TPU v7x, 32 devices: a whole 2x2x4 slice. The times are simulated.
32 devices in a mesh: group: 2 (over y), dom: 4 (over z), dp: 4 (over x, core).
Axes of the slice: x: 2, y: 2, z: 4, core: 2. Of those that a mesh axis runs over, the one named last changes fastest.
Arguments:
- node_latents: bfloat16 [8, 512, 512], P(('group', 'dp'), 'dom'), parts along dimension 0, may hold values from -6 to 6
- edge_latents: bfloat16 [8, 3072, 512], P(('group', 'dp'), 'dom'), parts along dimension 0, may hold values from -6 to 6
- agg_cotangent: bfloat16 [8, 512, 512], P(('group', 'dp'), 'dom'), parts along dimension 0, may hold values from -6 to 6
- weight_in: bfloat16 [1536, 512], replicated, may hold values from -0.15625 to 0.15625
- weight_out: bfloat16 [512, 512], replicated, may hold values from -0.25 to 0.25
- boundary: int32 [8, 4], P(('group', 'dom')), parts along dimension 0, may hold values from 0 to 1
- tile_src: int32 [96], P(('group', 'dom')), parts along dimension 0, may hold values from 0 to 5, as said below
- tile_dst: int32 [96], P(('group', 'dom')), parts along dimension 0, may hold values from 0 to 1
- edge_slot: int32 [96, 64], P(('group', 'dom')), parts along dimension 0, may hold values from 0 to 63
- tile_count: int32 [8], P(('group', 'dom')), parts along dimension 0, may hold values from 4 to 12, as said below
Outputs:
- aggregate: bfloat16 [8, 512, 512], P(('group', 'dp'), 'dom'), parts along dimension 0
- edge_grad: bfloat16 [8, 3072, 512], P(('group', 'dp'), 'dom'), parts along dimension 0
- node_grad: bfloat16 [8, 512, 512], P(('group', 'dp'), 'dom'), parts along dimension 0
- w_in_grad: float32 [3072, 512], P(('group', 'dp')), parts along dimension 0
- w_out_grad: float32 [1024, 512], P(('group', 'dp')), parts along dimension 0
There are 2 independent parts, one for each index of `group`. A program takes and returns all parts, laid end to end along the dimension named above; an argument that names none is the same for every part. Nothing has to cross between parts.
Inputs may be any that keep to these rules, and one draw needn't show every extreme that they name: `boundary`: block a partition sends to its partner at offset o_q, o = (1, -1, 2, -2), that is to partition d + o_q. `tile_src`: values below 2 name a block of the tile's own partition d; 2 + q names block boundary[d - o_q, q] of partition d - o_q, and only for partitions that exist. Tile j < 4 of a partition names 2 + j whenever partition d - o_j exists. The first tile_count[d] tiles of partition d are live; some partition has exactly 12 and some exactly 4.
All inputs are finite; a program needn't handle non-finite values.
Results may differ from a plain program's by a relative error of at most 0.0046.
Values may be sent and summed in bfloat16 or wider, within the bound.
No kernel may reach another device: no remote copies, remote signals or barrier semaphores. Data moves between devices by JAX's collectives and lax.ppermute only.
A program may use at most 64 MiB of HBM per device.

v0:
```python
import jax
import jax.numpy as jnp
from jax import lax
from jax.sharding import PartitionSpec as P

OFFSET_LIST = (1, -1, 2, -2)
EPSILON = 1e-05


def from_behind(array, axis, by):
    devices = lax.axis_size(axis)
    pairs = [(i, i + by) for i in range(devices) if 0 <= i + by < devices]
    return lax.ppermute(array, axis, pairs)


def pair_dot(left, right):
    return lax.dot_general(
        left, right, (((1,), (1,)), ((), ())), preferred_element_type=jnp.float32
    )


def outer_dot(left, right):
    return lax.dot_general(
        left, right, (((0,), (0,)), ((), ())), preferred_element_type=jnp.float32
    )


def send_blocks(outgoing):
    arrived = [from_behind(outgoing[which], "dom", OFFSET_LIST[which]) for which in range(4)]
    return jnp.stack(arrived)


def return_blocks(partial_grads):
    arrived = [
        from_behind(partial_grads[which].astype(jnp.bfloat16), "dom", -OFFSET_LIST[which]).astype(
            jnp.float32
        )
        for which in range(4)
    ]
    return jnp.stack(arrived)


def edge_pass(
    ext_nodes,
    edge_rows,
    cot_blocks,
    sources,
    targets,
    slot_table,
    live_tiles,
    weight_in,
    weight_out,
):
    tile_number = sources.shape[0]
    block_size = slot_table.shape[1]
    latent = edge_rows.shape[1]
    extent = ext_nodes.shape[0]
    owned_blocks = cot_blocks.shape[0]
    edge_total = tile_number * block_size
    pick_src = (sources[:, None] == jnp.arange(extent)[None, :]).astype(jnp.bfloat16)
    pick_dst = (targets[:, None] == jnp.arange(owned_blocks)[None, :]).astype(jnp.bfloat16)
    slot_hot = (slot_table[:, :, None] == jnp.arange(block_size)[None, None, :]).astype(
        jnp.bfloat16
    )
    src_blocks = jnp.einsum(
        "tb,bkl->tkl", pick_src, ext_nodes, preferred_element_type=jnp.float32
    ).astype(jnp.bfloat16)
    senders = jnp.einsum(
        "tks,tsl->tkl", slot_hot, src_blocks, preferred_element_type=jnp.float32
    ).astype(jnp.bfloat16)
    receivers = jnp.einsum(
        "tb,bkl->tkl", pick_dst, ext_nodes[:owned_blocks], preferred_element_type=jnp.float32
    ).astype(jnp.bfloat16)
    joined = jnp.concatenate(
        [edge_rows, senders.reshape(edge_total, latent), receivers.reshape(edge_total, latent)],
        axis=1,
    )
    preact = jnp.dot(joined, weight_in, preferred_element_type=jnp.float32)
    sigmoid_pre = jax.nn.sigmoid(preact)
    activated = (preact * sigmoid_pre).astype(jnp.bfloat16)
    projected = jnp.dot(activated, weight_out, preferred_element_type=jnp.float32)
    centered = projected - jnp.mean(projected, axis=1, keepdims=True)
    inv_scale = lax.rsqrt(jnp.mean(centered * centered, axis=1, keepdims=True) + EPSILON)
    message = centered * inv_scale
    row_live = jnp.repeat(live_tiles, block_size)[:, None]
    updated = (edge_rows.astype(jnp.float32) + message) * row_live
    hot_dst = pick_dst.astype(jnp.float32)
    aggregate = jnp.einsum(
        "tb,tkl->bkl",
        hot_dst,
        updated.reshape(tile_number, block_size, latent),
        precision=lax.Precision.HIGHEST,
    )
    upstream = (
        jnp.einsum("tb,bkl->tkl", pick_dst, cot_blocks, preferred_element_type=jnp.float32).reshape(
            edge_total, latent
        )
        * row_live
    )
    grad_project = inv_scale * (
        upstream
        - jnp.mean(upstream, axis=1, keepdims=True)
        - message * jnp.mean(upstream * message, axis=1, keepdims=True)
    )
    grad_project = grad_project.astype(jnp.bfloat16)
    grad_out = outer_dot(activated, grad_project)
    grad_act = pair_dot(grad_project, weight_out)
    grad_pre = (grad_act * sigmoid_pre * (1.0 + preact * (1.0 - sigmoid_pre))).astype(jnp.bfloat16)
    grad_in = outer_dot(joined, grad_pre)
    grad_edge = pair_dot(grad_pre, weight_in[:latent])
    grad_send = pair_dot(grad_pre, weight_in[latent : 2 * latent])
    grad_recv = pair_dot(grad_pre, weight_in[2 * latent :])
    edge_grad = (upstream + grad_edge).astype(jnp.bfloat16)
    slot_sums = jnp.einsum(
        "tks,tkl->tsl",
        slot_hot.astype(jnp.float32),
        grad_send.reshape(tile_number, block_size, latent),
        precision=lax.Precision.HIGHEST,
    )
    ext_grad = jnp.einsum(
        "tb,tsl->bsl", pick_src.astype(jnp.float32), slot_sums, precision=lax.Precision.HIGHEST
    )
    recv_grad = jnp.einsum(
        "tb,tkl->bkl",
        hot_dst,
        grad_recv.reshape(tile_number, block_size, latent),
        precision=lax.Precision.HIGHEST,
    )
    return (aggregate, edge_grad, ext_grad, recv_grad, grad_in, grad_out)


def body(
    node_latents,
    edge_latents,
    agg_cotangent,
    weight_in,
    weight_out,
    boundary,
    tile_src,
    tile_dst,
    edge_slot,
    tile_count,
):
    latent = node_latents.shape[2]
    block_size = edge_slot.shape[1]
    owned_blocks = node_latents.shape[1] // block_size
    tiles_here = tile_src.shape[0]
    node_blocks = node_latents[0].reshape(owned_blocks, block_size, latent)
    cot_blocks = agg_cotangent[0].reshape(owned_blocks, block_size, latent)
    chosen = boundary[0]
    outgoing = node_blocks[chosen]
    incoming = send_blocks(outgoing)
    ext_nodes = jnp.concatenate([node_blocks, incoming], axis=0)
    edge_rows = edge_latents[0]
    live_limit = tile_count[0]
    live_tiles = (jnp.arange(tiles_here) < live_limit).astype(jnp.float32)
    agg_sum, edge_grad, ext_grad, recv_grad, grad_in, grad_out = edge_pass(
        ext_nodes,
        edge_rows,
        cot_blocks,
        tile_src,
        tile_dst,
        edge_slot,
        live_tiles,
        weight_in,
        weight_out,
    )
    returned = return_blocks(ext_grad[owned_blocks:])
    node_grad = ext_grad[:owned_blocks] + recv_grad
    node_grad = node_grad.at[chosen].add(returned)
    dp_count = lax.axis_size("dp")
    dom_count = lax.axis_size("dom")
    in_rows = grad_in.shape[0] // dp_count
    stacked = jnp.concatenate(
        [grad_in.reshape(dp_count, -1, latent), grad_out.reshape(dp_count, -1, latent)], axis=1
    )
    arranged = (
        stacked.reshape(dp_count, dom_count, -1, latent).transpose(1, 0, 2, 3).reshape(-1, latent)
    )
    piece = lax.psum_scatter(arranged, ("dom", "dp"), scatter_dimension=0, tiled=True)
    mine = lax.all_gather(piece, "dom", axis=0, tiled=True)
    aggregate = agg_sum.reshape(1, owned_blocks * block_size, latent).astype(jnp.bfloat16)
    node_out = node_grad.reshape(1, owned_blocks * block_size, latent).astype(jnp.bfloat16)
    return (aggregate, edge_grad[None], node_out, mine[:in_rows], mine[in_rows:])


def solution(mesh):
    in_specs = (
        P(("group", "dp"), "dom", None),
        P(("group", "dp"), "dom", None),
        P(("group", "dp"), "dom", None),
        P(),
        P(),
        P(("group", "dom"), None),
        P(("group", "dom")),
        P(("group", "dom")),
        P(("group", "dom"), None),
        P(("group", "dom")),
    )
    out_specs = (
        P(("group", "dp"), "dom", None),
        P(("group", "dp"), "dom", None),
        P(("group", "dp"), "dom", None),
        P(("group", "dp"), None),
        P(("group", "dp"), None),
    )
    return jax.shard_map(body, mesh=mesh, in_specs=in_specs, out_specs=out_specs, check_vma=False)
```

profile of v0, /device:TPU:0, one launch (start us, length us, event | category | flops | bytes accessed | tf_op | source)
XLA Modules:
  0.0 164.0 jit_solution(14585928468454106703)
XLA Ops:
  8.0 1.5 gather_fusion
  9.5 1.3 collective-permute-start.3
  10.8 5.9 %collective-permute-start.2 = (bf16[64,512]{1,0:T(8,128)(2,1)S(1)}, bf16[64,512]{1,0:T(8,128)(2,1)S(1)}, u32[]{:S(2)}, u32[]{:S(2)}) collective-permute-start(bf16[64,512]{1,0:T(8,128)(2,1)S(1)} %get-tuple-element.13), channel_id=1, source_target_pairs={{0,8},{4,12},{1,9},{5,13},{2,10},{6,14},{3,11},{7,15},{16,24},{20,... | collective-permute-start | bytes 196616 | tf_op jit(solution)/shard_map/ppermute | solution.py:13
  16.7 1.3 collective-permute-start.1
  18.0 5.1 %collective-permute-start = (bf16[64,512]{1,0:T(8,128)(2,1)S(1)}, bf16[64,512]{1,0:T(8,128)(2,1)S(1)}, u32[]{:S(2)}, u32[]{:S(2)}) collective-permute-start(bf16[64,512]{1,0:T(8,128)(2,1)S(1)} %get-tuple-element.15), channel_id=1, source_target_pairs={{0,4},{4,8},{8,12},{1,5},{5,9},{9,13},{2,6},{6,10},{10,14},{3,7},{... | collective-permute-start | bytes 196616 | tf_op jit(solution)/shard_map/ppermute | solution.py:13
  23.8 1.5 convolution_convert_fusion
  25.3 1.9 %multiply_reduce_fusion = (f32[12,64]{0,1:T(8,128)S(1)}, f32[12,64,512]{2,0,1:T(8,128)}) fusion(f32[12]{0:T(128)S(1)} %compare_convert_fusion, bf16[2,64,512]{2,1,0:T(8,128)(2,1)S(1)} %bitcast.105, s32[12]{0:T(128)S(1)} %copy-done.9), kind=kOutput, calls=%fused_computation.10 | convolution fusion | flops 2358552 | bytes 1707104 | tf_op jit(solution)/shard_map/tb,bkl->tkl/dot_general | solution.py:95
  28.1 2.5 %copy.128 = f32[12,64,512]{2,1,0:T(8,128)S(1)} copy(f32[12,64,512]{2,0,1:T(8,128)} %get-tuple-element.21) | data formatting | bytes 3145728 | tf_op jit(solution)/shard_map/tb,bkl->tkl/dot_general | solution.py:95
  33.6 2.4 %concatenate.9 = bf16[6,64,512]{2,0,1:T(8,128)(2,1)S(1)} concatenate(bf16[2,64,512]{2,0,1:T(2,128)(2,1)S(1)} %copy.116, bf16[1,64,512]{2,0,1:T(2,128)(2,1)} %copy.117, bf16[1,64,512]{2,0,1:T(2,128)(2,1)} %copy.118, bf16[1,64,512]{2,0,1:T(2,128)(2,1)} %copy.119, bf16[1,64,512]{2,0,1:T(2,128)(2,1)} %copy.120), dimensions={0} | concatenate | bytes 786432 | tf_op jit(solution)/shard_map/concatenate | solution.py:153
  36.0 1.3 convolution_convert_fusion.1
  37.4 1.1 convolution_convert_fusion.2
  38.5 1.6 multiply_convert_fusion.2
  41.6 2.1 %multiply_convert_fusion.1 = (bf16[768,512]{1,0:T(8,128)(2,1)S(1)}, f32[768,512]{1,0:T(8,128)}, f32[768,512]{1,0:T(8,128)}) fusion(f32[12,64,512]{2,1,0:T(8,128)S(1)} %copy.128, f32[768,512]{1,0:T(8,128)S(1)} %get-tuple-element.19, f32[768]{0:T(1024)S(1)} %broadcast_multiply_fusion.1, f32[768]{0:T(1024)S(1)} %div.21, f32[768]{0:T(1024)S(1)} %mul.65, ...), kind=kLoop, calls=%fused_computation.14 | loop fusion | flops 4325376 | bytes 7879680 | tf_op jit(solution)/shard_map/convert_element_type | solution.py:105
  44.3 0.9 multiply_convert_fusion
  45.2 1.4 fusion.13
  47.1 2.4 %copy.133 = f32[4,4,128,512]{3,2,0,1:T(8,128)} copy(f32[4,4,128,512]{3,2,1,0:T(8,128)S(1)} %bitcast.90) | data formatting | bytes 8388608 | tf_op jit(solution)/shard_map/reshape | solution.py:178
  49.8 1.6 %fusion.18 = f32[768,512]{1,0:T(8,128)S(1)} fusion(bf16[768,512]{1,0:T(8,128)(2,1)S(1)} %multiply_convert_fusion, bf16[1536,512]{1,0:T(8,128)(2,1)} %param.13), kind=kOutput, calls=%fused_computation.32 | convolution fusion | flops 402653184 | bytes 2883584 | tf_op jit(solution)/shard_map/dot_general | solution.py:17
  51.4 0.9 fusion.21
  52.4 69.4 %reduce-scatter.2.cloned.1.call-done = f32[128,512]{1,0:T(8,128)} async-done(((f32[2048,512]{1,0:T(8,128)}), f32[128,512]{1,0:T(8,128)}) %reduce-scatter.2.cloned.1.call-update) | async-done | bytes 262160 | tf_op jit(solution)/shard_map/reduce_scatter | solution.py:180
  121.8 1.7 %fusion.45 = (bf16[6,64,512]{2,0,1:T(8,128)(2,1)S(1)}, f32[6,64,512]{2,0,1:T(8,128)S(1)}) fusion(f32[12,64,512]{2,1,0:T(8,128)S(1)} %fusion.21, s32[12]{0:T(128)S(1)} %copy-done.13), kind=kOutput, calls=%fused_computation.76 | convolution fusion | flops 28508232 | bytes 2752560 | tf_op jit(solution)/shard_map/tb,tsl->bsl/dot_general | solution.py:120
  124.1 2.8 %collective-permute-start.5 = (bf16[64,512]{1,0:T(8,128)(2,1)S(1)}, bf16[64,512]{1,0:T(8,128)(2,1)S(1)}, u32[]{:S(2)}, u32[]{:S(2)}) collective-permute-start(bf16[64,512]{1,0:T(8,128)(2,1)S(1)} %bitcast.119), channel_id=1, source_target_pairs={{0,4},{4,8},{8,12},{1,5},{5,9},{9,13},{2,6},{6,10},{10,14},{3,7},{... | collective-permute-start | bytes 196616 | tf_op jit(solution)/shard_map/ppermute | solution.py:13
  127.0 1.3 collective-permute-start.6
  128.3 5.4 %collective-permute-start.7 = (bf16[64,512]{1,0:T(8,128)(2,1)S(1)}, bf16[64,512]{1,0:T(8,128)(2,1)S(1)}, u32[]{:S(2)}, u32[]{:S(2)}) collective-permute-start(bf16[64,512]{1,0:T(8,128)(2,1)S(1)} %bitcast.111), channel_id=1, source_target_pairs={{0,8},{4,12},{1,9},{5,13},{2,10},{6,14},{3,11},{7,15},{16,24},{20,... | collective-permute-start | bytes 196616 | tf_op jit(solution)/shard_map/ppermute | solution.py:13
  133.7 1.3 collective-permute-start.4
  135.1 1.7 %fusion.10 = bf16[2,64,512]{2,0,1:T(2,128)(2,1)S(1)} fusion(f32[12,64,512]{2,1,0:T(8,128)S(1)} %bitcast.91, s32[12]{0:T(128)S(1)} %copy-done.10), kind=kOutput, calls=%fused_computation.26 | convolution fusion | flops 9502744 | bytes 1703984 | tf_op jit(solution)/shard_map/tb,tkl->bkl/dot_general | solution.py:88
  137.4 1.7 %fusion.7 = f32[2,64,512]{2,0,1:T(2,128)S(1)} fusion(f32[12,64,512]{2,1,0:T(8,128)S(1)} %bitcast.92, f32[6,64,512]{2,0,1:T(8,128)S(1)} %get-tuple-element.23, s32[12]{0:T(128)S(1)} %copy-done.10), kind=kOutput, calls=%fused_computation.25 | convolution fusion | flops 9502744 | bytes 2097200 | tf_op jit(solution)/shard_map/tb,tkl->bkl/dot_general | solution.py:123
  139.1 1.5 fusion.6
  141.3 1.4 collective-permute-done.4
  142.8 0.9 scatter_fusion
  144.4 9.0 %all-gather.2.cloned.1.call-done = f32[512,512]{1,0:T(8,128)} async-done(((f32[128,512]{1,0:T(8,128)}), f32[512,512]{1,0:T(8,128)}) %all-gather.2.cloned.1.call-update) | async-done | bytes 1048592 | tf_op jit(solution)/shard_map/all_gather | solution.py:181
  153.4 1.7 %slice.77 = f32[128,512]{1,0:T(8,128)} slice(f32[512,512]{1,0:T(8,128)} %all-gather.2.cloned.1.call-done), slice={[384:512], [0:512]} | slice | bytes 524288 | tf_op jit(solution)/shard_map/slice | solution.py:184
  155.0 2.1 %slice.76 = f32[384,512]{1,0:T(8,128)} slice(f32[512,512]{1,0:T(8,128)} %all-gather.2.cloned.1.call-done), slice={[0:384], [0:512]} | slice | bytes 1572864 | tf_op jit(solution)/shard_map/slice | solution.py:184
  (72 shorter events, 10.2 us)
Async XLA Ops:
  7.2 32.9 %copy-start = (bf16[512,512]{1,0:T(8,128)(2,1)S(1)}, bf16[512,512]{1,0:T(8,128)(2,1)}, u32[]{:S(2)}) copy-start(bf16[512,512]{1,0:T(8,128)(2,1)} %param.14) | copy-start | bytes 1572868
  7.2 18.1 %copy-start.9 = (s32[12]{0:T(128)S(1)}, s32[12]{0:T(128)}, u32[]{:S(2)}) copy-start(s32[12]{0:T(128)} %param.17) | copy-start | bytes 148
  7.2 18.1 %copy-start.7 = (bf16[1,128,512]{2,1,0:T(8,128)(2,1)S(1)}, bf16[1,128,512]{2,1,0:T(8,128)(2,1)}, u32[]{:S(2)}) copy-start(bf16[1,128,512]{2,1,0:T(8,128)(2,1)} %param.12) | copy-start | bytes 393220
  7.2 114.6 %reduce-scatter.2.cloned.1.call-start = ((), (), s32[]{:S(2)}) async-start(), calls=%async_computation.1 | async-start | bytes 4456448 | tf_op jit(solution)/shard_map/reduce_scatter | solution.py:180
  8.0 15.8 %copy-start.11 = (s32[4]{0:T(128)}, s32[4]{0:T(128)S(1)}, u32[]{:S(2)}) copy-start(s32[4]{0:T(128)S(1)} %fusion.35) | copy-start | bytes 52
  9.5 21.1 %collective-permute-start.3 = (bf16[64,512]{1,0:T(8,128)(2,1)S(1)}, bf16[64,512]{1,0:T(8,128)(2,1)S(1)}, u32[]{:S(2)}, u32[]{:S(2)}) collective-permute-start(bf16[64,512]{1,0:T(8,128)(2,1)S(1)} %get-tuple-element.12), channel_id=1, source_target_pairs={{8,0},{12,4},{9,1},{13,5},{10,2},{14,6},{11,3},{15,7},{24,16},{28,... | collective-permute-start | bytes 196616 | tf_op jit(solution)/shard_map/ppermute | solution.py:13
  10.8 20.6 %collective-permute-start.2 = (bf16[64,512]{1,0:T(8,128)(2,1)S(1)}, bf16[64,512]{1,0:T(8,128)(2,1)S(1)}, u32[]{:S(2)}, u32[]{:S(2)}) collective-permute-start(bf16[64,512]{1,0:T(8,128)(2,1)S(1)} %get-tuple-element.13), channel_id=1, source_target_pairs={{0,8},{4,12},{1,9},{5,13},{2,10},{6,14},{3,11},{7,15},{16,24},{20,... | collective-permute-start | bytes 196616 | tf_op jit(solution)/shard_map/ppermute | solution.py:13
  16.7 15.4 %collective-permute-start.1 = (bf16[64,512]{1,0:T(8,128)(2,1)S(1)}, bf16[64,512]{1,0:T(8,128)(2,1)S(1)}, u32[]{:S(2)}, u32[]{:S(2)}) collective-permute-start(bf16[64,512]{1,0:T(8,128)(2,1)S(1)} %get-tuple-element.14), channel_id=1, source_target_pairs={{4,0},{8,4},{12,8},{5,1},{9,5},{13,9},{6,2},{10,6},{14,10},{7,3},{... | collective-permute-start | bytes 196616 | tf_op jit(solution)/shard_map/ppermute | solution.py:13
  18.0 14.8 %collective-permute-start = (bf16[64,512]{1,0:T(8,128)(2,1)S(1)}, bf16[64,512]{1,0:T(8,128)(2,1)S(1)}, u32[]{:S(2)}, u32[]{:S(2)}) collective-permute-start(bf16[64,512]{1,0:T(8,128)(2,1)S(1)} %get-tuple-element.15), channel_id=1, source_target_pairs={{0,4},{4,8},{8,12},{1,5},{5,9},{9,13},{2,6},{6,10},{10,14},{3,7},{... | collective-permute-start | bytes 196616 | tf_op jit(solution)/shard_map/ppermute | solution.py:13
  23.8 3.5 %copy-start.3 = (bf16[1,128,512]{2,1,0:T(8,128)(2,1)S(1)}, bf16[1,128,512]{2,1,0:T(8,128)(2,1)}, u32[]{:S(2)}) copy-start(bf16[1,128,512]{2,1,0:T(8,128)(2,1)} %param.10) | copy-start | bytes 393220
  32.1 5.2 %copy-start.8 = (s32[12,64]{1,0:T(8,128)S(1)}, s32[12,64]{1,0:T(8,128)}, u32[]{:S(2)}) copy-start(s32[12,64]{1,0:T(8,128)} %param.18) | copy-start | bytes 9220
  36.0 2.4 %copy-start.4 = (bf16[1536,512]{1,0:T(8,128)(2,1)S(1)}, bf16[1536,512]{1,0:T(8,128)(2,1)}, u32[]{:S(2)}) copy-start(bf16[1536,512]{1,0:T(8,128)(2,1)} %param.13) | copy-start | bytes 4718596
  36.0 2.4 %copy-start.6 = (bf16[1,768,512]{2,1,0:T(8,128)(2,1)S(1)}, bf16[1,768,512]{2,1,0:T(8,128)(2,1)}, u32[]{:S(2)}) copy-start(bf16[1,768,512]{2,1,0:T(8,128)(2,1)} %param.11) | copy-start | bytes 2359300
  49.5 103.8 %all-gather.2.cloned.1.call-start = ((), (), s32[]{:S(2)}) async-start(), calls=%async_computation.2 | async-start | bytes 1310720 | tf_op jit(solution)/shard_map/all_gather | solution.py:181
  51.4 70.4 %copy-start.13 = (s32[12]{0:T(128)S(1)}, s32[12]{0:T(128)}, u32[]{:S(2)}) copy-start(s32[12]{0:T(128)} %param.16) | copy-start | bytes 148
  123.5 11.5 %copy-start.1 = (f32[768,512]{1,0:T(8,128)S(1)}, f32[768,512]{1,0:T(8,128)}, u32[]{:S(2)}) copy-start(f32[768,512]{1,0:T(8,128)} %get-tuple-element.6) | copy-start | bytes 4718596
  123.5 11.5 %copy-start.10 = (s32[12]{0:T(128)S(1)}, s32[12]{0:T(128)}, u32[]{:S(2)}) copy-start(s32[12]{0:T(128)} %param.17) | copy-start | bytes 148
  124.0 12.7 %copy-start.5 = (bf16[1536,512]{1,0:T(8,128)(2,1)S(1)}, bf16[1536,512]{1,0:T(8,128)(2,1)}, u32[]{:S(2)}) copy-start(bf16[1536,512]{1,0:T(8,128)(2,1)} %param.13) | copy-start | bytes 4718596
  124.1 17.2 %collective-permute-start.5 = (bf16[64,512]{1,0:T(8,128)(2,1)S(1)}, bf16[64,512]{1,0:T(8,128)(2,1)S(1)}, u32[]{:S(2)}, u32[]{:S(2)}) collective-permute-start(bf16[64,512]{1,0:T(8,128)(2,1)S(1)} %bitcast.119), channel_id=1, source_target_pairs={{0,4},{4,8},{8,12},{1,5},{5,9},{9,13},{2,6},{6,10},{10,14},{3,7},{... | collective-permute-start | bytes 196616 | tf_op jit(solution)/shard_map/ppermute | solution.py:13
  127.0 14.3 %collective-permute-start.6 = (bf16[64,512]{1,0:T(8,128)(2,1)S(1)}, bf16[64,512]{1,0:T(8,128)(2,1)S(1)}, u32[]{:S(2)}, u32[]{:S(2)}) collective-permute-start(bf16[64,512]{1,0:T(8,128)(2,1)S(1)} %bitcast.116), channel_id=1, source_target_pairs={{8,0},{12,4},{9,1},{13,5},{10,2},{14,6},{11,3},{15,7},{24,16},{28,... | collective-permute-start | bytes 196616 | tf_op jit(solution)/shard_map/ppermute | solution.py:13
  128.3 13.0 %collective-permute-start.7 = (bf16[64,512]{1,0:T(8,128)(2,1)S(1)}, bf16[64,512]{1,0:T(8,128)(2,1)S(1)}, u32[]{:S(2)}, u32[]{:S(2)}) collective-permute-start(bf16[64,512]{1,0:T(8,128)(2,1)S(1)} %bitcast.111), channel_id=1, source_target_pairs={{0,8},{4,12},{1,9},{5,13},{2,10},{6,14},{3,11},{7,15},{16,24},{20,... | collective-permute-start | bytes 196616 | tf_op jit(solution)/shard_map/ppermute | solution.py:13
  133.7 9.0 %collective-permute-start.4 = (bf16[64,512]{1,0:T(8,128)(2,1)S(1)}, bf16[64,512]{1,0:T(8,128)(2,1)S(1)}, u32[]{:S(2)}, u32[]{:S(2)}) collective-permute-start(bf16[64,512]{1,0:T(8,128)(2,1)S(1)} %bitcast.108), channel_id=1, source_target_pairs={{4,0},{8,4},{12,8},{5,1},{9,5},{13,9},{6,2},{10,6},{14,10},{7,3},{... | collective-permute-start | bytes 196616 | tf_op jit(solution)/shard_map/ppermute | solution.py:13
  137.4 1.7 %copy-start.2 = (f32[768,512]{1,0:T(8,128)S(1)}, f32[768,512]{1,0:T(8,128)}, u32[]{:S(2)}) copy-start(f32[768,512]{1,0:T(8,128)} %get-tuple-element.7) | copy-start | bytes 4718596
  140.6 2.2 %copy-start.12 = (s32[4]{0:T(128)S(1)}, s32[4]{0:T(128)}, u32[]{:S(2)}) copy-start(s32[4]{0:T(128)} %copy-done.11) | copy-start | bytes 52
Sparse Core Ops, SparseCore 0:
  49.7 72.0 reduce-scatter.1
  123.5 29.8 all-gather.1
where the time goes:
time: 165 us; the launch traced here: 164 us
  waiting for transfers between devices  79.9 us (48%)
  starting transfers between devices  24.7 us (15%)
  matrix products  20.7 us (13%)
  local copies, waits for them, and re-layouts  17.7 us (11%)
  between operations  15.2 us (9%)
  other arithmetic  5.72 us (3%)
    reduce_scatter x1, waiting for transfers between devices, body(): lax.psum_scatter(arranged, ('dom', 'dp'), scatter_dimension=0, tiled=True)  69.4 us
    ppermute x8, starting transfers between devices, from_behind(): return lax.ppermute(array, axis, pairs)  24.5 us
    all_gather x1, waiting for transfers between devices, body(): mine = lax.all_gather(piece, 'dom', axis=0, tiled=True)  9 us
    dot_general x4, matrix products, pair_dot(): lax.dot_general(left, right, (((1,), (1,)), ((), ())), preferred_element_...  4.68 us
  transfers between devices with their start and end apart: 10, of which 3 were waited for; matrix products, arithmetic and copies ran while one was open for 13% of the time, Pallas kernels for 0%

commit v1 on v0

--- a/solution.py
+++ b/solution.py
@@ -127,6 +127,46 @@
         precision=lax.Precision.HIGHEST,
     )
     return (aggregate, edge_grad, ext_grad, recv_grad, grad_in, grad_out)
+
+
+def halve_over_dp(stacked):
+    devices = lax.axis_size("dp")
+    if devices & (devices - 1):
+        return lax.psum_scatter(stacked, "dp", scatter_dimension=0, tiled=True)[0]
+    index = lax.axis_index("dp")
+    bit = 1
+    while bit < devices:
+        pairs = [(i, i ^ bit) for i in range(devices)]
+        mine = (index // bit) % 2
+        split = stacked.reshape((-1, 2) + stacked.shape[1:])
+        away = lax.dynamic_index_in_dim(split, 1 - mine, 1, keepdims=False).astype(jnp.bfloat16)
+        kept = lax.dynamic_index_in_dim(split, mine, 1, keepdims=False)
+        stacked = kept + lax.ppermute(away, "dp", pairs).astype(jnp.float32)
+        bit *= 2
+    return stacked[0]
+
+
+def sum_over_dom(rows):
+    devices = lax.axis_size("dom")
+    if devices > 4:
+        piece = lax.psum_scatter(rows, "dom", scatter_dimension=0, tiled=True)
+        return lax.all_gather(piece, "dom", axis=0, tiled=True)
+    index = lax.axis_index("dom")
+    pieces = rows.reshape((devices, -1) + rows.shape[1:])
+    narrow = pieces.astype(jnp.bfloat16)
+    total = lax.dynamic_index_in_dim(pieces, index, 0, keepdims=False)
+    for shift in range(1, devices):
+        pairs = [(i, (i + shift) % devices) for i in range(devices)]
+        away = lax.dynamic_index_in_dim(narrow, (index + shift) % devices, 0, keepdims=False)
+        total = total + lax.ppermute(away, "dom", pairs).astype(jnp.float32)
+    total = total.astype(jnp.bfloat16)
+    whole = jnp.zeros(pieces.shape, jnp.float32)
+    whole = lax.dynamic_update_index_in_dim(whole, total.astype(jnp.float32), index, 0)
+    for shift in range(1, devices):
+        pairs = [(i, (i + shift) % devices) for i in range(devices)]
+        came = lax.ppermute(total, "dom", pairs).astype(jnp.float32)
+        whole = lax.dynamic_update_index_in_dim(whole, came, (index - shift) % devices, 0)
+    return whole.reshape(rows.shape)
 
 
 def body(
@@ -169,16 +209,11 @@
     node_grad = ext_grad[:owned_blocks] + recv_grad
     node_grad = node_grad.at[chosen].add(returned)
     dp_count = lax.axis_size("dp")
-    dom_count = lax.axis_size("dom")
-    in_rows = grad_in.shape[0] // dp_count
     stacked = jnp.concatenate(
         [grad_in.reshape(dp_count, -1, latent), grad_out.reshape(dp_count, -1, latent)], axis=1
     )
-    arranged = (
-        stacked.reshape(dp_count, dom_count, -1, latent).transpose(1, 0, 2, 3).reshape(-1, latent)
-    )
-    piece = lax.psum_scatter(arranged, ("dom", "dp"), scatter_dimension=0, tiled=True)
-    mine = lax.all_gather(piece, "dom", axis=0, tiled=True)
+    in_rows = grad_in.shape[0] // dp_count
+    mine = sum_over_dom(halve_over_dp(stacked))
     aggregate = agg_sum.reshape(1, owned_blocks * block_size, latent).astype(jnp.bfloat16)
     node_out = node_grad.reshape(1, owned_blocks * block_size, latent).astype(jnp.bfloat16)
     return (aggregate, edge_grad[None], node_out, mine[:in_rows], mine[in_rows:])

time: 165 us -> 90.6 us (0.55)
  waiting for transfers between devices: 79.9 us -> 16.8 us
  between operations: 15.2 us -> 2.05 us
  starting transfers between devices: 24.7 us -> 35.5 us
  local copies, waits for them, and re-layouts: 17.7 us -> 11.1 us
    reduce_scatter x1 -> x0, waiting for transfers between devices: 69.4 us -> none  [body(): lax.psum_scatter(arranged, ('dom', 'dp'), scatter_dimension=0, tiled=True)]
    ppermute x0 -> x8, waiting for transfers between devices: none -> 16.8 us  [the longest x2 9.43 us: halve_over_dp(): stacked = kept + lax.ppermute(away, 'dp', pairs).astype(jnp.float32)]
    ppermute x0 -> x8, starting transfers between devices: none -> 12.7 us  [the longest x3 5.61 us: sum_over_dom(): total = total + lax.ppermute(away, 'dom', pairs).astype(jnp.float32)]
    all_gather x1 -> x0, waiting for transfers between devices: 9 us -> none  [body(): mine = lax.all_gather(piece, 'dom', axis=0, tiled=True)]
    another operation x4, local copies, waits for them, and re-layouts: 3.03 us -> 0.41 us  [send_blocks(): return jnp.stack(arrived)]
    reshape x1 -> x0, local copies, waits for them, and re-layouts: 2.4 us -> none  [body(): stacked.reshape(dp_count, dom_count, -1, latent).transpose(1, 0, 2, 3)]
  transfers between devices with their start and end apart: 10 -> 16, of which waited for: 3 -> 3; matrix products, arithmetic and copies ran while one was open for 13% -> 22% of each run, Pallas kernels for 0% -> 0%
where the time goes in v1:
time: 90.6 us; the launch traced here: 90.2 us
  starting transfers between devices  35.5 us (39%)
  matrix products  19.6 us (22%)
  waiting for transfers between devices  16.8 us (19%)
  local copies, waits for them, and re-layouts  11.1 us (12%)
  other arithmetic  5.12 us (6%)
  between operations  2.05 us (2%)
    ppermute x8, starting transfers between devices, from_behind(): return lax.ppermute(array, axis, pairs)  22.8 us
    ppermute x2, waiting for transfers between devices, halve_over_dp(): stacked = kept + lax.ppermute(away, 'dp', pairs).astype(jnp.float32)  9.43 us
    ppermute x3, starting transfers between devices, sum_over_dom(): total = total + lax.ppermute(away, 'dom', pairs).astype(jnp.float32)  5.61 us
    ppermute x3, starting transfers between devices, sum_over_dom(): came = lax.ppermute(total, 'dom', pairs).astype(jnp.float32)  5.44 us
    ppermute x3, waiting for transfers between devices, sum_over_dom(): came = lax.ppermute(total, 'dom', pairs).astype(jnp.float32)  5.06 us
    dot_general x4, matrix products, pair_dot(): lax.dot_general(left, right, (((1,), (1,)), ((), ())), preferred_element_...  3.62 us
    dot_general x1, local copies, waits for them, and re-layouts, edge_pass(): jnp.einsum('tb,bkl->tkl', pick_dst, cot_blocks, preferred_element_type=jn...  2.51 us
    ppermute x3, waiting for transfers between devices, sum_over_dom(): total = total + lax.ppermute(away, 'dom', pairs).astype(jnp.float32)  2.32 us
  transfers between devices with their start and end apart: 16, of which 3 were waited for; matrix products, arithmetic and copies ran while one was open for 22% of the time, Pallas kernels for 0%

profile of v1, /device:TPU:0, one launch (start us, length us, event | category | flops | bytes accessed | tf_op | source)
XLA Modules:
  0.0 90.2 jit_solution(13751784435164588520)
XLA Ops:
  1.4 1.5 %gather_fusion = bf16[4,64,512]{2,1,0:T(8,128)(2,1)S(1)} fusion(bf16[2,64,512]{2,1,0:T(8,128)(2,1)} %bitcast.131, s32[1024]{0:T(1024)S(1)} %pad_clamp_fusion), kind=kCustom, calls=%fused_computation | custom fusion | bytes 524304 | tf_op jit(solution)/shard_map/gather | solution.py:191
  3.6 4.9 %collective-permute-start = (bf16[64,512]{1,0:T(8,128)(2,1)}, bf16[64,512]{1,0:T(8,128)(2,1)S(1)}, u32[]{:S(2)}, u32[]{:S(2)}) collective-permute-start(bf16[64,512]{1,0:T(8,128)(2,1)} %get-tuple-element.20), channel_id=1, source_target_pairs={{0,4},{4,8},{8,12},{1,5},{5,9},{9,13},{2,6},{6,10},{10,14},{3,7},{... | collective-permute-start | bytes 196616 | tf_op jit(solution)/shard_map/ppermute | solution.py:13
  8.5 1.3 %collective-permute-start.1 = (bf16[64,512]{1,0:T(8,128)(2,1)}, bf16[64,512]{1,0:T(8,128)(2,1)S(1)}, u32[]{:S(2)}, u32[]{:S(2)}) collective-permute-start(bf16[64,512]{1,0:T(8,128)(2,1)} %get-tuple-element.19), channel_id=1, source_target_pairs={{4,0},{8,4},{12,8},{5,1},{9,5},{13,9},{6,2},{10,6},{14,10},{7,3},{... | collective-permute-start | bytes 196616 | tf_op jit(solution)/shard_map/ppermute | solution.py:13
  9.8 5.6 %collective-permute-start.2 = (bf16[64,512]{1,0:T(8,128)(2,1)}, bf16[64,512]{1,0:T(8,128)(2,1)S(1)}, u32[]{:S(2)}, u32[]{:S(2)}) collective-permute-start(bf16[64,512]{1,0:T(8,128)(2,1)} %get-tuple-element.18), channel_id=1, source_target_pairs={{0,8},{4,12},{1,9},{5,13},{2,10},{6,14},{3,11},{7,15},{16,24},{20,... | collective-permute-start | bytes 196616 | tf_op jit(solution)/shard_map/ppermute | solution.py:13
  15.4 1.3 %collective-permute-start.3 = (bf16[64,512]{1,0:T(8,128)(2,1)}, bf16[64,512]{1,0:T(8,128)(2,1)S(1)}, u32[]{:S(2)}, u32[]{:S(2)}) collective-permute-start(bf16[64,512]{1,0:T(8,128)(2,1)} %get-tuple-element.17), channel_id=1, source_target_pairs={{8,0},{12,4},{9,1},{13,5},{10,2},{14,6},{11,3},{15,7},{24,16},{28,... | collective-permute-start | bytes 196616 | tf_op jit(solution)/shard_map/ppermute | solution.py:13
  17.3 1.5 %convolution_convert_fusion = bf16[12,64,512]{2,0,1:T(8,128)(2,1)S(1)} fusion(s32[12]{0:T(128)} %param.17, bf16[2,64,512]{2,1,0:T(8,128)(2,1)} %bitcast.132), kind=kOutput, calls=%fused_computation.28 | convolution fusion | flops 1966104 | bytes 917552 | tf_op jit(solution)/shard_map/tb,bkl->tkl/dot_general | solution.py:71
  18.9 1.9 %multiply_reduce_fusion = (f32[12,64]{0,1:T(8,128)S(1)}, f32[12,64,512]{2,0,1:T(8,128)}) fusion(f32[12]{0:T(128)S(1)} %compare_convert_fusion, bf16[2,64,512]{2,1,0:T(8,128)(2,1)S(1)} %bitcast.141, s32[12]{0:T(128)S(1)} %copy-done.7), kind=kOutput, calls=%fused_computation.18 | convolution fusion | flops 2358552 | bytes 1707104 | tf_op jit(solution)/shard_map/tb,bkl->tkl/dot_general | solution.py:95
  21.1 2.5 %copy.121 = f32[12,64,512]{2,1,0:T(8,128)S(1)} copy(f32[12,64,512]{2,0,1:T(8,128)} %get-tuple-element.26) | data formatting | bytes 3145728 | tf_op jit(solution)/shard_map/tb,bkl->tkl/dot_general | solution.py:95
  23.6 1.3 %copy.117 = bf16[12,64,512]{2,1,0:T(8,128)(2,1)} copy(bf16[12,64,512]{2,0,1:T(8,128)(2,1)S(1)} %convolution_convert_fusion) | data formatting | bytes 1572864 | tf_op jit(solution)/shard_map/convert_element_type | solution.py:73
  25.6 1.0 %concatenate.14 = bf16[6,64,512]{2,0,1:T(8,128)(2,1)S(1)} concatenate(bf16[2,64,512]{2,0,1:T(2,128)(2,1)S(1)} %copy.109, bf16[1,64,512]{2,0,1:T(2,128)(2,1)S(1)} %copy.110, bf16[1,64,512]{2,0,1:T(2,128)(2,1)S(1)} %copy.111, bf16[1,64,512]{2,0,1:T(2,128)(2,1)S(1)} %copy.112, bf16[1,64,512]{2,0,1:T(2,128)(2,1)S(1)} %copy.113), dimensions={0} | concatenate | bytes 786432 | tf_op jit(solution)/shard_map/concatenate | solution.py:193
  26.7 1.3 %convolution_convert_fusion.1 = bf16[12,64,512]{2,0,1:T(8,128)(2,1)S(1)} fusion(bf16[6,64,512]{2,0,1:T(8,128)(2,1)S(1)} %concatenate.14, s32[12]{0:T(128)} %param.16), kind=kOutput, calls=%fused_computation.29 | convolution fusion | flops 5111880 | bytes 1179696 | tf_op jit(solution)/shard_map/tb,bkl->tkl/dot_general | solution.py:65
  28.1 1.1 %convolution_convert_fusion.2 = bf16[12,64,512]{2,1,0:T(8,128)(2,1)S(1)} fusion(bf16[12,64,512]{2,0,1:T(8,128)(2,1)S(1)} %convolution_convert_fusion.1, s32[12,64]{1,0:T(8,128)S(1)} %copy-done.6), kind=kOutput, calls=%fused_computation.31 | convolution fusion | flops 50774016 | bytes 1575936 | tf_op jit(solution)/shard_map/tks,tsl->tkl/dot_general | solution.py:68
  29.2 1.6 %multiply_convert_fusion.2 = (bf16[768,512]{1,0:T(8,128)(2,1)S(1)}, f32[768,512]{1,0:T(8,128)S(1)}) fusion(bf16[1536,512]{1,0:T(8,128)(2,1)S(1)} %copy-done.2, bf16[768,512]{1,0:T(8,128)(2,1)S(1)} %bitcast.136, bf16[768,512]{1,0:T(8,128)(2,1)S(1)} %bitcast.138, bf16[768,512]{1,0:T(8,128)(2,1)S(1)} %bitcast.134), kind=kOutput, calls=%fused_computation.26 | convolution fusion | flops 1217003520 | bytes 6291456 | tf_op jit(solution)/shard_map/dot_general | solution.py:78
  32.3 1.0 %multiply_convert_fusion.1 = (bf16[768,512]{1,0:T(8,128)(2,1)S(1)}, f32[768,512]{1,0:T(8,128)S(1)}, f32[768,512]{1,0:T(8,128)S(1)}) fusion(f32[12,64,512]{2,1,0:T(8,128)S(1)} %copy.121, f32[768,512]{1,0:T(8,128)S(1)} %get-tuple-element.24, f32[768]{0:T(1024)S(1)} %broadcast_multiply_fusion.1, f32[768]{0:T(1024)S(1)} %div.30, f32[768]{0:T(1024)S(1)} %mul.65, ...), kind=kLoop, calls=%fused_computation.22 | loop fusion | flops 4325376 | bytes 7879680 | tf_op jit(solution)/shard_map/convert_element_type | solution.py:105
  34.9 1.4 %fusion.19 = f32[1536,512]{1,0:T(8,128)S(1)} fusion(bf16[768,512]{1,0:T(8,128)(2,1)S(1)} %multiply_convert_fusion, bf16[768,512]{1,0:T(8,128)(2,1)S(1)} %bitcast.137, bf16[768,512]{1,0:T(8,128)(2,1)S(1)} %bitcast.139, bf16[768,512]{1,0:T(8,128)(2,1)S(1)} %bitcast.135), kind=kOutput, calls=%fused_computation.38 | convolution fusion | flops 1215037440 | bytes 6291456 | tf_op jit(solution)/shard_map/dot_general | solution.py:23
  38.7 1.7 %fusion.55 = (bf16[6,64,512]{2,0,1:T(8,128)(2,1)S(1)}, f32[6,64,512]{2,0,1:T(8,128)S(1)}) fusion(f32[12,64,512]{2,1,0:T(8,128)S(1)} %fusion.27, s32[12]{0:T(128)S(1)} %copy-done.11), kind=kOutput, calls=%fused_computation.99 | convolution fusion | flops 28508232 | bytes 2752560 | tf_op jit(solution)/shard_map/tb,tsl->bsl/dot_general | solution.py:120
  40.9 1.6 %collective-permute-start.9 = (bf16[1,512,512]{2,1,0:T(8,128)(2,1)S(1)}, bf16[1,512,512]{2,1,0:T(8,128)(2,1)S(1)}, u32[]{:S(2)}, u32[]{:S(2)}) collective-permute-start(bf16[1,512,512]{2,1,0:T(8,128)(2,1)S(1)} %dynamic-slice_convert_fusion), channel_id=1, source_target_pairs={{0,2},{1,3},{2,0},{3,1},{4,6},{5,7},{6,4},{7,5},{8,10},{9,11},{10,... | collective-permute-start | bytes 1572872 | tf_op jit(solution)/shard_map/ppermute | solution.py:144
  42.5 1.7 %fusion.15 = bf16[2,64,512]{2,0,1:T(2,128)(2,1)S(1)} fusion(f32[12,64,512]{2,1,0:T(8,128)S(1)} %bitcast.126, s32[12]{0:T(128)S(1)} %copy-done.8), kind=kOutput, calls=%fused_computation.34 | convolution fusion | flops 9502744 | bytes 1703984 | tf_op jit(solution)/shard_map/tb,tkl->bkl/dot_general | solution.py:88
  44.1 1.7 %fusion.12 = f32[2,64,512]{2,0,1:T(2,128)S(1)} fusion(f32[12,64,512]{2,1,0:T(8,128)S(1)} %bitcast.127, f32[6,64,512]{2,0,1:T(8,128)S(1)} %get-tuple-element.28, s32[12]{0:T(128)S(1)} %copy-done.8), kind=kOutput, calls=%fused_computation.33 | convolution fusion | flops 9502744 | bytes 2097200 | tf_op jit(solution)/shard_map/tb,tkl->bkl/dot_general | solution.py:123
  45.9 9.4 %collective-permute-done.9 = bf16[1,512,512]{2,1,0:T(8,128)(2,1)S(1)} collective-permute-done((bf16[1,512,512]{2,1,0:T(8,128)(2,1)S(1)}, bf16[1,512,512]{2,1,0:T(8,128)(2,1)S(1)}, u32[]{:S(2)}, u32[]{:S(2)}) %collective-permute-start.9) | collective-permute-done | bytes 524320 | tf_op jit(solution)/shard_map/ppermute | solution.py:144
  55.6 4.6 %collective-permute-start.12 = (bf16[128,512]{1,0:T(8,128)(2,1)S(1)}, bf16[128,512]{1,0:T(8,128)(2,1)S(1)}, u32[]{:S(2)}, u32[]{:S(2)}) collective-permute-start(bf16[128,512]{1,0:T(8,128)(2,1)S(1)} %get-tuple-element.11), channel_id=1, source_target_pairs={{0,12},{4,0},{8,4},{12,8},{1,13},{5,1},{9,5},{13,9},{2,14},{6,2},{... | collective-permute-start | bytes 393224 | tf_op jit(solution)/shard_map/ppermute | solution.py:161
  60.2 1.0 %collective-permute-start.10 = (bf16[128,512]{1,0:T(8,128)(2,1)S(1)}, bf16[128,512]{1,0:T(8,128)(2,1)S(1)}, u32[]{:S(2)}, u32[]{:S(2)}) collective-permute-start(bf16[128,512]{1,0:T(8,128)(2,1)S(1)} %get-tuple-element.10), channel_id=1, source_target_pairs={{0,4},{4,8},{8,12},{12,0},{1,5},{5,9},{9,13},{13,1},{2,6},{6,10},{... | collective-permute-start | bytes 393224 | tf_op jit(solution)/shard_map/ppermute | solution.py:161
  61.7 3.8 %collective-permute-start.7 = (bf16[64,512]{1,0:T(8,128)(2,1)S(1)}, bf16[64,512]{1,0:T(8,128)(2,1)S(1)}, u32[]{:S(2)}, u32[]{:S(2)}) collective-permute-start(bf16[64,512]{1,0:T(8,128)(2,1)S(1)} %bitcast.150), channel_id=1, source_target_pairs={{0,8},{4,12},{1,9},{5,13},{2,10},{6,14},{3,11},{7,15},{16,24},{20,... | collective-permute-start | bytes 196616 | tf_op jit(solution)/shard_map/ppermute | solution.py:13
  65.5 1.3 %collective-permute-start.6 = (bf16[64,512]{1,0:T(8,128)(2,1)S(1)}, bf16[64,512]{1,0:T(8,128)(2,1)S(1)}, u32[]{:S(2)}, u32[]{:S(2)}) collective-permute-start(bf16[64,512]{1,0:T(8,128)(2,1)S(1)} %bitcast.151), channel_id=1, source_target_pairs={{8,0},{12,4},{9,1},{13,5},{10,2},{14,6},{11,3},{15,7},{24,16},{28,... | collective-permute-start | bytes 196616 | tf_op jit(solution)/shard_map/ppermute | solution.py:13
  66.9 3.4 %collective-permute-start.5 = (bf16[64,512]{1,0:T(8,128)(2,1)S(1)}, bf16[64,512]{1,0:T(8,128)(2,1)S(1)}, u32[]{:S(2)}, u32[]{:S(2)}) collective-permute-start(bf16[64,512]{1,0:T(8,128)(2,1)S(1)} %bitcast.153), channel_id=1, source_target_pairs={{0,4},{4,8},{8,12},{1,5},{5,9},{9,13},{2,6},{6,10},{10,14},{3,7},{... | collective-permute-start | bytes 196616 | tf_op jit(solution)/shard_map/ppermute | solution.py:13
  70.3 2.3 %collective-permute-done.11 = bf16[128,512]{1,0:T(8,128)(2,1)S(1)} collective-permute-done((bf16[128,512]{1,0:T(8,128)(2,1)S(1)}, bf16[128,512]{1,0:T(8,128)(2,1)S(1)}, u32[]{:S(2)}, u32[]{:S(2)}) %collective-permute-start.11) | collective-permute-done | bytes 131104 | tf_op jit(solution)/shard_map/ppermute | solution.py:161
  72.6 1.3 %collective-permute-start.4 = (bf16[64,512]{1,0:T(8,128)(2,1)S(1)}, bf16[64,512]{1,0:T(8,128)(2,1)S(1)}, u32[]{:S(2)}, u32[]{:S(2)}) collective-permute-start(bf16[64,512]{1,0:T(8,128)(2,1)S(1)} %bitcast.152), channel_id=1, source_target_pairs={{4,0},{8,4},{12,8},{5,1},{9,5},{13,9},{6,2},{10,6},{14,10},{7,3},{... | collective-permute-start | bytes 196616 | tf_op jit(solution)/shard_map/ppermute | solution.py:13
  74.1 2.7 %collective-permute-start.13 = (bf16[128,512]{1,0:T(8,128)(2,1)S(1)}, bf16[128,512]{1,0:T(8,128)(2,1)S(1)}, u32[]{:S(2)}, u32[]{:S(2)}) collective-permute-start(bf16[128,512]{1,0:T(8,128)(2,1)S(1)} %get-tuple-element.6), channel_id=1, source_target_pairs={{0,4},{4,8},{8,12},{12,0},{1,5},{5,9},{9,13},{13,1},{2,6},{6,10},{... | collective-permute-start | bytes 393224 | tf_op jit(solution)/shard_map/ppermute | solution.py:167
  76.8 1.5 %fusion.11 = bf16[1,768,512]{2,1,0:T(8,128)(2,1)} fusion(f32[768,512]{1,0:T(8,128)S(1)} %get-tuple-element.9, bf16[768,512]{1,0:T(8,128)(2,1)S(1)} %multiply_convert_fusion, bf16[1536,512]{1,0:T(8,128)(2,1)S(1)} %copy-done.2), kind=kOutput, calls=%fused_computation.32 | convolution fusion | flops 403439616 | bytes 3670016 | tf_op jit(solution)/shard_map/dot_general | solution.py:17
  80.7 1.2 %collective-permute-start.14 = (bf16[128,512]{1,0:T(8,128)(2,1)S(1)}, bf16[128,512]{1,0:T(8,128)(2,1)S(1)}, u32[]{:S(2)}, u32[]{:S(2)}) collective-permute-start(bf16[128,512]{1,0:T(8,128)(2,1)S(1)} %get-tuple-element.6), channel_id=1, source_target_pairs={{0,8},{4,12},{8,0},{12,4},{1,9},{5,13},{9,1},{13,5},{2,10},{6,14},... | collective-permute-start | bytes 393224 | tf_op jit(solution)/shard_map/ppermute | solution.py:167
  81.9 1.5 %collective-permute-start.15 = (bf16[128,512]{1,0:T(8,128)(2,1)S(1)}, bf16[128,512]{1,0:T(8,128)(2,1)S(1)}, u32[]{:S(2)}, u32[]{:S(2)}) collective-permute-start(bf16[128,512]{1,0:T(8,128)(2,1)S(1)} %get-tuple-element.6), channel_id=1, source_target_pairs={{0,12},{4,0},{8,4},{12,8},{1,13},{5,1},{9,5},{13,9},{2,14},{6,2},{... | collective-permute-start | bytes 393224 | tf_op jit(solution)/shard_map/ppermute | solution.py:167
  83.4 5.1 %collective-permute-done.14 = bf16[128,512]{1,0:T(8,128)(2,1)S(1)} collective-permute-done((bf16[128,512]{1,0:T(8,128)(2,1)S(1)}, bf16[128,512]{1,0:T(8,128)(2,1)S(1)}, u32[]{:S(2)}, u32[]{:S(2)}) %collective-permute-start.14) | collective-permute-done | bytes 131104 | tf_op jit(solution)/shard_map/ppermute | solution.py:167
  (87 shorter events, 13.2 us)
Async XLA Ops:
  0.6 30.1 %copy-start = (bf16[512,512]{1,0:T(8,128)(2,1)S(1)}, bf16[512,512]{1,0:T(8,128)(2,1)}, u32[]{:S(2)}) copy-start(bf16[512,512]{1,0:T(8,128)(2,1)} %param.14) | copy-start | bytes 1572868
  0.6 18.2 %copy-start.7 = (s32[12]{0:T(128)S(1)}, s32[12]{0:T(128)}, u32[]{:S(2)}) copy-start(s32[12]{0:T(128)} %param.17) | copy-start | bytes 148
  0.7 18.2 %copy-start.5 = (bf16[1,128,512]{2,1,0:T(8,128)(2,1)S(1)}, bf16[1,128,512]{2,1,0:T(8,128)(2,1)}, u32[]{:S(2)}) copy-start(bf16[1,128,512]{2,1,0:T(8,128)(2,1)} %param.12) | copy-start | bytes 393220
  1.4 19.3 %copy-start.9 = (s32[4]{0:T(128)}, s32[4]{0:T(128)S(1)}, u32[]{:S(2)}) copy-start(s32[4]{0:T(128)S(1)} %fusion.44) | copy-start | bytes 52
  3.6 21.6 %collective-permute-start = (bf16[64,512]{1,0:T(8,128)(2,1)}, bf16[64,512]{1,0:T(8,128)(2,1)S(1)}, u32[]{:S(2)}, u32[]{:S(2)}) collective-permute-start(bf16[64,512]{1,0:T(8,128)(2,1)} %get-tuple-element.20), channel_id=1, source_target_pairs={{0,4},{4,8},{8,12},{1,5},{5,9},{9,13},{2,6},{6,10},{10,14},{3,7},{... | collective-permute-start | bytes 196616 | tf_op jit(solution)/shard_map/ppermute | solution.py:13
  8.5 16.7 %collective-permute-start.1 = (bf16[64,512]{1,0:T(8,128)(2,1)}, bf16[64,512]{1,0:T(8,128)(2,1)S(1)}, u32[]{:S(2)}, u32[]{:S(2)}) collective-permute-start(bf16[64,512]{1,0:T(8,128)(2,1)} %get-tuple-element.19), channel_id=1, source_target_pairs={{4,0},{8,4},{12,8},{5,1},{9,5},{13,9},{6,2},{10,6},{14,10},{7,3},{... | collective-permute-start | bytes 196616 | tf_op jit(solution)/shard_map/ppermute | solution.py:13
  9.8 15.6 %collective-permute-start.2 = (bf16[64,512]{1,0:T(8,128)(2,1)}, bf16[64,512]{1,0:T(8,128)(2,1)S(1)}, u32[]{:S(2)}, u32[]{:S(2)}) collective-permute-start(bf16[64,512]{1,0:T(8,128)(2,1)} %get-tuple-element.18), channel_id=1, source_target_pairs={{0,8},{4,12},{1,9},{5,13},{2,10},{6,14},{3,11},{7,15},{16,24},{20,... | collective-permute-start | bytes 196616 | tf_op jit(solution)/shard_map/ppermute | solution.py:13
  15.4 10.1 %collective-permute-start.3 = (bf16[64,512]{1,0:T(8,128)(2,1)}, bf16[64,512]{1,0:T(8,128)(2,1)S(1)}, u32[]{:S(2)}, u32[]{:S(2)}) collective-permute-start(bf16[64,512]{1,0:T(8,128)(2,1)} %get-tuple-element.17), channel_id=1, source_target_pairs={{8,0},{12,4},{9,1},{13,5},{10,2},{14,6},{11,3},{15,7},{24,16},{28,... | collective-permute-start | bytes 196616 | tf_op jit(solution)/shard_map/ppermute | solution.py:13
  17.3 3.5 %copy-start.1 = (bf16[1,128,512]{2,1,0:T(8,128)(2,1)S(1)}, bf16[1,128,512]{2,1,0:T(8,128)(2,1)}, u32[]{:S(2)}) copy-start(bf16[1,128,512]{2,1,0:T(8,128)(2,1)} %param.10) | copy-start | bytes 393220
  25.4 2.7 %copy-start.6 = (s32[12,64]{1,0:T(8,128)S(1)}, s32[12,64]{1,0:T(8,128)}, u32[]{:S(2)}) copy-start(s32[12,64]{1,0:T(8,128)} %param.18) | copy-start | bytes 9220
  26.7 2.5 %copy-start.2 = (bf16[1536,512]{1,0:T(8,128)(2,1)S(1)}, bf16[1536,512]{1,0:T(8,128)(2,1)}, u32[]{:S(2)}) copy-start(bf16[1536,512]{1,0:T(8,128)(2,1)} %param.13) | copy-start | bytes 4718596
  26.7 2.5 %copy-start.3 = (bf16[1,768,512]{2,1,0:T(8,128)(2,1)S(1)}, bf16[1,768,512]{2,1,0:T(8,128)(2,1)}, u32[]{:S(2)}) copy-start(bf16[1,768,512]{2,1,0:T(8,128)(2,1)} %param.11) | copy-start | bytes 2359300
  26.7 2.5 %copy-start.4 = (bf16[12,64,512]{2,1,0:T(8,128)(2,1)S(1)}, bf16[12,64,512]{2,1,0:T(8,128)(2,1)}, u32[]{:S(2)}) copy-start(bf16[12,64,512]{2,1,0:T(8,128)(2,1)} %copy.117) | copy-start | bytes 2359300
  36.5 4.0 %collective-permute-start.8 = (bf16[2,512,512]{2,1,0:T(8,128)(2,1)S(1)}, bf16[2,512,512]{2,1,0:T(8,128)(2,1)S(1)}, u32[]{:S(2)}, u32[]{:S(2)}) collective-permute-start(bf16[2,512,512]{2,1,0:T(8,128)(2,1)S(1)} %fusion.18), channel_id=1, source_target_pairs={{0,1},{1,0},{2,3},{3,2},{4,5},{5,4},{6,7},{7,6},{8,9},{9,8},{10,11... | collective-permute-start | bytes 3145736 | tf_op jit(solution)/shard_map/ppermute | solution.py:144
  37.8 1.0 %copy-start.11 = (s32[12]{0:T(128)S(1)}, s32[12]{0:T(128)}, u32[]{:S(2)}) copy-start(s32[12]{0:T(128)} %param.16) | copy-start | bytes 148
  40.4 2.0 %copy-start.8 = (s32[12]{0:T(128)S(1)}, s32[12]{0:T(128)}, u32[]{:S(2)}) copy-start(s32[12]{0:T(128)} %param.17) | copy-start | bytes 148
  40.9 14.4 %collective-permute-start.9 = (bf16[1,512,512]{2,1,0:T(8,128)(2,1)S(1)}, bf16[1,512,512]{2,1,0:T(8,128)(2,1)S(1)}, u32[]{:S(2)}, u32[]{:S(2)}) collective-permute-start(bf16[1,512,512]{2,1,0:T(8,128)(2,1)S(1)} %dynamic-slice_convert_fusion), channel_id=1, source_target_pairs={{0,2},{1,3},{2,0},{3,1},{4,6},{5,7},{6,4},{7,5},{8,10},{9,11},{10,... | collective-permute-start | bytes 1572872 | tf_op jit(solution)/shard_map/ppermute | solution.py:144
  55.6 11.3 %collective-permute-start.12 = (bf16[128,512]{1,0:T(8,128)(2,1)S(1)}, bf16[128,512]{1,0:T(8,128)(2,1)S(1)}, u32[]{:S(2)}, u32[]{:S(2)}) collective-permute-start(bf16[128,512]{1,0:T(8,128)(2,1)S(1)} %get-tuple-element.11), channel_id=1, source_target_pairs={{0,12},{4,0},{8,4},{12,8},{1,13},{5,1},{9,5},{13,9},{2,14},{6,2},{... | collective-permute-start | bytes 393224 | tf_op jit(solution)/shard_map/ppermute | solution.py:161
  60.2 12.4 %collective-permute-start.11 = (bf16[128,512]{1,0:T(8,128)(2,1)S(1)}, bf16[128,512]{1,0:T(8,128)(2,1)S(1)}, u32[]{:S(2)}, u32[]{:S(2)}) collective-permute-start(bf16[128,512]{1,0:T(8,128)(2,1)S(1)} %get-tuple-element.12), channel_id=1, source_target_pairs={{0,8},{4,12},{8,0},{12,4},{1,9},{5,13},{9,1},{13,5},{2,10},{6,14},... | collective-permute-start | bytes 393224 | tf_op jit(solution)/shard_map/ppermute | solution.py:161
  60.2 13.7 %collective-permute-start.10 = (bf16[128,512]{1,0:T(8,128)(2,1)S(1)}, bf16[128,512]{1,0:T(8,128)(2,1)S(1)}, u32[]{:S(2)}, u32[]{:S(2)}) collective-permute-start(bf16[128,512]{1,0:T(8,128)(2,1)S(1)} %get-tuple-element.10), channel_id=1, source_target_pairs={{0,4},{4,8},{8,12},{12,0},{1,5},{5,9},{9,13},{13,1},{2,6},{6,10},{... | collective-permute-start | bytes 393224 | tf_op jit(solution)/shard_map/ppermute | solution.py:161
  61.7 17.3 %collective-permute-start.7 = (bf16[64,512]{1,0:T(8,128)(2,1)S(1)}, bf16[64,512]{1,0:T(8,128)(2,1)S(1)}, u32[]{:S(2)}, u32[]{:S(2)}) collective-permute-start(bf16[64,512]{1,0:T(8,128)(2,1)S(1)} %bitcast.150), channel_id=1, source_target_pairs={{0,8},{4,12},{1,9},{5,13},{2,10},{6,14},{3,11},{7,15},{16,24},{20,... | collective-permute-start | bytes 196616 | tf_op jit(solution)/shard_map/ppermute | solution.py:13
  65.5 13.5 %collective-permute-start.6 = (bf16[64,512]{1,0:T(8,128)(2,1)S(1)}, bf16[64,512]{1,0:T(8,128)(2,1)S(1)}, u32[]{:S(2)}, u32[]{:S(2)}) collective-permute-start(bf16[64,512]{1,0:T(8,128)(2,1)S(1)} %bitcast.151), channel_id=1, source_target_pairs={{8,0},{12,4},{9,1},{13,5},{10,2},{14,6},{11,3},{15,7},{24,16},{28,... | collective-permute-start | bytes 196616 | tf_op jit(solution)/shard_map/ppermute | solution.py:13
  66.9 12.1 %collective-permute-start.5 = (bf16[64,512]{1,0:T(8,128)(2,1)S(1)}, bf16[64,512]{1,0:T(8,128)(2,1)S(1)}, u32[]{:S(2)}, u32[]{:S(2)}) collective-permute-start(bf16[64,512]{1,0:T(8,128)(2,1)S(1)} %bitcast.153), channel_id=1, source_target_pairs={{0,4},{4,8},{8,12},{1,5},{5,9},{9,13},{2,6},{6,10},{10,14},{3,7},{... | collective-permute-start | bytes 196616 | tf_op jit(solution)/shard_map/ppermute | solution.py:13
  72.6 6.4 %collective-permute-start.4 = (bf16[64,512]{1,0:T(8,128)(2,1)S(1)}, bf16[64,512]{1,0:T(8,128)(2,1)S(1)}, u32[]{:S(2)}, u32[]{:S(2)}) collective-permute-start(bf16[64,512]{1,0:T(8,128)(2,1)S(1)} %bitcast.152), channel_id=1, source_target_pairs={{4,0},{8,4},{12,8},{5,1},{9,5},{13,9},{6,2},{10,6},{14,10},{7,3},{... | collective-permute-start | bytes 196616 | tf_op jit(solution)/shard_map/ppermute | solution.py:13
  74.1 9.3 %collective-permute-start.13 = (bf16[128,512]{1,0:T(8,128)(2,1)S(1)}, bf16[128,512]{1,0:T(8,128)(2,1)S(1)}, u32[]{:S(2)}, u32[]{:S(2)}) collective-permute-start(bf16[128,512]{1,0:T(8,128)(2,1)S(1)} %get-tuple-element.6), channel_id=1, source_target_pairs={{0,4},{4,8},{8,12},{12,0},{1,5},{5,9},{9,13},{13,1},{2,6},{6,10},{... | collective-permute-start | bytes 393224 | tf_op jit(solution)/shard_map/ppermute | solution.py:167
  78.3 0.8 copy-start.10
  80.7 7.8 %collective-permute-start.14 = (bf16[128,512]{1,0:T(8,128)(2,1)S(1)}, bf16[128,512]{1,0:T(8,128)(2,1)S(1)}, u32[]{:S(2)}, u32[]{:S(2)}) collective-permute-start(bf16[128,512]{1,0:T(8,128)(2,1)S(1)} %get-tuple-element.6), channel_id=1, source_target_pairs={{0,8},{4,12},{8,0},{12,4},{1,9},{5,13},{9,1},{13,5},{2,10},{6,14},... | collective-permute-start | bytes 393224 | tf_op jit(solution)/shard_map/ppermute | solution.py:167
  81.9 6.6 %collective-permute-start.15 = (bf16[128,512]{1,0:T(8,128)(2,1)S(1)}, bf16[128,512]{1,0:T(8,128)(2,1)S(1)}, u32[]{:S(2)}, u32[]{:S(2)}) collective-permute-start(bf16[128,512]{1,0:T(8,128)(2,1)S(1)} %get-tuple-element.6), channel_id=1, source_target_pairs={{0,12},{4,0},{8,4},{12,8},{1,13},{5,1},{9,5},{13,9},{2,14},{6,2},{... | collective-permute-start | bytes 393224 | tf_op jit(solution)/shard_map/ppermute | solution.py:167

commit v2 on v0

v2 whole, which is shorter than its diff:
```python
import functools

import jax
import jax.numpy as jnp
from jax import lax
from jax.experimental import pallas as pl
from jax.experimental.pallas import tpu as pltpu
from jax.sharding import PartitionSpec as P

OFFSET_LIST = (1, -1, 2, -2)
EPSILON = 1e-05
VMEM = pl.BlockSpec(memory_space=pltpu.VMEM)
SMEM = pl.BlockSpec(memory_space=pltpu.SMEM)
F32 = jnp.float32
BF16 = jnp.bfloat16


def dot(left, right):
    return jnp.dot(left, right, preferred_element_type=F32)


def dot_t(left, right):
    return lax.dot_general(left, right, (((1,), (1,)), ((), ())), preferred_element_type=F32)


def t_dot(left, right):
    return lax.dot_general(left, right, (((0,), (0,)), ((), ())), preferred_element_type=F32)


def row_mean(array):
    return jnp.sum(array, axis=1, keepdims=True) * (1.0 / array.shape[1])


def rows_of(ref, block, size):
    return ref[pl.ds(pl.multiple_of(block * size, size), size), :]


def edge_kernel(
    parts,
    ways,
    arrivals,
    src_ref,
    dst_ref,
    count_ref,
    slot_ref,
    node_ref,
    *refs,
):
    arrived = refs[:arrivals]
    edge_ref, cot_ref, win_ref, wout_ref = refs[arrivals : arrivals + 4]
    (
        agg_out,
        gpre_ref,
        own_sums,
        back_sums,
        recv_sums,
        away_a,
        kept_a,
        away_b,
        kept_b,
    ) = refs[arrivals + 4 : arrivals + 13]
    ext_ref, send_ref, act_ref, proj_ref, pre_recv, cot_mid, agg_ref, sums_ref = refs[
        arrivals + 13 :
    ]
    tiles, block = slot_ref.shape
    latent = node_ref.shape[1]
    owned = node_ref.shape[0] // block
    part = lax.axis_index("dom")
    bit = lax.axis_index("dp") % 2
    live_count = count_ref[0]

    ext_ref[: owned * block, :] = node_ref[...]
    for which in range(arrivals):
        at = (owned + which) * block
        ext_ref[at : at + block, :] = arrived[which][...]
    pre_recv[...] = dot(node_ref[...], win_ref[2 * latent :, :])
    cot = cot_ref[...].astype(F32)
    cot_mid[...] = cot - row_mean(cot)
    agg_ref[...] = jnp.zeros_like(agg_ref)
    sums_ref[...] = jnp.zeros_like(sums_ref)
    recv_sums[...] = jnp.zeros_like(recv_sums)

    def hot(tile):
        source = src_ref[tile]
        which = source - owned
        reach = jnp.where(which >= 2, 2, 1)
        partner = part - jnp.where(which % 2 == 1, -reach, reach)
        exists = (source < owned) | ((partner >= 0) & (partner < parts))
        place = jnp.minimum(source, owned + arrivals - 1)
        there = jnp.where(exists, 1.0, 0.0)
        index = lax.broadcasted_iota(jnp.int32, (block, block), 0)
        return jnp.where(index == slot_ref[tile : tile + 1, :], there, 0.0).astype(BF16), place

    group = 4 if tiles % 4 == 0 else 1
    span = group * block
    for first in range(0, tiles, group):
        rows = slice(first * block, first * block + span)
        members = range(first, first + group)
        for tile in members:
            chosen, place = hot(tile)
            at = tile * block
            send_ref[at : at + block, :] = t_dot(chosen, rows_of(ext_ref, place, block)).astype(
                BF16
            )
        edges = edge_ref[rows, :]
        received = jnp.concatenate([rows_of(pre_recv, dst_ref[t], block) for t in members], axis=0)
        preact = (
            dot(edges, win_ref[:latent, :])
            + dot(send_ref[rows, :], win_ref[latent : 2 * latent, :])
            + received
        )
        gate = 0.5 * jnp.tanh(0.5 * preact) + 0.5
        activated = preact * gate
        slope = gate + activated * (1.0 - gate)
        activated = activated.astype(BF16)
        act_ref[rows, :] = activated
        projected = dot(activated, wout_ref[...])
        centered = projected - row_mean(projected)
        inv_scale = lax.rsqrt(row_mean(centered * centered) + EPSILON)
        message = centered * inv_scale
        updated = edges.astype(F32) + message
        upstream = []
        for number, tile in enumerate(members):
            live = jnp.where(tile < live_count, 1.0, 0.0)
            target = pl.ds(pl.multiple_of(dst_ref[tile] * block, block), block)
            agg_ref[target, :] += updated[number * block : (number + 1) * block] * live
            upstream.append(cot_mid[target, :] * live)
        upstream = jnp.concatenate(upstream, axis=0)
        grad_project = inv_scale * (upstream - message * row_mean(upstream * message))
        grad_project = grad_project.astype(BF16)
        proj_ref[rows, :] = grad_project
        grad_pre = (dot_t(grad_project, wout_ref[...]) * slope).astype(BF16)
        gpre_ref[rows, :] = grad_pre
        for number, tile in enumerate(members):
            chosen, place = hot(tile)
            mine = grad_pre[number * block : (number + 1) * block]
            target = pl.ds(pl.multiple_of(dst_ref[tile] * block, block), block)
            recv_sums[target, :] += mine.astype(F32)
            spot = pl.ds(pl.multiple_of(place * block, block), block)
            sums_ref[spot, :] += dot(chosen, mine)

    agg_out[...] = agg_ref[...].astype(BF16)
    own_sums[...] = sums_ref[: owned * block, :]
    for which in range(arrivals):
        at = (owned + which) * block
        back_sums[which] = sums_ref[at : at + block, :].astype(BF16)

    unit = latent // ways

    def put(owner, spot, value):
        away, kept = (away_a, kept_a) if spot < 2 else (away_b, kept_b)
        where = slice((spot % 2) * unit, (spot % 2 + 1) * unit)

        @pl.when(bit == owner % 2)
        def _():
            kept[owner // 2, where, :] = value

        @pl.when(bit != owner % 2)
        def _():
            away[owner // 2, where, :] = value.astype(BF16)

    step = 256
    for start in range(0, latent, step):
        value = t_dot(act_ref[:, start : start + step], proj_ref[...])
        for at in range(0, step, unit):
            put((start + at) // unit, 0, value[at : at + unit])
    sections = (
        (edge_ref, gpre_ref),
        (ext_ref, sums_ref),
        (node_ref, recv_sums),
    )
    for number, (left, right) in enumerate(sections):
        for start in range(0, latent, step):
            value = t_dot(left[:, start : start + step], right[...].astype(BF16))
            for at in range(0, step, unit):
                spot = (number * latent + start + at) // unit
                put(spot // 3, 1 + spot % 3, value[at : at + unit])


def edge_grad_kernel(block, dst_ref, count_ref, gpre_ref, cot_ref, win_ref, out_ref):
    latent = cot_ref.shape[1]
    tiles = gpre_ref.shape[0] // block
    group = 4 if tiles % 4 == 0 else 1
    for first in range(0, tiles, group):
        rows = slice(first * block, (first + group) * block)
        upstream = jnp.concatenate(
            [
                rows_of(cot_ref, dst_ref[t], block).astype(F32)
                * jnp.where(t < count_ref[0], 1.0, 0.0)
                for t in range(first, first + group)
            ],
            axis=0,
        )
        out_ref[rows, :] = (dot_t(gpre_ref[rows, :], win_ref[:latent, :]) + upstream).astype(BF16)


def node_grad_kernel(arrivals, chosen_ref, own_ref, recv_ref, win_ref, *refs):
    returned = refs[:arrivals]
    out_ref, total_ref = refs[arrivals:]
    latent = own_ref.shape[1]
    block = returned[0].shape[0]
    total_ref[...] = own_ref[...]
    for which in range(arrivals):
        spot = pl.ds(pl.multiple_of(chosen_ref[which] * block, block), block)
        total_ref[spot, :] += returned[which][...].astype(F32)

    def wide_dot(value, weight):
        high = value.astype(BF16)
        low = (value - high.astype(F32)).astype(BF16)
        return dot_t(high, weight) + dot_t(low, weight)

    out_ref[...] = (
        wide_dot(total_ref[...], win_ref[latent : 2 * latent, :])
        + wide_dot(recv_ref[...], win_ref[2 * latent :, :])
    ).astype(BF16)


def swap(array, axis, partner):
    devices = lax.axis_size(axis)
    return lax.ppermute(array, axis, [(i, partner(i)) for i in range(devices)])


def from_behind(array, axis, by):
    devices = lax.axis_size(axis)
    pairs = [(i, i + by) for i in range(devices) if 0 <= i + by < devices]
    return lax.ppermute(array, axis, pairs)


def partners_of_four(which):
    return ((1, 0, 3, 2), (0, 2, 1, 3), (2, 3, 0, 1))[which]


def exchange_of_four(first, second, third):
    return [
        swap(array, "dom", lambda i, which=which: partners_of_four(which)[i])
        for which, array in enumerate((first, second, third))
    ]


def sum_over_dp(away, kept):
    devices = lax.axis_size("dp")
    index = lax.axis_index("dp")
    total = kept + swap(away, "dp", lambda i: i ^ 1).astype(F32)
    bit = 2
    while bit < devices:
        mine = (index // bit) % 2
        split = total.reshape((-1, 2) + total.shape[1:])
        away = lax.dynamic_index_in_dim(split, 1 - mine, 1, keepdims=False).astype(BF16)
        kept = lax.dynamic_index_in_dim(split, mine, 1, keepdims=False)
        total = kept + swap(away, "dp", lambda i, bit=bit: i ^ bit).astype(F32)
        bit *= 2
    return total[0]


def sum_over_dom(rows):
    devices = lax.axis_size("dom")
    if devices != 4:
        piece = lax.psum_scatter(rows, "dom", scatter_dimension=0, tiled=True)
        return lax.all_gather(piece, "dom", axis=0, tiled=True)
    index = lax.axis_index("dom")
    inner = (index == 1) | (index == 2)
    low, high = jnp.split(rows, 2, axis=0)
    away = jnp.where(inner, high, low).astype(BF16)
    kept = jnp.where(inner, low, high)
    kept = (kept + swap(away, "dom", lambda i: i ^ 1).astype(F32)).astype(BF16)
    kept = (kept.astype(F32) + swap(kept, "dom", lambda i: 3 - i).astype(F32)).astype(BF16)
    other = swap(kept, "dom", lambda i: i ^ 1)
    low = jnp.where(inner, kept, other)
    high = jnp.where(inner, other, kept)
    return jnp.concatenate([low, high], axis=0).astype(F32)


def body(
    node_latents,
    edge_latents,
    agg_cotangent,
    weight_in,
    weight_out,
    boundary,
    tile_src,
    tile_dst,
    edge_slot,
    tile_count,
):
    tiles, block = edge_slot.shape
    edges, latent = edge_latents.shape[1:]
    nodes = node_latents.shape[1]
    parts = lax.axis_size("dom")
    ways = lax.axis_size("dp")
    part = lax.axis_index("dom")
    four = parts == 4
    node_rows = node_latents[0]
    chosen = boundary[0]

    def pick(which):
        return lax.dynamic_slice(node_rows, (chosen[which] * block, 0), (block, latent))

    if four:
        even = part % 2 == 0
        low = part < 2
        index = [
            jnp.where(even, chosen[0], chosen[1]),
            jnp.where(even, chosen[1], chosen[0]),
            jnp.where(low, chosen[2], chosen[3]),
        ]
        sent = [lax.dynamic_slice(node_rows, (i * block, 0), (block, latent)) for i in index]
        one, two, three = exchange_of_four(*sent)
        came = [jnp.where(even, two, one), jnp.where(even, one, two), three]
    else:
        came = [from_behind(pick(which), "dom", OFFSET_LIST[which]) for which in range(4)]
    arrivals = len(came)
    unit = latent // ways
    half = ways // 2

    agg, grad_pre, own_sums, back_sums, recv_sums, away_a, kept_a, away_b, kept_b = pl.pallas_call(
        functools.partial(edge_kernel, parts, ways, arrivals),
        out_shape=(
            jax.ShapeDtypeStruct((nodes, latent), BF16),
            jax.ShapeDtypeStruct((edges, latent), BF16),
            jax.ShapeDtypeStruct((nodes, latent), F32),
            jax.ShapeDtypeStruct((arrivals, block, latent), BF16),
            jax.ShapeDtypeStruct((nodes, latent), F32),
            jax.ShapeDtypeStruct((half, 2 * unit, latent), BF16),
            jax.ShapeDtypeStruct((half, 2 * unit, latent), F32),
            jax.ShapeDtypeStruct((half, 2 * unit, latent), BF16),
            jax.ShapeDtypeStruct((half, 2 * unit, latent), F32),
        ),
        in_specs=[SMEM] * 3 + [VMEM] * (6 + arrivals),
        out_specs=(VMEM,) * 9,
        scratch_shapes=[
            pltpu.VMEM((nodes + arrivals * block, latent), BF16),
            pltpu.VMEM((edges, latent), BF16),
            pltpu.VMEM((edges, latent), BF16),
            pltpu.VMEM((edges, latent), BF16),
            pltpu.VMEM((nodes, latent), F32),
            pltpu.VMEM((nodes, latent), F32),
            pltpu.VMEM((nodes, latent), F32),
            pltpu.VMEM((nodes + arrivals * block, latent), F32),
        ],
        compiler_params=pltpu.CompilerParams(vmem_limit_bytes=32 * 1024 * 1024),
        cost_estimate=pl.CostEstimate(
            flops=14 * edges * latent * latent,
            bytes_accessed=12_000_000,
            transcendentals=edges * latent,
        ),
        name="edge_block",
    )(
        tile_src,
        tile_dst,
        tile_count,
        edge_slot,
        node_rows,
        *came,
        edge_latents[0],
        agg_cotangent[0],
        weight_in,
        weight_out,
    )
    if four:
        first = jnp.where(even, back_sums[1], back_sums[0])
        second = jnp.where(even, back_sums[0], back_sums[1])
        returned = exchange_of_four(first, second, back_sums[2])
        spots = jnp.stack(index)
    else:
        returned = [
            from_behind(back_sums[which], "dom", -OFFSET_LIST[which]) for which in range(4)
        ]
        spots = chosen
    edge_grad = pl.pallas_call(
        functools.partial(edge_grad_kernel, block),
        out_shape=jax.ShapeDtypeStruct((edges, latent), BF16),
        in_specs=[SMEM] * 2 + [VMEM] * 3,
        out_specs=VMEM,
        compiler_params=pltpu.CompilerParams(vmem_limit_bytes=16 * 1024 * 1024),
        cost_estimate=pl.CostEstimate(
            flops=2 * edges * latent * latent, bytes_accessed=3_000_000, transcendentals=0
        ),
        name="edge_grads",
    )(tile_dst, tile_count, grad_pre, agg_cotangent[0], weight_in)
    node_out = pl.pallas_call(
        functools.partial(node_grad_kernel, arrivals),
        out_shape=jax.ShapeDtypeStruct((nodes, latent), BF16),
        in_specs=[SMEM] + [VMEM] * (3 + arrivals),
        out_specs=VMEM,
        scratch_shapes=[pltpu.VMEM((nodes, latent), F32)],
        compiler_params=pltpu.CompilerParams(vmem_limit_bytes=16 * 1024 * 1024),
        cost_estimate=pl.CostEstimate(
            flops=8 * nodes * latent * latent, bytes_accessed=2_000_000, transcendentals=0
        ),
        name="node_grads",
    )(spots, own_sums, recv_sums, weight_in, *returned)
    sum_a = sum_over_dom(sum_over_dp(away_a, kept_a))
    sum_b = sum_over_dom(sum_over_dp(away_b, kept_b))
    w_in_grad = jnp.concatenate([sum_a[unit:], sum_b], axis=0)
    return (agg[None], edge_grad[None], node_out[None], w_in_grad, sum_a[:unit])


def solution(mesh):
    in_specs = (
        P(("group", "dp"), "dom", None),
        P(("group", "dp"), "dom", None),
        P(("group", "dp"), "dom", None),
        P(),
        P(),
        P(("group", "dom"), None),
        P(("group", "dom")),
        P(("group", "dom")),
        P(("group", "dom"), None),
        P(("group", "dom")),
    )
    out_specs = (
        P(("group", "dp"), "dom", None),
        P(("group", "dp"), "dom", None),
        P(("group", "dp"), "dom", None),
        P(("group", "dp"), None),
        P(("group", "dp"), None),
    )
    return jax.shard_map(body, mesh=mesh, in_specs=in_specs, out_specs=out_specs, check_vma=False)
```

time: 165 us -> 84.6 us (0.51)
  waiting for transfers between devices: 79.9 us -> 20 us
  matrix products: 20.7 us -> 0 us
  Pallas kernels: 0 us -> 13.5 us
  between operations: 15.2 us -> 5.41 us
  local copies, waits for them, and re-layouts: 17.7 us -> 13 us
  starting transfers between devices: 24.7 us -> 27.6 us
    reduce_scatter x1 -> x0, waiting for transfers between devices: 69.4 us -> none  [body(): lax.psum_scatter(arranged, ('dom', 'dp'), scatter_dimension=0, tiled=True)]
    dot_general x16 -> x0, matrix products: 20.7 us -> none  [the longest x4 4.68 us: pair_dot(): lax.dot_general(left, right, (((1,), (1,)), ((), ())), preferred_element_...]
    ppermute x8 -> x16, waiting for transfers between devices: 1.45 us -> 20 us  [swap(): return lax.ppermute(array, axis, [(i, partner(i)) for i in range(devices)])]
    pallas_call x0 -> x3, Pallas kernels: none -> 13.5 us  [the longest x1 8.97 us: body(): pl.pallas_call(functools.partial(edge_kernel, parts, ways, arrivals), out...]
    unnamed x32 -> x34, local copies, waits for them, and re-layouts: 0.13 us -> 9.8 us
    all_gather x1 -> x0, waiting for transfers between devices: 9 us -> none  [body(): mine = lax.all_gather(piece, 'dom', axis=0, tiled=True)]
    another operation x5 -> x0, local copies, waits for them, and re-layouts: 3.17 us -> none  [the longest x4 3.03 us: send_blocks(): return jnp.stack(arrived)]
    ppermute x8 -> x16, starting transfers between devices: 24.5 us -> 27.6 us  [swap(): return lax.ppermute(array, axis, [(i, partner(i)) for i in range(devices)])]
  transfers between devices with their start and end apart: 10 -> 16, of which waited for: 3 -> 8; matrix products, arithmetic and copies ran while one was open for 13% -> 5% of each run, Pallas kernels for 0% -> 5%
where the time goes in v2:
time: 84.6 us; the launch traced here: 84 us
  starting transfers between devices  27.6 us (33%)
  waiting for transfers between devices  20 us (24%)
  Pallas kernels  13.5 us (16%)
  local copies, waits for them, and re-layouts  13 us (15%)
  between operations  5.41 us (6%)
  other arithmetic  4.65 us (5%)
    ppermute x16, starting transfers between devices, swap(): return lax.ppermute(array, axis, [(i, partner(i)) for i in range(devices)])  27.6 us
    ppermute x16, waiting for transfers between devices, swap(): return lax.ppermute(array, axis, [(i, partner(i)) for i in range(devices)])  20 us
    unnamed x34, local copies, waits for them, and re-layouts  9.8 us
    pallas_call x1, Pallas kernels, body(): pl.pallas_call(functools.partial(edge_kernel, parts, ways, arrivals), out...  8.97 us
    pallas_call x1, Pallas kernels, body(): pl.pallas_call(functools.partial(node_grad_kernel, arrivals), out_shape=j...  2.46 us
    add x2, other arithmetic, sum_over_dp(): total = kept + swap(away, 'dp', lambda i: i ^ 1).astype(F32)  2.42 us
    pallas_call x1, Pallas kernels, body(): pl.pallas_call(functools.partial(edge_grad_kernel, block), out_shape=jax....  2.03 us
  transfers between devices with their start and end apart: 16, of which 8 were waited for; matrix products, arithmetic and copies ran while one was open for 5% of the time, Pallas kernels for 5%

profile of v2, /device:TPU:0, one launch (start us, length us, event | category | flops | bytes accessed | tf_op | source)
XLA Modules:
  0.0 84.0 jit_solution(846417688859157392)
XLA Ops:
  0.6 1.4 %fusion.5 = (s32[1,1]{1,0:T(1,128)}, s32[1,1]{1,0:T(1,128)}, s32[1,1]{1,0:T(1,128)}, s32[1,1]{1,0:T(1,128)}) fusion(s32[1,4]{1,0:T(1,128)} %param.15), kind=kLoop, calls=%fused_computation.33 | loop fusion | bytes 32 | tf_op jit(solution)/shard_map/slice | solution.py:304
  5.9 0.9 %dynamic-slice_bitcast_fusion = (bf16[64,512]{1,0:T(8,128)(2,1)S(1)}, bf16[64,512]{1,0:T(8,128)(2,1)S(1)}, bf16[64,512]{1,0:T(8,128)(2,1)S(1)}) fusion(bf16[1,128,512]{2,1,0:T(8,128)(2,1)} %param.10, s32[]{:T(128)S(6)} %select_n.130, s32[]{:T(128)S(6)} %select_n.124, s32[]{:T(128)S(6)} %select_n.126), kind=kLoop, calls=%fused_computation.26 | loop fusion | bytes 393228 | tf_op jit(solution)/shard_map/dynamic_slice | solution.py:306
  7.6 5.9 %collective-permute-start.1 = (bf16[64,512]{1,0:T(8,128)(2,1)S(1)}, bf16[64,512]{1,0:T(8,128)(2,1)S(1)}, u32[]{:S(2)}, u32[]{:S(2)}) collective-permute-start(bf16[64,512]{1,0:T(8,128)(2,1)S(1)} %get-tuple-element.34), channel_id=1, source_target_pairs={{0,4},{4,0},{8,12},{12,8},{1,5},{5,1},{9,13},{13,9},{2,6},{6,2},{1... | collective-permute-start | bytes 196616 | tf_op jit(solution)/shard_map/ppermute | solution.py:220
  14.1 1.6 %collective-permute-done.1 = bf16[64,512]{1,0:T(8,128)(2,1)S(1)} collective-permute-done((bf16[64,512]{1,0:T(8,128)(2,1)S(1)}, bf16[64,512]{1,0:T(8,128)(2,1)S(1)}, u32[]{:S(2)}, u32[]{:S(2)}) %collective-permute-start.1) | collective-permute-done | bytes 65568 | tf_op jit(solution)/shard_map/ppermute | solution.py:220
  15.7 3.1 %collective-permute-done.2.refs_2_ = bf16[64,512]{1,0:T(8,128)(2,1)S(1)} collective-permute-done((bf16[64,512]{1,0:T(8,128)(2,1)S(1)}, bf16[64,512]{1,0:T(8,128)(2,1)S(1)}, u32[]{:S(2)}, u32[]{:S(2)}) %collective-permute-start.2) | collective-permute-done | bytes 65568 | tf_op jit(solution)/shard_map/ppermute | solution.py:220
  18.9 1.4 %copy-done = bf16[1536,512]{1,0:T(8,128)(2,1)S(1)} copy-done((bf16[1536,512]{1,0:T(8,128)(2,1)S(1)}, bf16[1536,512]{1,0:T(8,128)(2,1)}, u32[]{:S(2)}) %copy-start) | copy-done | bytes 1572888
  20.3 0.9 %copy-done.4 = bf16[1,128,512]{2,1,0:T(8,128)(2,1)S(1)} copy-done((bf16[1,128,512]{2,1,0:T(8,128)(2,1)S(1)}, bf16[1,128,512]{2,1,0:T(8,128)(2,1)}, u32[]{:S(2)}) %copy-start.4) | copy-done | bytes 131096
  21.2 0.9 %copy-done.9 = bf16[1,128,512]{2,1,0:T(8,128)(2,1)S(1)} copy-done((bf16[1,128,512]{2,1,0:T(8,128)(2,1)S(1)}, bf16[1,128,512]{2,1,0:T(8,128)(2,1)}, u32[]{:S(2)}) %copy-start.9) | copy-done | bytes 131096
  22.7 1.1 %copy-done.13 = bf16[1,768,512]{2,1,0:T(8,128)(2,1)S(1)} copy-done((bf16[1,768,512]{2,1,0:T(8,128)(2,1)S(1)}, bf16[1,768,512]{2,1,0:T(8,128)(2,1)}, u32[]{:S(2)}) %copy-start.13) | copy-done | bytes 786456
  23.9 1.0 %copy-done.14 = bf16[512,512]{1,0:T(8,128)(2,1)S(1)} copy-done((bf16[512,512]{1,0:T(8,128)(2,1)S(1)}, bf16[512,512]{1,0:T(8,128)(2,1)}, u32[]{:S(2)}) %copy-start.14) | copy-done | bytes 524312
  26.3 9.0 %edge_block.1 = (bf16[128,512]{1,0:T(8,128)(2,1)}, bf16[768,512]{1,0:T(8,128)(2,1)S(1)}, f32[128,512]{1,0:T(8,128)S(1)}, bf16[3,64,512]{2,1,0:T(8,128)(2,1)S(1)}...) custom-call(s32[12]{0:T(128)S(1)} %copy-done.16, ...), custom_call_target="tpu_custom_call" | custom-call | flops 2818572288 | bytes 12000000 | tf_op jit(solution)/shard_map/edge_block/pallas_call | solution.py:315
  35.2 1.0 %copy-done.2 = f32[2,256,512]{2,1,0:T(8,128)} copy-done((f32[2,256,512]{2,1,0:T(8,128)}, f32[2,256,512]{2,1,0:T(8,128)S(1)}, u32[]{:S(2)}) %copy-start.2) | copy-done | bytes 1048600
  36.9 0.7 copy-done.7
  38.9 1.9 %collective-permute-start.3 = (bf16[64,512]{1,0:T(8,128)(2,1)}, bf16[64,512]{1,0:T(8,128)(2,1)}, u32[]{:S(2)}, u32[]{:S(2)}) collective-permute-start(bf16[64,512]{1,0:T(8,128)(2,1)} %get-tuple-element.30), channel_id=1, source_target_pairs={{0,4},{4,0},{8,12},{12,8},{1,5},{5,1},{9,13},{13,9},{2,6},{6,2},{1... | collective-permute-start | bytes 196616 | tf_op jit(solution)/shard_map/ppermute | solution.py:220
  40.8 2.1 %collective-permute-start.4 = (bf16[64,512]{1,0:T(8,128)(2,1)}, bf16[64,512]{1,0:T(8,128)(2,1)}, u32[]{:S(2)}, u32[]{:S(2)}) collective-permute-start(bf16[64,512]{1,0:T(8,128)(2,1)} %get-tuple-element.31), channel_id=1, source_target_pairs={{0,0},{4,8},{8,4},{12,12},{1,1},{5,9},{9,5},{13,13},{2,2},{6,10},{... | collective-permute-start | bytes 196616 | tf_op jit(solution)/shard_map/ppermute | solution.py:220
  43.0 2.0 %edge_grads.1 = bf16[768,512]{1,0:T(8,128)(2,1)} custom-call(s32[12]{0:T(128)S(1)} %copy-done.12, s32[1]{0:T(128)S(6)} %copy.15.count_ref, bf16[768,512]{1,0:T(8,128)(2,1)S(1)} %get-tuple-element.15.gpre_ref, bf16[128,512]{1,0:T(8,128)(2,1)S(1)} %bitcast.39, bf16[1536,512]{1,0:T(8,128)(2,1)S(1)} %copy-done.1), custom_call_target="tpu_custom_call" | custom-call | flops 402653184 | bytes 3000000 | tf_op jit(solution)/shard_map/edge_grads/pallas_call | solution.py:369
  45.1 2.5 %node_grads.1 = bf16[128,512]{1,0:T(8,128)(2,1)} custom-call(s32[3]{0:T(128)S(1)} %pad_add_fusion.chosen_ref, f32[128,512]{1,0:T(8,128)S(1)} %copy-done.6, f32[128,512]{1,0:T(8,128)S(1)} %copy-done.8, bf16[1536,512]{1,0:T(8,128)(2,1)S(1)} %copy-done.1, bf16[64,512]{1,0:T(8,128)(2,1)} %collective-permute-done.3.refs_0_, ...), custom_call_target="tpu_custom_call" | custom-call | flops 268435456 | bytes 2000000 | tf_op jit(solution)/shard_map/node_grads/pallas_call | solution.py:380
  47.6 1.2 %convert_add_fusion.1 = f32[2,256,512]{2,1,0:T(8,128)S(1)} fusion(f32[2,256,512]{2,1,0:T(8,128)S(1)} %copy-done.3, bf16[2,256,512]{2,1,0:T(8,128)(2,1)} %collective-permute-done.6), kind=kLoop, calls=%fused_computation.1 | loop fusion | flops 524288 | bytes 2621440 | tf_op jit(solution)/shard_map/add | solution.py:243
  48.8 1.6 %collective-permute-start.7 = (bf16[1,256,512]{2,1,0:T(8,128)(2,1)S(1)}, bf16[1,256,512]{2,1,0:T(8,128)(2,1)S(1)}, u32[]{:S(2)}, u32[]{:S(2)}) collective-permute-start(bf16[1,256,512]{2,1,0:T(8,128)(2,1)S(1)} %dynamic-slice_convert_fusion.1), channel_id=1, source_target_pairs={{0,2},{1,3},{2,0},{3,1},{4,6},{5,7},{6,4},{7,5},{8,10},{9,11},{10,... | collective-permute-start | bytes 786440 | tf_op jit(solution)/shard_map/ppermute | solution.py:220
  50.4 1.2 %convert_add_fusion = f32[2,256,512]{2,1,0:T(8,128)S(1)} fusion(f32[2,256,512]{2,1,0:T(8,128)S(1)} %get-tuple-element.21, bf16[2,256,512]{2,1,0:T(8,128)(2,1)} %collective-permute-done.11), kind=kLoop, calls=%fused_computation | loop fusion | flops 524288 | bytes 2621440 | tf_op jit(solution)/shard_map/add | solution.py:243
  52.3 5.7 %collective-permute-done.7 = bf16[1,256,512]{2,1,0:T(8,128)(2,1)S(1)} collective-permute-done((bf16[1,256,512]{2,1,0:T(8,128)(2,1)S(1)}, bf16[1,256,512]{2,1,0:T(8,128)(2,1)S(1)}, u32[]{:S(2)}, u32[]{:S(2)}) %collective-permute-start.7) | collective-permute-done | bytes 262176 | tf_op jit(solution)/shard_map/ppermute | solution.py:220
  58.1 2.4 %collective-permute-start.8 = (bf16[128,512]{1,0:T(8,128)(2,1)S(1)}, bf16[128,512]{1,0:T(8,128)(2,1)S(1)}, u32[]{:S(2)}, u32[]{:S(2)}) collective-permute-start(bf16[128,512]{1,0:T(8,128)(2,1)S(1)} %fusion.2), channel_id=1, source_target_pairs={{0,4},{4,0},{8,12},{12,8},{1,5},{5,1},{9,13},{13,9},{2,6},{6,2},{1... | collective-permute-start | bytes 393224 | tf_op jit(solution)/shard_map/ppermute | solution.py:220
  60.5 2.7 %collective-permute-done.12 = bf16[1,256,512]{2,1,0:T(8,128)(2,1)S(1)} collective-permute-done((bf16[1,256,512]{2,1,0:T(8,128)(2,1)S(1)}, bf16[1,256,512]{2,1,0:T(8,128)(2,1)S(1)}, u32[]{:S(2)}, u32[]{:S(2)}) %collective-permute-start.12) | collective-permute-done | bytes 262176 | tf_op jit(solution)/shard_map/ppermute | solution.py:220
  63.3 0.9 %collective-permute-start.13 = (bf16[128,512]{1,0:T(8,128)(2,1)S(1)}, bf16[128,512]{1,0:T(8,128)(2,1)S(1)}, u32[]{:S(2)}, u32[]{:S(2)}) collective-permute-start(bf16[128,512]{1,0:T(8,128)(2,1)S(1)} %fusion.3), channel_id=1, source_target_pairs={{0,4},{4,0},{8,12},{12,8},{1,5},{5,1},{9,13},{13,9},{2,6},{6,2},{1... | collective-permute-start | bytes 393224 | tf_op jit(solution)/shard_map/ppermute | solution.py:220
  64.3 2.1 %collective-permute-start.9 = (bf16[128,512]{1,0:T(8,128)(2,1)S(1)}, bf16[128,512]{1,0:T(8,128)(2,1)S(1)}, u32[]{:S(2)}, u32[]{:S(2)}) collective-permute-start(bf16[128,512]{1,0:T(8,128)(2,1)S(1)} %fusion.1), channel_id=1, source_target_pairs={{0,12},{4,8},{8,4},{12,0},{1,13},{5,9},{9,5},{13,1},{2,14},{6,10},... | collective-permute-start | bytes 393224 | tf_op jit(solution)/shard_map/ppermute | solution.py:220
  66.4 3.1 %collective-permute-done.13 = bf16[128,512]{1,0:T(8,128)(2,1)S(1)} collective-permute-done((bf16[128,512]{1,0:T(8,128)(2,1)S(1)}, bf16[128,512]{1,0:T(8,128)(2,1)S(1)}, u32[]{:S(2)}, u32[]{:S(2)}) %collective-permute-start.13) | collective-permute-done | bytes 131104 | tf_op jit(solution)/shard_map/ppermute | solution.py:220
  69.6 1.8 %collective-permute-start.14 = (bf16[128,512]{1,0:T(8,128)(2,1)S(1)}, bf16[128,512]{1,0:T(8,128)(2,1)S(1)}, u32[]{:S(2)}, u32[]{:S(2)}) collective-permute-start(bf16[128,512]{1,0:T(8,128)(2,1)S(1)} %fusion), channel_id=1, source_target_pairs={{0,12},{4,8},{8,4},{12,0},{1,13},{5,9},{9,5},{13,1},{2,14},{6,10},... | collective-permute-start | bytes 393224 | tf_op jit(solution)/shard_map/ppermute | solution.py:220
  72.0 5.2 %collective-permute-start.10 = (bf16[128,512]{1,0:T(8,128)(2,1)S(1)}, bf16[128,512]{1,0:T(8,128)(2,1)S(1)}, u32[]{:S(2)}, u32[]{:S(2)}) collective-permute-start(bf16[128,512]{1,0:T(8,128)(2,1)S(1)} %add_convert_fusion.1), channel_id=1, source_target_pairs={{0,4},{4,0},{8,12},{12,8},{1,5},{5,1},{9,13},{13,9},{2,6},{6,2},{1... | collective-permute-start | bytes 393224 | tf_op jit(solution)/shard_map/ppermute | solution.py:220
  77.3 1.7 %collective-permute-start.15 = (bf16[128,512]{1,0:T(8,128)(2,1)S(1)}, bf16[128,512]{1,0:T(8,128)(2,1)S(1)}, u32[]{:S(2)}, u32[]{:S(2)}) collective-permute-start(bf16[128,512]{1,0:T(8,128)(2,1)S(1)} %add_convert_fusion), channel_id=1, source_target_pairs={{0,4},{4,0},{8,12},{12,8},{1,5},{5,1},{9,13},{13,9},{2,6},{6,2},{1... | collective-permute-start | bytes 393224 | tf_op jit(solution)/shard_map/ppermute | solution.py:220
  79.0 2.6 %collective-permute-done.10 = bf16[128,512]{1,0:T(8,128)(2,1)S(1)} collective-permute-done((bf16[128,512]{1,0:T(8,128)(2,1)S(1)}, bf16[128,512]{1,0:T(8,128)(2,1)S(1)}, u32[]{:S(2)}, u32[]{:S(2)}) %collective-permute-start.10) | collective-permute-done | bytes 131104 | tf_op jit(solution)/shard_map/ppermute | solution.py:220
  81.6 0.7 fusion.4
  83.1 0.9 %pad_maximum_fusion = f32[384,512]{1,0:T(8,128)} fusion(f32[256,512]{1,0:T(8,128)S(1)} %maximum_convert_fusion.1, f32[128,512]{1,0:T(8,128)S(1)} %get-tuple-element.24), kind=kLoop, calls=%fused_computation.2 | loop fusion | flops 196608 | bytes 1572864 | tf_op jit(solution)/shard_map/concatenate | solution.py:394
  (60 shorter events, 7.1 us)
Async XLA Ops:
  6.9 7.2 %collective-permute-start = (bf16[64,512]{1,0:T(8,128)(2,1)S(1)}, bf16[64,512]{1,0:T(8,128)(2,1)S(1)}, u32[]{:S(2)}, u32[]{:S(2)}) collective-permute-start(bf16[64,512]{1,0:T(8,128)(2,1)S(1)} %get-tuple-element.33), channel_id=1, source_target_pairs={{0,0},{4,8},{8,4},{12,12},{1,1},{5,9},{9,5},{13,13},{2,2},{6,10},{... | collective-permute-start | bytes 196616 | tf_op jit(solution)/shard_map/ppermute | solution.py:220
  7.6 8.2 %collective-permute-start.1 = (bf16[64,512]{1,0:T(8,128)(2,1)S(1)}, bf16[64,512]{1,0:T(8,128)(2,1)S(1)}, u32[]{:S(2)}, u32[]{:S(2)}) collective-permute-start(bf16[64,512]{1,0:T(8,128)(2,1)S(1)} %get-tuple-element.34), channel_id=1, source_target_pairs={{0,4},{4,0},{8,12},{12,8},{1,5},{5,1},{9,13},{13,9},{2,6},{6,2},{1... | collective-permute-start | bytes 196616 | tf_op jit(solution)/shard_map/ppermute | solution.py:220
  13.5 5.4 %collective-permute-start.2 = (bf16[64,512]{1,0:T(8,128)(2,1)S(1)}, bf16[64,512]{1,0:T(8,128)(2,1)S(1)}, u32[]{:S(2)}, u32[]{:S(2)}) collective-permute-start(bf16[64,512]{1,0:T(8,128)(2,1)S(1)} %get-tuple-element.32), channel_id=1, source_target_pairs={{0,8},{4,12},{8,0},{12,4},{1,9},{5,13},{9,1},{13,5},{2,10},{6,14},... | collective-permute-start | bytes 196616 | tf_op jit(solution)/shard_map/ppermute | solution.py:220
  18.9 1.4 %copy-start = (bf16[1536,512]{1,0:T(8,128)(2,1)S(1)}, bf16[1536,512]{1,0:T(8,128)(2,1)}, u32[]{:S(2)}) copy-start(bf16[1536,512]{1,0:T(8,128)(2,1)} %win_ref.3) | copy-start | bytes 4718596
  20.3 0.9 %copy-start.4 = (bf16[1,128,512]{2,1,0:T(8,128)(2,1)S(1)}, bf16[1,128,512]{2,1,0:T(8,128)(2,1)}, u32[]{:S(2)}) copy-start(bf16[1,128,512]{2,1,0:T(8,128)(2,1)} %param.10) | copy-start | bytes 393220
  21.2 0.9 %copy-start.9 = (bf16[1,128,512]{2,1,0:T(8,128)(2,1)S(1)}, bf16[1,128,512]{2,1,0:T(8,128)(2,1)}, u32[]{:S(2)}) copy-start(bf16[1,128,512]{2,1,0:T(8,128)(2,1)} %param.12) | copy-start | bytes 393220
  22.1 0.7 copy-start.11
  22.7 1.1 %copy-start.13 = (bf16[1,768,512]{2,1,0:T(8,128)(2,1)S(1)}, bf16[1,768,512]{2,1,0:T(8,128)(2,1)}, u32[]{:S(2)}) copy-start(bf16[1,768,512]{2,1,0:T(8,128)(2,1)} %param.11) | copy-start | bytes 2359300
  23.9 1.0 %copy-start.14 = (bf16[512,512]{1,0:T(8,128)(2,1)S(1)}, bf16[512,512]{1,0:T(8,128)(2,1)}, u32[]{:S(2)}) copy-start(bf16[512,512]{1,0:T(8,128)(2,1)} %refs_6_.1) | copy-start | bytes 1572868
  24.9 0.7 copy-start.15
  26.3 16.7 %copy-start.1 = (bf16[1536,512]{1,0:T(8,128)(2,1)S(1)}, bf16[1536,512]{1,0:T(8,128)(2,1)}, u32[]{:S(2)}) copy-start(bf16[1536,512]{1,0:T(8,128)(2,1)} %win_ref.3) | copy-start | bytes 4718596
  26.3 16.7 %copy-start.10 = (bf16[1,128,512]{2,1,0:T(8,128)(2,1)S(1)}, bf16[1,128,512]{2,1,0:T(8,128)(2,1)}, u32[]{:S(2)}) copy-start(bf16[1,128,512]{2,1,0:T(8,128)(2,1)} %param.12) | copy-start | bytes 393220
  26.3 16.7 %copy-start.12 = (s32[12]{0:T(128)S(1)}, s32[12]{0:T(128)}, u32[]{:S(2)}) copy-start(s32[12]{0:T(128)} %dst_ref.3) | copy-start | bytes 148
  35.2 1.0 %copy-start.2 = (f32[2,256,512]{2,1,0:T(8,128)}, f32[2,256,512]{2,1,0:T(8,128)S(1)}, u32[]{:S(2)}) copy-start(f32[2,256,512]{2,1,0:T(8,128)S(1)} %get-tuple-element.19) | copy-start | bytes 3145732
  36.2 0.7 copy-start.5
  36.9 0.7 copy-start.7
  37.6 9.9 %collective-permute-start.6 = (bf16[2,256,512]{2,1,0:T(8,128)(2,1)}, bf16[2,256,512]{2,1,0:T(8,128)(2,1)}, u32[]{:S(2)}, u32[]{:S(2)}) collective-permute-start(bf16[2,256,512]{2,1,0:T(8,128)(2,1)} %get-tuple-element.20), channel_id=1, source_target_pairs={{0,1},{1,0},{2,3},{3,2},{4,5},{5,4},{6,7},{7,6},{8,9},{9,8},{10,11... | collective-permute-start | bytes 1572872 | tf_op jit(solution)/shard_map/ppermute | solution.py:220
  38.3 6.8 %collective-permute-start.5 = (bf16[64,512]{1,0:T(8,128)(2,1)}, bf16[64,512]{1,0:T(8,128)(2,1)}, u32[]{:S(2)}, u32[]{:S(2)}) collective-permute-start(bf16[64,512]{1,0:T(8,128)(2,1)} %get-tuple-element.29), channel_id=1, source_target_pairs={{0,8},{4,12},{8,0},{12,4},{1,9},{5,13},{9,1},{13,5},{2,10},{6,14},... | collective-permute-start | bytes 196616 | tf_op jit(solution)/shard_map/ppermute | solution.py:220
  38.9 6.2 %collective-permute-start.3 = (bf16[64,512]{1,0:T(8,128)(2,1)}, bf16[64,512]{1,0:T(8,128)(2,1)}, u32[]{:S(2)}, u32[]{:S(2)}) collective-permute-start(bf16[64,512]{1,0:T(8,128)(2,1)} %get-tuple-element.30), channel_id=1, source_target_pairs={{0,4},{4,0},{8,12},{12,8},{1,5},{5,1},{9,13},{13,9},{2,6},{6,2},{1... | collective-permute-start | bytes 196616 | tf_op jit(solution)/shard_map/ppermute | solution.py:220
  40.8 4.3 %collective-permute-start.4 = (bf16[64,512]{1,0:T(8,128)(2,1)}, bf16[64,512]{1,0:T(8,128)(2,1)}, u32[]{:S(2)}, u32[]{:S(2)}) collective-permute-start(bf16[64,512]{1,0:T(8,128)(2,1)} %get-tuple-element.31), channel_id=1, source_target_pairs={{0,0},{4,8},{8,4},{12,12},{1,1},{5,9},{9,5},{13,13},{2,2},{6,10},{... | collective-permute-start | bytes 196616 | tf_op jit(solution)/shard_map/ppermute | solution.py:220
  42.9 7.5 %collective-permute-start.11 = (bf16[2,256,512]{2,1,0:T(8,128)(2,1)}, bf16[2,256,512]{2,1,0:T(8,128)(2,1)}, u32[]{:S(2)}, u32[]{:S(2)}) collective-permute-start(bf16[2,256,512]{2,1,0:T(8,128)(2,1)} %get-tuple-element.22), channel_id=1, source_target_pairs={{0,1},{1,0},{2,3},{3,2},{4,5},{5,4},{6,7},{7,6},{8,9},{9,8},{10,11... | collective-permute-start | bytes 1572872 | tf_op jit(solution)/shard_map/ppermute | solution.py:220
  43.0 2.1 %copy-start.6 = (f32[128,512]{1,0:T(8,128)S(1)}, f32[128,512]{1,0:T(8,128)}, u32[]{:S(2)}) copy-start(f32[128,512]{1,0:T(8,128)} %copy-done.5) | copy-start | bytes 786436
  43.0 2.1 %copy-start.8 = (f32[128,512]{1,0:T(8,128)S(1)}, f32[128,512]{1,0:T(8,128)}, u32[]{:S(2)}) copy-start(f32[128,512]{1,0:T(8,128)} %copy-done.7) | copy-start | bytes 786436
  45.1 2.5 %copy-start.3 = (f32[2,256,512]{2,1,0:T(8,128)S(1)}, f32[2,256,512]{2,1,0:T(8,128)}, u32[]{:S(2)}) copy-start(f32[2,256,512]{2,1,0:T(8,128)} %copy-done.2) | copy-start | bytes 3145732
  48.8 9.2 %collective-permute-start.7 = (bf16[1,256,512]{2,1,0:T(8,128)(2,1)S(1)}, bf16[1,256,512]{2,1,0:T(8,128)(2,1)S(1)}, u32[]{:S(2)}, u32[]{:S(2)}) collective-permute-start(bf16[1,256,512]{2,1,0:T(8,128)(2,1)S(1)} %dynamic-slice_convert_fusion.1), channel_id=1, source_target_pairs={{0,2},{1,3},{2,0},{3,1},{4,6},{5,7},{6,4},{7,5},{8,10},{9,11},{10,... | collective-permute-start | bytes 786440 | tf_op jit(solution)/shard_map/ppermute | solution.py:220
  51.7 11.6 %collective-permute-start.12 = (bf16[1,256,512]{2,1,0:T(8,128)(2,1)S(1)}, bf16[1,256,512]{2,1,0:T(8,128)(2,1)S(1)}, u32[]{:S(2)}, u32[]{:S(2)}) collective-permute-start(bf16[1,256,512]{2,1,0:T(8,128)(2,1)S(1)} %dynamic-slice_convert_fusion), channel_id=1, source_target_pairs={{0,2},{1,3},{2,0},{3,1},{4,6},{5,7},{6,4},{7,5},{8,10},{9,11},{10,... | collective-permute-start | bytes 786440 | tf_op jit(solution)/shard_map/ppermute | solution.py:220
  58.1 6.2 %collective-permute-start.8 = (bf16[128,512]{1,0:T(8,128)(2,1)S(1)}, bf16[128,512]{1,0:T(8,128)(2,1)S(1)}, u32[]{:S(2)}, u32[]{:S(2)}) collective-permute-start(bf16[128,512]{1,0:T(8,128)(2,1)S(1)} %fusion.2), channel_id=1, source_target_pairs={{0,4},{4,0},{8,12},{12,8},{1,5},{5,1},{9,13},{13,9},{2,6},{6,2},{1... | collective-permute-start | bytes 393224 | tf_op jit(solution)/shard_map/ppermute | solution.py:220
  63.3 6.2 %collective-permute-start.13 = (bf16[128,512]{1,0:T(8,128)(2,1)S(1)}, bf16[128,512]{1,0:T(8,128)(2,1)S(1)}, u32[]{:S(2)}, u32[]{:S(2)}) collective-permute-start(bf16[128,512]{1,0:T(8,128)(2,1)S(1)} %fusion.3), channel_id=1, source_target_pairs={{0,4},{4,0},{8,12},{12,8},{1,5},{5,1},{9,13},{13,9},{2,6},{6,2},{1... | collective-permute-start | bytes 393224 | tf_op jit(solution)/shard_map/ppermute | solution.py:220
  64.3 7.6 %collective-permute-start.9 = (bf16[128,512]{1,0:T(8,128)(2,1)S(1)}, bf16[128,512]{1,0:T(8,128)(2,1)S(1)}, u32[]{:S(2)}, u32[]{:S(2)}) collective-permute-start(bf16[128,512]{1,0:T(8,128)(2,1)S(1)} %fusion.1), channel_id=1, source_target_pairs={{0,12},{4,8},{8,4},{12,0},{1,13},{5,9},{9,5},{13,1},{2,14},{6,10},... | collective-permute-start | bytes 393224 | tf_op jit(solution)/shard_map/ppermute | solution.py:220
  69.6 7.6 %collective-permute-start.14 = (bf16[128,512]{1,0:T(8,128)(2,1)S(1)}, bf16[128,512]{1,0:T(8,128)(2,1)S(1)}, u32[]{:S(2)}, u32[]{:S(2)}) collective-permute-start(bf16[128,512]{1,0:T(8,128)(2,1)S(1)} %fusion), channel_id=1, source_target_pairs={{0,12},{4,8},{8,4},{12,0},{1,13},{5,9},{9,5},{13,1},{2,14},{6,10},... | collective-permute-start | bytes 393224 | tf_op jit(solution)/shard_map/ppermute | solution.py:220
  72.0 9.5 %collective-permute-start.10 = (bf16[128,512]{1,0:T(8,128)(2,1)S(1)}, bf16[128,512]{1,0:T(8,128)(2,1)S(1)}, u32[]{:S(2)}, u32[]{:S(2)}) collective-permute-start(bf16[128,512]{1,0:T(8,128)(2,1)S(1)} %add_convert_fusion.1), channel_id=1, source_target_pairs={{0,4},{4,0},{8,12},{12,8},{1,5},{5,1},{9,13},{13,9},{2,6},{6,2},{1... | collective-permute-start | bytes 393224 | tf_op jit(solution)/shard_map/ppermute | solution.py:220
  77.3 5.7 %collective-permute-start.15 = (bf16[128,512]{1,0:T(8,128)(2,1)S(1)}, bf16[128,512]{1,0:T(8,128)(2,1)S(1)}, u32[]{:S(2)}, u32[]{:S(2)}) collective-permute-start(bf16[128,512]{1,0:T(8,128)(2,1)S(1)} %add_convert_fusion), channel_id=1, source_target_pairs={{0,4},{4,0},{8,12},{12,8},{1,5},{5,1},{9,13},{13,9},{2,6},{6,2},{1... | collective-permute-start | bytes 393224 | tf_op jit(solution)/shard_map/ppermute | solution.py:220
  (1 other events, 0.7 us)

commit v3 on v2

v3 whole, which is shorter than its diff:
```python
import functools

import jax
import jax.numpy as jnp
from jax import lax
from jax.experimental import pallas as pl
from jax.experimental.pallas import tpu as pltpu
from jax.sharding import PartitionSpec as P

OFFSET_LIST = (1, -1, 2, -2)
EPSILON = 1e-05
VMEM = pl.BlockSpec(memory_space=pltpu.VMEM)
HBM = pl.BlockSpec(memory_space=pltpu.HBM)
SMEM = pl.BlockSpec(memory_space=pltpu.SMEM)
ANY = pl.BlockSpec(memory_space=pl.ANY)
F32 = jnp.float32
BF16 = jnp.bfloat16


def dot(left, right):
    return jnp.dot(left, right, preferred_element_type=F32)


def dot_t(left, right):
    return lax.dot_general(left, right, (((1,), (1,)), ((), ())), preferred_element_type=F32)


def t_dot(left, right):
    return lax.dot_general(left, right, (((0,), (0,)), ((), ())), preferred_element_type=F32)


def row_mean(array):
    return jnp.sum(array, axis=1, keepdims=True) * (1.0 / array.shape[1])


def rows_of(ref, block, size):
    return ref[pl.ds(pl.multiple_of(block * size, size), size), :]


def load_small(source, target, sem):
    copy = pltpu.make_async_copy(source, target, sem)
    copy.start()
    return copy


def boundary_places(boundary_ref, part, four):
    taken = [boundary_ref[0, which] for which in range(4)]
    if not four:
        return taken
    even = part % 2 == 0
    return [
        jnp.where(even, taken[0], taken[1]),
        jnp.where(even, taken[1], taken[0]),
        jnp.where(part < 2, taken[2], taken[3]),
    ]


def arrival_places(part, four, arrivals):
    if not four:
        return list(range(arrivals))
    even = part % 2 == 0
    return [jnp.where(even, 1, 0), jnp.where(even, 0, 1), 2]


def pick_kernel(four, block, boundary_hbm, node_hbm, *refs):
    count = 3 if four else 4
    outs = refs[:count]
    boundary_ref, small_sem, sems = refs[count:]
    load_small(boundary_hbm, boundary_ref, small_sem).wait()
    copies = []
    for which, place in enumerate(boundary_places(boundary_ref, lax.axis_index("dom"), four)):
        spot = pl.ds(pl.multiple_of(place * block, block), block)
        copies.append(pltpu.make_async_copy(node_hbm.at[spot, :], outs[which], sems.at[which]))
        copies[-1].start()
    for copy in copies:
        copy.wait()


def prep_kernel(
    parts,
    arrivals,
    src_hbm,
    dst_hbm,
    slot_hbm,
    node_hbm,
    edge_hbm,
    cot_hbm,
    win_hbm,
    wout_hbm,
    node_ref,
    edge_ref,
    cot_ref,
    win_ref,
    wout_ref,
    pre_ref,
    mid_ref,
    hot_ref,
    hot_turned,
    src_ref,
    dst_ref,
    slot_ref,
    recv_ref,
    sems,
):
    tiles, block = slot_ref.shape
    nodes, latent = node_ref.shape
    owned = nodes // block
    extent = hot_turned.shape[0]
    pairs = (
        (src_hbm, src_ref),
        (dst_hbm, dst_ref),
        (slot_hbm, slot_ref),
        (node_hbm, node_ref),
        (win_hbm.at[2 * latent :, :], win_ref.at[2 * latent :, :]),
        (win_hbm.at[:latent, :], win_ref.at[:latent, :]),
        (edge_hbm, edge_ref),
        (cot_hbm, cot_ref),
        (win_hbm.at[latent : 2 * latent, :], win_ref.at[latent : 2 * latent, :]),
        (wout_hbm, wout_ref),
    )
    copies = [load_small(*pair, sems.at[number]) for number, pair in enumerate(pairs)]
    part = lax.axis_index("dom")
    for copy in copies[:3]:
        copy.wait()
    index = lax.broadcasted_iota(jnp.int32, (extent, 2 * block), 0)
    first = lax.broadcasted_iota(jnp.int32, (1, 2 * block), 1) < block
    for tile in range(0, tiles, 2):
        wanted = []
        for member in (tile, tile + 1):
            source = src_ref[member]
            which = source - owned
            reach = jnp.where(which >= 2, 2, 1)
            partner = part - jnp.where(which % 2 == 1, -reach, reach)
            exists = (source < owned) | ((partner >= 0) & (partner < parts))
            place = jnp.minimum(source, owned + arrivals - 1)
            wanted.append(jnp.where(exists, place * block, -2 * extent))
        slots = jnp.concatenate(
            [slot_ref[tile : tile + 1, :], slot_ref[tile + 1 : tile + 2, :]], axis=1
        )
        row = slots + jnp.where(first, wanted[0], wanted[1])
        hot = jnp.where(index == row, 1.0, 0.0)
        at = slice(tile * block, (tile + 2) * block)
        hot_turned[:, at] = hot.astype(BF16)
        hot_ref[at, :] = hot.T.astype(BF16)
    copies[3].wait()
    copies[4].wait()
    recv_ref[...] = dot(node_ref[...], win_ref[2 * latent :, :])
    copies[5].wait()
    copies[6].wait()
    group = 4 if tiles % 4 == 0 else 2
    for tile in range(0, tiles, group):
        rows = slice(tile * block, (tile + group) * block)
        received = jnp.concatenate(
            [rows_of(recv_ref, dst_ref[t], block) for t in range(tile, tile + group)], axis=0
        )
        pre_ref[rows, :] = dot(edge_ref[rows, :], win_ref[:latent, :]) + received
    copies[7].wait()
    cot = cot_ref[...].astype(F32)
    mid_ref[...] = cot - row_mean(cot)
    copies[8].wait()
    copies[9].wait()


def edge_kernel(
    ways,
    arrivals,
    four,
    block,
    dst_hbm,
    count_ref,
    *refs,
):
    arrived = refs[:arrivals]
    (
        node_ref,
        edge_ref,
        win_ref,
        wout_ref,
        pre_ref,
        mid_ref,
        hot_ref,
        hot_turned,
        agg_hbm,
        gpre_ref,
        own_sums,
        recv_sums,
    ) = refs[arrivals : arrivals + 12]
    back_sums = refs[arrivals + 12 : 2 * arrivals + 12]
    away_a, kept_a, away_b, kept_b = refs[2 * arrivals + 12 : 2 * arrivals + 16]
    (
        dst_ref,
        ext_ref,
        act_ref,
        proj_ref,
        agg_ref,
        agg_bf16,
        sums_ref,
        sems,
    ) = refs[2 * arrivals + 16 :]
    nodes, latent = node_ref.shape
    edges = edge_ref.shape[0]
    tiles = edges // block
    owned = nodes // block
    part = lax.axis_index("dom")
    bit = lax.axis_index("dp") % 2
    dst_copy = load_small(dst_hbm, dst_ref, sems.at[0])
    places = arrival_places(part, four, arrivals)

    ext_ref[:nodes, :] = node_ref[...]
    for which in range(arrivals):
        at = pl.multiple_of((owned + places[which]) * block, block)
        ext_ref[pl.ds(at, block), :] = arrived[which][...]
    filled = nodes + arrivals * block
    if filled < ext_ref.shape[0]:
        ext_ref[filled:, :] = jnp.zeros((ext_ref.shape[0] - filled, latent), BF16)
    agg_ref[...] = jnp.zeros_like(agg_ref)
    recv_sums[...] = jnp.zeros_like(recv_sums)

    group = 4 if tiles % 4 == 0 else 1
    span = group * block
    for first in range(0, tiles, group):
        rows = slice(first * block, first * block + span)
        members = range(first, first + group)
        edge_rows = edge_ref[rows, :]
        senders = dot(hot_ref[rows, :], ext_ref[...]).astype(BF16)
        preact = pre_ref[rows, :] + dot(senders, win_ref[latent : 2 * latent, :])
        gate = 0.5 * jnp.tanh(0.5 * preact) + 0.5
        activated = preact * gate
        slope = gate + activated * (1.0 - gate)
        activated = activated.astype(BF16)
        act_ref[rows, :] = activated
        projected = dot(activated, wout_ref[...])
        centered = projected - row_mean(projected)
        inv_scale = lax.rsqrt(row_mean(centered * centered) + EPSILON)
        message = centered * inv_scale
        updated = edge_rows.astype(F32) + message
        if first == 0:
            dst_copy.wait()
        upstream = []
        for number, tile in enumerate(members):
            live = jnp.where(tile < count_ref[0], 1.0, 0.0)
            target = pl.ds(pl.multiple_of(dst_ref[tile] * block, block), block)
            agg_ref[target, :] += updated[number * block : (number + 1) * block] * live
            upstream.append(mid_ref[target, :] * live)
        upstream = jnp.concatenate(upstream, axis=0)
        grad_project = inv_scale * (upstream - message * row_mean(upstream * message))
        grad_project = grad_project.astype(BF16)
        proj_ref[rows, :] = grad_project
        grad_pre = (dot_t(grad_project, wout_ref[...]) * slope).astype(BF16)
        gpre_ref[rows, :] = grad_pre
        for number, tile in enumerate(members):
            mine = grad_pre[number * block : (number + 1) * block]
            target = pl.ds(pl.multiple_of(dst_ref[tile] * block, block), block)
            recv_sums[target, :] += mine.astype(F32)

    agg_bf16[...] = agg_ref[...].astype(BF16)
    agg_copy = load_small(agg_bf16, agg_hbm, sems.at[1])
    sums_ref[...] = dot(hot_turned[...], gpre_ref[...])
    own_sums[...] = sums_ref[:nodes, :]
    for which in range(arrivals):
        at = pl.multiple_of((owned + places[which]) * block, block)
        back_sums[which][...] = sums_ref[pl.ds(at, block), :].astype(BF16)

    unit = latent // ways

    def put(owner, spot, value):
        away, kept = (away_a, kept_a) if spot < 2 else (away_b, kept_b)
        where = slice((spot % 2) * unit, (spot % 2 + 1) * unit)

        @pl.when(bit == owner % 2)
        def _():
            kept[owner // 2, where, :] = value

        @pl.when(bit != owner % 2)
        def _():
            away[owner // 2, where, :] = value.astype(BF16)

    step = 256
    for start in range(0, latent, step):
        value = t_dot(act_ref[:, start : start + step], proj_ref[...])
        for at in range(0, step, unit):
            put((start + at) // unit, 0, value[at : at + unit])
    sections = (
        (edge_ref, gpre_ref),
        (ext_ref, sums_ref),
        (node_ref, recv_sums),
    )
    for number, (left, right) in enumerate(sections):
        for start in range(0, latent, step):
            value = t_dot(left[:, start : start + step], right[...].astype(BF16))
            for at in range(0, step, unit):
                spot = (number * latent + start + at) // unit
                put(spot // 3, 1 + spot % 3, value[at : at + unit])
    agg_copy.wait()


def edge_grad_kernel(
    block, dst_hbm, count_ref, after, gpre_ref, cot_ref, win_ref, out_ref, dst_ref, sem
):
    latent = cot_ref.shape[1]
    tiles = gpre_ref.shape[0] // block
    group = 4 if tiles % 4 == 0 else 1
    load_small(dst_hbm, dst_ref, sem).wait()
    for first in range(0, tiles, group):
        rows = slice(first * block, (first + group) * block)
        upstream = jnp.concatenate(
            [
                rows_of(cot_ref, dst_ref[t], block).astype(F32)
                * jnp.where(t < count_ref[0], 1.0, 0.0)
                for t in range(first, first + group)
            ],
            axis=0,
        )
        out_ref[rows, :] = (dot_t(gpre_ref[rows, :], win_ref[:latent, :]) + upstream).astype(BF16)


def node_grad_kernel(arrivals, four, boundary_hbm, after, own_ref, recv_ref, win_ref, *refs):
    returned = refs[:arrivals]
    out_ref, total_ref, boundary_ref, sem = refs[arrivals:]
    latent = own_ref.shape[1]
    block = returned[0].shape[0]
    copy = load_small(boundary_hbm, boundary_ref, sem)
    total_ref[...] = own_ref[...]
    copy.wait()
    for which, place in enumerate(boundary_places(boundary_ref, lax.axis_index("dom"), four)):
        spot = pl.ds(pl.multiple_of(place * block, block), block)
        total_ref[spot, :] += returned[which][...].astype(F32)

    def wide_dot(value, weight):
        high = value.astype(BF16)
        low = (value - high.astype(F32)).astype(BF16)
        return dot_t(high, weight) + dot_t(low, weight)

    out_ref[...] = (
        wide_dot(total_ref[...], win_ref[latent : 2 * latent, :])
        + wide_dot(recv_ref[...], win_ref[2 * latent :, :])
    ).astype(BF16)


def last_kernel(own_a, other_a, own_b, other_b, in_ref, out_ref):
    unit = out_ref.shape[0]
    part = lax.axis_index("dom")
    inner = (part == 1) | (part == 2)

    def write(low_a, high_a, low_b, high_b):
        out_ref[...] = low_a[...].astype(F32)
        in_ref[:unit, :] = high_a[...].astype(F32)
        in_ref[unit : 2 * unit, :] = low_b[...].astype(F32)
        in_ref[2 * unit :, :] = high_b[...].astype(F32)

    @pl.when(inner)
    def _():
        write(own_a, other_a, own_b, other_b)

    @pl.when(jnp.logical_not(inner))
    def _():
        write(other_a, own_a, other_b, own_b)


def swap(array, axis, partner):
    devices = lax.axis_size(axis)
    return lax.ppermute(array, axis, [(i, partner(i)) for i in range(devices)])


def from_behind(array, axis, by):
    devices = lax.axis_size(axis)
    pairs = [(i, i + by) for i in range(devices) if 0 <= i + by < devices]
    return lax.ppermute(array, axis, pairs)


def partners_of_four(which):
    return ((1, 0, 3, 2), (0, 2, 1, 3), (2, 3, 0, 1))[which]


def exchange_of_four(first, second, third):
    return [
        swap(array, "dom", lambda i, which=which: partners_of_four(which)[i])
        for which, array in enumerate((first, second, third))
    ]


def sum_over_dp(away, kept):
    devices = lax.axis_size("dp")
    index = lax.axis_index("dp")
    bit = 1
    while True:
        came = swap(away, "dp", lambda i, bit=bit: i ^ bit)
        bit *= 2
        if bit >= devices:
            return kept[0] + came[0].astype(F32), away
        mine = (index // bit) % 2

        def half(array, side):
            split = array.reshape((-1, 2) + array.shape[1:])
            return lax.dynamic_index_in_dim(split, side, 1, keepdims=False)

        away = (half(kept, 1 - mine) + half(came, 1 - mine).astype(F32)).astype(BF16)
        kept = half(kept, mine) + half(came, mine).astype(F32)


def sum_over_four(rows):
    index = lax.axis_index("dom")
    inner = (index == 1) | (index == 2)
    low, high = jnp.split(rows, 2, axis=0)
    away = jnp.where(inner, high, low).astype(BF16)
    kept = jnp.where(inner, low, high)
    kept = (kept + swap(away, "dom", lambda i: i ^ 1).astype(F32)).astype(BF16)
    kept = (kept.astype(F32) + swap(kept, "dom", lambda i: 3 - i).astype(F32)).astype(BF16)
    return kept, swap(kept, "dom", lambda i: i ^ 1)


def sum_over_dom(rows):
    piece = lax.psum_scatter(rows, "dom", scatter_dimension=0, tiled=True)
    return lax.all_gather(piece, "dom", axis=0, tiled=True)


def in_vmem(array):
    return pltpu.with_memory_space_constraint(array, pltpu.VMEM)


def in_hbm(array):
    return pltpu.with_memory_space_constraint(array, pltpu.HBM)


def body(
    node_latents,
    edge_latents,
    agg_cotangent,
    weight_in,
    weight_out,
    boundary,
    tile_src,
    tile_dst,
    edge_slot,
    tile_count,
):
    tiles, block = edge_slot.shape
    edges, latent = edge_latents.shape[1:]
    nodes = node_latents.shape[1]
    parts = lax.axis_size("dom")
    ways = lax.axis_size("dp")
    four = parts == 4
    arrivals = 3 if four else 4
    boundary = in_hbm(boundary)
    tile_dst = in_hbm(tile_dst)
    node_rows = in_hbm(node_latents[0])
    block_shape = pltpu.VMEM((block, latent), BF16)
    small = pltpu.CompilerParams(vmem_limit_bytes=8 * 1024 * 1024)

    sent = pl.pallas_call(
        functools.partial(pick_kernel, four, block),
        out_shape=(block_shape,) * arrivals,
        in_specs=[HBM] * 2,
        out_specs=(VMEM,) * arrivals,
        scratch_shapes=[
            pltpu.SMEM(boundary.shape, jnp.int32),
            pltpu.SemaphoreType.DMA,
            pltpu.SemaphoreType.DMA((arrivals,)),
        ],
        compiler_params=small,
        cost_estimate=pl.CostEstimate(flops=0, bytes_accessed=400_000, transcendentals=0),
        name="pick_blocks",
    )(boundary, node_rows)
    if four:
        came = exchange_of_four(*sent)
    else:
        came = [from_behind(sent[which], "dom", OFFSET_LIST[which]) for which in range(4)]
    unit = latent // ways
    half = ways // 2
    extent = -(-(nodes + arrivals * block) // 128) * 128

    node_v, edge_v, cot_v, win_v, wout_v, pre, mid, hot, turned = pl.pallas_call(
        functools.partial(prep_kernel, parts, arrivals),
        out_shape=(
            pltpu.VMEM((nodes, latent), BF16),
            pltpu.VMEM((edges, latent), BF16),
            pltpu.VMEM((nodes, latent), BF16),
            pltpu.VMEM(weight_in.shape, BF16),
            pltpu.VMEM(weight_out.shape, BF16),
            pltpu.VMEM((edges, latent), F32),
            pltpu.VMEM((nodes, latent), F32),
            pltpu.VMEM((edges, extent), BF16),
            pltpu.VMEM((extent, edges), BF16),
        ),
        in_specs=[HBM] * 8,
        out_specs=(VMEM,) * 9,
        scratch_shapes=[
            pltpu.SMEM((tiles,), jnp.int32),
            pltpu.SMEM((tiles,), jnp.int32),
            pltpu.VMEM((tiles, block), jnp.int32),
            pltpu.VMEM((nodes, latent), F32),
            pltpu.SemaphoreType.DMA((10,)),
        ],
        compiler_params=small,
        cost_estimate=pl.CostEstimate(
            flops=2 * edges * latent * latent, bytes_accessed=8_000_000, transcendentals=0
        ),
        name="prepare",
    )(
        in_hbm(tile_src),
        tile_dst,
        in_hbm(edge_slot),
        node_rows,
        in_hbm(edge_latents[0]),
        in_hbm(agg_cotangent[0]),
        in_hbm(weight_in),
        in_hbm(weight_out),
    )
    outs = pl.pallas_call(
        functools.partial(edge_kernel, ways, arrivals, four, block),
        out_shape=(
            jax.ShapeDtypeStruct((nodes, latent), BF16),
            pltpu.VMEM((edges, latent), BF16),
            pltpu.VMEM((nodes, latent), F32),
            pltpu.VMEM((nodes, latent), F32),
            *[block_shape] * arrivals,
            pltpu.VMEM((half, 2 * unit, latent), BF16),
            pltpu.VMEM((half, 2 * unit, latent), F32),
            pltpu.VMEM((half, 2 * unit, latent), BF16),
            pltpu.VMEM((half, 2 * unit, latent), F32),
        ),
        in_specs=[HBM, SMEM] + [VMEM] * (8 + arrivals),
        out_specs=(HBM,) + (VMEM,) * (7 + arrivals),
        scratch_shapes=[
            pltpu.SMEM((tiles,), jnp.int32),
            pltpu.VMEM((extent, latent), BF16),
            pltpu.VMEM((edges, latent), BF16),
            pltpu.VMEM((edges, latent), BF16),
            pltpu.VMEM((nodes, latent), F32),
            pltpu.VMEM((nodes, latent), BF16),
            pltpu.VMEM((extent, latent), F32),
            pltpu.SemaphoreType.DMA((2,)),
        ],
        compiler_params=pltpu.CompilerParams(vmem_limit_bytes=16 * 1024 * 1024),
        cost_estimate=pl.CostEstimate(
            flops=14 * edges * latent * latent,
            bytes_accessed=12_000_000,
            transcendentals=edges * latent,
        ),
        name="edge_block",
    )(
        tile_dst,
        tile_count,
        *[
            in_vmem(array)
            for array in (*came, node_v, edge_v, win_v, wout_v, pre, mid, hot, turned)
        ],
    )
    agg, grad_pre, own_sums, recv_sums = outs[:4]
    back_sums = outs[4 : 4 + arrivals]
    away_a, kept_a, away_b, kept_b = outs[4 + arrivals :]
    rows_a, sent_a = sum_over_dp(away_a, kept_a)
    rows_b, _ = sum_over_dp(away_b, kept_b)
    if four:
        returned = exchange_of_four(*back_sums)
    else:
        returned = [
            from_behind(back_sums[which], "dom", -OFFSET_LIST[which]) for which in range(4)
        ]
    edge_grad = pl.pallas_call(
        functools.partial(edge_grad_kernel, block),
        out_shape=jax.ShapeDtypeStruct((edges, latent), BF16),
        in_specs=[HBM, SMEM, ANY] + [VMEM] * 3,
        out_specs=VMEM,
        scratch_shapes=[
            pltpu.SMEM((tiles,), jnp.int32),
            pltpu.SemaphoreType.DMA,
        ],
        compiler_params=small,
        cost_estimate=pl.CostEstimate(
            flops=2 * edges * latent * latent, bytes_accessed=3_000_000, transcendentals=0
        ),
        name="edge_grads",
    )(tile_dst, tile_count, sent_a, in_vmem(grad_pre), in_vmem(cot_v), in_vmem(win_v))
    node_out = pl.pallas_call(
        functools.partial(node_grad_kernel, arrivals, four),
        out_shape=jax.ShapeDtypeStruct((nodes, latent), BF16),
        in_specs=[HBM, ANY] + [VMEM] * (3 + arrivals),
        out_specs=VMEM,
        scratch_shapes=[
            pltpu.VMEM((nodes, latent), F32),
            pltpu.SMEM(boundary.shape, jnp.int32),
            pltpu.SemaphoreType.DMA,
        ],
        compiler_params=small,
        cost_estimate=pl.CostEstimate(
            flops=8 * nodes * latent * latent, bytes_accessed=2_000_000, transcendentals=0
        ),
        name="node_grads",
    )(
        boundary,
        sent_a,
        *[in_vmem(array) for array in (own_sums, recv_sums, win_v, *returned)],
    )
    if four:
        w_in_grad, w_out_grad = pl.pallas_call(
            last_kernel,
            out_shape=(
                jax.ShapeDtypeStruct((3 * unit, latent), F32),
                jax.ShapeDtypeStruct((unit, latent), F32),
            ),
            in_specs=[VMEM] * 4,
            out_specs=(VMEM,) * 2,
            compiler_params=small,
            cost_estimate=pl.CostEstimate(flops=0, bytes_accessed=1_500_000, transcendentals=0),
            name="widen",
        )(*sum_over_four(rows_a), *sum_over_four(rows_b))
    else:
        sum_a, sum_b = sum_over_dom(rows_a), sum_over_dom(rows_b)
        w_in_grad = jnp.concatenate([sum_a[unit:], sum_b], axis=0)
        w_out_grad = sum_a[:unit]
    return (agg[None], edge_grad[None], node_out[None], w_in_grad, w_out_grad)


def solution(mesh):
    in_specs = (
        P(("group", "dp"), "dom", None),
        P(("group", "dp"), "dom", None),
        P(("group", "dp"), "dom", None),
        P(),
        P(),
        P(("group", "dom"), None),
        P(("group", "dom")),
        P(("group", "dom")),
        P(("group", "dom"), None),
        P(("group", "dom")),
    )
    out_specs = (
        P(("group", "dp"), "dom", None),
        P(("group", "dp"), "dom", None),
        P(("group", "dp"), "dom", None),
        P(("group", "dp"), None),
        P(("group", "dp"), None),
    )
    return jax.shard_map(body, mesh=mesh, in_specs=in_specs, out_specs=out_specs, check_vma=False)
```

time: 84.6 us -> 74.3 us (0.88)
  local copies, waits for them, and re-layouts: 13 us -> 3.79 us
  between operations: 5.41 us -> 1.49 us
  Pallas kernels: 13.5 us -> 17.2 us
  waiting for transfers between devices: 20 us -> 16.5 us
  starting transfers between devices: 27.6 us -> 30.2 us
    unnamed x34 -> x18, local copies, waits for them, and re-layouts: 9.8 us -> 3.79 us
    pallas_call x2 -> x5, Pallas kernels: 11.4 us -> 15.1 us  [the longest x1 7.94 us: body(): pl.pallas_call(functools.partial(edge_kernel, ways, arrivals, four, block...]
    ppermute x16, waiting for transfers between devices: 20 us -> 16.5 us  [swap(): return lax.ppermute(array, axis, [(i, partner(i)) for i in range(devices)])]
    ppermute x16, starting transfers between devices: 27.6 us -> 30.2 us  [swap(): return lax.ppermute(array, axis, [(i, partner(i)) for i in range(devices)])]
    slice x2 -> x0, local copies, waits for them, and re-layouts: 2.14 us -> none  [the longest x1 1.4 us: body(): chosen[3]]
    convert_element_type x8, other arithmetic: 0.34 us -> 2.42 us  [the longest x2 2.19 us: sum_over_dp(): (half(kept, 1 - mine) + half(came, 1 - mine).astype(F32)).astype(BF16)]
    dynamic_slice x1 -> x0, local copies, waits for them, and re-layouts: 0.94 us -> none  [body(): lax.dynamic_slice(node_rows, (i * block, 0), (block, latent))]
    concatenate x1 -> x0, other arithmetic: 0.93 us -> none  [body(): w_in_grad = jnp.concatenate([sum_a[unit:], sum_b], axis=0)]
  transfers between devices with their start and end apart: 16 -> 16, of which waited for: 8 -> 8; matrix products, arithmetic and copies ran while one was open for 5% -> 6% of each run, Pallas kernels for 5% -> 9%
where the time goes in v3:
time: 74.3 us; the launch traced here: 74 us
  starting transfers between devices  30.2 us (41%)
  Pallas kernels  17.2 us (23%)
  waiting for transfers between devices  16.5 us (22%)
  other arithmetic  4.75 us (6%)
  local copies, waits for them, and re-layouts  3.79 us (5%)
  between operations  1.49 us (2%)
    ppermute x16, starting transfers between devices, swap(): return lax.ppermute(array, axis, [(i, partner(i)) for i in range(devices)])  30.2 us
    ppermute x16, waiting for transfers between devices, swap(): return lax.ppermute(array, axis, [(i, partner(i)) for i in range(devices)])  16.5 us
    pallas_call x1, Pallas kernels, body(): pl.pallas_call(functools.partial(edge_kernel, ways, arrivals, four, block...  7.94 us
    unnamed x18, local copies, waits for them, and re-layouts  3.79 us
    add x2, other arithmetic, sum_over_dp(): return (kept[0] + came[0].astype(F32), away)  2.33 us
    pallas_call x1, Pallas kernels, body(): pl.pallas_call(functools.partial(prep_kernel, parts, arrivals), out_shape...  2.32 us
    convert_element_type x2, other arithmetic, sum_over_dp(): (half(kept, 1 - mine) + half(came, 1 - mine).astype(F32)).astype(BF16)  2.19 us
    pallas_call x1, Pallas kernels, body(): pl.pallas_call(functools.partial(edge_grad_kernel, block), out_shape=jax....  2.17 us
  transfers between devices with their start and end apart: 16, of which 8 were waited for; matrix products, arithmetic and copies ran while one was open for 6% of the time, Pallas kernels for 9%

profile of v3, /device:TPU:0, one launch (start us, length us, event | category | flops | bytes accessed | tf_op | source)
XLA Modules:
  0.0 74.0 jit_solution(11541571351756080494)
XLA Ops:
  0.6 1.6 %pick_blocks.1 = (bf16[64,512]{1,0:T(8,128)(2,1)S(1)}, bf16[64,512]{1,0:T(8,128)(2,1)S(1)}, bf16[64,512]{1,0:T(8,128)(2,1)S(1)}) custom-call(s32[1,4]{1,0:T(1,128)} %boundary_hbm.3, bf16[128,512]{1,0:T(8,128)(2,1)} %bitcast.20), custom_call_target="tpu_custom_call" | custom-call | bytes 400000 | tf_op jit(solution)/shard_map/pick_blocks/pallas_call | solution.py:450
  2.3 3.1 %collective-permute-start = (bf16[64,512]{1,0:T(8,128)(2,1)S(1)}, bf16[64,512]{1,0:T(8,128)(2,1)S(1)}, u32[]{:S(2)}, u32[]{:S(2)}) collective-permute-start(bf16[64,512]{1,0:T(8,128)(2,1)S(1)} %get-tuple-element.30), channel_id=1, source_target_pairs={{0,4},{4,0},{8,12},{12,8},{1,5},{5,1},{9,13},{13,9},{2,6},{6,2},{1... | collective-permute-start | bytes 196616 | tf_op jit(solution)/shard_map/ppermute | solution.py:362
  5.4 0.7 collective-permute-start.1
  6.1 3.9 %collective-permute-start.2 = (bf16[64,512]{1,0:T(8,128)(2,1)S(1)}, bf16[64,512]{1,0:T(8,128)(2,1)S(1)}, u32[]{:S(2)}, u32[]{:S(2)}) collective-permute-start(bf16[64,512]{1,0:T(8,128)(2,1)S(1)} %get-tuple-element.32), channel_id=1, source_target_pairs={{0,8},{4,12},{8,0},{12,4},{1,9},{5,13},{9,1},{13,5},{2,10},{6,14},... | collective-permute-start | bytes 196616 | tf_op jit(solution)/shard_map/ppermute | solution.py:362
  10.6 2.3 %prepare.1 = (bf16[128,512]{1,0:T(8,128)(2,1)S(1)}, bf16[768,512]{1,0:T(8,128)(2,1)S(1)}, bf16[128,512]{1,0:T(8,128)(2,1)S(1)}, bf16[1536,512]{1,0:T(8,128)(2,1)...) custom-call(s32[12]{0:T(128)} %src_hbm.1, ...), custom_call_target="tpu_custom_call" | custom-call | flops 402653184 | bytes 8000000 | tf_op jit(solution)/shard_map/prepare/pallas_call | solution.py:472
  12.9 0.8 %collective-permute-done.2.refs_2_ = bf16[64,512]{1,0:T(8,128)(2,1)S(1)} collective-permute-done((bf16[64,512]{1,0:T(8,128)(2,1)S(1)}, bf16[64,512]{1,0:T(8,128)(2,1)S(1)}, u32[]{:S(2)}, u32[]{:S(2)}) %collective-permute-start.2) | collective-permute-done | bytes 65568 | tf_op jit(solution)/shard_map/ppermute | solution.py:362
  13.8 7.9 %edge_block.1 = (bf16[128,512]{1,0:T(8,128)(2,1)}, bf16[768,512]{1,0:T(8,128)(2,1)S(1)}, f32[128,512]{1,0:T(8,128)S(1)}, f32[128,512]{1,0:T(8,128)S(1)}, bf16[64...) custom-call(s32[12]{0:T(128)} %dst_hbm.5, ...), custom_call_target="tpu_custom_call" | custom-call | flops 2818572288 | bytes 12000000 | tf_op jit(solution)/shard_map/edge_block/pallas_call | solution.py:509
  21.7 1.0 %copy-done = f32[2,256,512]{2,1,0:T(8,128)} copy-done((f32[2,256,512]{2,1,0:T(8,128)}, f32[2,256,512]{2,1,0:T(8,128)S(1)}, u32[]{:S(2)}) %copy-start) | copy-done | bytes 1048600
  22.7 0.9 %copy-done.1 = bf16[768,512]{1,0:T(8,128)(2,1)} copy-done((bf16[768,512]{1,0:T(8,128)(2,1)}, bf16[768,512]{1,0:T(8,128)(2,1)S(1)}, u32[]{:S(2)}) %copy-start.1) | copy-done | bytes 786456
  26.0 1.7 %collective-permute-done.3 = bf16[2,256,512]{2,1,0:T(8,128)(2,1)} collective-permute-done((bf16[2,256,512]{2,1,0:T(8,128)(2,1)}, bf16[2,256,512]{2,1,0:T(8,128)(2,1)}, u32[]{:S(2)}, u32[]{:S(2)}) %collective-permute-start.3) | collective-permute-done | bytes 524320 | tf_op jit(solution)/shard_map/ppermute | solution.py:362
  27.7 1.2 %add_convert_fusion.1.after = bf16[1,256,512]{2,1,0:T(8,128)(2,1)S(1)} fusion(f32[2,256,512]{2,1,0:T(8,128)} %copy-done, s32[]{:T(128)S(6)} %select_n.58, bf16[2,256,512]{2,1,0:T(8,128)(2,1)} %collective-permute-done.3), kind=kLoop, calls=%fused_computation.3 | loop fusion | flops 393216 | bytes 1048580 | tf_op jit(solution)/shard_map/convert_element_type | solution.py:397
  28.9 1.6 %collective-permute-start.7 = (bf16[1,256,512]{2,1,0:T(8,128)(2,1)S(1)}, bf16[1,256,512]{2,1,0:T(8,128)(2,1)}, u32[]{:S(2)}, u32[]{:S(2)}) collective-permute-start(bf16[1,256,512]{2,1,0:T(8,128)(2,1)S(1)} %add_convert_fusion.1.after), channel_id=1, source_target_pairs={{0,2},{1,3},{2,0},{3,1},{4,6},{5,7},{6,4},{7,5},{8,10},{9,11},{10,... | collective-permute-start | bytes 786440 | tf_op jit(solution)/shard_map/ppermute | solution.py:362
  30.5 1.0 %add_convert_fusion = bf16[1,256,512]{2,1,0:T(8,128)(2,1)S(1)} fusion(f32[2,256,512]{2,1,0:T(8,128)S(1)} %get-tuple-element.51, s32[]{:T(128)S(6)} %select_n.58, bf16[2,256,512]{2,1,0:T(8,128)(2,1)} %collective-permute-done.11), kind=kLoop, calls=%fused_computation.1 | loop fusion | flops 393216 | bytes 1048580 | tf_op jit(solution)/shard_map/convert_element_type | solution.py:397
  32.1 6.1 %collective-permute-done.7 = bf16[1,256,512]{2,1,0:T(8,128)(2,1)} collective-permute-done((bf16[1,256,512]{2,1,0:T(8,128)(2,1)S(1)}, bf16[1,256,512]{2,1,0:T(8,128)(2,1)}, u32[]{:S(2)}, u32[]{:S(2)}) %collective-permute-start.7) | collective-permute-done | bytes 262176 | tf_op jit(solution)/shard_map/ppermute | solution.py:362
  38.2 1.3 %convert_add_fusion.1 = f32[1,256,512]{2,1,0:T(8,128)S(1)} fusion(bf16[1,256,512]{2,1,0:T(8,128)(2,1)} %collective-permute-done.7, f32[2,256,512]{2,1,0:T(8,128)} %copy-done, s32[]{:T(128)S(6)} %select_n.60, bf16[2,256,512]{2,1,0:T(8,128)(2,1)} %collective-permute-done.3), kind=kLoop, calls=%fused_computation.2 | loop fusion | flops 524288 | bytes 1572868 | tf_op jit(solution)/shard_map/add | solution.py:390
  39.6 2.0 %collective-permute-start.8 = (bf16[128,512]{1,0:T(8,128)(2,1)S(1)}, bf16[128,512]{1,0:T(8,128)(2,1)S(1)}, u32[]{:S(2)}, u32[]{:S(2)}) collective-permute-start(bf16[128,512]{1,0:T(8,128)(2,1)S(1)} %fusion.2), channel_id=1, source_target_pairs={{0,4},{4,0},{8,12},{12,8},{1,5},{5,1},{9,13},{13,9},{2,6},{6,2},{1... | collective-permute-start | bytes 393224 | tf_op jit(solution)/shard_map/ppermute | solution.py:362
  41.5 1.4 %collective-permute-done.12 = bf16[1,256,512]{2,1,0:T(8,128)(2,1)S(1)} collective-permute-done((bf16[1,256,512]{2,1,0:T(8,128)(2,1)S(1)}, bf16[1,256,512]{2,1,0:T(8,128)(2,1)S(1)}, u32[]{:S(2)}, u32[]{:S(2)}) %collective-permute-start.12) | collective-permute-done | bytes 262176 | tf_op jit(solution)/shard_map/ppermute | solution.py:362
  42.9 1.0 %convert_add_fusion = f32[1,256,512]{2,1,0:T(8,128)S(1)} fusion(bf16[1,256,512]{2,1,0:T(8,128)(2,1)S(1)} %collective-permute-done.12, f32[2,256,512]{2,1,0:T(8,128)S(1)} %get-tuple-element.51, s32[]{:T(128)S(6)} %select_n.60, bf16[2,256,512]{2,1,0:T(8,128)(2,1)} %collective-permute-done.11), kind=kLoop, calls=%fused_computation | loop fusion | flops 524288 | bytes 1572868 | tf_op jit(solution)/shard_map/add | solution.py:390
  44.1 2.0 %collective-permute-start.13 = (bf16[128,512]{1,0:T(8,128)(2,1)S(1)}, bf16[128,512]{1,0:T(8,128)(2,1)S(1)}, u32[]{:S(2)}, u32[]{:S(2)}) collective-permute-start(bf16[128,512]{1,0:T(8,128)(2,1)S(1)} %fusion.3), channel_id=1, source_target_pairs={{0,4},{4,0},{8,12},{12,8},{1,5},{5,1},{9,13},{13,9},{2,6},{6,2},{1... | collective-permute-start | bytes 393224 | tf_op jit(solution)/shard_map/ppermute | solution.py:362
  46.1 2.0 %collective-permute-start.9 = (bf16[128,512]{1,0:T(8,128)(2,1)S(1)}, bf16[128,512]{1,0:T(8,128)(2,1)S(1)}, u32[]{:S(2)}, u32[]{:S(2)}) collective-permute-start(bf16[128,512]{1,0:T(8,128)(2,1)S(1)} %fusion.1), channel_id=1, source_target_pairs={{0,12},{4,8},{8,4},{12,0},{1,13},{5,9},{9,5},{13,1},{2,14},{6,10},... | collective-permute-start | bytes 393224 | tf_op jit(solution)/shard_map/ppermute | solution.py:362
  48.0 1.8 %collective-permute-done.13 = bf16[128,512]{1,0:T(8,128)(2,1)S(1)} collective-permute-done((bf16[128,512]{1,0:T(8,128)(2,1)S(1)}, bf16[128,512]{1,0:T(8,128)(2,1)S(1)}, u32[]{:S(2)}, u32[]{:S(2)}) %collective-permute-start.13) | collective-permute-done | bytes 131104 | tf_op jit(solution)/shard_map/ppermute | solution.py:362
  49.9 3.8 %collective-permute-start.14 = (bf16[128,512]{1,0:T(8,128)(2,1)S(1)}, bf16[128,512]{1,0:T(8,128)(2,1)S(1)}, u32[]{:S(2)}, u32[]{:S(2)}) collective-permute-start(bf16[128,512]{1,0:T(8,128)(2,1)S(1)} %fusion), channel_id=1, source_target_pairs={{0,12},{4,8},{8,4},{12,0},{1,13},{5,9},{9,5},{13,1},{2,14},{6,10},... | collective-permute-start | bytes 393224 | tf_op jit(solution)/shard_map/ppermute | solution.py:362
  53.7 0.7 %collective-permute-done.9 = bf16[128,512]{1,0:T(8,128)(2,1)S(1)} collective-permute-done((bf16[128,512]{1,0:T(8,128)(2,1)S(1)}, bf16[128,512]{1,0:T(8,128)(2,1)S(1)}, u32[]{:S(2)}, u32[]{:S(2)}) %collective-permute-start.9) | collective-permute-done | bytes 131104 | tf_op jit(solution)/shard_map/ppermute | solution.py:362
  54.5 2.4 %collective-permute-start.10 = (bf16[128,512]{1,0:T(8,128)(2,1)S(1)}, bf16[128,512]{1,0:T(8,128)(2,1)S(1)}, u32[]{:S(2)}, u32[]{:S(2)}) collective-permute-start(bf16[128,512]{1,0:T(8,128)(2,1)S(1)} %add_convert_fusion.3.own_a), channel_id=1, source_target_pairs={{0,4},{4,0},{8,12},{12,8},{1,5},{5,1},{9,13},{13,9},{2,6},{6,2},{1... | collective-permute-start | bytes 393224 | tf_op jit(solution)/shard_map/ppermute | solution.py:362
  56.9 0.8 %collective-permute-done.14 = bf16[128,512]{1,0:T(8,128)(2,1)S(1)} collective-permute-done((bf16[128,512]{1,0:T(8,128)(2,1)S(1)}, bf16[128,512]{1,0:T(8,128)(2,1)S(1)}, u32[]{:S(2)}, u32[]{:S(2)}) %collective-permute-start.14) | collective-permute-done | bytes 131104 | tf_op jit(solution)/shard_map/ppermute | solution.py:362
  57.7 2.4 %collective-permute-start.15 = (bf16[128,512]{1,0:T(8,128)(2,1)S(1)}, bf16[128,512]{1,0:T(8,128)(2,1)S(1)}, u32[]{:S(2)}, u32[]{:S(2)}) collective-permute-start(bf16[128,512]{1,0:T(8,128)(2,1)S(1)} %add_convert_fusion.2.own_b), channel_id=1, source_target_pairs={{0,4},{4,0},{8,12},{12,8},{1,5},{5,1},{9,13},{13,9},{2,6},{6,2},{1... | collective-permute-start | bytes 393224 | tf_op jit(solution)/shard_map/ppermute | solution.py:362
  60.2 0.7 collective-permute-start.5
  60.9 4.7 %collective-permute-start.6 = (bf16[64,512]{1,0:T(8,128)(2,1)S(1)}, bf16[64,512]{1,0:T(8,128)(2,1)S(1)}, u32[]{:S(2)}, u32[]{:S(2)}) collective-permute-start(bf16[64,512]{1,0:T(8,128)(2,1)S(1)} %copy-done.4), channel_id=1, source_target_pairs={{0,8},{4,12},{8,0},{12,4},{1,9},{5,13},{9,1},{13,5},{2,10},{6,14},... | collective-permute-start | bytes 196616 | tf_op jit(solution)/shard_map/ppermute | solution.py:362
  65.6 3.0 %collective-permute-done.6.refs_2_ = bf16[64,512]{1,0:T(8,128)(2,1)S(1)} collective-permute-done((bf16[64,512]{1,0:T(8,128)(2,1)S(1)}, bf16[64,512]{1,0:T(8,128)(2,1)S(1)}, u32[]{:S(2)}, u32[]{:S(2)}) %collective-permute-start.6) | collective-permute-done | bytes 65568 | tf_op jit(solution)/shard_map/ppermute | solution.py:362
  68.6 2.1 %node_grads.1 = bf16[128,512]{1,0:T(8,128)(2,1)} custom-call(s32[1,4]{1,0:T(1,128)} %boundary_hbm.3, bf16[1,256,512]{2,1,0:T(8,128)(2,1)S(1)} %add_convert_fusion.1.after, f32[128,512]{1,0:T(8,128)S(1)} %get-tuple-element.46.own_ref, f32[128,512]{1,0:T(8,128)S(1)} %get-tuple-element.47.recv_ref, bf16[1536,512]{1,0:T(8,128)(2,1)S(1)} %get-tuple-element.35.refs_5_.win_ref, ...), custom_call_target="tpu_custom_call" | custom-call | flops 268435456 | bytes 2000000 | tf_op jit(solution)/shard_map/node_grads/pallas_call | solution.py:575
  70.7 2.2 %edge_grads.1 = bf16[768,512]{1,0:T(8,128)(2,1)} custom-call(s32[12]{0:T(128)} %dst_hbm.5, s32[1]{0:T(128)S(6)} %copy.15.count_ref, bf16[1,256,512]{2,1,0:T(8,128)(2,1)S(1)} %add_convert_fusion.1.after, bf16[768,512]{1,0:T(8,128)(2,1)S(1)} %copy-done.2, bf16[128,512]{1,0:T(8,128)(2,1)S(1)} %get-tuple-element.45.cot_ref, ...), custom_call_target="tpu_custom_call" | custom-call | flops 402653184 | bytes 3000000 | tf_op jit(solution)/shard_map/edge_grads/pallas_call | solution.py:560
  72.9 1.0 %widen.1 = (f32[384,512]{1,0:T(8,128)}, f32[128,512]{1,0:T(8,128)}) custom-call(bf16[128,512]{1,0:T(8,128)(2,1)S(1)} %add_convert_fusion.3.own_a, bf16[128,512]{1,0:T(8,128)(2,1)S(1)} %collective-permute-done.10.other_a, bf16[128,512]{1,0:T(8,128)(2,1)S(1)} %add_convert_fusion.2.own_b, bf16[128,512]{1,0:T(8,128)(2,1)S(1)} %collective-permute-done.15.other_b), custom_call_target="tpu_custom_call" | custom-call | bytes 1500000 | tf_op jit(solution)/shard_map/widen/pallas_call | solution.py:596
  (34 shorter events, 3.3 us)
Async XLA Ops:
  2.3 10.6 %collective-permute-start = (bf16[64,512]{1,0:T(8,128)(2,1)S(1)}, bf16[64,512]{1,0:T(8,128)(2,1)S(1)}, u32[]{:S(2)}, u32[]{:S(2)}) collective-permute-start(bf16[64,512]{1,0:T(8,128)(2,1)S(1)} %get-tuple-element.30), channel_id=1, source_target_pairs={{0,4},{4,0},{8,12},{12,8},{1,5},{5,1},{9,13},{13,9},{2,6},{6,2},{1... | collective-permute-start | bytes 196616 | tf_op jit(solution)/shard_map/ppermute | solution.py:362
  5.4 7.5 %collective-permute-start.1 = (bf16[64,512]{1,0:T(8,128)(2,1)S(1)}, bf16[64,512]{1,0:T(8,128)(2,1)S(1)}, u32[]{:S(2)}, u32[]{:S(2)}) collective-permute-start(bf16[64,512]{1,0:T(8,128)(2,1)S(1)} %get-tuple-element.31), channel_id=1, source_target_pairs={{0,0},{4,8},{8,4},{12,12},{1,1},{5,9},{9,5},{13,13},{2,2},{6,10},{... | collective-permute-start | bytes 196616 | tf_op jit(solution)/shard_map/ppermute | solution.py:362
  6.1 7.7 %collective-permute-start.2 = (bf16[64,512]{1,0:T(8,128)(2,1)S(1)}, bf16[64,512]{1,0:T(8,128)(2,1)S(1)}, u32[]{:S(2)}, u32[]{:S(2)}) collective-permute-start(bf16[64,512]{1,0:T(8,128)(2,1)S(1)} %get-tuple-element.32), channel_id=1, source_target_pairs={{0,8},{4,12},{8,0},{12,4},{1,9},{5,13},{9,1},{13,5},{2,10},{6,14},... | collective-permute-start | bytes 196616 | tf_op jit(solution)/shard_map/ppermute | solution.py:362
  21.7 1.0 %copy-start = (f32[2,256,512]{2,1,0:T(8,128)}, f32[2,256,512]{2,1,0:T(8,128)S(1)}, u32[]{:S(2)}) copy-start(f32[2,256,512]{2,1,0:T(8,128)S(1)} %get-tuple-element.42) | copy-start | bytes 3145732
  22.7 0.9 %copy-start.1 = (bf16[768,512]{1,0:T(8,128)(2,1)}, bf16[768,512]{1,0:T(8,128)(2,1)S(1)}, u32[]{:S(2)}) copy-start(bf16[768,512]{1,0:T(8,128)(2,1)S(1)} %get-tuple-element.44.gpre_ref) | copy-start | bytes 2359300
  23.6 0.6 copy-start.3
  24.2 0.6 copy-start.5
  24.8 0.6 copy-start.7
  25.5 2.3 %collective-permute-start.3 = (bf16[2,256,512]{2,1,0:T(8,128)(2,1)}, bf16[2,256,512]{2,1,0:T(8,128)(2,1)}, u32[]{:S(2)}, u32[]{:S(2)}) collective-permute-start(bf16[2,256,512]{2,1,0:T(8,128)(2,1)} %get-tuple-element.43), channel_id=1, source_target_pairs={{0,1},{1,0},{2,3},{3,2},{4,5},{5,4},{6,7},{7,6},{8,9},{9,8},{10,11... | collective-permute-start | bytes 1572872 | tf_op jit(solution)/shard_map/ppermute | solution.py:362
  25.5 5.0 %collective-permute-start.11 = (bf16[2,256,512]{2,1,0:T(8,128)(2,1)}, bf16[2,256,512]{2,1,0:T(8,128)(2,1)}, u32[]{:S(2)}, u32[]{:S(2)}) collective-permute-start(bf16[2,256,512]{2,1,0:T(8,128)(2,1)} %get-tuple-element.52), channel_id=1, source_target_pairs={{0,1},{1,0},{2,3},{3,2},{4,5},{5,4},{6,7},{7,6},{8,9},{9,8},{10,11... | collective-permute-start | bytes 1572872 | tf_op jit(solution)/shard_map/ppermute | solution.py:362
  28.9 9.3 %collective-permute-start.7 = (bf16[1,256,512]{2,1,0:T(8,128)(2,1)S(1)}, bf16[1,256,512]{2,1,0:T(8,128)(2,1)}, u32[]{:S(2)}, u32[]{:S(2)}) collective-permute-start(bf16[1,256,512]{2,1,0:T(8,128)(2,1)S(1)} %add_convert_fusion.1.after), channel_id=1, source_target_pairs={{0,2},{1,3},{2,0},{3,1},{4,6},{5,7},{6,4},{7,5},{8,10},{9,11},{10,... | collective-permute-start | bytes 786440 | tf_op jit(solution)/shard_map/ppermute | solution.py:362
  31.5 11.4 %collective-permute-start.12 = (bf16[1,256,512]{2,1,0:T(8,128)(2,1)S(1)}, bf16[1,256,512]{2,1,0:T(8,128)(2,1)S(1)}, u32[]{:S(2)}, u32[]{:S(2)}) collective-permute-start(bf16[1,256,512]{2,1,0:T(8,128)(2,1)S(1)} %add_convert_fusion), channel_id=1, source_target_pairs={{0,2},{1,3},{2,0},{3,1},{4,6},{5,7},{6,4},{7,5},{8,10},{9,11},{10,... | collective-permute-start | bytes 786440 | tf_op jit(solution)/shard_map/ppermute | solution.py:362
  39.6 6.5 %collective-permute-start.8 = (bf16[128,512]{1,0:T(8,128)(2,1)S(1)}, bf16[128,512]{1,0:T(8,128)(2,1)S(1)}, u32[]{:S(2)}, u32[]{:S(2)}) collective-permute-start(bf16[128,512]{1,0:T(8,128)(2,1)S(1)} %fusion.2), channel_id=1, source_target_pairs={{0,4},{4,0},{8,12},{12,8},{1,5},{5,1},{9,13},{13,9},{2,6},{6,2},{1... | collective-permute-start | bytes 393224 | tf_op jit(solution)/shard_map/ppermute | solution.py:362
  44.0 16.1 %copy-start.8 = (bf16[64,512]{1,0:T(8,128)(2,1)S(1)}, bf16[64,512]{1,0:T(8,128)(2,1)}, u32[]{:S(2)}) copy-start(bf16[64,512]{1,0:T(8,128)(2,1)} %copy-done.7) | copy-start | bytes 196612
  44.0 16.2 %copy-start.6 = (bf16[64,512]{1,0:T(8,128)(2,1)S(1)}, bf16[64,512]{1,0:T(8,128)(2,1)}, u32[]{:S(2)}) copy-start(bf16[64,512]{1,0:T(8,128)(2,1)} %copy-done.5) | copy-start | bytes 196612
  44.0 16.8 %copy-start.4 = (bf16[64,512]{1,0:T(8,128)(2,1)S(1)}, bf16[64,512]{1,0:T(8,128)(2,1)}, u32[]{:S(2)}) copy-start(bf16[64,512]{1,0:T(8,128)(2,1)} %copy-done.3) | copy-start | bytes 196612
  44.1 5.8 %collective-permute-start.13 = (bf16[128,512]{1,0:T(8,128)(2,1)S(1)}, bf16[128,512]{1,0:T(8,128)(2,1)S(1)}, u32[]{:S(2)}, u32[]{:S(2)}) collective-permute-start(bf16[128,512]{1,0:T(8,128)(2,1)S(1)} %fusion.3), channel_id=1, source_target_pairs={{0,4},{4,0},{8,12},{12,8},{1,5},{5,1},{9,13},{13,9},{2,6},{6,2},{1... | collective-permute-start | bytes 393224 | tf_op jit(solution)/shard_map/ppermute | solution.py:362
  46.1 8.4 %collective-permute-start.9 = (bf16[128,512]{1,0:T(8,128)(2,1)S(1)}, bf16[128,512]{1,0:T(8,128)(2,1)S(1)}, u32[]{:S(2)}, u32[]{:S(2)}) collective-permute-start(bf16[128,512]{1,0:T(8,128)(2,1)S(1)} %fusion.1), channel_id=1, source_target_pairs={{0,12},{4,8},{8,4},{12,0},{1,13},{5,9},{9,5},{13,1},{2,14},{6,10},... | collective-permute-start | bytes 393224 | tf_op jit(solution)/shard_map/ppermute | solution.py:362
  49.9 7.8 %collective-permute-start.14 = (bf16[128,512]{1,0:T(8,128)(2,1)S(1)}, bf16[128,512]{1,0:T(8,128)(2,1)S(1)}, u32[]{:S(2)}, u32[]{:S(2)}) collective-permute-start(bf16[128,512]{1,0:T(8,128)(2,1)S(1)} %fusion), channel_id=1, source_target_pairs={{0,12},{4,8},{8,4},{12,0},{1,13},{5,9},{9,5},{13,1},{2,14},{6,10},... | collective-permute-start | bytes 393224 | tf_op jit(solution)/shard_map/ppermute | solution.py:362
  54.5 16.2 %copy-start.2 = (bf16[768,512]{1,0:T(8,128)(2,1)S(1)}, bf16[768,512]{1,0:T(8,128)(2,1)}, u32[]{:S(2)}) copy-start(bf16[768,512]{1,0:T(8,128)(2,1)} %copy-done.1) | copy-start | bytes 2359300
  54.5 18.4 %collective-permute-start.10 = (bf16[128,512]{1,0:T(8,128)(2,1)S(1)}, bf16[128,512]{1,0:T(8,128)(2,1)S(1)}, u32[]{:S(2)}, u32[]{:S(2)}) collective-permute-start(bf16[128,512]{1,0:T(8,128)(2,1)S(1)} %add_convert_fusion.3.own_a), channel_id=1, source_target_pairs={{0,4},{4,0},{8,12},{12,8},{1,5},{5,1},{9,13},{13,9},{2,6},{6,2},{1... | collective-permute-start | bytes 393224 | tf_op jit(solution)/shard_map/ppermute | solution.py:362
  57.7 15.2 %collective-permute-start.15 = (bf16[128,512]{1,0:T(8,128)(2,1)S(1)}, bf16[128,512]{1,0:T(8,128)(2,1)S(1)}, u32[]{:S(2)}, u32[]{:S(2)}) collective-permute-start(bf16[128,512]{1,0:T(8,128)(2,1)S(1)} %add_convert_fusion.2.own_b), channel_id=1, source_target_pairs={{0,4},{4,0},{8,12},{12,8},{1,5},{5,1},{9,13},{13,9},{2,6},{6,2},{1... | collective-permute-start | bytes 393224 | tf_op jit(solution)/shard_map/ppermute | solution.py:362
  60.1 5.5 %collective-permute-start.4 = (bf16[64,512]{1,0:T(8,128)(2,1)S(1)}, bf16[64,512]{1,0:T(8,128)(2,1)S(1)}, u32[]{:S(2)}, u32[]{:S(2)}) collective-permute-start(bf16[64,512]{1,0:T(8,128)(2,1)S(1)} %copy-done.8), channel_id=1, source_target_pairs={{0,4},{4,0},{8,12},{12,8},{1,5},{5,1},{9,13},{13,9},{2,6},{6,2},{1... | collective-permute-start | bytes 196616 | tf_op jit(solution)/shard_map/ppermute | solution.py:362
  60.2 5.4 %collective-permute-start.5 = (bf16[64,512]{1,0:T(8,128)(2,1)S(1)}, bf16[64,512]{1,0:T(8,128)(2,1)S(1)}, u32[]{:S(2)}, u32[]{:S(2)}) collective-permute-start(bf16[64,512]{1,0:T(8,128)(2,1)S(1)} %copy-done.6), channel_id=1, source_target_pairs={{0,0},{4,8},{8,4},{12,12},{1,1},{5,9},{9,5},{13,13},{2,2},{6,10},{... | collective-permute-start | bytes 196616 | tf_op jit(solution)/shard_map/ppermute | solution.py:362
  60.9 7.7 %collective-permute-start.6 = (bf16[64,512]{1,0:T(8,128)(2,1)S(1)}, bf16[64,512]{1,0:T(8,128)(2,1)S(1)}, u32[]{:S(2)}, u32[]{:S(2)}) collective-permute-start(bf16[64,512]{1,0:T(8,128)(2,1)S(1)} %copy-done.4), channel_id=1, source_target_pairs={{0,8},{4,12},{8,0},{12,4},{1,9},{5,13},{9,1},{13,5},{2,10},{6,14},... | collective-permute-start | bytes 196616 | tf_op jit(solution)/shard_map/ppermute | solution.py:362

commit v4 on v3

--- a/solution.py
+++ b/solution.py
@@ -182,21 +182,20 @@
         hot_turned,
         agg_hbm,
         gpre_ref,
-        own_sums,
+        sums_ref,
         recv_sums,
-    ) = refs[arrivals : arrivals + 12]
-    back_sums = refs[arrivals + 12 : 2 * arrivals + 12]
-    away_a, kept_a, away_b, kept_b = refs[2 * arrivals + 12 : 2 * arrivals + 16]
-    (
+        away_a,
+        kept_a,
+        away_b,
+        kept_b,
         dst_ref,
         ext_ref,
         act_ref,
         proj_ref,
         agg_ref,
         agg_bf16,
-        sums_ref,
         sems,
-    ) = refs[2 * arrivals + 16 :]
+    ) = refs[arrivals:]
     nodes, latent = node_ref.shape
     edges = edge_ref.shape[0]
     tiles = edges // block
@@ -256,10 +255,6 @@
     agg_bf16[...] = agg_ref[...].astype(BF16)
     agg_copy = load_small(agg_bf16, agg_hbm, sems.at[1])
     sums_ref[...] = dot(hot_turned[...], gpre_ref[...])
-    own_sums[...] = sums_ref[:nodes, :]
-    for which in range(arrivals):
-        at = pl.multiple_of((owned + places[which]) * block, block)
-        back_sums[which][...] = sums_ref[pl.ds(at, block), :].astype(BF16)
 
     unit = latent // ways
 
@@ -295,12 +290,30 @@
 
 
 def edge_grad_kernel(
-    block, dst_hbm, count_ref, after, gpre_ref, cot_ref, win_ref, out_ref, dst_ref, sem
+    block,
+    arrivals,
+    four,
+    dst_hbm,
+    count_ref,
+    after,
+    gpre_ref,
+    sums_ref,
+    cot_ref,
+    win_ref,
+    out_ref,
+    *refs,
 ):
-    latent = cot_ref.shape[1]
+    back_sums = refs[:arrivals]
+    dst_ref, sem = refs[arrivals:]
+    copy = load_small(dst_hbm, dst_ref, sem)
+    nodes, latent = cot_ref.shape
     tiles = gpre_ref.shape[0] // block
     group = 4 if tiles % 4 == 0 else 1
-    load_small(dst_hbm, dst_ref, sem).wait()
+    places = arrival_places(lax.axis_index("dom"), four, arrivals)
+    for which in range(arrivals):
+        at = pl.multiple_of(nodes + places[which] * block, block)
+        back_sums[which][...] = sums_ref[pl.ds(at, block), :].astype(BF16)
+    copy.wait()
     for first in range(0, tiles, group):
         rows = slice(first * block, (first + group) * block)
         upstream = jnp.concatenate(
@@ -314,13 +327,31 @@
         out_ref[rows, :] = (dot_t(gpre_ref[rows, :], win_ref[:latent, :]) + upstream).astype(BF16)
 
 
-def node_grad_kernel(arrivals, four, boundary_hbm, after, own_ref, recv_ref, win_ref, *refs):
+def halve_kernel(bit, came_ref, kept_ref, after, away_ref, left_ref):
+    mine = (lax.axis_index("dp") // bit) % 2
+    for slot in range(left_ref.shape[0]):
+        there, here = 2 * slot + 1 - mine, 2 * slot + mine
+        away_ref[slot] = (kept_ref[there] + came_ref[there].astype(F32)).astype(BF16)
+        left_ref[slot] = kept_ref[here] + came_ref[here].astype(F32)
+
+
+def split_kernel(came_ref, kept_ref, after, away_ref, left_ref):
+    part = lax.axis_index("dom")
+    inner = (part == 1) | (part == 2)
+    rows = left_ref.shape[0]
+    here = pl.ds(pl.multiple_of(jnp.where(inner, 0, rows), rows), rows)
+    there = pl.ds(pl.multiple_of(jnp.where(inner, rows, 0), rows), rows)
+    away_ref[...] = (kept_ref[0, there, :] + came_ref[0, there, :].astype(F32)).astype(BF16)
+    left_ref[...] = kept_ref[0, here, :] + came_ref[0, here, :].astype(F32)
+
+
+def node_grad_kernel(arrivals, four, boundary_hbm, sums_ref, recv_ref, win_ref, *refs):
     returned = refs[:arrivals]
     out_ref, total_ref, boundary_ref, sem = refs[arrivals:]
-    latent = own_ref.shape[1]
+    nodes, latent = recv_ref.shape
     block = returned[0].shape[0]
     copy = load_small(boundary_hbm, boundary_ref, sem)
-    total_ref[...] = own_ref[...]
+    total_ref[...] = sums_ref[:nodes, :]
     copy.wait()
     for which, place in enumerate(boundary_places(boundary_ref, lax.axis_index("dom"), four)):
         spot = pl.ds(pl.multiple_of(place * block, block), block)
@@ -379,31 +410,45 @@
     ]
 
 
-def sum_over_dp(away, kept):
+def halve(bit, came, kept, after):
+    slots, rows, latent = kept.shape
+    return pl.pallas_call(
+        functools.partial(halve_kernel, bit),
+        out_shape=(
+            pltpu.VMEM((slots // 2, rows, latent), BF16),
+            pltpu.VMEM((slots // 2, rows, latent), F32),
+        ),
+        in_specs=[VMEM] * 3,
+        out_specs=(VMEM,) * 2,
+        cost_estimate=pl.CostEstimate(flops=0, bytes_accessed=500_000, transcendentals=0),
+        name="halve",
+    )(in_vmem(came), in_vmem(kept), in_vmem(after))
+
+
+def sum_over_dp(away, kept, after):
     devices = lax.axis_size("dp")
-    index = lax.axis_index("dp")
     bit = 1
     while True:
         came = swap(away, "dp", lambda i, bit=bit: i ^ bit)
         bit *= 2
         if bit >= devices:
-            return kept[0] + came[0].astype(F32), away
-        mine = (index // bit) % 2
-
-        def half(array, side):
-            split = array.reshape((-1, 2) + array.shape[1:])
-            return lax.dynamic_index_in_dim(split, side, 1, keepdims=False)
-
-        away = (half(kept, 1 - mine) + half(came, 1 - mine).astype(F32)).astype(BF16)
-        kept = half(kept, mine) + half(came, mine).astype(F32)
-
-
-def sum_over_four(rows):
-    index = lax.axis_index("dom")
-    inner = (index == 1) | (index == 2)
-    low, high = jnp.split(rows, 2, axis=0)
-    away = jnp.where(inner, high, low).astype(BF16)
-    kept = jnp.where(inner, low, high)
+            return came, kept, away
+        away, kept = halve(bit, came, kept, after)
+
+
+def sum_over_four(came, kept, after):
+    rows, latent = kept.shape[1:]
+    away, kept = pl.pallas_call(
+        split_kernel,
+        out_shape=(
+            pltpu.VMEM((rows // 2, latent), BF16),
+            pltpu.VMEM((rows // 2, latent), F32),
+        ),
+        in_specs=[VMEM] * 2 + [HBM],
+        out_specs=(VMEM,) * 2,
+        cost_estimate=pl.CostEstimate(flops=0, bytes_accessed=500_000, transcendentals=0),
+        name="split",
+    )(in_vmem(came), in_vmem(kept), in_hbm(after))
     kept = (kept + swap(away, "dom", lambda i: i ^ 1).astype(F32)).astype(BF16)
     kept = (kept.astype(F32) + swap(kept, "dom", lambda i: 3 - i).astype(F32)).astype(BF16)
     return kept, swap(kept, "dom", lambda i: i ^ 1)
@@ -511,16 +556,15 @@
         out_shape=(
             jax.ShapeDtypeStruct((nodes, latent), BF16),
             pltpu.VMEM((edges, latent), BF16),
+            pltpu.VMEM((extent, latent), F32),
             pltpu.VMEM((nodes, latent), F32),
-            pltpu.VMEM((nodes, latent), F32),
-            *[block_shape] * arrivals,
             pltpu.VMEM((half, 2 * unit, latent), BF16),
             pltpu.VMEM((half, 2 * unit, latent), F32),
             pltpu.VMEM((half, 2 * unit, latent), BF16),
             pltpu.VMEM((half, 2 * unit, latent), F32),
         ),
         in_specs=[HBM, SMEM] + [VMEM] * (8 + arrivals),
-        out_specs=(HBM,) + (VMEM,) * (7 + arrivals),
+        out_specs=(HBM,) + (VMEM,) * 7,
         scratch_shapes=[
             pltpu.SMEM((tiles,), jnp.int32),
             pltpu.VMEM((extent, latent), BF16),
@@ -528,7 +572,6 @@
             pltpu.VMEM((edges, latent), BF16),
             pltpu.VMEM((nodes, latent), F32),
             pltpu.VMEM((nodes, latent), BF16),
-            pltpu.VMEM((extent, latent), F32),
             pltpu.SemaphoreType.DMA((2,)),
         ],
         compiler_params=pltpu.CompilerParams(vmem_limit_bytes=16 * 1024 * 1024),
@@ -546,22 +589,13 @@
             for array in (*came, node_v, edge_v, win_v, wout_v, pre, mid, hot, turned)
         ],
     )
-    agg, grad_pre, own_sums, recv_sums = outs[:4]
-    back_sums = outs[4 : 4 + arrivals]
-    away_a, kept_a, away_b, kept_b = outs[4 + arrivals :]
-    rows_a, sent_a = sum_over_dp(away_a, kept_a)
-    rows_b, _ = sum_over_dp(away_b, kept_b)
-    if four:
-        returned = exchange_of_four(*back_sums)
-    else:
-        returned = [
-            from_behind(back_sums[which], "dom", -OFFSET_LIST[which]) for which in range(4)
-        ]
-    edge_grad = pl.pallas_call(
-        functools.partial(edge_grad_kernel, block),
-        out_shape=jax.ShapeDtypeStruct((edges, latent), BF16),
-        in_specs=[HBM, SMEM, ANY] + [VMEM] * 3,
-        out_specs=VMEM,
+    agg, grad_pre, sums, recv_sums, away_a, kept_a, away_b, kept_b = outs
+    came_a, kept_a, sent_a = sum_over_dp(away_a, kept_a, cot_v)
+    edge_grad, *back_sums = pl.pallas_call(
+        functools.partial(edge_grad_kernel, block, arrivals, four),
+        out_shape=(jax.ShapeDtypeStruct((edges, latent), BF16),) + (block_shape,) * arrivals,
+        in_specs=[HBM, SMEM] + [VMEM] * 5,
+        out_specs=(VMEM,) * (1 + arrivals),
         scratch_shapes=[
             pltpu.SMEM((tiles,), jnp.int32),
             pltpu.SemaphoreType.DMA,
@@ -571,11 +605,22 @@
             flops=2 * edges * latent * latent, bytes_accessed=3_000_000, transcendentals=0
         ),
         name="edge_grads",
-    )(tile_dst, tile_count, sent_a, in_vmem(grad_pre), in_vmem(cot_v), in_vmem(win_v))
+    )(
+        tile_dst,
+        tile_count,
+        *[in_vmem(array) for array in (sent_a, grad_pre, sums, cot_v, win_v)],
+    )
+    came_b, kept_b, _ = sum_over_dp(away_b, kept_b, back_sums[0])
+    if four:
+        returned = exchange_of_four(*back_sums)
+    else:
+        returned = [
+            from_behind(back_sums[which], "dom", -OFFSET_LIST[which]) for which in range(4)
+        ]
     node_out = pl.pallas_call(
         functools.partial(node_grad_kernel, arrivals, four),
         out_shape=jax.ShapeDtypeStruct((nodes, latent), BF16),
-        in_specs=[HBM, ANY] + [VMEM] * (3 + arrivals),
+        in_specs=[HBM] + [VMEM] * (3 + arrivals),
         out_specs=VMEM,
         scratch_shapes=[
             pltpu.VMEM((nodes, latent), F32),
@@ -587,11 +632,7 @@
             flops=8 * nodes * latent * latent, bytes_accessed=2_000_000, transcendentals=0
         ),
         name="node_grads",
-    )(
-        boundary,
-        sent_a,
-        *[in_vmem(array) for array in (own_sums, recv_sums, win_v, *returned)],
-    )
+    )(boundary, *[in_vmem(array) for array in (sums, recv_sums, win_v, *returned)])
     if four:
         w_in_grad, w_out_grad = pl.pallas_call(
             last_kernel,
@@ -604,9 +645,10 @@
             compiler_params=small,
             cost_estimate=pl.CostEstimate(flops=0, bytes_accessed=1_500_000, transcendentals=0),
             name="widen",
-        )(*sum_over_four(rows_a), *sum_over_four(rows_b))
+        )(*sum_over_four(came_a, kept_a, edge_grad), *sum_over_four(came_b, kept_b, node_out))
     else:
-        sum_a, sum_b = sum_over_dom(rows_a), sum_over_dom(rows_b)
+        sum_a = sum_over_dom(kept_a[0] + came_a[0].astype(F32))
+        sum_b = sum_over_dom(kept_b[0] + came_b[0].astype(F32))
         w_in_grad = jnp.concatenate([sum_a[unit:], sum_b], axis=0)
         w_out_grad = sum_a[:unit]
     return (agg[None], edge_grad[None], node_out[None], w_in_grad, w_out_grad)

time: 74.3 us -> 78.3 us (1.054)
  Pallas kernels: 17.2 us -> 22.6 us
  local copies, waits for them, and re-layouts: 3.79 us -> 9.14 us
  other arithmetic: 4.75 us -> 1.08 us
  starting transfers between devices: 30.2 us -> 27.2 us
    pallas_call x1 -> x5, Pallas kernels: 2.17 us -> 7.79 us  [the longest x1 3.19 us: body(): pl.pallas_call(functools.partial(edge_grad_kernel, block, arrivals, four)...]
    unnamed x18 -> x34, local copies, waits for them, and re-layouts: 3.79 us -> 9.14 us
    ppermute x16, starting transfers between devices: 30.2 us -> 27.2 us  [swap(): return lax.ppermute(array, axis, [(i, partner(i)) for i in range(devices)])]
    add x2 -> x0, other arithmetic: 2.33 us -> none  [sum_over_dp(): return (kept[0] + came[0].astype(F32), away)]
    convert_element_type x4 -> x0, other arithmetic: 2.25 us -> none  [the longest x2 2.19 us: sum_over_dp(): (half(kept, 1 - mine) + half(came, 1 - mine).astype(F32)).astype(BF16)]
    convert_element_type x2, other arithmetic: 0.11 us -> 1.01 us  [sum_over_four(): kept = (kept + swap(away, 'dom', lambda i: i ^ 1).astype(F32)).astype(BF16)]
  transfers between devices with their start and end apart: 16 -> 16, of which waited for: 8 -> 8; matrix products, arithmetic and copies ran while one was open for 6% -> 1% of each run, Pallas kernels for 9% -> 16%
where the time goes in v4:
time: 78.3 us; the launch traced here: 77.8 us
  starting transfers between devices  27.2 us (35%)
  Pallas kernels  22.6 us (29%)
  waiting for transfers between devices  16.3 us (21%)
  local copies, waits for them, and re-layouts  9.14 us (12%)
  between operations  1.48 us (2%)
  other arithmetic  1.08 us (1%)
    ppermute x16, starting transfers between devices, swap(): return lax.ppermute(array, axis, [(i, partner(i)) for i in range(devices)])  27.2 us
    ppermute x16, waiting for transfers between devices, swap(): return lax.ppermute(array, axis, [(i, partner(i)) for i in range(devices)])  16.3 us
    unnamed x34, local copies, waits for them, and re-layouts  9.14 us
    pallas_call x1, Pallas kernels, body(): pl.pallas_call(functools.partial(edge_kernel, ways, arrivals, four, block...  7.7 us
    pallas_call x1, Pallas kernels, body(): pl.pallas_call(functools.partial(edge_grad_kernel, block, arrivals, four)...  3.19 us
    pallas_call x2, Pallas kernels, halve(): pl.pallas_call(functools.partial(halve_kernel, bit), out_shape=(pltpu.VME...  2.61 us
    pallas_call x1, Pallas kernels, body(): pl.pallas_call(functools.partial(prep_kernel, parts, arrivals), out_shape...  2.32 us
    pallas_call x1, Pallas kernels, body(): pl.pallas_call(functools.partial(node_grad_kernel, arrivals, four), out_s...  2.13 us
  transfers between devices with their start and end apart: 16, of which 8 were waited for; matrix products, arithmetic and copies ran while one was open for 1% of the time, Pallas kernels for 16%

profile of v4, /device:TPU:0, one launch (start us, length us, event | category | flops | bytes accessed | tf_op | source)
XLA Modules:
  0.0 77.8 jit_solution(4738274823453300450)
XLA Ops:
  0.6 1.6 %pick_blocks.1 = (bf16[64,512]{1,0:T(8,128)(2,1)S(1)}, bf16[64,512]{1,0:T(8,128)(2,1)S(1)}, bf16[64,512]{1,0:T(8,128)(2,1)S(1)}) custom-call(s32[1,4]{1,0:T(1,128)} %boundary_hbm.3, bf16[128,512]{1,0:T(8,128)(2,1)} %bitcast.9), custom_call_target="tpu_custom_call" | custom-call | bytes 400000 | tf_op jit(solution)/shard_map/pick_blocks/pallas_call | solution.py:495
  2.3 3.1 %collective-permute-start = (bf16[64,512]{1,0:T(8,128)(2,1)S(1)}, bf16[64,512]{1,0:T(8,128)(2,1)S(1)}, u32[]{:S(2)}, u32[]{:S(2)}) collective-permute-start(bf16[64,512]{1,0:T(8,128)(2,1)S(1)} %get-tuple-element.39), channel_id=1, source_target_pairs={{0,4},{4,0},{8,12},{12,8},{1,5},{5,1},{9,13},{13,9},{2,6},{6,2},{1... | collective-permute-start | bytes 196616 | tf_op jit(solution)/shard_map/ppermute | solution.py:393
  6.0 3.9 %collective-permute-start.2 = (bf16[64,512]{1,0:T(8,128)(2,1)S(1)}, bf16[64,512]{1,0:T(8,128)(2,1)S(1)}, u32[]{:S(2)}, u32[]{:S(2)}) collective-permute-start(bf16[64,512]{1,0:T(8,128)(2,1)S(1)} %get-tuple-element.41), channel_id=1, source_target_pairs={{0,8},{4,12},{8,0},{12,4},{1,9},{5,13},{9,1},{13,5},{2,10},{6,14},... | collective-permute-start | bytes 196616 | tf_op jit(solution)/shard_map/ppermute | solution.py:393
  10.6 2.3 %prepare.1 = (bf16[128,512]{1,0:T(8,128)(2,1)S(1)}, bf16[768,512]{1,0:T(8,128)(2,1)S(1)}, bf16[128,512]{1,0:T(8,128)(2,1)S(1)}, bf16[1536,512]{1,0:T(8,128)(2,1)...) custom-call(s32[12]{0:T(128)} %src_hbm.1, ...), custom_call_target="tpu_custom_call" | custom-call | flops 402653184 | bytes 8000000 | tf_op jit(solution)/shard_map/prepare/pallas_call | solution.py:517
  12.9 0.8 %collective-permute-done.2.refs_2_ = bf16[64,512]{1,0:T(8,128)(2,1)S(1)} collective-permute-done((bf16[64,512]{1,0:T(8,128)(2,1)S(1)}, bf16[64,512]{1,0:T(8,128)(2,1)S(1)}, u32[]{:S(2)}, u32[]{:S(2)}) %collective-permute-start.2) | collective-permute-done | bytes 65568 | tf_op jit(solution)/shard_map/ppermute | solution.py:393
  13.8 7.7 %edge_block.1 = (bf16[128,512]{1,0:T(8,128)(2,1)}, bf16[768,512]{1,0:T(8,128)(2,1)S(1)}, f32[384,512]{1,0:T(8,128)S(1)}, f32[128,512]{1,0:T(8,128)S(1)}, bf16[2,...) custom-call(s32[12]{0:T(128)} %dst_hbm.5, ...), custom_call_target="tpu_custom_call" | custom-call | flops 2818572288 | bytes 12000000 | tf_op jit(solution)/shard_map/edge_block/pallas_call | solution.py:554
  21.5 1.0 %copy-done.3 = f32[2,256,512]{2,1,0:T(8,128)} copy-done((f32[2,256,512]{2,1,0:T(8,128)}, f32[2,256,512]{2,1,0:T(8,128)S(1)}, u32[]{:S(2)}) %copy-start.3) | copy-done | bytes 1048600
  22.5 0.9 %copy-done.5 = bf16[768,512]{1,0:T(8,128)(2,1)} copy-done((bf16[768,512]{1,0:T(8,128)(2,1)}, bf16[768,512]{1,0:T(8,128)(2,1)S(1)}, u32[]{:S(2)}) %copy-start.5) | copy-done | bytes 786456
  24.5 2.1 %collective-permute-done.3.came_ref = bf16[2,256,512]{2,1,0:T(8,128)(2,1)S(1)} collective-permute-done((bf16[2,256,512]{2,1,0:T(8,128)(2,1)S(1)}, bf16[2,256,512]{2,1,0:T(8,128)(2,1)S(1)}, u32[]{:S(2)}, u32[]{:S(2)}) %collective-permute-start.3) | collective-permute-done | bytes 524320 | tf_op jit(solution)/shard_map/ppermute | solution.py:393
  27.4 1.5 %collective-permute-start.7 = (bf16[1,256,512]{2,1,0:T(8,128)(2,1)}, bf16[1,256,512]{2,1,0:T(8,128)(2,1)}, u32[]{:S(2)}, u32[]{:S(2)}) collective-permute-start(bf16[1,256,512]{2,1,0:T(8,128)(2,1)} %get-tuple-element.54.after), channel_id=1, source_target_pairs={{0,2},{1,3},{2,0},{3,1},{4,6},{5,7},{6,4},{7,5},{8,10},{9,11},{10,... | collective-permute-start | bytes 786440 | tf_op jit(solution)/shard_map/ppermute | solution.py:393
  28.9 1.4 %copy-done.1 = bf16[1536,512]{1,0:T(8,128)(2,1)S(1)} copy-done((bf16[1536,512]{1,0:T(8,128)(2,1)S(1)}, bf16[1536,512]{1,0:T(8,128)(2,1)}, u32[]{:S(2)}) %copy-start.1) | copy-done | bytes 1572888
  30.4 1.1 %copy-done.6 = bf16[768,512]{1,0:T(8,128)(2,1)S(1)} copy-done((bf16[768,512]{1,0:T(8,128)(2,1)S(1)}, bf16[768,512]{1,0:T(8,128)(2,1)}, u32[]{:S(2)}) %copy-start.6) | copy-done | bytes 786456
  31.5 3.2 %edge_grads.1 = (bf16[768,512]{1,0:T(8,128)(2,1)}, bf16[64,512]{1,0:T(8,128)(2,1)S(1)}, bf16[64,512]{1,0:T(8,128)(2,1)S(1)}, bf16[64,512]{1,0:T(8,128)(2,1)S(1)}) custom-call(s32[12]{0:T(128)} %dst_hbm.5, s32[1]{0:T(128)S(6)} %copy.15.count_ref, bf16[1,256,512]{2,1,0:T(8,128)(2,1)} %get-tuple-element.54.after, bf16[768,512]{1,0:T(8,128)(2,1)S(1)} %copy-done.6, ...), custom_call_target="tpu_custom_call" | custom-call | flops 402653184 | bytes 3000000 | tf_op jit(solution)/shard_map/edge_grads/pallas_call | solution.py:594
  35.9 1.8 %halve.3 = (bf16[1,256,512]{2,1,0:T(8,128)(2,1)}, f32[1,256,512]{2,1,0:T(8,128)S(1)}) custom-call(bf16[2,256,512]{2,1,0:T(8,128)(2,1)} %collective-permute-done.11.came_ref, f32[2,256,512]{2,1,0:T(8,128)S(1)} %copy-done.4, bf16[64,512]{1,0:T(8,128)(2,1)S(1)} %get-tuple-element.59.after), custom_call_target="tpu_custom_call" | custom-call | bytes 500000 | tf_op jit(solution)/shard_map/halve/pallas_call | solution.py:415
  39.1 1.0 %copy-done.8 = f32[1,256,512]{2,1,0:T(8,128)S(1)} copy-done((f32[1,256,512]{2,1,0:T(8,128)S(1)}, f32[1,256,512]{2,1,0:T(8,128)}, u32[]{:S(2)}) %copy-start.8) | copy-done | bytes 524312
  40.1 1.0 %split.2 = (bf16[128,512]{1,0:T(8,128)(2,1)S(1)}, f32[128,512]{1,0:T(8,128)S(1)}) custom-call(bf16[1,256,512]{2,1,0:T(8,128)(2,1)} %collective-permute-done.7.came_ref, f32[1,256,512]{2,1,0:T(8,128)S(1)} %copy-done.8, bf16[768,512]{1,0:T(8,128)(2,1)} %get-tuple-element.57.after), custom_call_target="tpu_custom_call" | custom-call | bytes 500000 | tf_op jit(solution)/shard_map/split/pallas_call | solution.py:441
  41.2 2.0 %collective-permute-start.8 = (bf16[128,512]{1,0:T(8,128)(2,1)S(1)}, bf16[128,512]{1,0:T(8,128)(2,1)S(1)}, u32[]{:S(2)}, u32[]{:S(2)}) collective-permute-start(bf16[128,512]{1,0:T(8,128)(2,1)S(1)} %get-tuple-element.64), channel_id=1, source_target_pairs={{0,4},{4,0},{8,12},{12,8},{1,5},{5,1},{9,13},{13,9},{2,6},{6,2},{1... | collective-permute-start | bytes 393224 | tf_op jit(solution)/shard_map/ppermute | solution.py:393
  43.1 1.5 %collective-permute-start.5 = (bf16[64,512]{1,0:T(8,128)(2,1)}, bf16[64,512]{1,0:T(8,128)(2,1)S(1)}, u32[]{:S(2)}, u32[]{:S(2)}) collective-permute-start(bf16[64,512]{1,0:T(8,128)(2,1)} %copy-done.16), channel_id=1, source_target_pairs={{0,0},{4,8},{8,4},{12,12},{1,1},{5,9},{9,5},{13,13},{2,2},{6,10},{... | collective-permute-start | bytes 196616 | tf_op jit(solution)/shard_map/ppermute | solution.py:393
  44.6 2.5 %collective-permute-start.6 = (bf16[64,512]{1,0:T(8,128)(2,1)}, bf16[64,512]{1,0:T(8,128)(2,1)S(1)}, u32[]{:S(2)}, u32[]{:S(2)}) collective-permute-start(bf16[64,512]{1,0:T(8,128)(2,1)} %copy-done.15), channel_id=1, source_target_pairs={{0,8},{4,12},{8,0},{12,4},{1,9},{5,13},{9,1},{13,5},{2,10},{6,14},... | collective-permute-start | bytes 196616 | tf_op jit(solution)/shard_map/ppermute | solution.py:393
  47.8 3.3 %collective-permute-done.6.refs_2_ = bf16[64,512]{1,0:T(8,128)(2,1)S(1)} collective-permute-done((bf16[64,512]{1,0:T(8,128)(2,1)}, bf16[64,512]{1,0:T(8,128)(2,1)S(1)}, u32[]{:S(2)}, u32[]{:S(2)}) %collective-permute-start.6) | collective-permute-done | bytes 65568 | tf_op jit(solution)/shard_map/ppermute | solution.py:393
  51.7 0.9 %copy-done.12 = f32[128,512]{1,0:T(8,128)S(1)} copy-done((f32[128,512]{1,0:T(8,128)S(1)}, f32[128,512]{1,0:T(8,128)}, u32[]{:S(2)}) %copy-start.12) | copy-done | bytes 262168
  52.7 2.1 %node_grads.1.after = bf16[128,512]{1,0:T(8,128)(2,1)} custom-call(s32[1,4]{1,0:T(1,128)} %boundary_hbm.3, f32[384,512]{1,0:T(8,128)S(1)} %get-tuple-element.56.sums_ref, f32[128,512]{1,0:T(8,128)S(1)} %copy-done.12, bf16[1536,512]{1,0:T(8,128)(2,1)S(1)} %copy-done.2, bf16[64,512]{1,0:T(8,128)(2,1)S(1)} %collective-permute-done.4.refs_0_, ...), custom_call_target="tpu_custom_call" | custom-call | flops 268435456 | bytes 2000000 | tf_op jit(solution)/shard_map/node_grads/pallas_call | solution.py:620
  54.9 1.0 %split.3 = (bf16[128,512]{1,0:T(8,128)(2,1)S(1)}, f32[128,512]{1,0:T(8,128)S(1)}) custom-call(bf16[1,256,512]{2,1,0:T(8,128)(2,1)} %collective-permute-done.12.came_ref, f32[1,256,512]{2,1,0:T(8,128)S(1)} %copy-done.10, bf16[128,512]{1,0:T(8,128)(2,1)} %node_grads.1.after), custom_call_target="tpu_custom_call" | custom-call | bytes 500000 | tf_op jit(solution)/shard_map/split/pallas_call | solution.py:441
  55.8 1.4 %collective-permute-start.13 = (bf16[128,512]{1,0:T(8,128)(2,1)S(1)}, bf16[128,512]{1,0:T(8,128)(2,1)S(1)}, u32[]{:S(2)}, u32[]{:S(2)}) collective-permute-start(bf16[128,512]{1,0:T(8,128)(2,1)S(1)} %get-tuple-element.70), channel_id=1, source_target_pairs={{0,4},{4,0},{8,12},{12,8},{1,5},{5,1},{9,13},{13,9},{2,6},{6,2},{1... | collective-permute-start | bytes 393224 | tf_op jit(solution)/shard_map/ppermute | solution.py:393
  57.2 1.0 %add_convert_fusion.3 = bf16[128,512]{1,0:T(8,128)(2,1)S(1)} fusion(f32[128,512]{1,0:T(8,128)} %copy-done.13, bf16[128,512]{1,0:T(8,128)(2,1)S(1)} %collective-permute-done.8), kind=kLoop, calls=%fused_computation.3 | loop fusion | flops 196608 | bytes 524288 | tf_op jit(solution)/shard_map/convert_element_type | solution.py:452
  58.2 2.2 %collective-permute-start.9 = (bf16[128,512]{1,0:T(8,128)(2,1)S(1)}, bf16[128,512]{1,0:T(8,128)(2,1)S(1)}, u32[]{:S(2)}, u32[]{:S(2)}) collective-permute-start(bf16[128,512]{1,0:T(8,128)(2,1)S(1)} %add_convert_fusion.3), channel_id=1, source_target_pairs={{0,12},{4,8},{8,4},{12,0},{1,13},{5,9},{9,5},{13,1},{2,14},{6,10},... | collective-permute-start | bytes 393224 | tf_op jit(solution)/shard_map/ppermute | solution.py:393
  60.4 1.2 %collective-permute-done.13 = bf16[128,512]{1,0:T(8,128)(2,1)S(1)} collective-permute-done((bf16[128,512]{1,0:T(8,128)(2,1)S(1)}, bf16[128,512]{1,0:T(8,128)(2,1)S(1)}, u32[]{:S(2)}, u32[]{:S(2)}) %collective-permute-start.13) | collective-permute-done | bytes 131104 | tf_op jit(solution)/shard_map/ppermute | solution.py:393
  61.7 6.6 %collective-permute-start.14 = (bf16[128,512]{1,0:T(8,128)(2,1)S(1)}, bf16[128,512]{1,0:T(8,128)(2,1)S(1)}, u32[]{:S(2)}, u32[]{:S(2)}) collective-permute-start(bf16[128,512]{1,0:T(8,128)(2,1)S(1)} %add_convert_fusion.1), channel_id=1, source_target_pairs={{0,12},{4,8},{8,4},{12,0},{1,13},{5,9},{9,5},{13,1},{2,14},{6,10},... | collective-permute-start | bytes 393224 | tf_op jit(solution)/shard_map/ppermute | solution.py:393
  68.4 3.3 %collective-permute-done.14 = bf16[128,512]{1,0:T(8,128)(2,1)S(1)} collective-permute-done((bf16[128,512]{1,0:T(8,128)(2,1)S(1)}, bf16[128,512]{1,0:T(8,128)(2,1)S(1)}, u32[]{:S(2)}, u32[]{:S(2)}) %collective-permute-start.14) | collective-permute-done | bytes 131104 | tf_op jit(solution)/shard_map/ppermute | solution.py:393
  71.8 1.5 %collective-permute-done.10.other_a = bf16[128,512]{1,0:T(8,128)(2,1)S(1)} collective-permute-done((bf16[128,512]{1,0:T(8,128)(2,1)S(1)}, bf16[128,512]{1,0:T(8,128)(2,1)S(1)}, u32[]{:S(2)}, u32[]{:S(2)}) %collective-permute-start.10) | collective-permute-done | bytes 131104 | tf_op jit(solution)/shard_map/ppermute | solution.py:393
  73.3 3.5 %collective-permute-done.15.other_b = bf16[128,512]{1,0:T(8,128)(2,1)S(1)} collective-permute-done((bf16[128,512]{1,0:T(8,128)(2,1)S(1)}, bf16[128,512]{1,0:T(8,128)(2,1)S(1)}, u32[]{:S(2)}, u32[]{:S(2)}) %collective-permute-start.15) | collective-permute-done | bytes 131104 | tf_op jit(solution)/shard_map/ppermute | solution.py:393
  76.8 1.0 %widen.1 = (f32[384,512]{1,0:T(8,128)}, f32[128,512]{1,0:T(8,128)}) custom-call(bf16[128,512]{1,0:T(8,128)(2,1)S(1)} %add_convert_fusion.2.own_a, bf16[128,512]{1,0:T(8,128)(2,1)S(1)} %collective-permute-done.10.other_a, bf16[128,512]{1,0:T(8,128)(2,1)S(1)} %add_convert_fusion.own_b, bf16[128,512]{1,0:T(8,128)(2,1)S(1)} %collective-permute-done.15.other_b), custom_call_target="tpu_custom_call" | custom-call | bytes 1500000 | tf_op jit(solution)/shard_map/widen/pallas_call | solution.py:637
  (48 shorter events, 6.9 us)
Async XLA Ops:
  2.3 10.6 %collective-permute-start = (bf16[64,512]{1,0:T(8,128)(2,1)S(1)}, bf16[64,512]{1,0:T(8,128)(2,1)S(1)}, u32[]{:S(2)}, u32[]{:S(2)}) collective-permute-start(bf16[64,512]{1,0:T(8,128)(2,1)S(1)} %get-tuple-element.39), channel_id=1, source_target_pairs={{0,4},{4,0},{8,12},{12,8},{1,5},{5,1},{9,13},{13,9},{2,6},{6,2},{1... | collective-permute-start | bytes 196616 | tf_op jit(solution)/shard_map/ppermute | solution.py:393
  5.4 7.6 %collective-permute-start.1 = (bf16[64,512]{1,0:T(8,128)(2,1)S(1)}, bf16[64,512]{1,0:T(8,128)(2,1)S(1)}, u32[]{:S(2)}, u32[]{:S(2)}) collective-permute-start(bf16[64,512]{1,0:T(8,128)(2,1)S(1)} %get-tuple-element.40), channel_id=1, source_target_pairs={{0,0},{4,8},{8,4},{12,12},{1,1},{5,9},{9,5},{13,13},{2,2},{6,10},{... | collective-permute-start | bytes 196616 | tf_op jit(solution)/shard_map/ppermute | solution.py:393
  6.0 7.7 %collective-permute-start.2 = (bf16[64,512]{1,0:T(8,128)(2,1)S(1)}, bf16[64,512]{1,0:T(8,128)(2,1)S(1)}, u32[]{:S(2)}, u32[]{:S(2)}) collective-permute-start(bf16[64,512]{1,0:T(8,128)(2,1)S(1)} %get-tuple-element.41), channel_id=1, source_target_pairs={{0,8},{4,12},{8,0},{12,4},{1,9},{5,13},{9,1},{13,5},{2,10},{6,14},... | collective-permute-start | bytes 196616 | tf_op jit(solution)/shard_map/ppermute | solution.py:393
  12.9 8.6 %copy-start = (bf16[1536,512]{1,0:T(8,128)(2,1)}, bf16[1536,512]{1,0:T(8,128)(2,1)S(1)}, u32[]{:S(2)}) copy-start(bf16[1536,512]{1,0:T(8,128)(2,1)S(1)} %get-tuple-element.44.refs_5_.win_ref) | copy-start | bytes 4718596
  21.5 1.0 %copy-start.3 = (f32[2,256,512]{2,1,0:T(8,128)}, f32[2,256,512]{2,1,0:T(8,128)S(1)}, u32[]{:S(2)}) copy-start(f32[2,256,512]{2,1,0:T(8,128)S(1)} %get-tuple-element.66.kept_ref) | copy-start | bytes 3145732
  22.4 0.9 %copy-start.5 = (bf16[768,512]{1,0:T(8,128)(2,1)}, bf16[768,512]{1,0:T(8,128)(2,1)S(1)}, u32[]{:S(2)}) copy-start(bf16[768,512]{1,0:T(8,128)(2,1)S(1)} %get-tuple-element.55.gpre_ref) | copy-start | bytes 2359300
  23.3 0.7 copy-start.11
  24.0 2.6 %collective-permute-start.3 = (bf16[2,256,512]{2,1,0:T(8,128)(2,1)S(1)}, bf16[2,256,512]{2,1,0:T(8,128)(2,1)S(1)}, u32[]{:S(2)}, u32[]{:S(2)}) collective-permute-start(bf16[2,256,512]{2,1,0:T(8,128)(2,1)S(1)} %get-tuple-element.51), channel_id=1, source_target_pairs={{0,1},{1,0},{2,3},{3,2},{4,5},{5,4},{6,7},{7,6},{8,9},{9,8},{10,11... | collective-permute-start | bytes 1572872 | tf_op jit(solution)/shard_map/ppermute | solution.py:393
  24.0 11.9 %collective-permute-start.11 = (bf16[2,256,512]{2,1,0:T(8,128)(2,1)}, bf16[2,256,512]{2,1,0:T(8,128)(2,1)}, u32[]{:S(2)}, u32[]{:S(2)}) collective-permute-start(bf16[2,256,512]{2,1,0:T(8,128)(2,1)} %get-tuple-element.65), channel_id=1, source_target_pairs={{0,1},{1,0},{2,3},{3,2},{4,5},{5,4},{6,7},{7,6},{8,9},{9,8},{10,11... | collective-permute-start | bytes 1572872 | tf_op jit(solution)/shard_map/ppermute | solution.py:393
  27.4 7.3 %copy-start.7 = (f32[1,256,512]{2,1,0:T(8,128)}, f32[1,256,512]{2,1,0:T(8,128)S(1)}, u32[]{:S(2)}) copy-start(f32[1,256,512]{2,1,0:T(8,128)S(1)} %get-tuple-element.62.kept_ref) | copy-start | bytes 1572868
  27.4 11.7 %collective-permute-start.7 = (bf16[1,256,512]{2,1,0:T(8,128)(2,1)}, bf16[1,256,512]{2,1,0:T(8,128)(2,1)}, u32[]{:S(2)}, u32[]{:S(2)}) collective-permute-start(bf16[1,256,512]{2,1,0:T(8,128)(2,1)} %get-tuple-element.54.after), channel_id=1, source_target_pairs={{0,2},{1,3},{2,0},{3,1},{4,6},{5,7},{6,4},{7,5},{8,10},{9,11},{10,... | collective-permute-start | bytes 786440 | tf_op jit(solution)/shard_map/ppermute | solution.py:393
  28.9 1.4 %copy-start.1 = (bf16[1536,512]{1,0:T(8,128)(2,1)S(1)}, bf16[1536,512]{1,0:T(8,128)(2,1)}, u32[]{:S(2)}) copy-start(bf16[1536,512]{1,0:T(8,128)(2,1)} %copy-done) | copy-start | bytes 4718596
  30.4 1.1 %copy-start.6 = (bf16[768,512]{1,0:T(8,128)(2,1)S(1)}, bf16[768,512]{1,0:T(8,128)(2,1)}, u32[]{:S(2)}) copy-start(bf16[768,512]{1,0:T(8,128)(2,1)} %copy-done.5) | copy-start | bytes 2359300
  31.5 4.5 %copy-start.4 = (f32[2,256,512]{2,1,0:T(8,128)S(1)}, f32[2,256,512]{2,1,0:T(8,128)}, u32[]{:S(2)}) copy-start(f32[2,256,512]{2,1,0:T(8,128)} %copy-done.3) | copy-start | bytes 3145732
  35.3 0.6 copy-start.16
  35.9 3.2 %copy-start.14 = (bf16[64,512]{1,0:T(8,128)(2,1)}, bf16[64,512]{1,0:T(8,128)(2,1)S(1)}, u32[]{:S(2)}) copy-start(bf16[64,512]{1,0:T(8,128)(2,1)S(1)} %get-tuple-element.59.after) | copy-start | bytes 196612
  37.8 0.8 %copy-start.9 = (f32[1,256,512]{2,1,0:T(8,128)}, f32[1,256,512]{2,1,0:T(8,128)S(1)}, u32[]{:S(2)}) copy-start(f32[1,256,512]{2,1,0:T(8,128)S(1)} %get-tuple-element.68.kept_ref) | copy-start | bytes 1572868
  38.6 13.2 %copy-start.2 = (bf16[1536,512]{1,0:T(8,128)(2,1)S(1)}, bf16[1536,512]{1,0:T(8,128)(2,1)}, u32[]{:S(2)}) copy-start(bf16[1536,512]{1,0:T(8,128)(2,1)} %copy-done) | copy-start | bytes 4718596
  38.6 16.3 %collective-permute-start.12 = (bf16[1,256,512]{2,1,0:T(8,128)(2,1)}, bf16[1,256,512]{2,1,0:T(8,128)(2,1)}, u32[]{:S(2)}, u32[]{:S(2)}) collective-permute-start(bf16[1,256,512]{2,1,0:T(8,128)(2,1)} %get-tuple-element.67), channel_id=1, source_target_pairs={{0,2},{1,3},{2,0},{3,1},{4,6},{5,7},{6,4},{7,5},{8,10},{9,11},{10,... | collective-permute-start | bytes 786440 | tf_op jit(solution)/shard_map/ppermute | solution.py:393
  39.1 1.0 %copy-start.8 = (f32[1,256,512]{2,1,0:T(8,128)S(1)}, f32[1,256,512]{2,1,0:T(8,128)}, u32[]{:S(2)}) copy-start(f32[1,256,512]{2,1,0:T(8,128)} %copy-done.7) | copy-start | bytes 1572868
  41.1 13.7 %copy-start.13 = (f32[128,512]{1,0:T(8,128)}, f32[128,512]{1,0:T(8,128)S(1)}, u32[]{:S(2)}) copy-start(f32[128,512]{1,0:T(8,128)S(1)} %get-tuple-element.63) | copy-start | bytes 786436
  41.2 13.7 %copy-start.10 = (f32[1,256,512]{2,1,0:T(8,128)S(1)}, f32[1,256,512]{2,1,0:T(8,128)}, u32[]{:S(2)}) copy-start(f32[1,256,512]{2,1,0:T(8,128)} %copy-done.9) | copy-start | bytes 1572868
  41.2 16.1 %collective-permute-start.8 = (bf16[128,512]{1,0:T(8,128)(2,1)S(1)}, bf16[128,512]{1,0:T(8,128)(2,1)S(1)}, u32[]{:S(2)}, u32[]{:S(2)}) collective-permute-start(bf16[128,512]{1,0:T(8,128)(2,1)S(1)} %get-tuple-element.64), channel_id=1, source_target_pairs={{0,4},{4,0},{8,12},{12,8},{1,5},{5,1},{9,13},{13,9},{2,6},{6,2},{1... | collective-permute-start | bytes 393224 | tf_op jit(solution)/shard_map/ppermute | solution.py:393
  43.1 4.6 %collective-permute-start.5 = (bf16[64,512]{1,0:T(8,128)(2,1)}, bf16[64,512]{1,0:T(8,128)(2,1)S(1)}, u32[]{:S(2)}, u32[]{:S(2)}) collective-permute-start(bf16[64,512]{1,0:T(8,128)(2,1)} %copy-done.16), channel_id=1, source_target_pairs={{0,0},{4,8},{8,4},{12,12},{1,1},{5,9},{9,5},{13,13},{2,2},{6,10},{... | collective-permute-start | bytes 196616 | tf_op jit(solution)/shard_map/ppermute | solution.py:393
  44.6 6.4 %collective-permute-start.6 = (bf16[64,512]{1,0:T(8,128)(2,1)}, bf16[64,512]{1,0:T(8,128)(2,1)S(1)}, u32[]{:S(2)}, u32[]{:S(2)}) collective-permute-start(bf16[64,512]{1,0:T(8,128)(2,1)} %copy-done.15), channel_id=1, source_target_pairs={{0,8},{4,12},{8,0},{12,4},{1,9},{5,13},{9,1},{13,5},{2,10},{6,14},... | collective-permute-start | bytes 196616 | tf_op jit(solution)/shard_map/ppermute | solution.py:393
  47.1 4.6 %collective-permute-start.4 = (bf16[64,512]{1,0:T(8,128)(2,1)}, bf16[64,512]{1,0:T(8,128)(2,1)S(1)}, u32[]{:S(2)}, u32[]{:S(2)}) collective-permute-start(bf16[64,512]{1,0:T(8,128)(2,1)} %copy-done.14), channel_id=1, source_target_pairs={{0,4},{4,0},{8,12},{12,8},{1,5},{5,1},{9,13},{13,9},{2,6},{6,2},{1... | collective-permute-start | bytes 196616 | tf_op jit(solution)/shard_map/ppermute | solution.py:393
  51.7 1.0 %copy-start.12 = (f32[128,512]{1,0:T(8,128)S(1)}, f32[128,512]{1,0:T(8,128)}, u32[]{:S(2)}) copy-start(f32[128,512]{1,0:T(8,128)} %copy-done.11) | copy-start | bytes 786436
  55.8 5.8 %collective-permute-start.13 = (bf16[128,512]{1,0:T(8,128)(2,1)S(1)}, bf16[128,512]{1,0:T(8,128)(2,1)S(1)}, u32[]{:S(2)}, u32[]{:S(2)}) collective-permute-start(bf16[128,512]{1,0:T(8,128)(2,1)S(1)} %get-tuple-element.70), channel_id=1, source_target_pairs={{0,4},{4,0},{8,12},{12,8},{1,5},{5,1},{9,13},{13,9},{2,6},{6,2},{1... | collective-permute-start | bytes 393224 | tf_op jit(solution)/shard_map/ppermute | solution.py:393
  58.2 10.0 %collective-permute-start.9 = (bf16[128,512]{1,0:T(8,128)(2,1)S(1)}, bf16[128,512]{1,0:T(8,128)(2,1)S(1)}, u32[]{:S(2)}, u32[]{:S(2)}) collective-permute-start(bf16[128,512]{1,0:T(8,128)(2,1)S(1)} %add_convert_fusion.3), channel_id=1, source_target_pairs={{0,12},{4,8},{8,4},{12,0},{1,13},{5,9},{9,5},{13,1},{2,14},{6,10},... | collective-permute-start | bytes 393224 | tf_op jit(solution)/shard_map/ppermute | solution.py:393
  61.7 10.0 %collective-permute-start.14 = (bf16[128,512]{1,0:T(8,128)(2,1)S(1)}, bf16[128,512]{1,0:T(8,128)(2,1)S(1)}, u32[]{:S(2)}, u32[]{:S(2)}) collective-permute-start(bf16[128,512]{1,0:T(8,128)(2,1)S(1)} %add_convert_fusion.1), channel_id=1, source_target_pairs={{0,12},{4,8},{8,4},{12,0},{1,13},{5,9},{9,5},{13,1},{2,14},{6,10},... | collective-permute-start | bytes 393224 | tf_op jit(solution)/shard_map/ppermute | solution.py:393
  68.3 5.0 %collective-permute-start.10 = (bf16[128,512]{1,0:T(8,128)(2,1)S(1)}, bf16[128,512]{1,0:T(8,128)(2,1)S(1)}, u32[]{:S(2)}, u32[]{:S(2)}) collective-permute-start(bf16[128,512]{1,0:T(8,128)(2,1)S(1)} %add_convert_fusion.2.own_a), channel_id=1, source_target_pairs={{0,4},{4,0},{8,12},{12,8},{1,5},{5,1},{9,13},{13,9},{2,6},{6,2},{1... | collective-permute-start | bytes 393224 | tf_op jit(solution)/shard_map/ppermute | solution.py:393
  71.7 5.0 %collective-permute-start.15 = (bf16[128,512]{1,0:T(8,128)(2,1)S(1)}, bf16[128,512]{1,0:T(8,128)(2,1)S(1)}, u32[]{:S(2)}, u32[]{:S(2)}) collective-permute-start(bf16[128,512]{1,0:T(8,128)(2,1)S(1)} %add_convert_fusion.own_b), channel_id=1, source_target_pairs={{0,4},{4,0},{8,12},{12,8},{1,5},{5,1},{9,13},{13,9},{2,6},{6,2},{1... | collective-permute-start | bytes 393224 | tf_op jit(solution)/shard_map/ppermute | solution.py:393
  (1 other events, 0.6 us)

commit v5 on v4

--- a/solution.py
+++ b/solution.py
@@ -335,7 +335,8 @@
         left_ref[slot] = kept_ref[here] + came_ref[here].astype(F32)
 
 
-def split_kernel(came_ref, kept_ref, after, away_ref, left_ref):
+def split_kernel(came_ref, kept_ref, *refs):
+    away_ref, left_ref = refs[-2:]
     part = lax.axis_index("dom")
     inner = (part == 1) | (part == 2)
     rows = left_ref.shape[0]
@@ -345,7 +346,7 @@
     left_ref[...] = kept_ref[0, here, :] + came_ref[0, here, :].astype(F32)
 
 
-def node_grad_kernel(arrivals, four, boundary_hbm, sums_ref, recv_ref, win_ref, *refs):
+def node_grad_kernel(arrivals, four, boundary_hbm, after, sums_ref, recv_ref, win_ref, *refs):
     returned = refs[:arrivals]
     out_ref, total_ref, boundary_ref, sem = refs[arrivals:]
     nodes, latent = recv_ref.shape
@@ -368,7 +369,7 @@
     ).astype(BF16)
 
 
-def last_kernel(own_a, other_a, own_b, other_b, in_ref, out_ref):
+def last_kernel(after, own_a, other_a, own_b, other_b, in_ref, out_ref):
     unit = out_ref.shape[0]
     part = lax.axis_index("dom")
     inner = (part == 1) | (part == 2)
@@ -420,6 +421,7 @@
         ),
         in_specs=[VMEM] * 3,
         out_specs=(VMEM,) * 2,
+        compiler_params=pltpu.CompilerParams(vmem_limit_bytes=4 * 1024 * 1024),
         cost_estimate=pl.CostEstimate(flops=0, bytes_accessed=500_000, transcendentals=0),
         name="halve",
     )(in_vmem(came), in_vmem(kept), in_vmem(after))
@@ -436,20 +438,27 @@
         away, kept = halve(bit, came, kept, after)
 
 
-def sum_over_four(came, kept, after):
+def split(came, kept, after):
     rows, latent = kept.shape[1:]
-    away, kept = pl.pallas_call(
+    return pl.pallas_call(
         split_kernel,
         out_shape=(
             pltpu.VMEM((rows // 2, latent), BF16),
             pltpu.VMEM((rows // 2, latent), F32),
         ),
-        in_specs=[VMEM] * 2 + [HBM],
+        in_specs=[VMEM] * (2 + len(after)),
         out_specs=(VMEM,) * 2,
+        compiler_params=pltpu.CompilerParams(vmem_limit_bytes=4 * 1024 * 1024),
         cost_estimate=pl.CostEstimate(flops=0, bytes_accessed=500_000, transcendentals=0),
         name="split",
-    )(in_vmem(came), in_vmem(kept), in_hbm(after))
-    kept = (kept + swap(away, "dom", lambda i: i ^ 1).astype(F32)).astype(BF16)
+    )(in_vmem(came), in_vmem(kept), *[in_vmem(array) for array in after])
+
+
+def sum_of_pair(away, kept):
+    return (kept + swap(away, "dom", lambda i: i ^ 1).astype(F32)).astype(BF16)
+
+
+def sum_of_four(kept):
     kept = (kept.astype(F32) + swap(kept, "dom", lambda i: 3 - i).astype(F32)).astype(BF16)
     return kept, swap(kept, "dom", lambda i: i ^ 1)
 
@@ -617,10 +626,16 @@
         returned = [
             from_behind(back_sums[which], "dom", -OFFSET_LIST[which]) for which in range(4)
         ]
+    if four:
+        pair_a = sum_of_pair(*split(came_a, kept_a, returned))
+        pair_b = sum_of_pair(*split(came_b, kept_b, ()))
+        late = pair_b
+    else:
+        late = sent_a
     node_out = pl.pallas_call(
         functools.partial(node_grad_kernel, arrivals, four),
         out_shape=jax.ShapeDtypeStruct((nodes, latent), BF16),
-        in_specs=[HBM] + [VMEM] * (3 + arrivals),
+        in_specs=[HBM] + [VMEM] * (4 + arrivals),
         out_specs=VMEM,
         scratch_shapes=[
             pltpu.VMEM((nodes, latent), F32),
@@ -632,7 +647,7 @@
             flops=8 * nodes * latent * latent, bytes_accessed=2_000_000, transcendentals=0
         ),
         name="node_grads",
-    )(boundary, *[in_vmem(array) for array in (sums, recv_sums, win_v, *returned)])
+    )(boundary, *[in_vmem(array) for array in (late, sums, recv_sums, win_v, *returned)])
     if four:
         w_in_grad, w_out_grad = pl.pallas_call(
             last_kernel,
@@ -640,12 +655,12 @@
                 jax.ShapeDtypeStruct((3 * unit, latent), F32),
                 jax.ShapeDtypeStruct((unit, latent), F32),
             ),
-            in_specs=[VMEM] * 4,
+            in_specs=[HBM] + [VMEM] * 4,
             out_specs=(VMEM,) * 2,
             compiler_params=small,
             cost_estimate=pl.CostEstimate(flops=0, bytes_accessed=1_500_000, transcendentals=0),
             name="widen",
-        )(*sum_over_four(came_a, kept_a, edge_grad), *sum_over_four(came_b, kept_b, node_out))
+        )(in_hbm(node_out), *sum_of_four(pair_a), *sum_of_four(pair_b))
     else:
         sum_a = sum_over_dom(kept_a[0] + came_a[0].astype(F32))
         sum_b = sum_over_dom(kept_b[0] + came_b[0].astype(F32))

time: 78.3 us -> 59.9 us (0.77)
  local copies, waits for them, and re-layouts: 9.14 us -> 0 us
  Pallas kernels: 22.6 us -> 16.5 us
  waiting for transfers between devices: 16.3 us -> 14.5 us
  other arithmetic: 1.08 us -> 0.12 us
    unnamed x34 -> x0, local copies, waits for them, and re-layouts: 9.14 us -> none
    pallas_call x2, Pallas kernels: 2.61 us -> 0.19 us  [halve(): pl.pallas_call(functools.partial(halve_kernel, bit), out_shape=(pltpu.VME...]
    pallas_call x2, Pallas kernels: 1.99 us -> 0.08 us  [split(): pl.pallas_call(split_kernel, out_shape=(pltpu.VMEM((rows // 2, latent), B...]
    ppermute x16, waiting for transfers between devices: 16.3 us -> 14.5 us  [swap(): return lax.ppermute(array, axis, [(i, partner(i)) for i in range(devices)])]
    pallas_call x1, Pallas kernels: 3.19 us -> 2.16 us  [body(): pl.pallas_call(functools.partial(edge_grad_kernel, block, arrivals, four)...]
    convert_element_type x4, other arithmetic: 1.08 us -> 0.12 us  [the longest x2 0.07 us: sum_of_four(): (kept.astype(F32) + swap(kept, 'dom', lambda i: 3 - i).astype(F32)).astyp...]
  transfers between devices with their start and end apart: 16 -> 16, of which waited for: 8 -> 7; matrix products, arithmetic and copies ran while one was open for 1% -> 0% of each run, Pallas kernels for 16% -> 12%
where the time goes in v5:
time: 59.9 us; the launch traced here: 59.7 us
  starting transfers between devices  27.1 us (45%)
  Pallas kernels  16.5 us (28%)
  waiting for transfers between devices  14.5 us (24%)
  between operations  1.43 us (2%)
    ppermute x16, starting transfers between devices, swap(): return lax.ppermute(array, axis, [(i, partner(i)) for i in range(devices)])  27.1 us
    ppermute x16, waiting for transfers between devices, swap(): return lax.ppermute(array, axis, [(i, partner(i)) for i in range(devices)])  14.5 us
    pallas_call x1, Pallas kernels, body(): pl.pallas_call(functools.partial(edge_kernel, ways, arrivals, four, block...  6.92 us
    pallas_call x1, Pallas kernels, body(): pl.pallas_call(functools.partial(prep_kernel, parts, arrivals), out_shape...  2.32 us
    pallas_call x1, Pallas kernels, body(): pl.pallas_call(functools.partial(edge_grad_kernel, block, arrivals, four)...  2.16 us
    pallas_call x1, Pallas kernels, body(): pl.pallas_call(functools.partial(node_grad_kernel, arrivals, four), out_s...  2.13 us
    pallas_call x1, Pallas kernels, body(): pl.pallas_call(functools.partial(pick_kernel, four, block), out_shape=(bl...  1.67 us
  transfers between devices with their start and end apart: 16, of which 7 were waited for; matrix products, arithmetic and copies ran while one was open for 0% of the time, Pallas kernels for 12%

profile of v5, /device:TPU:0, one launch (start us, length us, event | category | flops | bytes accessed | tf_op | source)
XLA Modules:
  0.0 59.7 jit_solution(13221170581246069933)
XLA Ops:
  0.6 1.7 %pick_blocks.1 = (bf16[64,512]{1,0:T(8,128)(2,1)S(1)}, bf16[64,512]{1,0:T(8,128)(2,1)S(1)}, bf16[64,512]{1,0:T(8,128)(2,1)S(1)}) custom-call(s32[1,4]{1,0:T(1,128)} %boundary_hbm.3, bf16[128,512]{1,0:T(8,128)(2,1)} %bitcast.8), custom_call_target="tpu_custom_call" | custom-call | bytes 400000 | tf_op jit(solution)/shard_map/pick_blocks/pallas_call | solution.py:504
  2.3 3.1 %collective-permute-start = (bf16[64,512]{1,0:T(8,128)(2,1)S(1)}, bf16[64,512]{1,0:T(8,128)(2,1)S(1)}, u32[]{:S(2)}, u32[]{:S(2)}) collective-permute-start(bf16[64,512]{1,0:T(8,128)(2,1)S(1)} %get-tuple-element.39), channel_id=1, source_target_pairs={{0,4},{4,0},{8,12},{12,8},{1,5},{5,1},{9,13},{13,9},{2,6},{6,2},{1... | collective-permute-start | bytes 196616 | tf_op jit(solution)/shard_map/ppermute | solution.py:394
  5.4 0.7 %collective-permute-start.1 = (bf16[64,512]{1,0:T(8,128)(2,1)S(1)}, bf16[64,512]{1,0:T(8,128)(2,1)S(1)}, u32[]{:S(2)}, u32[]{:S(2)}) collective-permute-start(bf16[64,512]{1,0:T(8,128)(2,1)S(1)} %get-tuple-element.40), channel_id=1, source_target_pairs={{0,0},{4,8},{8,4},{12,12},{1,1},{5,9},{9,5},{13,13},{2,2},{6,10},{... | collective-permute-start | bytes 196616 | tf_op jit(solution)/shard_map/ppermute | solution.py:394
  6.1 3.9 %collective-permute-start.2 = (bf16[64,512]{1,0:T(8,128)(2,1)S(1)}, bf16[64,512]{1,0:T(8,128)(2,1)S(1)}, u32[]{:S(2)}, u32[]{:S(2)}) collective-permute-start(bf16[64,512]{1,0:T(8,128)(2,1)S(1)} %get-tuple-element.41), channel_id=1, source_target_pairs={{0,8},{4,12},{8,0},{12,4},{1,9},{5,13},{9,1},{13,5},{2,10},{6,14},... | collective-permute-start | bytes 196616 | tf_op jit(solution)/shard_map/ppermute | solution.py:394
  10.6 2.3 %prepare.1 = (bf16[128,512]{1,0:T(8,128)(2,1)S(1)}, bf16[768,512]{1,0:T(8,128)(2,1)S(1)}, bf16[128,512]{1,0:T(8,128)(2,1)S(1)}, bf16[1536,512]{1,0:T(8,128)(2,1)...) custom-call(s32[12]{0:T(128)} %src_hbm.1, ...), custom_call_target="tpu_custom_call" | custom-call | flops 402653184 | bytes 8000000 | tf_op jit(solution)/shard_map/prepare/pallas_call | solution.py:526
  12.9 0.0 collective-permute-done.refs_0_
  12.9 0.0 collective-permute-done.1.refs_1_
  12.9 0.8 %collective-permute-done.2.refs_2_ = bf16[64,512]{1,0:T(8,128)(2,1)S(1)} collective-permute-done((bf16[64,512]{1,0:T(8,128)(2,1)S(1)}, bf16[64,512]{1,0:T(8,128)(2,1)S(1)}, u32[]{:S(2)}, u32[]{:S(2)}) %collective-permute-start.2) | collective-permute-done | bytes 65568 | tf_op jit(solution)/shard_map/ppermute | solution.py:394
  13.8 6.9 %edge_block.1 = (bf16[128,512]{1,0:T(8,128)(2,1)}, bf16[768,512]{1,0:T(8,128)(2,1)S(1)}, f32[384,512]{1,0:T(8,128)S(1)}, f32[128,512]{1,0:T(8,128)S(1)}, bf16[2,...) custom-call(s32[12]{0:T(128)} %dst_hbm.5, ...), custom_call_target="tpu_custom_call" | custom-call | flops 2818572288 | bytes 12000000 | tf_op jit(solution)/shard_map/edge_block/pallas_call | solution.py:563
  20.7 0.1 collective-permute-start.3
  20.8 0.5 collective-permute-start.4
  21.3 1.4 %collective-permute-done.3.came_ref = bf16[2,256,512]{2,1,0:T(8,128)(2,1)S(1)} collective-permute-done((bf16[2,256,512]{2,1,0:T(8,128)(2,1)S(1)}, bf16[2,256,512]{2,1,0:T(8,128)(2,1)S(1)}, u32[]{:S(2)}, u32[]{:S(2)}) %collective-permute-start.3) | collective-permute-done | bytes 524320 | tf_op jit(solution)/shard_map/ppermute | solution.py:394
  22.7 0.1 halve.2
  22.8 1.6 %collective-permute-start.10 = (bf16[1,256,512]{2,1,0:T(8,128)(2,1)S(1)}, bf16[1,256,512]{2,1,0:T(8,128)(2,1)S(1)}, u32[]{:S(2)}, u32[]{:S(2)}) collective-permute-start(bf16[1,256,512]{2,1,0:T(8,128)(2,1)S(1)} %get-tuple-element.54.after), channel_id=1, source_target_pairs={{0,2},{1,3},{2,0},{3,1},{4,6},{5,7},{6,4},{7,5},{8,10},{9,11},{10,... | collective-permute-start | bytes 786440 | tf_op jit(solution)/shard_map/ppermute | solution.py:394
  24.3 2.2 %edge_grads.1 = (bf16[768,512]{1,0:T(8,128)(2,1)}, bf16[64,512]{1,0:T(8,128)(2,1)S(1)}, bf16[64,512]{1,0:T(8,128)(2,1)S(1)}, bf16[64,512]{1,0:T(8,128)(2,1)S(1)}) custom-call(s32[12]{0:T(128)} %dst_hbm.5, s32[1]{0:T(128)S(6)} %copy.15.count_ref, bf16[1,256,512]{2,1,0:T(8,128)(2,1)S(1)} %get-tuple-element.54.after, ...), custom_call_target="tpu_custom_call" | custom-call | flops 402653184 | bytes 3000000 | tf_op jit(solution)/shard_map/edge_grads/pallas_call | solution.py:603
  26.5 0.1 halve.3
  26.6 0.6 collective-permute-start.5
  27.2 0.7 %collective-permute-start.8 = (bf16[64,512]{1,0:T(8,128)(2,1)S(1)}, bf16[64,512]{1,0:T(8,128)(2,1)S(1)}, u32[]{:S(2)}, u32[]{:S(2)}) collective-permute-start(bf16[64,512]{1,0:T(8,128)(2,1)S(1)} %get-tuple-element.66), channel_id=1, source_target_pairs={{0,0},{4,8},{8,4},{12,12},{1,1},{5,9},{9,5},{13,13},{2,2},{6,10},{... | collective-permute-start | bytes 196616 | tf_op jit(solution)/shard_map/ppermute | solution.py:394
  27.9 4.7 %collective-permute-start.9 = (bf16[64,512]{1,0:T(8,128)(2,1)S(1)}, bf16[64,512]{1,0:T(8,128)(2,1)S(1)}, u32[]{:S(2)}, u32[]{:S(2)}) collective-permute-start(bf16[64,512]{1,0:T(8,128)(2,1)S(1)} %get-tuple-element.67), channel_id=1, source_target_pairs={{0,8},{4,12},{8,0},{12,4},{1,9},{5,13},{9,1},{13,5},{2,10},{6,14},... | collective-permute-start | bytes 196616 | tf_op jit(solution)/shard_map/ppermute | solution.py:394
  32.5 4.4 %collective-permute-done.9.refs_2_ = bf16[64,512]{1,0:T(8,128)(2,1)S(1)} collective-permute-done((bf16[64,512]{1,0:T(8,128)(2,1)S(1)}, bf16[64,512]{1,0:T(8,128)(2,1)S(1)}, u32[]{:S(2)}, u32[]{:S(2)}) %collective-permute-start.9) | collective-permute-done | bytes 65568 | tf_op jit(solution)/shard_map/ppermute | solution.py:394
  36.9 0.5 collective-permute-done.7.refs_0_
  37.4 0.2 collective-permute-start.11
  37.6 2.0 %collective-permute-start.6 = (bf16[128,512]{1,0:T(8,128)(2,1)S(1)}, bf16[128,512]{1,0:T(8,128)(2,1)S(1)}, u32[]{:S(2)}, u32[]{:S(2)}) collective-permute-start(bf16[128,512]{1,0:T(8,128)(2,1)S(1)} %get-tuple-element.64), channel_id=1, source_target_pairs={{0,4},{4,0},{8,12},{12,8},{1,5},{5,1},{9,13},{13,9},{2,6},{6,2},{1... | collective-permute-start | bytes 393224 | tf_op jit(solution)/shard_map/ppermute | solution.py:394
  39.7 2.8 %collective-permute-done.11 = bf16[128,512]{1,0:T(8,128)(2,1)S(1)} collective-permute-done((bf16[128,512]{1,0:T(8,128)(2,1)S(1)}, bf16[128,512]{1,0:T(8,128)(2,1)S(1)}, u32[]{:S(2)}, u32[]{:S(2)}) %collective-permute-start.11) | collective-permute-done | bytes 131104 | tf_op jit(solution)/shard_map/ppermute | solution.py:394
  42.5 1.9 %collective-permute-start.12 = (bf16[128,512]{1,0:T(8,128)(2,1)S(1)}, bf16[128,512]{1,0:T(8,128)(2,1)S(1)}, u32[]{:S(2)}, u32[]{:S(2)}) collective-permute-start(bf16[128,512]{1,0:T(8,128)(2,1)S(1)} %add_convert_fusion.2), channel_id=1, source_target_pairs={{0,12},{4,8},{8,4},{12,0},{1,13},{5,9},{9,5},{13,1},{2,14},{6,10},... | collective-permute-start | bytes 393224 | tf_op jit(solution)/shard_map/ppermute | solution.py:394
  44.5 2.6 %collective-permute-start.14 = (bf16[128,512]{1,0:T(8,128)(2,1)S(1)}, bf16[128,512]{1,0:T(8,128)(2,1)S(1)}, u32[]{:S(2)}, u32[]{:S(2)}) collective-permute-start(bf16[128,512]{1,0:T(8,128)(2,1)S(1)} %add_convert_fusion.3.after), channel_id=1, source_target_pairs={{0,12},{4,8},{8,4},{12,0},{1,13},{5,9},{9,5},{13,1},{2,14},{6,10},... | collective-permute-start | bytes 393224 | tf_op jit(solution)/shard_map/ppermute | solution.py:394
  47.0 3.1 %collective-permute-done.12 = bf16[128,512]{1,0:T(8,128)(2,1)S(1)} collective-permute-done((bf16[128,512]{1,0:T(8,128)(2,1)S(1)}, bf16[128,512]{1,0:T(8,128)(2,1)S(1)}, u32[]{:S(2)}, u32[]{:S(2)}) %collective-permute-start.12) | collective-permute-done | bytes 131104 | tf_op jit(solution)/shard_map/ppermute | solution.py:394
  50.1 3.4 %collective-permute-start.13 = (bf16[128,512]{1,0:T(8,128)(2,1)S(1)}, bf16[128,512]{1,0:T(8,128)(2,1)S(1)}, u32[]{:S(2)}, u32[]{:S(2)}) collective-permute-start(bf16[128,512]{1,0:T(8,128)(2,1)S(1)} %add_convert_fusion.1.own_a), channel_id=1, source_target_pairs={{0,4},{4,0},{8,12},{12,8},{1,5},{5,1},{9,13},{13,9},{2,6},{6,2},{1... | collective-permute-start | bytes 393224 | tf_op jit(solution)/shard_map/ppermute | solution.py:394
  53.6 1.4 %collective-permute-start.15 = (bf16[128,512]{1,0:T(8,128)(2,1)S(1)}, bf16[128,512]{1,0:T(8,128)(2,1)S(1)}, u32[]{:S(2)}, u32[]{:S(2)}) collective-permute-start(bf16[128,512]{1,0:T(8,128)(2,1)S(1)} %add_convert_fusion.own_b), channel_id=1, source_target_pairs={{0,4},{4,0},{8,12},{12,8},{1,5},{5,1},{9,13},{13,9},{2,6},{6,2},{1... | collective-permute-start | bytes 393224 | tf_op jit(solution)/shard_map/ppermute | solution.py:394
  55.0 2.1 %node_grads.1.after = bf16[128,512]{1,0:T(8,128)(2,1)} custom-call(s32[1,4]{1,0:T(1,128)} %boundary_hbm.3, bf16[128,512]{1,0:T(8,128)(2,1)S(1)} %add_convert_fusion.3.after, f32[384,512]{1,0:T(8,128)S(1)} %get-tuple-element.56.sums_ref, f32[128,512]{1,0:T(8,128)S(1)} %get-tuple-element.65.recv_ref, bf16[1536,512]{1,0:T(8,128)(2,1)S(1)} %get-tuple-element.44.refs_5_.win_ref, ...), custom_call_target="tpu_custom_call" | custom-call | flops 268435456 | bytes 2000000 | tf_op jit(solution)/shard_map/node_grads/pallas_call | solution.py:635
  57.1 1.5 %collective-permute-done.15.other_b = bf16[128,512]{1,0:T(8,128)(2,1)S(1)} collective-permute-done((bf16[128,512]{1,0:T(8,128)(2,1)S(1)}, bf16[128,512]{1,0:T(8,128)(2,1)S(1)}, u32[]{:S(2)}, u32[]{:S(2)}) %collective-permute-start.15) | collective-permute-done | bytes 131104 | tf_op jit(solution)/shard_map/ppermute | solution.py:394
  58.6 1.0 %widen.1 = (f32[384,512]{1,0:T(8,128)}, f32[128,512]{1,0:T(8,128)}) custom-call(bf16[128,512]{1,0:T(8,128)(2,1)} %node_grads.1.after, bf16[128,512]{1,0:T(8,128)(2,1)S(1)} %add_convert_fusion.1.own_a, bf16[128,512]{1,0:T(8,128)(2,1)S(1)} %collective-permute-done.13.other_a, bf16[128,512]{1,0:T(8,128)(2,1)S(1)} %add_convert_fusion.own_b, ...), custom_call_target="tpu_custom_call" | custom-call | bytes 1500000 | tf_op jit(solution)/shard_map/widen/pallas_call | solution.py:652
  (14 shorter events, 0.2 us)
Async XLA Ops:
  2.3 10.6 %collective-permute-start = (bf16[64,512]{1,0:T(8,128)(2,1)S(1)}, bf16[64,512]{1,0:T(8,128)(2,1)S(1)}, u32[]{:S(2)}, u32[]{:S(2)}) collective-permute-start(bf16[64,512]{1,0:T(8,128)(2,1)S(1)} %get-tuple-element.39), channel_id=1, source_target_pairs={{0,4},{4,0},{8,12},{12,8},{1,5},{5,1},{9,13},{13,9},{2,6},{6,2},{1... | collective-permute-start | bytes 196616 | tf_op jit(solution)/shard_map/ppermute | solution.py:394
  5.4 7.5 %collective-permute-start.1 = (bf16[64,512]{1,0:T(8,128)(2,1)S(1)}, bf16[64,512]{1,0:T(8,128)(2,1)S(1)}, u32[]{:S(2)}, u32[]{:S(2)}) collective-permute-start(bf16[64,512]{1,0:T(8,128)(2,1)S(1)} %get-tuple-element.40), channel_id=1, source_target_pairs={{0,0},{4,8},{8,4},{12,12},{1,1},{5,9},{9,5},{13,13},{2,2},{6,10},{... | collective-permute-start | bytes 196616 | tf_op jit(solution)/shard_map/ppermute | solution.py:394
  6.1 7.7 %collective-permute-start.2 = (bf16[64,512]{1,0:T(8,128)(2,1)S(1)}, bf16[64,512]{1,0:T(8,128)(2,1)S(1)}, u32[]{:S(2)}, u32[]{:S(2)}) collective-permute-start(bf16[64,512]{1,0:T(8,128)(2,1)S(1)} %get-tuple-element.41), channel_id=1, source_target_pairs={{0,8},{4,12},{8,0},{12,4},{1,9},{5,13},{9,1},{13,5},{2,10},{6,14},... | collective-permute-start | bytes 196616 | tf_op jit(solution)/shard_map/ppermute | solution.py:394
  20.7 2.0 %collective-permute-start.3 = (bf16[2,256,512]{2,1,0:T(8,128)(2,1)S(1)}, bf16[2,256,512]{2,1,0:T(8,128)(2,1)S(1)}, u32[]{:S(2)}, u32[]{:S(2)}) collective-permute-start(bf16[2,256,512]{2,1,0:T(8,128)(2,1)S(1)} %get-tuple-element.51), channel_id=1, source_target_pairs={{0,1},{1,0},{2,3},{3,2},{4,5},{5,4},{6,7},{7,6},{8,9},{9,8},{10,11... | collective-permute-start | bytes 1572872 | tf_op jit(solution)/shard_map/ppermute | solution.py:394
  20.8 5.7 %collective-permute-start.4 = (bf16[2,256,512]{2,1,0:T(8,128)(2,1)S(1)}, bf16[2,256,512]{2,1,0:T(8,128)(2,1)S(1)}, u32[]{:S(2)}, u32[]{:S(2)}) collective-permute-start(bf16[2,256,512]{2,1,0:T(8,128)(2,1)S(1)} %get-tuple-element.58), channel_id=1, source_target_pairs={{0,1},{1,0},{2,3},{3,2},{4,5},{5,4},{6,7},{7,6},{8,9},{9,8},{10,11... | collective-permute-start | bytes 1572872 | tf_op jit(solution)/shard_map/ppermute | solution.py:394
  22.8 14.6 %collective-permute-start.10 = (bf16[1,256,512]{2,1,0:T(8,128)(2,1)S(1)}, bf16[1,256,512]{2,1,0:T(8,128)(2,1)S(1)}, u32[]{:S(2)}, u32[]{:S(2)}) collective-permute-start(bf16[1,256,512]{2,1,0:T(8,128)(2,1)S(1)} %get-tuple-element.54.after), channel_id=1, source_target_pairs={{0,2},{1,3},{2,0},{3,1},{4,6},{5,7},{6,4},{7,5},{8,10},{9,11},{10,... | collective-permute-start | bytes 786440 | tf_op jit(solution)/shard_map/ppermute | solution.py:394
  26.6 11.0 %collective-permute-start.5 = (bf16[1,256,512]{2,1,0:T(8,128)(2,1)S(1)}, bf16[1,256,512]{2,1,0:T(8,128)(2,1)S(1)}, u32[]{:S(2)}, u32[]{:S(2)}) collective-permute-start(bf16[1,256,512]{2,1,0:T(8,128)(2,1)S(1)} %get-tuple-element.61), channel_id=1, source_target_pairs={{0,2},{1,3},{2,0},{3,1},{4,6},{5,7},{6,4},{7,5},{8,10},{9,11},{10,... | collective-permute-start | bytes 786440 | tf_op jit(solution)/shard_map/ppermute | solution.py:394
  27.2 5.3 %collective-permute-start.8 = (bf16[64,512]{1,0:T(8,128)(2,1)S(1)}, bf16[64,512]{1,0:T(8,128)(2,1)S(1)}, u32[]{:S(2)}, u32[]{:S(2)}) collective-permute-start(bf16[64,512]{1,0:T(8,128)(2,1)S(1)} %get-tuple-element.66), channel_id=1, source_target_pairs={{0,0},{4,8},{8,4},{12,12},{1,1},{5,9},{9,5},{13,13},{2,2},{6,10},{... | collective-permute-start | bytes 196616 | tf_op jit(solution)/shard_map/ppermute | solution.py:394
  27.9 9.0 %collective-permute-start.9 = (bf16[64,512]{1,0:T(8,128)(2,1)S(1)}, bf16[64,512]{1,0:T(8,128)(2,1)S(1)}, u32[]{:S(2)}, u32[]{:S(2)}) collective-permute-start(bf16[64,512]{1,0:T(8,128)(2,1)S(1)} %get-tuple-element.67), channel_id=1, source_target_pairs={{0,8},{4,12},{8,0},{12,4},{1,9},{5,13},{9,1},{13,5},{2,10},{6,14},... | collective-permute-start | bytes 196616 | tf_op jit(solution)/shard_map/ppermute | solution.py:394
  32.5 4.9 %collective-permute-start.7 = (bf16[64,512]{1,0:T(8,128)(2,1)S(1)}, bf16[64,512]{1,0:T(8,128)(2,1)S(1)}, u32[]{:S(2)}, u32[]{:S(2)}) collective-permute-start(bf16[64,512]{1,0:T(8,128)(2,1)S(1)} %get-tuple-element.60.after), channel_id=1, source_target_pairs={{0,4},{4,0},{8,12},{12,8},{1,5},{5,1},{9,13},{13,9},{2,6},{6,2},{1... | collective-permute-start | bytes 196616 | tf_op jit(solution)/shard_map/ppermute | solution.py:394
  37.4 5.0 %collective-permute-start.11 = (bf16[128,512]{1,0:T(8,128)(2,1)S(1)}, bf16[128,512]{1,0:T(8,128)(2,1)S(1)}, u32[]{:S(2)}, u32[]{:S(2)}) collective-permute-start(bf16[128,512]{1,0:T(8,128)(2,1)S(1)} %get-tuple-element.70), channel_id=1, source_target_pairs={{0,4},{4,0},{8,12},{12,8},{1,5},{5,1},{9,13},{13,9},{2,6},{6,2},{1... | collective-permute-start | bytes 393224 | tf_op jit(solution)/shard_map/ppermute | solution.py:394
  37.6 6.8 %collective-permute-start.6 = (bf16[128,512]{1,0:T(8,128)(2,1)S(1)}, bf16[128,512]{1,0:T(8,128)(2,1)S(1)}, u32[]{:S(2)}, u32[]{:S(2)}) collective-permute-start(bf16[128,512]{1,0:T(8,128)(2,1)S(1)} %get-tuple-element.64), channel_id=1, source_target_pairs={{0,4},{4,0},{8,12},{12,8},{1,5},{5,1},{9,13},{13,9},{2,6},{6,2},{1... | collective-permute-start | bytes 393224 | tf_op jit(solution)/shard_map/ppermute | solution.py:394
  42.5 7.6 %collective-permute-start.12 = (bf16[128,512]{1,0:T(8,128)(2,1)S(1)}, bf16[128,512]{1,0:T(8,128)(2,1)S(1)}, u32[]{:S(2)}, u32[]{:S(2)}) collective-permute-start(bf16[128,512]{1,0:T(8,128)(2,1)S(1)} %add_convert_fusion.2), channel_id=1, source_target_pairs={{0,12},{4,8},{8,4},{12,0},{1,13},{5,9},{9,5},{13,1},{2,14},{6,10},... | collective-permute-start | bytes 393224 | tf_op jit(solution)/shard_map/ppermute | solution.py:394
  44.5 9.1 %collective-permute-start.14 = (bf16[128,512]{1,0:T(8,128)(2,1)S(1)}, bf16[128,512]{1,0:T(8,128)(2,1)S(1)}, u32[]{:S(2)}, u32[]{:S(2)}) collective-permute-start(bf16[128,512]{1,0:T(8,128)(2,1)S(1)} %add_convert_fusion.3.after), channel_id=1, source_target_pairs={{0,12},{4,8},{8,4},{12,0},{1,13},{5,9},{9,5},{13,1},{2,14},{6,10},... | collective-permute-start | bytes 393224 | tf_op jit(solution)/shard_map/ppermute | solution.py:394
  50.1 7.0 %collective-permute-start.13 = (bf16[128,512]{1,0:T(8,128)(2,1)S(1)}, bf16[128,512]{1,0:T(8,128)(2,1)S(1)}, u32[]{:S(2)}, u32[]{:S(2)}) collective-permute-start(bf16[128,512]{1,0:T(8,128)(2,1)S(1)} %add_convert_fusion.1.own_a), channel_id=1, source_target_pairs={{0,4},{4,0},{8,12},{12,8},{1,5},{5,1},{9,13},{13,9},{2,6},{6,2},{1... | collective-permute-start | bytes 393224 | tf_op jit(solution)/shard_map/ppermute | solution.py:394
  53.6 5.0 %collective-permute-start.15 = (bf16[128,512]{1,0:T(8,128)(2,1)S(1)}, bf16[128,512]{1,0:T(8,128)(2,1)S(1)}, u32[]{:S(2)}, u32[]{:S(2)}) collective-permute-start(bf16[128,512]{1,0:T(8,128)(2,1)S(1)} %add_convert_fusion.own_b), channel_id=1, source_target_pairs={{0,4},{4,0},{8,12},{12,8},{1,5},{5,1},{9,13},{13,9},{2,6},{6,2},{1... | collective-permute-start | bytes 393224 | tf_op jit(solution)/shard_map/ppermute | solution.py:394

commit v6 on v4

--- a/solution.py
+++ b/solution.py
@@ -79,6 +79,7 @@
 def prep_kernel(
     parts,
     arrivals,
+    count_ref,
     src_hbm,
     dst_hbm,
     slot_hbm,
@@ -93,19 +94,20 @@
     win_ref,
     wout_ref,
     pre_ref,
-    mid_ref,
+    up_ref,
     hot_ref,
     hot_turned,
     src_ref,
     dst_ref,
     slot_ref,
     recv_ref,
+    mid_ref,
     sems,
 ):
     tiles, block = slot_ref.shape
     nodes, latent = node_ref.shape
     owned = nodes // block
-    extent = hot_turned.shape[0]
+    extent = hot_ref.shape[1]
     pairs = (
         (src_hbm, src_ref),
         (dst_hbm, dst_ref),
@@ -123,7 +125,10 @@
     for copy in copies[:3]:
         copy.wait()
     index = lax.broadcasted_iota(jnp.int32, (extent, 2 * block), 0)
-    first = lax.broadcasted_iota(jnp.int32, (1, 2 * block), 1) < block
+    lane = lax.broadcasted_iota(jnp.int32, (1, 2 * block), 1)
+    first = lane < block
+    within = jnp.where(first, lane, lane - block)
+    node_index = lax.broadcasted_iota(jnp.int32, (nodes, 2 * block), 0)
     for tile in range(0, tiles, 2):
         wanted = []
         for member in (tile, tile + 1):
@@ -140,7 +145,9 @@
         row = slots + jnp.where(first, wanted[0], wanted[1])
         hot = jnp.where(index == row, 1.0, 0.0)
         at = slice(tile * block, (tile + 2) * block)
-        hot_turned[:, at] = hot.astype(BF16)
+        hot_turned[:extent, at] = hot.astype(BF16)
+        target = within + jnp.where(first, dst_ref[tile] * block, dst_ref[tile + 1] * block)
+        hot_turned[extent:, at] = jnp.where(node_index == target, 1.0, 0.0).astype(BF16)
         hot_ref[at, :] = hot.T.astype(BF16)
     copies[3].wait()
     copies[4].wait()
@@ -157,19 +164,62 @@
     copies[7].wait()
     cot = cot_ref[...].astype(F32)
     mid_ref[...] = cot - row_mean(cot)
+    for tile in range(tiles):
+        live = jnp.where(tile < count_ref[0], 1.0, 0.0)
+        up_ref[tile * block : (tile + 1) * block, :] = rows_of(mid_ref, dst_ref[tile], block) * live
     copies[8].wait()
     copies[9].wait()
 
 
-def edge_kernel(
-    ways,
-    arrivals,
-    four,
-    block,
-    dst_hbm,
-    count_ref,
-    *refs,
-):
+def put_units(chunk, ways, bit, away, kept, sections):
+    latent = sections[0][0].shape[1]
+    unit = latent // ways
+    step = 128
+
+    def wanted(number, start):
+        if number == 0:
+            return [(start + at) // unit for at in range(0, step, unit)] if chunk == 0 else []
+        found = []
+        for at in range(0, step, unit):
+            spot = ((number - 1) * latent + start + at) // unit
+            if (1 + spot % 3) // 2 == chunk:
+                found.append(spot)
+        return found
+
+    for number, (left, right) in enumerate(sections):
+        value_right = right()
+        start = 0
+        while start < latent:
+            size = step
+            if start + 2 * step <= latent and wanted(number, start + step):
+                size = 2 * step
+            if wanted(number, start):
+                value = t_dot(left[:, start : start + size], value_right)
+                for at in range(0, size, unit):
+                    if number == 0:
+                        owner, spot = (start + at) // unit, 0
+                    else:
+                        place = ((number - 1) * latent + start + at) // unit
+                        owner, spot = place // 3, 1 + place % 3
+                    if spot // 2 != chunk:
+                        continue
+                    part = value[at : at + unit]
+                    where = slice((spot % 2) * unit, (spot % 2 + 1) * unit)
+
+                    @pl.when(bit == owner % 2)
+                    def _(owner=owner, where=where, part=part):
+                        kept[owner // 2, where, :] = part
+
+                    @pl.when(bit != owner % 2)
+                    def _(owner=owner, where=where, part=part):
+                        away[owner // 2, where, :] = part.astype(BF16)
+
+                start += size
+            else:
+                start += step
+
+
+def edge_kernel(ways, arrivals, four, block, *refs):
     arrived = refs[:arrivals]
     (
         node_ref,
@@ -177,50 +227,34 @@
         win_ref,
         wout_ref,
         pre_ref,
-        mid_ref,
+        up_ref,
         hot_ref,
         hot_turned,
-        agg_hbm,
         gpre_ref,
+        message_ref,
         sums_ref,
-        recv_sums,
-        away_a,
-        kept_a,
-        away_b,
-        kept_b,
-        dst_ref,
         ext_ref,
+        away_ref,
+        kept_ref,
         act_ref,
         proj_ref,
-        agg_ref,
-        agg_bf16,
-        sems,
     ) = refs[arrivals:]
     nodes, latent = node_ref.shape
     edges = edge_ref.shape[0]
-    tiles = edges // block
-    owned = nodes // block
-    part = lax.axis_index("dom")
-    bit = lax.axis_index("dp") % 2
-    dst_copy = load_small(dst_hbm, dst_ref, sems.at[0])
-    places = arrival_places(part, four, arrivals)
+    extent = ext_ref.shape[0]
+    places = arrival_places(lax.axis_index("dom"), four, arrivals)
 
     ext_ref[:nodes, :] = node_ref[...]
     for which in range(arrivals):
-        at = pl.multiple_of((owned + places[which]) * block, block)
+        at = pl.multiple_of(nodes + places[which] * block, block)
         ext_ref[pl.ds(at, block), :] = arrived[which][...]
     filled = nodes + arrivals * block
-    if filled < ext_ref.shape[0]:
-        ext_ref[filled:, :] = jnp.zeros((ext_ref.shape[0] - filled, latent), BF16)
-    agg_ref[...] = jnp.zeros_like(agg_ref)
-    recv_sums[...] = jnp.zeros_like(recv_sums)
-
-    group = 4 if tiles % 4 == 0 else 1
-    span = group * block
-    for first in range(0, tiles, group):
-        rows = slice(first * block, first * block + span)
-        members = range(first, first + group)
-        edge_rows = edge_ref[rows, :]
+    if filled < extent:
+        ext_ref[filled:, :] = jnp.zeros((extent - filled, latent), BF16)
+
+    span = 256 if edges % 256 == 0 else block
+    for start in range(0, edges, span):
+        rows = slice(start, start + span)
         senders = dot(hot_ref[rows, :], ext_ref[...]).astype(BF16)
         preact = pre_ref[rows, :] + dot(senders, win_ref[latent : 2 * latent, :])
         gate = 0.5 * jnp.tanh(0.5 * preact) + 0.5
@@ -232,61 +266,32 @@
         centered = projected - row_mean(projected)
         inv_scale = lax.rsqrt(row_mean(centered * centered) + EPSILON)
         message = centered * inv_scale
-        updated = edge_rows.astype(F32) + message
-        if first == 0:
-            dst_copy.wait()
-        upstream = []
-        for number, tile in enumerate(members):
-            live = jnp.where(tile < count_ref[0], 1.0, 0.0)
-            target = pl.ds(pl.multiple_of(dst_ref[tile] * block, block), block)
-            agg_ref[target, :] += updated[number * block : (number + 1) * block] * live
-            upstream.append(mid_ref[target, :] * live)
-        upstream = jnp.concatenate(upstream, axis=0)
+        message_ref[rows, :] = message
+        upstream = up_ref[rows, :]
         grad_project = inv_scale * (upstream - message * row_mean(upstream * message))
         grad_project = grad_project.astype(BF16)
         proj_ref[rows, :] = grad_project
-        grad_pre = (dot_t(grad_project, wout_ref[...]) * slope).astype(BF16)
-        gpre_ref[rows, :] = grad_pre
-        for number, tile in enumerate(members):
-            mine = grad_pre[number * block : (number + 1) * block]
-            target = pl.ds(pl.multiple_of(dst_ref[tile] * block, block), block)
-            recv_sums[target, :] += mine.astype(F32)
-
-    agg_bf16[...] = agg_ref[...].astype(BF16)
-    agg_copy = load_small(agg_bf16, agg_hbm, sems.at[1])
+        gpre_ref[rows, :] = (dot_t(grad_project, wout_ref[...]) * slope).astype(BF16)
+
     sums_ref[...] = dot(hot_turned[...], gpre_ref[...])
-
-    unit = latent // ways
-
-    def put(owner, spot, value):
-        away, kept = (away_a, kept_a) if spot < 2 else (away_b, kept_b)
-        where = slice((spot % 2) * unit, (spot % 2 + 1) * unit)
-
-        @pl.when(bit == owner % 2)
-        def _():
-            kept[owner // 2, where, :] = value
-
-        @pl.when(bit != owner % 2)
-        def _():
-            away[owner // 2, where, :] = value.astype(BF16)
-
-    step = 256
-    for start in range(0, latent, step):
-        value = t_dot(act_ref[:, start : start + step], proj_ref[...])
-        for at in range(0, step, unit):
-            put((start + at) // unit, 0, value[at : at + unit])
     sections = (
-        (edge_ref, gpre_ref),
-        (ext_ref, sums_ref),
-        (node_ref, recv_sums),
+        (act_ref, lambda: proj_ref[...]),
+        (edge_ref, lambda: gpre_ref[...]),
+        (ext_ref, lambda: sums_ref[:extent, :].astype(BF16)),
+        (node_ref, lambda: sums_ref[extent:, :].astype(BF16)),
     )
-    for number, (left, right) in enumerate(sections):
-        for start in range(0, latent, step):
-            value = t_dot(left[:, start : start + step], right[...].astype(BF16))
-            for at in range(0, step, unit):
-                spot = (number * latent + start + at) // unit
-                put(spot // 3, 1 + spot % 3, value[at : at + unit])
-    agg_copy.wait()
+    put_units(0, ways, lax.axis_index("dp") % 2, away_ref, kept_ref, sections)
+
+
+def rest_kernel(ways, node_ref, edge_ref, ext_ref, gpre_ref, sums_ref, away_ref, kept_ref):
+    extent = ext_ref.shape[0]
+    sections = (
+        (edge_ref, lambda: None),
+        (edge_ref, lambda: gpre_ref[...]),
+        (ext_ref, lambda: sums_ref[:extent, :].astype(BF16)),
+        (node_ref, lambda: sums_ref[extent:, :].astype(BF16)),
+    )
+    put_units(1, ways, lax.axis_index("dp") % 2, away_ref, kept_ref, sections)
 
 
 def edge_grad_kernel(
@@ -300,11 +305,14 @@
     sums_ref,
     cot_ref,
     win_ref,
+    edge_ref,
+    message_ref,
     out_ref,
+    agg_out,
     *refs,
 ):
     back_sums = refs[:arrivals]
-    dst_ref, sem = refs[arrivals:]
+    dst_ref, agg_ref, sem = refs[arrivals:]
     copy = load_small(dst_hbm, dst_ref, sem)
     nodes, latent = cot_ref.shape
     tiles = gpre_ref.shape[0] // block
@@ -313,6 +321,7 @@
     for which in range(arrivals):
         at = pl.multiple_of(nodes + places[which] * block, block)
         back_sums[which][...] = sums_ref[pl.ds(at, block), :].astype(BF16)
+    agg_ref[...] = jnp.zeros_like(agg_ref)
     copy.wait()
     for first in range(0, tiles, group):
         rows = slice(first * block, (first + group) * block)
@@ -325,6 +334,13 @@
             axis=0,
         )
         out_ref[rows, :] = (dot_t(gpre_ref[rows, :], win_ref[:latent, :]) + upstream).astype(BF16)
+        for t in range(first, first + group):
+            live = jnp.where(t < count_ref[0], 1.0, 0.0)
+            mine = slice(t * block, (t + 1) * block)
+            updated = edge_ref[mine, :].astype(F32) + message_ref[mine, :]
+            target = pl.ds(pl.multiple_of(dst_ref[t] * block, block), block)
+            agg_ref[target, :] += updated * live
+    agg_out[...] = agg_ref[...].astype(BF16)
 
 
 def halve_kernel(bit, came_ref, kept_ref, after, away_ref, left_ref):
@@ -335,20 +351,34 @@
         left_ref[slot] = kept_ref[here] + came_ref[here].astype(F32)
 
 
-def split_kernel(came_ref, kept_ref, after, away_ref, left_ref):
+def quarter_kernel(came_ref, kept_ref, after, cross_ref, over_ref, beside_ref, left_ref):
     part = lax.axis_index("dom")
+    mine = lax.axis_index("dp") // 2
     inner = (part == 1) | (part == 2)
     rows = left_ref.shape[0]
     here = pl.ds(pl.multiple_of(jnp.where(inner, 0, rows), rows), rows)
     there = pl.ds(pl.multiple_of(jnp.where(inner, rows, 0), rows), rows)
-    away_ref[...] = (kept_ref[0, there, :] + came_ref[0, there, :].astype(F32)).astype(BF16)
-    left_ref[...] = kept_ref[0, here, :] + came_ref[0, here, :].astype(F32)
-
-
-def node_grad_kernel(arrivals, four, boundary_hbm, sums_ref, recv_ref, win_ref, *refs):
+
+    def total(slot, where):
+        return kept_ref[slot, where, :] + came_ref[slot, where, :].astype(F32)
+
+    cross_ref[...] = total(1 - mine, there).astype(BF16)
+    over_ref[...] = total(1 - mine, here).astype(BF16)
+    beside_ref[...] = total(mine, there).astype(BF16)
+    left_ref[...] = total(mine, here)
+
+
+def add_kernel(left_ref, cross_ref, over_ref, beside_ref, *refs):
+    out_ref = refs[-1]
+    terms = [ref[...].astype(F32) for ref in (cross_ref, over_ref, beside_ref)]
+    out_ref[...] = ((left_ref[...] + terms[1]) + (terms[0] + terms[2])).astype(BF16)
+
+
+def node_grad_kernel(arrivals, four, boundary_hbm, after, sums_ref, win_ref, *refs):
     returned = refs[:arrivals]
     out_ref, total_ref, boundary_ref, sem = refs[arrivals:]
-    nodes, latent = recv_ref.shape
+    nodes, latent = out_ref.shape
+    extent = sums_ref.shape[0] - nodes
     block = returned[0].shape[0]
     copy = load_small(boundary_hbm, boundary_ref, sem)
     total_ref[...] = sums_ref[:nodes, :]
@@ -364,11 +394,11 @@
 
     out_ref[...] = (
         wide_dot(total_ref[...], win_ref[latent : 2 * latent, :])
-        + wide_dot(recv_ref[...], win_ref[2 * latent :, :])
+        + wide_dot(sums_ref[extent:, :], win_ref[2 * latent :, :])
     ).astype(BF16)
 
 
-def last_kernel(own_a, other_a, own_b, other_b, in_ref, out_ref):
+def last_kernel(after, own_a, other_a, own_b, other_b, in_ref, out_ref):
     unit = out_ref.shape[0]
     part = lax.axis_index("dom")
     inner = (part == 1) | (part == 2)
@@ -404,10 +434,10 @@
 
 
 def exchange_of_four(first, second, third):
-    return [
-        swap(array, "dom", lambda i, which=which: partners_of_four(which)[i])
-        for which, array in enumerate((first, second, third))
-    ]
+    third = swap(third, "dom", lambda i: partners_of_four(2)[i])
+    second = swap(second, "dom", lambda i: partners_of_four(1)[i])
+    first = swap(first, "dom", lambda i: partners_of_four(0)[i])
+    return [first, second, third]
 
 
 def halve(bit, came, kept, after):
@@ -420,6 +450,7 @@
         ),
         in_specs=[VMEM] * 3,
         out_specs=(VMEM,) * 2,
+        compiler_params=pltpu.CompilerParams(vmem_limit_bytes=4 * 1024 * 1024),
         cost_estimate=pl.CostEstimate(flops=0, bytes_accessed=500_000, transcendentals=0),
         name="halve",
     )(in_vmem(came), in_vmem(kept), in_vmem(after))
@@ -436,20 +467,47 @@
         away, kept = halve(bit, came, kept, after)
 
 
-def sum_over_four(came, kept, after):
-    rows, latent = kept.shape[1:]
-    away, kept = pl.pallas_call(
-        split_kernel,
-        out_shape=(
-            pltpu.VMEM((rows // 2, latent), BF16),
-            pltpu.VMEM((rows // 2, latent), F32),
-        ),
-        in_specs=[VMEM] * 2 + [HBM],
-        out_specs=(VMEM,) * 2,
-        cost_estimate=pl.CostEstimate(flops=0, bytes_accessed=500_000, transcendentals=0),
-        name="split",
-    )(in_vmem(came), in_vmem(kept), in_hbm(after))
-    kept = (kept + swap(away, "dom", lambda i: i ^ 1).astype(F32)).astype(BF16)
+def sum_of_square(away, kept, after):
+    slots, rows, latent = kept.shape
+    came = swap(away, "dp", lambda i: i ^ 1)
+    piece = pltpu.VMEM((rows // 2, latent), BF16)
+    limit = pltpu.CompilerParams(vmem_limit_bytes=4 * 1024 * 1024)
+    cost = pl.CostEstimate(flops=0, bytes_accessed=500_000, transcendentals=0)
+    cross, over, beside, left = pl.pallas_call(
+        quarter_kernel,
+        out_shape=(piece, piece, piece, pltpu.VMEM((rows // 2, latent), F32)),
+        in_specs=[VMEM] * 3,
+        out_specs=(VMEM,) * 4,
+        compiler_params=limit,
+        cost_estimate=cost,
+        name="quarter",
+    )(in_vmem(came), in_vmem(kept), in_vmem(after))
+    ways = lax.axis_size("dp")
+    parts = lax.axis_size("dom")
+    diagonal = [
+        (d * ways + p, (d ^ 1) * ways + (p ^ 2)) for d in range(parts) for p in range(ways)
+    ]
+    arrived = [
+        lax.ppermute(cross, ("dom", "dp"), diagonal),
+        swap(over, "dp", lambda i: i ^ 2),
+        swap(beside, "dom", lambda i: i ^ 1),
+    ]
+
+    def finish(*late):
+        return pl.pallas_call(
+            add_kernel,
+            out_shape=piece,
+            in_specs=[VMEM] * (4 + len(late)),
+            out_specs=VMEM,
+            compiler_params=limit,
+            cost_estimate=cost,
+            name="add_terms",
+        )(*[in_vmem(array) for array in (left, *arrived, *late)])
+
+    return cross, finish
+
+
+def sum_of_four(kept):
     kept = (kept.astype(F32) + swap(kept, "dom", lambda i: 3 - i).astype(F32)).astype(BF16)
     return kept, swap(kept, "dom", lambda i: i ^ 1)
 
@@ -484,7 +542,7 @@
     nodes = node_latents.shape[1]
     parts = lax.axis_size("dom")
     ways = lax.axis_size("dp")
-    four = parts == 4
+    four = parts == 4 and ways == 4
     arrivals = 3 if four else 4
     boundary = in_hbm(boundary)
     tile_dst = in_hbm(tile_dst)
@@ -514,7 +572,7 @@
     half = ways // 2
     extent = -(-(nodes + arrivals * block) // 128) * 128
 
-    node_v, edge_v, cot_v, win_v, wout_v, pre, mid, hot, turned = pl.pallas_call(
+    node_v, edge_v, cot_v, win_v, wout_v, pre, up, hot, turned = pl.pallas_call(
         functools.partial(prep_kernel, parts, arrivals),
         out_shape=(
             pltpu.VMEM((nodes, latent), BF16),
@@ -523,16 +581,17 @@
             pltpu.VMEM(weight_in.shape, BF16),
             pltpu.VMEM(weight_out.shape, BF16),
             pltpu.VMEM((edges, latent), F32),
-            pltpu.VMEM((nodes, latent), F32),
+            pltpu.VMEM((edges, latent), F32),
             pltpu.VMEM((edges, extent), BF16),
-            pltpu.VMEM((extent, edges), BF16),
+            pltpu.VMEM((extent + nodes, edges), BF16),
         ),
-        in_specs=[HBM] * 8,
+        in_specs=[SMEM] + [HBM] * 8,
         out_specs=(VMEM,) * 9,
         scratch_shapes=[
             pltpu.SMEM((tiles,), jnp.int32),
             pltpu.SMEM((tiles,), jnp.int32),
             pltpu.VMEM((tiles, block), jnp.int32),
+            pltpu.VMEM((nodes, latent), F32),
             pltpu.VMEM((nodes, latent), F32),
             pltpu.SemaphoreType.DMA((10,)),
         ],
@@ -542,6 +601,7 @@
         ),
         name="prepare",
     )(
+        tile_count,
         in_hbm(tile_src),
         tile_dst,
         in_hbm(edge_slot),
@@ -551,53 +611,64 @@
         in_hbm(weight_in),
         in_hbm(weight_out),
     )
-    outs = pl.pallas_call(
+    sent_shape = pltpu.VMEM((half, 2 * unit, latent), BF16)
+    kept_shape = pltpu.VMEM((half, 2 * unit, latent), F32)
+    grad_pre, message, sums, ext, away_a, kept_a = pl.pallas_call(
         functools.partial(edge_kernel, ways, arrivals, four, block),
         out_shape=(
-            jax.ShapeDtypeStruct((nodes, latent), BF16),
             pltpu.VMEM((edges, latent), BF16),
-            pltpu.VMEM((extent, latent), F32),
-            pltpu.VMEM((nodes, latent), F32),
-            pltpu.VMEM((half, 2 * unit, latent), BF16),
-            pltpu.VMEM((half, 2 * unit, latent), F32),
-            pltpu.VMEM((half, 2 * unit, latent), BF16),
-            pltpu.VMEM((half, 2 * unit, latent), F32),
+            pltpu.VMEM((edges, latent), F32),
+            pltpu.VMEM((extent + nodes, latent), F32),
+            pltpu.VMEM((extent, latent), BF16),
+            sent_shape,
+            kept_shape,
         ),
-        in_specs=[HBM, SMEM] + [VMEM] * (8 + arrivals),
-        out_specs=(HBM,) + (VMEM,) * 7,
+        in_specs=[VMEM] * (8 + arrivals),
+        out_specs=(VMEM,) * 6,
         scratch_shapes=[
-            pltpu.SMEM((tiles,), jnp.int32),
-            pltpu.VMEM((extent, latent), BF16),
             pltpu.VMEM((edges, latent), BF16),
             pltpu.VMEM((edges, latent), BF16),
-            pltpu.VMEM((nodes, latent), F32),
-            pltpu.VMEM((nodes, latent), BF16),
-            pltpu.SemaphoreType.DMA((2,)),
         ],
         compiler_params=pltpu.CompilerParams(vmem_limit_bytes=16 * 1024 * 1024),
         cost_estimate=pl.CostEstimate(
-            flops=14 * edges * latent * latent,
+            flops=12 * edges * latent * latent,
             bytes_accessed=12_000_000,
             transcendentals=edges * latent,
         ),
         name="edge_block",
     )(
-        tile_dst,
-        tile_count,
         *[
             in_vmem(array)
-            for array in (*came, node_v, edge_v, win_v, wout_v, pre, mid, hot, turned)
+            for array in (*came, node_v, edge_v, win_v, wout_v, pre, up, hot, turned)
         ],
     )
-    agg, grad_pre, sums, recv_sums, away_a, kept_a, away_b, kept_b = outs
-    came_a, kept_a, sent_a = sum_over_dp(away_a, kept_a, cot_v)
-    edge_grad, *back_sums = pl.pallas_call(
+    away_b, kept_b = pl.pallas_call(
+        functools.partial(rest_kernel, ways),
+        out_shape=(sent_shape, kept_shape),
+        in_specs=[VMEM] * 5,
+        out_specs=(VMEM,) * 2,
+        compiler_params=small,
+        cost_estimate=pl.CostEstimate(
+            flops=2 * edges * latent * latent, bytes_accessed=4_000_000, transcendentals=0
+        ),
+        name="rest_weights",
+    )(*[in_vmem(array) for array in (node_v, edge_v, ext, grad_pre, sums)])
+    if four:
+        sent_a, finish_a = sum_of_square(away_a, kept_a, cot_v)
+    else:
+        came_a, kept_a, sent_a = sum_over_dp(away_a, kept_a, cot_v)
+    edge_grad, agg, *back_sums = pl.pallas_call(
         functools.partial(edge_grad_kernel, block, arrivals, four),
-        out_shape=(jax.ShapeDtypeStruct((edges, latent), BF16),) + (block_shape,) * arrivals,
-        in_specs=[HBM, SMEM] + [VMEM] * 5,
-        out_specs=(VMEM,) * (1 + arrivals),
+        out_shape=(
+            jax.ShapeDtypeStruct((edges, latent), BF16),
+            jax.ShapeDtypeStruct((nodes, latent), BF16),
+        )
+        + (block_shape,) * arrivals,
+        in_specs=[HBM, SMEM] + [VMEM] * 7,
+        out_specs=(VMEM,) * (2 + arrivals),
         scratch_shapes=[
             pltpu.SMEM((tiles,), jnp.int32),
+            pltpu.VMEM((nodes, latent), F32),
             pltpu.SemaphoreType.DMA,
         ],
         compiler_params=small,
@@ -608,15 +679,20 @@
     )(
         tile_dst,
         tile_count,
-        *[in_vmem(array) for array in (sent_a, grad_pre, sums, cot_v, win_v)],
+        *[in_vmem(array) for array in (sent_a, grad_pre, sums, cot_v, win_v, edge_v, message)],
     )
-    came_b, kept_b, _ = sum_over_dp(away_b, kept_b, back_sums[0])
     if four:
         returned = exchange_of_four(*back_sums)
+        _, finish_b = sum_of_square(away_b, kept_b, back_sums[0])
+        pair_a = finish_a()
+        pair_b = finish_b(*returned)
+        late = pair_b
     else:
         returned = [
             from_behind(back_sums[which], "dom", -OFFSET_LIST[which]) for which in range(4)
         ]
+        came_b, kept_b, _ = sum_over_dp(away_b, kept_b, back_sums[0])
+        late = sent_a
     node_out = pl.pallas_call(
         functools.partial(node_grad_kernel, arrivals, four),
         out_shape=jax.ShapeDtypeStruct((nodes, latent), BF16),
@@ -632,7 +708,7 @@
             flops=8 * nodes * latent * latent, bytes_accessed=2_000_000, transcendentals=0
         ),
         name="node_grads",
-    )(boundary, *[in_vmem(array) for array in (sums, recv_sums, win_v, *returned)])
+    )(boundary, *[in_vmem(array) for array in (late, sums, win_v, *returned)])
     if four:
         w_in_grad, w_out_grad = pl.pallas_call(
             last_kernel,
@@ -640,12 +716,12 @@
                 jax.ShapeDtypeStruct((3 * unit, latent), F32),
                 jax.ShapeDtypeStruct((unit, latent), F32),
             ),
-            in_specs=[VMEM] * 4,
+            in_specs=[HBM] + [VMEM] * 4,
             out_specs=(VMEM,) * 2,
             compiler_params=small,
             cost_estimate=pl.CostEstimate(flops=0, bytes_accessed=1_500_000, transcendentals=0),
             name="widen",
-        )(*sum_over_four(came_a, kept_a, edge_grad), *sum_over_four(came_b, kept_b, node_out))
+        )(in_hbm(node_out), *sum_of_four(pair_a), *sum_of_four(pair_b))
     else:
         sum_a = sum_over_dom(kept_a[0] + came_a[0].astype(F32))
         sum_b = sum_over_dom(kept_b[0] + came_b[0].astype(F32))

time: 78.3 us -> 60.1 us (0.77)
  local copies, waits for them, and re-layouts: 9.14 us -> 0 us
  Pallas kernels: 22.6 us -> 17 us
  starting transfers between devices: 27.2 us -> 24.2 us
  other arithmetic: 1.08 us -> 0.07 us
  waiting for transfers between devices: 16.3 us -> 17.2 us
    unnamed x34 -> x0, local copies, waits for them, and re-layouts: 9.14 us -> none
    ppermute x16, starting transfers between devices: 27.2 us -> 23.8 us  [swap(): return lax.ppermute(array, axis, [(i, partner(i)) for i in range(devices)])]
    pallas_call x4 -> x5, Pallas kernels: 4.6 us -> 1.79 us  [the longest x1 1.49 us: body(): pl.pallas_call(functools.partial(rest_kernel, ways), out_shape=(sent_shap...]
    pallas_call x1, Pallas kernels: 7.7 us -> 5.74 us  [body(): pl.pallas_call(functools.partial(edge_kernel, ways, arrivals, four, block...]
    convert_element_type x4 -> x2, other arithmetic: 1.08 us -> 0.07 us  [sum_of_four(): (kept.astype(F32) + swap(kept, 'dom', lambda i: 3 - i).astype(F32)).astyp...]
    pallas_call x1, Pallas kernels: 3.19 us -> 2.21 us  [body(): pl.pallas_call(functools.partial(edge_grad_kernel, block, arrivals, four)...]
    ppermute x16, waiting for transfers between devices: 16.3 us -> 17.2 us  [swap(): return lax.ppermute(array, axis, [(i, partner(i)) for i in range(devices)])]
  transfers between devices with their start and end apart: 16 -> 18, of which waited for: 8 -> 4; matrix products, arithmetic and copies ran while one was open for 1% -> 0% of each run, Pallas kernels for 16% -> 14%
where the time goes in v6:
time: 60.1 us; the launch traced here: 59.9 us
  starting transfers between devices  24.2 us (40%)
  waiting for transfers between devices  17.2 us (29%)
  Pallas kernels  17 us (28%)
  between operations  1.46 us (2%)
    ppermute x16, starting transfers between devices, swap(): return lax.ppermute(array, axis, [(i, partner(i)) for i in range(devices)])  23.8 us
    ppermute x16, waiting for transfers between devices, swap(): return lax.ppermute(array, axis, [(i, partner(i)) for i in range(devices)])  17.2 us
    pallas_call x1, Pallas kernels, body(): pl.pallas_call(functools.partial(edge_kernel, ways, arrivals, four, block...  5.74 us
    pallas_call x1, Pallas kernels, body(): pl.pallas_call(functools.partial(prep_kernel, parts, arrivals), out_shape...  2.42 us
    pallas_call x1, Pallas kernels, body(): pl.pallas_call(functools.partial(edge_grad_kernel, block, arrivals, four)...  2.21 us
    pallas_call x1, Pallas kernels, body(): pl.pallas_call(functools.partial(node_grad_kernel, arrivals, four), out_s...  2.14 us
    pallas_call x1, Pallas kernels, body(): pl.pallas_call(functools.partial(pick_kernel, four, block), out_shape=(bl...  1.63 us
    pallas_call x1, Pallas kernels, body(): pl.pallas_call(functools.partial(rest_kernel, ways), out_shape=(sent_shap...  1.49 us
  transfers between devices with their start and end apart: 18, of which 4 were waited for; matrix products, arithmetic and copies ran while one was open for 0% of the time, Pallas kernels for 14%

profile of v6, /device:TPU:0, one launch (start us, length us, event | category | flops | bytes accessed | tf_op | source)
XLA Modules:
  0.0 59.9 jit_solution(15105893656716549040)
XLA Ops:
  0.6 1.6 %pick_blocks.1 = (bf16[64,512]{1,0:T(8,128)(2,1)S(1)}, bf16[64,512]{1,0:T(8,128)(2,1)S(1)}, bf16[64,512]{1,0:T(8,128)(2,1)S(1)}) custom-call(s32[1,4]{1,0:T(1,128)} %boundary_hbm.3, bf16[128,512]{1,0:T(8,128)(2,1)} %bitcast.8), custom_call_target="tpu_custom_call" | custom-call | bytes 400000 | tf_op jit(solution)/shard_map/pick_blocks/pallas_call | solution.py:553
  2.3 3.1 %collective-permute-start = (bf16[64,512]{1,0:T(8,128)(2,1)S(1)}, bf16[64,512]{1,0:T(8,128)(2,1)S(1)}, u32[]{:S(2)}, u32[]{:S(2)}) collective-permute-start(bf16[64,512]{1,0:T(8,128)(2,1)S(1)} %get-tuple-element.40), channel_id=1, source_target_pairs={{0,4},{4,0},{8,12},{12,8},{1,5},{5,1},{9,13},{13,9},{2,6},{6,2},{1... | collective-permute-start | bytes 196616 | tf_op jit(solution)/shard_map/ppermute | solution.py:423
  5.4 0.7 %collective-permute-start.1 = (bf16[64,512]{1,0:T(8,128)(2,1)S(1)}, bf16[64,512]{1,0:T(8,128)(2,1)S(1)}, u32[]{:S(2)}, u32[]{:S(2)}) collective-permute-start(bf16[64,512]{1,0:T(8,128)(2,1)S(1)} %get-tuple-element.41), channel_id=1, source_target_pairs={{0,0},{4,8},{8,4},{12,12},{1,1},{5,9},{9,5},{13,13},{2,2},{6,10},{... | collective-permute-start | bytes 196616 | tf_op jit(solution)/shard_map/ppermute | solution.py:423
  6.0 3.9 %collective-permute-start.2 = (bf16[64,512]{1,0:T(8,128)(2,1)S(1)}, bf16[64,512]{1,0:T(8,128)(2,1)S(1)}, u32[]{:S(2)}, u32[]{:S(2)}) collective-permute-start(bf16[64,512]{1,0:T(8,128)(2,1)S(1)} %get-tuple-element.42), channel_id=1, source_target_pairs={{0,8},{4,12},{8,0},{12,4},{1,9},{5,13},{9,1},{13,5},{2,10},{6,14},... | collective-permute-start | bytes 196616 | tf_op jit(solution)/shard_map/ppermute | solution.py:423
  10.6 2.4 %prepare.1 = (bf16[128,512]{1,0:T(8,128)(2,1)S(1)}, bf16[768,512]{1,0:T(8,128)(2,1)S(1)}, bf16[128,512]{1,0:T(8,128)(2,1)S(1)}, bf16[1536,512]{1,0:T(8,128)(2,1)...) custom-call(s32[1]{0:T(128)S(6)} %copy.15.count_ref, ...), custom_call_target="tpu_custom_call" | custom-call | flops 402653184 | bytes 8000000 | tf_op jit(solution)/shard_map/prepare/pallas_call | solution.py:575
  13.0 0.7 %collective-permute-done.2.refs_2_ = bf16[64,512]{1,0:T(8,128)(2,1)S(1)} collective-permute-done((bf16[64,512]{1,0:T(8,128)(2,1)S(1)}, bf16[64,512]{1,0:T(8,128)(2,1)S(1)}, u32[]{:S(2)}, u32[]{:S(2)}) %collective-permute-start.2) | collective-permute-done | bytes 65568 | tf_op jit(solution)/shard_map/ppermute | solution.py:423
  13.8 5.7 %edge_block.1 = (bf16[768,512]{1,0:T(8,128)(2,1)S(1)}, f32[768,512]{1,0:T(8,128)S(1)}, f32[512,512]{1,0:T(8,128)S(1)}, bf16[384,512]{1,0:T(8,128)(2,1)S(1)}, bf1...) custom-call(bf16[64,512]{1,0:T(8,128)(2,1)S(1)} %collective-permute-done.refs_0_, ...), custom_call_target="tpu_custom_call" | custom-call | flops 2415919104 | bytes 12000000 | tf_op jit(solution)/shard_map/edge_block/pallas_call | solution.py:616
  19.5 0.1 collective-permute-start.3
  19.6 1.5 %rest_weights.1 = (bf16[2,256,512]{2,1,0:T(8,128)(2,1)S(1)}, f32[2,256,512]{2,1,0:T(8,128)S(1)}) custom-call(bf16[128,512]{1,0:T(8,128)(2,1)S(1)} %get-tuple-element.43.refs_3_.node_ref, bf16[768,512]{1,0:T(8,128)(2,1)S(1)} %get-tuple-element.44.refs_4_.edge_ref, bf16[384,512]{1,0:T(8,128)(2,1)S(1)} %get-tuple-element.60.ext_ref, ...), custom_call_target="tpu_custom_call" | custom-call | flops 402653184 | bytes 4000000 | tf_op jit(solution)/shard_map/rest_weights/pallas_call | solution.py:645
  21.1 0.6 collective-permute-start.4
  21.7 0.1 quarter.2
  21.8 1.6 %collective-permute-start.12 = (bf16[128,512]{1,0:T(8,128)(2,1)S(1)}, bf16[128,512]{1,0:T(8,128)(2,1)S(1)}, u32[]{:S(2)}, u32[]{:S(2)}) collective-permute-start(bf16[128,512]{1,0:T(8,128)(2,1)S(1)} %get-tuple-element.71), channel_id=1, source_target_pairs={{0,2},{1,3},{2,0},{3,1},{4,6},{5,7},{6,4},{7,5},{8,10},{9,11},{10,... | collective-permute-start | bytes 393224 | tf_op jit(solution)/shard_map/ppermute | solution.py:423
  23.3 1.9 %collective-permute-start.13 = (bf16[128,512]{1,0:T(8,128)(2,1)S(1)}, bf16[128,512]{1,0:T(8,128)(2,1)S(1)}, u32[]{:S(2)}, u32[]{:S(2)}) collective-permute-start(bf16[128,512]{1,0:T(8,128)(2,1)S(1)} %get-tuple-element.72), channel_id=1, source_target_pairs={{0,4},{4,0},{8,12},{12,8},{1,5},{5,1},{9,13},{13,9},{2,6},{6,2},{1... | collective-permute-start | bytes 393224 | tf_op jit(solution)/shard_map/ppermute | solution.py:423
  25.2 0.1 collective-permute-start.11
  25.3 2.2 %edge_grads.1 = (bf16[768,512]{1,0:T(8,128)(2,1)}, bf16[128,512]{1,0:T(8,128)(2,1)}, bf16[64,512]{1,0:T(8,128)(2,1)S(1)}, bf16[64,512]{1,0:T(8,128)(2,1)S(1)}, bf16[64,512]{1,0:T(8,128)(2,1)S(1)}) custom-call(s32[12]{0:T(128)} %dst_hbm.3, s32[1]{0:T(128)S(6)} %copy.15.count_ref, bf16[128,512]{1,0:T(8,128)(2,1)S(1)} %get-tuple-element.54.after, ...), custom_call_target="tpu_custom_call" | custom-call | flops 402653184 | bytes 3000000 | tf_op jit(solution)/shard_map/edge_grads/pallas_call | solution.py:660
  27.5 0.7 %collective-permute-start.9 = (bf16[64,512]{1,0:T(8,128)(2,1)S(1)}, bf16[64,512]{1,0:T(8,128)(2,1)S(1)}, u32[]{:S(2)}, u32[]{:S(2)}) collective-permute-start(bf16[64,512]{1,0:T(8,128)(2,1)S(1)} %get-tuple-element.68), channel_id=1, source_target_pairs={{0,0},{4,8},{8,4},{12,12},{1,1},{5,9},{9,5},{13,13},{2,2},{6,10},{... | collective-permute-start | bytes 196616 | tf_op jit(solution)/shard_map/ppermute | solution.py:423
  28.2 4.7 %collective-permute-start.10 = (bf16[64,512]{1,0:T(8,128)(2,1)S(1)}, bf16[64,512]{1,0:T(8,128)(2,1)S(1)}, u32[]{:S(2)}, u32[]{:S(2)}) collective-permute-start(bf16[64,512]{1,0:T(8,128)(2,1)S(1)} %get-tuple-element.69), channel_id=1, source_target_pairs={{0,8},{4,12},{8,0},{12,4},{1,9},{5,13},{9,1},{13,5},{2,10},{6,14},... | collective-permute-start | bytes 196616 | tf_op jit(solution)/shard_map/ppermute | solution.py:423
  32.9 0.1 quarter.3
  33.0 0.3 collective-permute-start.5
  33.3 1.4 %collective-permute-start.6 = (bf16[128,512]{1,0:T(8,128)(2,1)S(1)}, bf16[128,512]{1,0:T(8,128)(2,1)S(1)}, u32[]{:S(2)}, u32[]{:S(2)}) collective-permute-start(bf16[128,512]{1,0:T(8,128)(2,1)S(1)} %get-tuple-element.66), channel_id=1, source_target_pairs={{0,2},{1,3},{2,0},{3,1},{4,6},{5,7},{6,4},{7,5},{8,10},{9,11},{10,... | collective-permute-start | bytes 393224 | tf_op jit(solution)/shard_map/ppermute | solution.py:423
  34.6 1.9 %collective-permute-start.7 = (bf16[128,512]{1,0:T(8,128)(2,1)S(1)}, bf16[128,512]{1,0:T(8,128)(2,1)S(1)}, u32[]{:S(2)}, u32[]{:S(2)}) collective-permute-start(bf16[128,512]{1,0:T(8,128)(2,1)S(1)} %get-tuple-element.67), channel_id=1, source_target_pairs={{0,4},{4,0},{8,12},{12,8},{1,5},{5,1},{9,13},{13,9},{2,6},{6,2},{1... | collective-permute-start | bytes 393224 | tf_op jit(solution)/shard_map/ppermute | solution.py:423
  36.5 0.1 add_terms.3
  36.6 1.5 %collective-permute-start.14 = (bf16[128,512]{1,0:T(8,128)(2,1)S(1)}, bf16[128,512]{1,0:T(8,128)(2,1)S(1)}, u32[]{:S(2)}, u32[]{:S(2)}) collective-permute-start(bf16[128,512]{1,0:T(8,128)(2,1)S(1)} %add_terms.3), channel_id=1, source_target_pairs={{0,12},{4,8},{8,4},{12,0},{1,13},{5,9},{9,5},{13,1},{2,14},{6,10},... | collective-permute-start | bytes 393224 | tf_op jit(solution)/shard_map/ppermute | solution.py:423
  38.2 7.6 %collective-permute-done.8.refs_0_ = bf16[64,512]{1,0:T(8,128)(2,1)S(1)} collective-permute-done((bf16[64,512]{1,0:T(8,128)(2,1)S(1)}, bf16[64,512]{1,0:T(8,128)(2,1)S(1)}, u32[]{:S(2)}, u32[]{:S(2)}) %collective-permute-start.8) | collective-permute-done | bytes 65568 | tf_op jit(solution)/shard_map/ppermute | solution.py:423
  45.8 0.1 add_terms.2.after
  45.8 1.8 %collective-permute-start.16 = (bf16[128,512]{1,0:T(8,128)(2,1)S(1)}, bf16[128,512]{1,0:T(8,128)(2,1)S(1)}, u32[]{:S(2)}, u32[]{:S(2)}) collective-permute-start(bf16[128,512]{1,0:T(8,128)(2,1)S(1)} %add_terms.2.after), channel_id=1, source_target_pairs={{0,12},{4,8},{8,4},{12,0},{1,13},{5,9},{9,5},{13,1},{2,14},{6,10},... | collective-permute-start | bytes 393224 | tf_op jit(solution)/shard_map/ppermute | solution.py:423
  47.6 0.1 collective-permute-start.15
  47.7 6.1 %collective-permute-done.16 = bf16[128,512]{1,0:T(8,128)(2,1)S(1)} collective-permute-done((bf16[128,512]{1,0:T(8,128)(2,1)S(1)}, bf16[128,512]{1,0:T(8,128)(2,1)S(1)}, u32[]{:S(2)}, u32[]{:S(2)}) %collective-permute-start.16) | collective-permute-done | bytes 131104 | tf_op jit(solution)/shard_map/ppermute | solution.py:423
  53.8 0.1 collective-permute-start.17
  53.9 2.1 %node_grads.1.after = bf16[128,512]{1,0:T(8,128)(2,1)} custom-call(s32[1,4]{1,0:T(1,128)} %boundary_hbm.3, bf16[128,512]{1,0:T(8,128)(2,1)S(1)} %add_terms.2.after, f32[512,512]{1,0:T(8,128)S(1)} %get-tuple-element.56.sums_ref, bf16[1536,512]{1,0:T(8,128)(2,1)S(1)} %get-tuple-element.45.refs_5_.win_ref, bf16[64,512]{1,0:T(8,128)(2,1)S(1)} %collective-permute-done.8.refs_0_, ...), custom_call_target="tpu_custom_call" | custom-call | flops 268435456 | bytes 2000000 | tf_op jit(solution)/shard_map/node_grads/pallas_call | solution.py:696
  56.1 2.8 %collective-permute-done.17.other_b = bf16[128,512]{1,0:T(8,128)(2,1)S(1)} collective-permute-done((bf16[128,512]{1,0:T(8,128)(2,1)S(1)}, bf16[128,512]{1,0:T(8,128)(2,1)S(1)}, u32[]{:S(2)}, u32[]{:S(2)}) %collective-permute-start.17) | collective-permute-done | bytes 131104 | tf_op jit(solution)/shard_map/ppermute | solution.py:423
  58.9 1.0 %widen.1 = (f32[384,512]{1,0:T(8,128)}, f32[128,512]{1,0:T(8,128)}) custom-call(bf16[128,512]{1,0:T(8,128)(2,1)} %node_grads.1.after, bf16[128,512]{1,0:T(8,128)(2,1)S(1)} %add_convert_fusion.1.own_a, bf16[128,512]{1,0:T(8,128)(2,1)S(1)} %collective-permute-done.15.other_a, bf16[128,512]{1,0:T(8,128)(2,1)S(1)} %add_convert_fusion.own_b, ...), custom_call_target="tpu_custom_call" | custom-call | bytes 1500000 | tf_op jit(solution)/shard_map/widen/pallas_call | solution.py:713
  (17 shorter events, 0.1 us)
Async XLA Ops:
  2.3 10.7 %collective-permute-start = (bf16[64,512]{1,0:T(8,128)(2,1)S(1)}, bf16[64,512]{1,0:T(8,128)(2,1)S(1)}, u32[]{:S(2)}, u32[]{:S(2)}) collective-permute-start(bf16[64,512]{1,0:T(8,128)(2,1)S(1)} %get-tuple-element.40), channel_id=1, source_target_pairs={{0,4},{4,0},{8,12},{12,8},{1,5},{5,1},{9,13},{13,9},{2,6},{6,2},{1... | collective-permute-start | bytes 196616 | tf_op jit(solution)/shard_map/ppermute | solution.py:423
  5.4 7.7 %collective-permute-start.1 = (bf16[64,512]{1,0:T(8,128)(2,1)S(1)}, bf16[64,512]{1,0:T(8,128)(2,1)S(1)}, u32[]{:S(2)}, u32[]{:S(2)}) collective-permute-start(bf16[64,512]{1,0:T(8,128)(2,1)S(1)} %get-tuple-element.41), channel_id=1, source_target_pairs={{0,0},{4,8},{8,4},{12,12},{1,1},{5,9},{9,5},{13,13},{2,2},{6,10},{... | collective-permute-start | bytes 196616 | tf_op jit(solution)/shard_map/ppermute | solution.py:423
  6.0 7.7 %collective-permute-start.2 = (bf16[64,512]{1,0:T(8,128)(2,1)S(1)}, bf16[64,512]{1,0:T(8,128)(2,1)S(1)}, u32[]{:S(2)}, u32[]{:S(2)}) collective-permute-start(bf16[64,512]{1,0:T(8,128)(2,1)S(1)} %get-tuple-element.42), channel_id=1, source_target_pairs={{0,8},{4,12},{8,0},{12,4},{1,9},{5,13},{9,1},{13,5},{2,10},{6,14},... | collective-permute-start | bytes 196616 | tf_op jit(solution)/shard_map/ppermute | solution.py:423
  19.5 2.2 %collective-permute-start.3 = (bf16[2,256,512]{2,1,0:T(8,128)(2,1)S(1)}, bf16[2,256,512]{2,1,0:T(8,128)(2,1)S(1)}, u32[]{:S(2)}, u32[]{:S(2)}) collective-permute-start(bf16[2,256,512]{2,1,0:T(8,128)(2,1)S(1)} %get-tuple-element.51), channel_id=1, source_target_pairs={{0,1},{1,0},{2,3},{3,2},{4,5},{5,4},{6,7},{7,6},{8,9},{9,8},{10,11... | collective-permute-start | bytes 1572872 | tf_op jit(solution)/shard_map/ppermute | solution.py:423
  21.1 7.1 %collective-permute-start.4 = (bf16[2,256,512]{2,1,0:T(8,128)(2,1)S(1)}, bf16[2,256,512]{2,1,0:T(8,128)(2,1)S(1)}, u32[]{:S(2)}, u32[]{:S(2)}) collective-permute-start(bf16[2,256,512]{2,1,0:T(8,128)(2,1)S(1)} %get-tuple-element.61), channel_id=1, source_target_pairs={{0,1},{1,0},{2,3},{3,2},{4,5},{5,4},{6,7},{7,6},{8,9},{9,8},{10,11... | collective-permute-start | bytes 1572872 | tf_op jit(solution)/shard_map/ppermute | solution.py:423
  21.8 11.2 %collective-permute-start.12 = (bf16[128,512]{1,0:T(8,128)(2,1)S(1)}, bf16[128,512]{1,0:T(8,128)(2,1)S(1)}, u32[]{:S(2)}, u32[]{:S(2)}) collective-permute-start(bf16[128,512]{1,0:T(8,128)(2,1)S(1)} %get-tuple-element.71), channel_id=1, source_target_pairs={{0,2},{1,3},{2,0},{3,1},{4,6},{5,7},{6,4},{7,5},{8,10},{9,11},{10,... | collective-permute-start | bytes 393224 | tf_op jit(solution)/shard_map/ppermute | solution.py:423
  23.3 9.9 %collective-permute-start.13 = (bf16[128,512]{1,0:T(8,128)(2,1)S(1)}, bf16[128,512]{1,0:T(8,128)(2,1)S(1)}, u32[]{:S(2)}, u32[]{:S(2)}) collective-permute-start(bf16[128,512]{1,0:T(8,128)(2,1)S(1)} %get-tuple-element.72), channel_id=1, source_target_pairs={{0,4},{4,0},{8,12},{12,8},{1,5},{5,1},{9,13},{13,9},{2,6},{6,2},{1... | collective-permute-start | bytes 393224 | tf_op jit(solution)/shard_map/ppermute | solution.py:423
  25.2 9.4 %collective-permute-start.11 = (bf16[128,512]{1,0:T(8,128)(2,1)S(1)}, bf16[128,512]{1,0:T(8,128)(2,1)S(1)}, u32[]{:S(2)}, u32[]{:S(2)}) collective-permute-start(bf16[128,512]{1,0:T(8,128)(2,1)S(1)} %get-tuple-element.54.after), channel_id=1, source_target_pairs={{0,6},{1,7},{2,4},{3,5},{4,2},{5,3},{6,0},{7,1},{8,14},{9,15},{10,... | collective-permute-start | bytes 393224 | tf_op jit(solution)/shard_map/ppermute | solution.py:491
  27.5 9.1 %collective-permute-start.9 = (bf16[64,512]{1,0:T(8,128)(2,1)S(1)}, bf16[64,512]{1,0:T(8,128)(2,1)S(1)}, u32[]{:S(2)}, u32[]{:S(2)}) collective-permute-start(bf16[64,512]{1,0:T(8,128)(2,1)S(1)} %get-tuple-element.68), channel_id=1, source_target_pairs={{0,0},{4,8},{8,4},{12,12},{1,1},{5,9},{9,5},{13,13},{2,2},{6,10},{... | collective-permute-start | bytes 196616 | tf_op jit(solution)/shard_map/ppermute | solution.py:423
  28.2 9.9 %collective-permute-start.10 = (bf16[64,512]{1,0:T(8,128)(2,1)S(1)}, bf16[64,512]{1,0:T(8,128)(2,1)S(1)}, u32[]{:S(2)}, u32[]{:S(2)}) collective-permute-start(bf16[64,512]{1,0:T(8,128)(2,1)S(1)} %get-tuple-element.69), channel_id=1, source_target_pairs={{0,8},{4,12},{8,0},{12,4},{1,9},{5,13},{9,1},{13,5},{2,10},{6,14},... | collective-permute-start | bytes 196616 | tf_op jit(solution)/shard_map/ppermute | solution.py:423
  33.0 12.8 %collective-permute-start.5 = (bf16[128,512]{1,0:T(8,128)(2,1)S(1)}, bf16[128,512]{1,0:T(8,128)(2,1)S(1)}, u32[]{:S(2)}, u32[]{:S(2)}) collective-permute-start(bf16[128,512]{1,0:T(8,128)(2,1)S(1)} %get-tuple-element.65), channel_id=1, source_target_pairs={{0,6},{1,7},{2,4},{3,5},{4,2},{5,3},{6,0},{7,1},{8,14},{9,15},{10,... | collective-permute-start | bytes 393224 | tf_op jit(solution)/shard_map/ppermute | solution.py:491
  33.3 12.5 %collective-permute-start.6 = (bf16[128,512]{1,0:T(8,128)(2,1)S(1)}, bf16[128,512]{1,0:T(8,128)(2,1)S(1)}, u32[]{:S(2)}, u32[]{:S(2)}) collective-permute-start(bf16[128,512]{1,0:T(8,128)(2,1)S(1)} %get-tuple-element.66), channel_id=1, source_target_pairs={{0,2},{1,3},{2,0},{3,1},{4,6},{5,7},{6,4},{7,5},{8,10},{9,11},{10,... | collective-permute-start | bytes 393224 | tf_op jit(solution)/shard_map/ppermute | solution.py:423
  34.6 11.1 %collective-permute-start.7 = (bf16[128,512]{1,0:T(8,128)(2,1)S(1)}, bf16[128,512]{1,0:T(8,128)(2,1)S(1)}, u32[]{:S(2)}, u32[]{:S(2)}) collective-permute-start(bf16[128,512]{1,0:T(8,128)(2,1)S(1)} %get-tuple-element.67), channel_id=1, source_target_pairs={{0,4},{4,0},{8,12},{12,8},{1,5},{5,1},{9,13},{13,9},{2,6},{6,2},{1... | collective-permute-start | bytes 393224 | tf_op jit(solution)/shard_map/ppermute | solution.py:423
  36.6 11.0 %collective-permute-start.14 = (bf16[128,512]{1,0:T(8,128)(2,1)S(1)}, bf16[128,512]{1,0:T(8,128)(2,1)S(1)}, u32[]{:S(2)}, u32[]{:S(2)}) collective-permute-start(bf16[128,512]{1,0:T(8,128)(2,1)S(1)} %add_terms.3), channel_id=1, source_target_pairs={{0,12},{4,8},{8,4},{12,0},{1,13},{5,9},{9,5},{13,1},{2,14},{6,10},... | collective-permute-start | bytes 393224 | tf_op jit(solution)/shard_map/ppermute | solution.py:423
  38.2 7.6 %collective-permute-start.8 = (bf16[64,512]{1,0:T(8,128)(2,1)S(1)}, bf16[64,512]{1,0:T(8,128)(2,1)S(1)}, u32[]{:S(2)}, u32[]{:S(2)}) collective-permute-start(bf16[64,512]{1,0:T(8,128)(2,1)S(1)} %get-tuple-element.63.after), channel_id=1, source_target_pairs={{0,4},{4,0},{8,12},{12,8},{1,5},{5,1},{9,13},{13,9},{2,6},{6,2},{1... | collective-permute-start | bytes 196616 | tf_op jit(solution)/shard_map/ppermute | solution.py:423
  45.8 8.0 %collective-permute-start.16 = (bf16[128,512]{1,0:T(8,128)(2,1)S(1)}, bf16[128,512]{1,0:T(8,128)(2,1)S(1)}, u32[]{:S(2)}, u32[]{:S(2)}) collective-permute-start(bf16[128,512]{1,0:T(8,128)(2,1)S(1)} %add_terms.2.after), channel_id=1, source_target_pairs={{0,12},{4,8},{8,4},{12,0},{1,13},{5,9},{9,5},{13,1},{2,14},{6,10},... | collective-permute-start | bytes 393224 | tf_op jit(solution)/shard_map/ppermute | solution.py:423
  47.6 8.4 %collective-permute-start.15 = (bf16[128,512]{1,0:T(8,128)(2,1)S(1)}, bf16[128,512]{1,0:T(8,128)(2,1)S(1)}, u32[]{:S(2)}, u32[]{:S(2)}) collective-permute-start(bf16[128,512]{1,0:T(8,128)(2,1)S(1)} %add_convert_fusion.1.own_a), channel_id=1, source_target_pairs={{0,4},{4,0},{8,12},{12,8},{1,5},{5,1},{9,13},{13,9},{2,6},{6,2},{1... | collective-permute-start | bytes 393224 | tf_op jit(solution)/shard_map/ppermute | solution.py:423
  53.8 5.0 %collective-permute-start.17 = (bf16[128,512]{1,0:T(8,128)(2,1)S(1)}, bf16[128,512]{1,0:T(8,128)(2,1)S(1)}, u32[]{:S(2)}, u32[]{:S(2)}) collective-permute-start(bf16[128,512]{1,0:T(8,128)(2,1)S(1)} %add_convert_fusion.own_b), channel_id=1, source_target_pairs={{0,4},{4,0},{8,12},{12,8},{1,5},{5,1},{9,13},{13,9},{2,6},{6,2},{1... | collective-permute-start | bytes 393224 | tf_op jit(solution)/shard_map/ppermute | solution.py:423

commit v7 on v6

--- a/solution.py
+++ b/solution.py
@@ -311,16 +311,16 @@
     agg_out,
     *refs,
 ):
-    back_sums = refs[:arrivals]
-    dst_ref, agg_ref, sem = refs[arrivals:]
+    back_sums = refs[:-3]
+    dst_ref, agg_ref, sem = refs[-3:]
     copy = load_small(dst_hbm, dst_ref, sem)
     nodes, latent = cot_ref.shape
     tiles = gpre_ref.shape[0] // block
     group = 4 if tiles % 4 == 0 else 1
-    places = arrival_places(lax.axis_index("dom"), four, arrivals)
-    for which in range(arrivals):
-        at = pl.multiple_of(nodes + places[which] * block, block)
-        back_sums[which][...] = sums_ref[pl.ds(at, block), :].astype(BF16)
+    places = arrival_places(lax.axis_index("dom"), four, arrivals)[-len(back_sums) :]
+    for place, back_ref in zip(places, back_sums):
+        at = pl.multiple_of(nodes + place * block, block)
+        back_ref[...] = sums_ref[pl.ds(at, block), :].astype(BF16)
     agg_ref[...] = jnp.zeros_like(agg_ref)
     copy.wait()
     for first in range(0, tiles, group):
@@ -351,27 +351,47 @@
         left_ref[slot] = kept_ref[here] + came_ref[here].astype(F32)
 
 
-def quarter_kernel(came_ref, kept_ref, after, cross_ref, over_ref, beside_ref, left_ref):
+def quarter_kernel(
+    nodes,
+    block,
+    came_a,
+    kept_a,
+    came_b,
+    kept_b,
+    sums_ref,
+    cross_ref,
+    over_ref,
+    beside_ref,
+    left_ref,
+):
     part = lax.axis_index("dom")
     mine = lax.axis_index("dp") // 2
     inner = (part == 1) | (part == 2)
-    rows = left_ref.shape[0]
+    rows = left_ref.shape[0] // 2
     here = pl.ds(pl.multiple_of(jnp.where(inner, 0, rows), rows), rows)
     there = pl.ds(pl.multiple_of(jnp.where(inner, rows, 0), rows), rows)
-
-    def total(slot, where):
-        return kept_ref[slot, where, :] + came_ref[slot, where, :].astype(F32)
-
-    cross_ref[...] = total(1 - mine, there).astype(BF16)
-    over_ref[...] = total(1 - mine, here).astype(BF16)
-    beside_ref[...] = total(mine, there).astype(BF16)
-    left_ref[...] = total(mine, here)
+    for number, (came_ref, kept_ref) in enumerate(((came_a, kept_a), (came_b, kept_b))):
+        spot = slice(number * rows, (number + 1) * rows)
+
+        def total(slot, where, came_ref=came_ref, kept_ref=kept_ref):
+            return kept_ref[slot, where, :] + came_ref[slot, where, :].astype(F32)
+
+        cross_ref[spot, :] = total(1 - mine, there).astype(BF16)
+        over_ref[spot, :] = total(1 - mine, here).astype(BF16)
+        beside_ref[spot, :] = total(mine, there).astype(BF16)
+        left_ref[spot, :] = total(mine, here)
+    place = arrival_places(part, True, 3)[0]
+    back = pl.ds(pl.multiple_of(nodes + place * block, block), block)
+    beside_ref[2 * rows :, :] = sums_ref[back, :].astype(BF16)
 
 
 def add_kernel(left_ref, cross_ref, over_ref, beside_ref, *refs):
-    out_ref = refs[-1]
-    terms = [ref[...].astype(F32) for ref in (cross_ref, over_ref, beside_ref)]
-    out_ref[...] = ((left_ref[...] + terms[1]) + (terms[0] + terms[2])).astype(BF16)
+    out_refs = refs[-2:]
+    rows = out_refs[0].shape[0]
+    for number, out_ref in enumerate(out_refs):
+        spot = slice(number * rows, (number + 1) * rows)
+        terms = [ref[spot, :].astype(F32) for ref in (cross_ref, over_ref, beside_ref)]
+        out_ref[...] = ((left_ref[spot, :] + terms[1]) + (terms[0] + terms[2])).astype(BF16)
 
 
 def node_grad_kernel(arrivals, four, boundary_hbm, after, sums_ref, win_ref, *refs):
@@ -379,13 +399,13 @@
     out_ref, total_ref, boundary_ref, sem = refs[arrivals:]
     nodes, latent = out_ref.shape
     extent = sums_ref.shape[0] - nodes
-    block = returned[0].shape[0]
+    block = returned[-1].shape[0]
     copy = load_small(boundary_hbm, boundary_ref, sem)
     total_ref[...] = sums_ref[:nodes, :]
     copy.wait()
     for which, place in enumerate(boundary_places(boundary_ref, lax.axis_index("dom"), four)):
         spot = pl.ds(pl.multiple_of(place * block, block), block)
-        total_ref[spot, :] += returned[which][...].astype(F32)
+        total_ref[spot, :] += returned[which][-block:, :].astype(F32)
 
     def wide_dot(value, weight):
         high = value.astype(BF16)
@@ -467,21 +487,27 @@
         away, kept = halve(bit, came, kept, after)
 
 
-def sum_of_square(away, kept, after):
-    slots, rows, latent = kept.shape
-    came = swap(away, "dp", lambda i: i ^ 1)
-    piece = pltpu.VMEM((rows // 2, latent), BF16)
+def sum_of_square(nodes, block, chunks, sums):
+    slots, rows, latent = chunks[0][1].shape
+    operands = []
+    for away, kept in chunks:
+        operands += [swap(away, "dp", lambda i: i ^ 1), kept]
     limit = pltpu.CompilerParams(vmem_limit_bytes=4 * 1024 * 1024)
     cost = pl.CostEstimate(flops=0, bytes_accessed=500_000, transcendentals=0)
     cross, over, beside, left = pl.pallas_call(
-        quarter_kernel,
-        out_shape=(piece, piece, piece, pltpu.VMEM((rows // 2, latent), F32)),
-        in_specs=[VMEM] * 3,
+        functools.partial(quarter_kernel, nodes, block),
+        out_shape=(
+            pltpu.VMEM((rows, latent), BF16),
+            pltpu.VMEM((rows, latent), BF16),
+            pltpu.VMEM((rows + block, latent), BF16),
+            pltpu.VMEM((rows, latent), F32),
+        ),
+        in_specs=[VMEM] * 5,
         out_specs=(VMEM,) * 4,
         compiler_params=limit,
         cost_estimate=cost,
         name="quarter",
-    )(in_vmem(came), in_vmem(kept), in_vmem(after))
+    )(*[in_vmem(array) for array in (*operands, sums)])
     ways = lax.axis_size("dp")
     parts = lax.axis_size("dom")
     diagonal = [
@@ -496,15 +522,15 @@
     def finish(*late):
         return pl.pallas_call(
             add_kernel,
-            out_shape=piece,
+            out_shape=(pltpu.VMEM((rows // 2, latent), BF16),) * 2,
             in_specs=[VMEM] * (4 + len(late)),
-            out_specs=VMEM,
+            out_specs=(VMEM,) * 2,
             compiler_params=limit,
             cost_estimate=cost,
             name="add_terms",
         )(*[in_vmem(array) for array in (left, *arrived, *late)])
 
-    return cross, finish
+    return cross, arrived[2], finish
 
 
 def sum_of_four(kept):
@@ -653,8 +679,12 @@
         ),
         name="rest_weights",
     )(*[in_vmem(array) for array in (node_v, edge_v, ext, grad_pre, sums)])
+    backs = arrivals
     if four:
-        sent_a, finish_a = sum_of_square(away_a, kept_a, cot_v)
+        sent_a, beside, finish = sum_of_square(
+            nodes, block, ((away_a, kept_a), (away_b, kept_b)), sums
+        )
+        backs = 2
     else:
         came_a, kept_a, sent_a = sum_over_dp(away_a, kept_a, cot_v)
     edge_grad, agg, *back_sums = pl.pallas_call(
@@ -663,9 +693,9 @@
             jax.ShapeDtypeStruct((edges, latent), BF16),
             jax.ShapeDtypeStruct((nodes, latent), BF16),
         )
-        + (block_shape,) * arrivals,
+        + (block_shape,) * backs,
         in_specs=[HBM, SMEM] + [VMEM] * 7,
-        out_specs=(VMEM,) * (2 + arrivals),
+        out_specs=(VMEM,) * (2 + backs),
         scratch_shapes=[
             pltpu.SMEM((tiles,), jnp.int32),
             pltpu.VMEM((nodes, latent), F32),
@@ -682,10 +712,10 @@
         *[in_vmem(array) for array in (sent_a, grad_pre, sums, cot_v, win_v, edge_v, message)],
     )
     if four:
-        returned = exchange_of_four(*back_sums)
-        _, finish_b = sum_of_square(away_b, kept_b, back_sums[0])
-        pair_a = finish_a()
-        pair_b = finish_b(*returned)
+        far = swap(back_sums[1], "dom", lambda i: partners_of_four(2)[i])
+        near = swap(back_sums[0], "dom", lambda i: partners_of_four(1)[i])
+        pair_a, pair_b = finish(near, far)
+        returned = [beside, near, far]
         late = pair_b
     else:
         returned = [

time: 60.1 us -> 61.8 us (1.028)
  starting transfers between devices: 24.2 us -> 28.7 us
  waiting for transfers between devices: 17.2 us -> 14.4 us
    ppermute x16 -> x13, starting transfers between devices: 23.8 us -> 28.6 us  [swap(): return lax.ppermute(array, axis, [(i, partner(i)) for i in range(devices)])]
    ppermute x16 -> x13, waiting for transfers between devices: 17.2 us -> 12.8 us  [swap(): return lax.ppermute(array, axis, [(i, partner(i)) for i in range(devices)])]
    ppermute x2 -> x1, waiting for transfers between devices: 0.01 us -> 1.69 us  [sum_of_square(): lax.ppermute(cross, ('dom', 'dp'), diagonal)]
  transfers between devices with their start and end apart: 18 -> 14, of which waited for: 4 -> 7; matrix products, arithmetic and copies ran while one was open for 0% -> 0% of each run, Pallas kernels for 14% -> 13%
where the time goes in v7:
time: 61.8 us; the launch traced here: 61.6 us
  starting transfers between devices  28.7 us (46%)
  Pallas kernels  16.9 us (27%)
  waiting for transfers between devices  14.4 us (23%)
  between operations  1.4 us (2%)
    ppermute x13, starting transfers between devices, swap(): return lax.ppermute(array, axis, [(i, partner(i)) for i in range(devices)])  28.6 us
    ppermute x13, waiting for transfers between devices, swap(): return lax.ppermute(array, axis, [(i, partner(i)) for i in range(devices)])  12.8 us
    pallas_call x1, Pallas kernels, body(): pl.pallas_call(functools.partial(edge_kernel, ways, arrivals, four, block...  5.74 us
    pallas_call x1, Pallas kernels, body(): pl.pallas_call(functools.partial(prep_kernel, parts, arrivals), out_shape...  2.42 us
    pallas_call x1, Pallas kernels, body(): pl.pallas_call(functools.partial(edge_grad_kernel, block, arrivals, four)...  2.21 us
    pallas_call x1, Pallas kernels, body(): pl.pallas_call(functools.partial(node_grad_kernel, arrivals, four), out_s...  2.14 us
    ppermute x1, waiting for transfers between devices, sum_of_square(): lax.ppermute(cross, ('dom', 'dp'), diagonal)  1.69 us
    pallas_call x1, Pallas kernels, body(): pl.pallas_call(functools.partial(pick_kernel, four, block), out_shape=(bl...  1.63 us
  transfers between devices with their start and end apart: 14, of which 7 were waited for; matrix products, arithmetic and copies ran while one was open for 0% of the time, Pallas kernels for 13%

profile of v7, /device:TPU:0, one launch (start us, length us, event | category | flops | bytes accessed | tf_op | source)
XLA Modules:
  0.0 61.6 jit_solution(14996848543067285187)
XLA Ops:
  0.6 1.6 %pick_blocks.1 = (bf16[64,512]{1,0:T(8,128)(2,1)S(1)}, bf16[64,512]{1,0:T(8,128)(2,1)S(1)}, bf16[64,512]{1,0:T(8,128)(2,1)S(1)}) custom-call(s32[1,4]{1,0:T(1,128)} %boundary_hbm.3, bf16[128,512]{1,0:T(8,128)(2,1)} %bitcast.8), custom_call_target="tpu_custom_call" | custom-call | bytes 400000 | tf_op jit(solution)/shard_map/pick_blocks/pallas_call | solution.py:579
  2.3 3.1 %collective-permute-start = (bf16[64,512]{1,0:T(8,128)(2,1)S(1)}, bf16[64,512]{1,0:T(8,128)(2,1)S(1)}, u32[]{:S(2)}, u32[]{:S(2)}) collective-permute-start(bf16[64,512]{1,0:T(8,128)(2,1)S(1)} %get-tuple-element.37), channel_id=1, source_target_pairs={{0,4},{4,0},{8,12},{12,8},{1,5},{5,1},{9,13},{13,9},{2,6},{6,2},{1... | collective-permute-start | bytes 196616 | tf_op jit(solution)/shard_map/ppermute | solution.py:443
  5.4 0.7 %collective-permute-start.1 = (bf16[64,512]{1,0:T(8,128)(2,1)S(1)}, bf16[64,512]{1,0:T(8,128)(2,1)S(1)}, u32[]{:S(2)}, u32[]{:S(2)}) collective-permute-start(bf16[64,512]{1,0:T(8,128)(2,1)S(1)} %get-tuple-element.38), channel_id=1, source_target_pairs={{0,0},{4,8},{8,4},{12,12},{1,1},{5,9},{9,5},{13,13},{2,2},{6,10},{... | collective-permute-start | bytes 196616 | tf_op jit(solution)/shard_map/ppermute | solution.py:443
  6.0 3.9 %collective-permute-start.2 = (bf16[64,512]{1,0:T(8,128)(2,1)S(1)}, bf16[64,512]{1,0:T(8,128)(2,1)S(1)}, u32[]{:S(2)}, u32[]{:S(2)}) collective-permute-start(bf16[64,512]{1,0:T(8,128)(2,1)S(1)} %get-tuple-element.39), channel_id=1, source_target_pairs={{0,8},{4,12},{8,0},{12,4},{1,9},{5,13},{9,1},{13,5},{2,10},{6,14},... | collective-permute-start | bytes 196616 | tf_op jit(solution)/shard_map/ppermute | solution.py:443
  10.6 2.4 %prepare.1 = (bf16[128,512]{1,0:T(8,128)(2,1)S(1)}, bf16[768,512]{1,0:T(8,128)(2,1)S(1)}, bf16[128,512]{1,0:T(8,128)(2,1)S(1)}, bf16[1536,512]{1,0:T(8,128)(2,1)...) custom-call(s32[1]{0:T(128)S(6)} %copy.15.count_ref, ...), custom_call_target="tpu_custom_call" | custom-call | flops 402653184 | bytes 8000000 | tf_op jit(solution)/shard_map/prepare/pallas_call | solution.py:601
  13.0 0.0 collective-permute-done.refs_0_
  13.0 0.0 collective-permute-done.1.refs_1_
  13.0 0.7 %collective-permute-done.2.refs_2_ = bf16[64,512]{1,0:T(8,128)(2,1)S(1)} collective-permute-done((bf16[64,512]{1,0:T(8,128)(2,1)S(1)}, bf16[64,512]{1,0:T(8,128)(2,1)S(1)}, u32[]{:S(2)}, u32[]{:S(2)}) %collective-permute-start.2) | collective-permute-done | bytes 65568 | tf_op jit(solution)/shard_map/ppermute | solution.py:443
  13.8 5.7 %edge_block.1 = (bf16[768,512]{1,0:T(8,128)(2,1)S(1)}, f32[768,512]{1,0:T(8,128)S(1)}, f32[512,512]{1,0:T(8,128)S(1)}, bf16[384,512]{1,0:T(8,128)(2,1)S(1)}, bf1...) custom-call(bf16[64,512]{1,0:T(8,128)(2,1)S(1)} %collective-permute-done.refs_0_, ...), custom_call_target="tpu_custom_call" | custom-call | flops 2415919104 | bytes 12000000 | tf_op jit(solution)/shard_map/edge_block/pallas_call | solution.py:642
  19.5 0.1 collective-permute-start.3
  19.6 1.5 %rest_weights.1 = (bf16[2,256,512]{2,1,0:T(8,128)(2,1)S(1)}, f32[2,256,512]{2,1,0:T(8,128)S(1)}) custom-call(bf16[128,512]{1,0:T(8,128)(2,1)S(1)} %get-tuple-element.40.refs_3_.node_ref, bf16[768,512]{1,0:T(8,128)(2,1)S(1)} %get-tuple-element.41.refs_4_.edge_ref, bf16[384,512]{1,0:T(8,128)(2,1)S(1)} %get-tuple-element.50.ext_ref, ...), custom_call_target="tpu_custom_call" | custom-call | flops 402653184 | bytes 4000000 | tf_op jit(solution)/shard_map/rest_weights/pallas_call | solution.py:671
  21.1 0.6 collective-permute-start.4
  21.7 1.5 %collective-permute-done.4.came_b = bf16[2,256,512]{2,1,0:T(8,128)(2,1)S(1)} collective-permute-done((bf16[2,256,512]{2,1,0:T(8,128)(2,1)S(1)}, bf16[2,256,512]{2,1,0:T(8,128)(2,1)S(1)}, u32[]{:S(2)}, u32[]{:S(2)}) %collective-permute-start.4) | collective-permute-done | bytes 524320 | tf_op jit(solution)/shard_map/ppermute | solution.py:443
  23.2 0.2 quarter.1
  23.4 2.0 %collective-permute-start.7 = (bf16[320,512]{1,0:T(8,128)(2,1)S(1)}, bf16[320,512]{1,0:T(8,128)(2,1)S(1)}, u32[]{:S(2)}, u32[]{:S(2)}) collective-permute-start(bf16[320,512]{1,0:T(8,128)(2,1)S(1)} %get-tuple-element.62), channel_id=1, source_target_pairs={{0,4},{4,0},{8,12},{12,8},{1,5},{5,1},{9,13},{13,9},{2,6},{6,2},{1... | collective-permute-start | bytes 983048 | tf_op jit(solution)/shard_map/ppermute | solution.py:443
  25.3 1.5 %collective-permute-start.6 = (bf16[256,512]{1,0:T(8,128)(2,1)S(1)}, bf16[256,512]{1,0:T(8,128)(2,1)S(1)}, u32[]{:S(2)}, u32[]{:S(2)}) collective-permute-start(bf16[256,512]{1,0:T(8,128)(2,1)S(1)} %get-tuple-element.61), channel_id=1, source_target_pairs={{0,2},{1,3},{2,0},{3,1},{4,6},{5,7},{6,4},{7,5},{8,10},{9,11},{10,... | collective-permute-start | bytes 786440 | tf_op jit(solution)/shard_map/ppermute | solution.py:443
  26.9 0.1 collective-permute-start.5
  26.9 2.2 %edge_grads.1 = (bf16[768,512]{1,0:T(8,128)(2,1)}, bf16[128,512]{1,0:T(8,128)(2,1)}, bf16[64,512]{1,0:T(8,128)(2,1)S(1)}, bf16[64,512]{1,0:T(8,128)(2,1)S(1)}) custom-call(s32[12]{0:T(128)} %dst_hbm.3, s32[1]{0:T(128)S(6)} %copy.15.count_ref, bf16[256,512]{1,0:T(8,128)(2,1)S(1)} %get-tuple-element.55.after, bf16[768,512]{1,0:T(8,128)(2,1)S(1)} %get-tuple-element.51.gpre_ref, ...), custom_call_target="tpu_custom_call" | custom-call | flops 402653184 | bytes 3000000 | tf_op jit(solution)/shard_map/edge_grads/pallas_call | solution.py:690
  29.2 0.7 %collective-permute-start.8 = (bf16[64,512]{1,0:T(8,128)(2,1)S(1)}, bf16[64,512]{1,0:T(8,128)(2,1)S(1)}, u32[]{:S(2)}, u32[]{:S(2)}) collective-permute-start(bf16[64,512]{1,0:T(8,128)(2,1)S(1)} %get-tuple-element.63), channel_id=1, source_target_pairs={{0,0},{4,8},{8,4},{12,12},{1,1},{5,9},{9,5},{13,13},{2,2},{6,10},{... | collective-permute-start | bytes 196616 | tf_op jit(solution)/shard_map/ppermute | solution.py:443
  29.8 4.7 %collective-permute-start.9 = (bf16[64,512]{1,0:T(8,128)(2,1)S(1)}, bf16[64,512]{1,0:T(8,128)(2,1)S(1)}, u32[]{:S(2)}, u32[]{:S(2)}) collective-permute-start(bf16[64,512]{1,0:T(8,128)(2,1)S(1)} %get-tuple-element.64), channel_id=1, source_target_pairs={{0,8},{4,12},{8,0},{12,4},{1,9},{5,13},{9,1},{13,5},{2,10},{6,14},... | collective-permute-start | bytes 196616 | tf_op jit(solution)/shard_map/ppermute | solution.py:443
  34.5 5.4 %collective-permute-done.9.refs_1_.refs_2_ = bf16[64,512]{1,0:T(8,128)(2,1)S(1)} collective-permute-done((bf16[64,512]{1,0:T(8,128)(2,1)S(1)}, bf16[64,512]{1,0:T(8,128)(2,1)S(1)}, u32[]{:S(2)}, u32[]{:S(2)}) %collective-permute-start.9) | collective-permute-done | bytes 65568 | tf_op jit(solution)/shard_map/ppermute | solution.py:443
  39.9 1.7 %collective-permute-done.5.cross_ref = bf16[256,512]{1,0:T(8,128)(2,1)S(1)} collective-permute-done((bf16[256,512]{1,0:T(8,128)(2,1)S(1)}, bf16[256,512]{1,0:T(8,128)(2,1)S(1)}, u32[]{:S(2)}, u32[]{:S(2)}) %collective-permute-start.5) | collective-permute-done | bytes 262176 | tf_op jit(solution)/shard_map/ppermute | solution.py:517
  41.6 0.1 add_terms.1
  41.7 3.2 %collective-permute-start.10 = (bf16[128,512]{1,0:T(8,128)(2,1)S(1)}, bf16[128,512]{1,0:T(8,128)(2,1)S(1)}, u32[]{:S(2)}, u32[]{:S(2)}) collective-permute-start(bf16[128,512]{1,0:T(8,128)(2,1)S(1)} %get-tuple-element.66), channel_id=1, source_target_pairs={{0,12},{4,8},{8,4},{12,0},{1,13},{5,9},{9,5},{13,1},{2,14},{6,10},... | collective-permute-start | bytes 393224 | tf_op jit(solution)/shard_map/ppermute | solution.py:443
  44.9 0.7 %collective-permute-start.12 = (bf16[128,512]{1,0:T(8,128)(2,1)S(1)}, bf16[128,512]{1,0:T(8,128)(2,1)S(1)}, u32[]{:S(2)}, u32[]{:S(2)}) collective-permute-start(bf16[128,512]{1,0:T(8,128)(2,1)S(1)} %get-tuple-element.65.after), channel_id=1, source_target_pairs={{0,12},{4,8},{8,4},{12,0},{1,13},{5,9},{9,5},{13,1},{2,14},{6,10},... | collective-permute-start | bytes 393224 | tf_op jit(solution)/shard_map/ppermute | solution.py:443
  45.6 3.3 %collective-permute-done.10 = bf16[128,512]{1,0:T(8,128)(2,1)S(1)} collective-permute-done((bf16[128,512]{1,0:T(8,128)(2,1)S(1)}, bf16[128,512]{1,0:T(8,128)(2,1)S(1)}, u32[]{:S(2)}, u32[]{:S(2)}) %collective-permute-start.10) | collective-permute-done | bytes 131104 | tf_op jit(solution)/shard_map/ppermute | solution.py:443
  48.9 6.1 %collective-permute-start.11 = (bf16[128,512]{1,0:T(8,128)(2,1)S(1)}, bf16[128,512]{1,0:T(8,128)(2,1)S(1)}, u32[]{:S(2)}, u32[]{:S(2)}) collective-permute-start(bf16[128,512]{1,0:T(8,128)(2,1)S(1)} %add_convert_fusion.1.own_a), channel_id=1, source_target_pairs={{0,4},{4,0},{8,12},{12,8},{1,5},{5,1},{9,13},{13,9},{2,6},{6,2},{1... | collective-permute-start | bytes 393224 | tf_op jit(solution)/shard_map/ppermute | solution.py:443
  55.0 1.6 %collective-permute-start.13 = (bf16[128,512]{1,0:T(8,128)(2,1)S(1)}, bf16[128,512]{1,0:T(8,128)(2,1)S(1)}, u32[]{:S(2)}, u32[]{:S(2)}) collective-permute-start(bf16[128,512]{1,0:T(8,128)(2,1)S(1)} %add_convert_fusion.own_b), channel_id=1, source_target_pairs={{0,4},{4,0},{8,12},{12,8},{1,5},{5,1},{9,13},{13,9},{2,6},{6,2},{1... | collective-permute-start | bytes 393224 | tf_op jit(solution)/shard_map/ppermute | solution.py:443
  56.6 2.1 %node_grads.1.after = bf16[128,512]{1,0:T(8,128)(2,1)} custom-call(s32[1,4]{1,0:T(1,128)} %boundary_hbm.3, bf16[128,512]{1,0:T(8,128)(2,1)S(1)} %get-tuple-element.65.after, f32[512,512]{1,0:T(8,128)S(1)} %get-tuple-element.52.sums_ref, bf16[1536,512]{1,0:T(8,128)(2,1)S(1)} %get-tuple-element.42.refs_5_.win_ref, ...), custom_call_target="tpu_custom_call" | custom-call | flops 268435456 | bytes 2000000 | tf_op jit(solution)/shard_map/node_grads/pallas_call | solution.py:726
  58.7 0.4 collective-permute-done.11.other_a
  59.1 1.4 %collective-permute-done.13.other_b = bf16[128,512]{1,0:T(8,128)(2,1)S(1)} collective-permute-done((bf16[128,512]{1,0:T(8,128)(2,1)S(1)}, bf16[128,512]{1,0:T(8,128)(2,1)S(1)}, u32[]{:S(2)}, u32[]{:S(2)}) %collective-permute-start.13) | collective-permute-done | bytes 131104 | tf_op jit(solution)/shard_map/ppermute | solution.py:443
  60.6 1.0 %widen.1 = (f32[384,512]{1,0:T(8,128)}, f32[128,512]{1,0:T(8,128)}) custom-call(bf16[128,512]{1,0:T(8,128)(2,1)} %node_grads.1.after, bf16[128,512]{1,0:T(8,128)(2,1)S(1)} %add_convert_fusion.1.own_a, bf16[128,512]{1,0:T(8,128)(2,1)S(1)} %collective-permute-done.11.other_a, bf16[128,512]{1,0:T(8,128)(2,1)S(1)} %add_convert_fusion.own_b, ...), custom_call_target="tpu_custom_call" | custom-call | bytes 1500000 | tf_op jit(solution)/shard_map/widen/pallas_call | solution.py:743
  (7 shorter events, 0.1 us)
Async XLA Ops:
  2.3 10.7 %collective-permute-start = (bf16[64,512]{1,0:T(8,128)(2,1)S(1)}, bf16[64,512]{1,0:T(8,128)(2,1)S(1)}, u32[]{:S(2)}, u32[]{:S(2)}) collective-permute-start(bf16[64,512]{1,0:T(8,128)(2,1)S(1)} %get-tuple-element.37), channel_id=1, source_target_pairs={{0,4},{4,0},{8,12},{12,8},{1,5},{5,1},{9,13},{13,9},{2,6},{6,2},{1... | collective-permute-start | bytes 196616 | tf_op jit(solution)/shard_map/ppermute | solution.py:443
  5.4 7.7 %collective-permute-start.1 = (bf16[64,512]{1,0:T(8,128)(2,1)S(1)}, bf16[64,512]{1,0:T(8,128)(2,1)S(1)}, u32[]{:S(2)}, u32[]{:S(2)}) collective-permute-start(bf16[64,512]{1,0:T(8,128)(2,1)S(1)} %get-tuple-element.38), channel_id=1, source_target_pairs={{0,0},{4,8},{8,4},{12,12},{1,1},{5,9},{9,5},{13,13},{2,2},{6,10},{... | collective-permute-start | bytes 196616 | tf_op jit(solution)/shard_map/ppermute | solution.py:443
  6.0 7.7 %collective-permute-start.2 = (bf16[64,512]{1,0:T(8,128)(2,1)S(1)}, bf16[64,512]{1,0:T(8,128)(2,1)S(1)}, u32[]{:S(2)}, u32[]{:S(2)}) collective-permute-start(bf16[64,512]{1,0:T(8,128)(2,1)S(1)} %get-tuple-element.39), channel_id=1, source_target_pairs={{0,8},{4,12},{8,0},{12,4},{1,9},{5,13},{9,1},{13,5},{2,10},{6,14},... | collective-permute-start | bytes 196616 | tf_op jit(solution)/shard_map/ppermute | solution.py:443
  19.5 2.2 %collective-permute-start.3 = (bf16[2,256,512]{2,1,0:T(8,128)(2,1)S(1)}, bf16[2,256,512]{2,1,0:T(8,128)(2,1)S(1)}, u32[]{:S(2)}, u32[]{:S(2)}) collective-permute-start(bf16[2,256,512]{2,1,0:T(8,128)(2,1)S(1)} %get-tuple-element.48), channel_id=1, source_target_pairs={{0,1},{1,0},{2,3},{3,2},{4,5},{5,4},{6,7},{7,6},{8,9},{9,8},{10,11... | collective-permute-start | bytes 1572872 | tf_op jit(solution)/shard_map/ppermute | solution.py:443
  21.1 2.1 %collective-permute-start.4 = (bf16[2,256,512]{2,1,0:T(8,128)(2,1)S(1)}, bf16[2,256,512]{2,1,0:T(8,128)(2,1)S(1)}, u32[]{:S(2)}, u32[]{:S(2)}) collective-permute-start(bf16[2,256,512]{2,1,0:T(8,128)(2,1)S(1)} %get-tuple-element.53), channel_id=1, source_target_pairs={{0,1},{1,0},{2,3},{3,2},{4,5},{5,4},{6,7},{7,6},{8,9},{9,8},{10,11... | collective-permute-start | bytes 1572872 | tf_op jit(solution)/shard_map/ppermute | solution.py:443
  23.4 18.2 %collective-permute-start.7 = (bf16[320,512]{1,0:T(8,128)(2,1)S(1)}, bf16[320,512]{1,0:T(8,128)(2,1)S(1)}, u32[]{:S(2)}, u32[]{:S(2)}) collective-permute-start(bf16[320,512]{1,0:T(8,128)(2,1)S(1)} %get-tuple-element.62), channel_id=1, source_target_pairs={{0,4},{4,0},{8,12},{12,8},{1,5},{5,1},{9,13},{13,9},{2,6},{6,2},{1... | collective-permute-start | bytes 983048 | tf_op jit(solution)/shard_map/ppermute | solution.py:443
  25.3 14.5 %collective-permute-start.6 = (bf16[256,512]{1,0:T(8,128)(2,1)S(1)}, bf16[256,512]{1,0:T(8,128)(2,1)S(1)}, u32[]{:S(2)}, u32[]{:S(2)}) collective-permute-start(bf16[256,512]{1,0:T(8,128)(2,1)S(1)} %get-tuple-element.61), channel_id=1, source_target_pairs={{0,2},{1,3},{2,0},{3,1},{4,6},{5,7},{6,4},{7,5},{8,10},{9,11},{10,... | collective-permute-start | bytes 786440 | tf_op jit(solution)/shard_map/ppermute | solution.py:443
  26.9 14.7 %collective-permute-start.5 = (bf16[256,512]{1,0:T(8,128)(2,1)S(1)}, bf16[256,512]{1,0:T(8,128)(2,1)S(1)}, u32[]{:S(2)}, u32[]{:S(2)}) collective-permute-start(bf16[256,512]{1,0:T(8,128)(2,1)S(1)} %get-tuple-element.55.after), channel_id=1, source_target_pairs={{0,6},{1,7},{2,4},{3,5},{4,2},{5,3},{6,0},{7,1},{8,14},{9,15},{10,... | collective-permute-start | bytes 786440 | tf_op jit(solution)/shard_map/ppermute | solution.py:517
  29.2 5.3 %collective-permute-start.8 = (bf16[64,512]{1,0:T(8,128)(2,1)S(1)}, bf16[64,512]{1,0:T(8,128)(2,1)S(1)}, u32[]{:S(2)}, u32[]{:S(2)}) collective-permute-start(bf16[64,512]{1,0:T(8,128)(2,1)S(1)} %get-tuple-element.63), channel_id=1, source_target_pairs={{0,0},{4,8},{8,4},{12,12},{1,1},{5,9},{9,5},{13,13},{2,2},{6,10},{... | collective-permute-start | bytes 196616 | tf_op jit(solution)/shard_map/ppermute | solution.py:443
  29.8 10.0 %collective-permute-start.9 = (bf16[64,512]{1,0:T(8,128)(2,1)S(1)}, bf16[64,512]{1,0:T(8,128)(2,1)S(1)}, u32[]{:S(2)}, u32[]{:S(2)}) collective-permute-start(bf16[64,512]{1,0:T(8,128)(2,1)S(1)} %get-tuple-element.64), channel_id=1, source_target_pairs={{0,8},{4,12},{8,0},{12,4},{1,9},{5,13},{9,1},{13,5},{2,10},{6,14},... | collective-permute-start | bytes 196616 | tf_op jit(solution)/shard_map/ppermute | solution.py:443
  41.7 7.2 %collective-permute-start.10 = (bf16[128,512]{1,0:T(8,128)(2,1)S(1)}, bf16[128,512]{1,0:T(8,128)(2,1)S(1)}, u32[]{:S(2)}, u32[]{:S(2)}) collective-permute-start(bf16[128,512]{1,0:T(8,128)(2,1)S(1)} %get-tuple-element.66), channel_id=1, source_target_pairs={{0,12},{4,8},{8,4},{12,0},{1,13},{5,9},{9,5},{13,1},{2,14},{6,10},... | collective-permute-start | bytes 393224 | tf_op jit(solution)/shard_map/ppermute | solution.py:443
  44.9 10.1 %collective-permute-start.12 = (bf16[128,512]{1,0:T(8,128)(2,1)S(1)}, bf16[128,512]{1,0:T(8,128)(2,1)S(1)}, u32[]{:S(2)}, u32[]{:S(2)}) collective-permute-start(bf16[128,512]{1,0:T(8,128)(2,1)S(1)} %get-tuple-element.65.after), channel_id=1, source_target_pairs={{0,12},{4,8},{8,4},{12,0},{1,13},{5,9},{9,5},{13,1},{2,14},{6,10},... | collective-permute-start | bytes 393224 | tf_op jit(solution)/shard_map/ppermute | solution.py:443
  48.9 10.3 %collective-permute-start.11 = (bf16[128,512]{1,0:T(8,128)(2,1)S(1)}, bf16[128,512]{1,0:T(8,128)(2,1)S(1)}, u32[]{:S(2)}, u32[]{:S(2)}) collective-permute-start(bf16[128,512]{1,0:T(8,128)(2,1)S(1)} %add_convert_fusion.1.own_a), channel_id=1, source_target_pairs={{0,4},{4,0},{8,12},{12,8},{1,5},{5,1},{9,13},{13,9},{2,6},{6,2},{1... | collective-permute-start | bytes 393224 | tf_op jit(solution)/shard_map/ppermute | solution.py:443
  55.0 5.6 %collective-permute-start.13 = (bf16[128,512]{1,0:T(8,128)(2,1)S(1)}, bf16[128,512]{1,0:T(8,128)(2,1)S(1)}, u32[]{:S(2)}, u32[]{:S(2)}) collective-permute-start(bf16[128,512]{1,0:T(8,128)(2,1)S(1)} %add_convert_fusion.own_b), channel_id=1, source_target_pairs={{0,4},{4,0},{8,12},{12,8},{1,5},{5,1},{9,13},{13,9},{2,6},{6,2},{1... | collective-permute-start | bytes 393224 | tf_op jit(solution)/shard_map/ppermute | solution.py:443

commit v8 on v6

--- a/solution.py
+++ b/solution.py
@@ -311,16 +311,16 @@
     agg_out,
     *refs,
 ):
-    back_sums = refs[:arrivals]
-    dst_ref, agg_ref, sem = refs[arrivals:]
+    back_sums = refs[:-3]
+    dst_ref, agg_ref, sem = refs[-3:]
     copy = load_small(dst_hbm, dst_ref, sem)
     nodes, latent = cot_ref.shape
     tiles = gpre_ref.shape[0] // block
     group = 4 if tiles % 4 == 0 else 1
     places = arrival_places(lax.axis_index("dom"), four, arrivals)
-    for which in range(arrivals):
-        at = pl.multiple_of(nodes + places[which] * block, block)
-        back_sums[which][...] = sums_ref[pl.ds(at, block), :].astype(BF16)
+    for place, back_ref in zip(places, back_sums):
+        at = pl.multiple_of(nodes + place * block, block)
+        back_ref[...] = sums_ref[pl.ds(at, block), :].astype(BF16)
     agg_ref[...] = jnp.zeros_like(agg_ref)
     copy.wait()
     for first in range(0, tiles, group):
@@ -351,27 +351,33 @@
         left_ref[slot] = kept_ref[here] + came_ref[here].astype(F32)
 
 
-def quarter_kernel(came_ref, kept_ref, after, cross_ref, over_ref, beside_ref, left_ref):
+def send_back_kernel(nodes, block, came_ref, kept_ref, sums_ref, away_ref, left_ref, *back_refs):
+    halve_kernel(2, came_ref, kept_ref, None, away_ref, left_ref)
+    for place, back_ref in zip(arrival_places(lax.axis_index("dom"), True, 3)[1:], back_refs):
+        at = pl.multiple_of(nodes + place * block, block)
+        back_ref[...] = sums_ref[pl.ds(at, block), :].astype(BF16)
+
+
+def split_kernel(nodes, block, came_ref, kept_ref, *refs):
+    away_ref, left_ref = refs[-2:]
     part = lax.axis_index("dom")
-    mine = lax.axis_index("dp") // 2
     inner = (part == 1) | (part == 2)
     rows = left_ref.shape[0]
     here = pl.ds(pl.multiple_of(jnp.where(inner, 0, rows), rows), rows)
     there = pl.ds(pl.multiple_of(jnp.where(inner, rows, 0), rows), rows)
-
-    def total(slot, where):
-        return kept_ref[slot, where, :] + came_ref[slot, where, :].astype(F32)
-
-    cross_ref[...] = total(1 - mine, there).astype(BF16)
-    over_ref[...] = total(1 - mine, here).astype(BF16)
-    beside_ref[...] = total(mine, there).astype(BF16)
-    left_ref[...] = total(mine, here)
-
-
-def add_kernel(left_ref, cross_ref, over_ref, beside_ref, *refs):
+    away_ref[:rows, :] = (kept_ref[0, there, :] + came_ref[0, there, :].astype(F32)).astype(BF16)
+    left_ref[...] = kept_ref[0, here, :] + came_ref[0, here, :].astype(F32)
+    if away_ref.shape[0] > rows:
+        sums_ref = refs[0]
+        place = arrival_places(part, True, 3)[0]
+        at = pl.multiple_of(nodes + place * block, block)
+        away_ref[rows:, :] = sums_ref[pl.ds(at, block), :].astype(BF16)
+
+
+def add_kernel(left_ref, came_ref, *refs):
     out_ref = refs[-1]
-    terms = [ref[...].astype(F32) for ref in (cross_ref, over_ref, beside_ref)]
-    out_ref[...] = ((left_ref[...] + terms[1]) + (terms[0] + terms[2])).astype(BF16)
+    rows = out_ref.shape[0]
+    out_ref[...] = (left_ref[...] + came_ref[:rows, :].astype(F32)).astype(BF16)
 
 
 def node_grad_kernel(arrivals, four, boundary_hbm, after, sums_ref, win_ref, *refs):
@@ -379,13 +385,13 @@
     out_ref, total_ref, boundary_ref, sem = refs[arrivals:]
     nodes, latent = out_ref.shape
     extent = sums_ref.shape[0] - nodes
-    block = returned[0].shape[0]
+    block = returned[-1].shape[0]
     copy = load_small(boundary_hbm, boundary_ref, sem)
     total_ref[...] = sums_ref[:nodes, :]
     copy.wait()
     for which, place in enumerate(boundary_places(boundary_ref, lax.axis_index("dom"), four)):
         spot = pl.ds(pl.multiple_of(place * block, block), block)
-        total_ref[spot, :] += returned[which][...].astype(F32)
+        total_ref[spot, :] += returned[which][-block:, :].astype(F32)
 
     def wide_dot(value, weight):
         high = value.astype(BF16)
@@ -467,48 +473,41 @@
         away, kept = halve(bit, came, kept, after)
 
 
-def sum_of_square(away, kept, after):
-    slots, rows, latent = kept.shape
-    came = swap(away, "dp", lambda i: i ^ 1)
-    piece = pltpu.VMEM((rows // 2, latent), BF16)
-    limit = pltpu.CompilerParams(vmem_limit_bytes=4 * 1024 * 1024)
-    cost = pl.CostEstimate(flops=0, bytes_accessed=500_000, transcendentals=0)
-    cross, over, beside, left = pl.pallas_call(
-        quarter_kernel,
-        out_shape=(piece, piece, piece, pltpu.VMEM((rows // 2, latent), F32)),
-        in_specs=[VMEM] * 3,
-        out_specs=(VMEM,) * 4,
-        compiler_params=limit,
-        cost_estimate=cost,
-        name="quarter",
-    )(in_vmem(came), in_vmem(kept), in_vmem(after))
-    ways = lax.axis_size("dp")
-    parts = lax.axis_size("dom")
-    diagonal = [
-        (d * ways + p, (d ^ 1) * ways + (p ^ 2)) for d in range(parts) for p in range(ways)
-    ]
-    arrived = [
-        lax.ppermute(cross, ("dom", "dp"), diagonal),
-        swap(over, "dp", lambda i: i ^ 2),
-        swap(beside, "dom", lambda i: i ^ 1),
-    ]
-
-    def finish(*late):
-        return pl.pallas_call(
-            add_kernel,
-            out_shape=piece,
-            in_specs=[VMEM] * (4 + len(late)),
-            out_specs=VMEM,
-            compiler_params=limit,
-            cost_estimate=cost,
-            name="add_terms",
-        )(*[in_vmem(array) for array in (left, *arrived, *late)])
-
-    return cross, finish
+def small_call(kernel, name, out_shape, *operands):
+    many = isinstance(out_shape, tuple)
+    return pl.pallas_call(
+        kernel,
+        out_shape=out_shape,
+        in_specs=[VMEM] * len(operands),
+        out_specs=(VMEM,) * len(out_shape) if many else VMEM,
+        compiler_params=pltpu.CompilerParams(vmem_limit_bytes=4 * 1024 * 1024),
+        cost_estimate=pl.CostEstimate(flops=0, bytes_accessed=500_000, transcendentals=0),
+        name=name,
+    )(*[in_vmem(array) for array in operands])
+
+
+def sum_of_pair(nodes, block, came, kept, sums, after, last):
+    rows, latent = kept.shape[1:]
+    half = rows // 2
+    sent = half if sums is None else half + block
+    extra = after if sums is None else (sums, *after)
+    away, left = small_call(
+        functools.partial(split_kernel, nodes, block),
+        "split",
+        (pltpu.VMEM((sent, latent), BF16), pltpu.VMEM((half, latent), F32)),
+        came,
+        kept,
+        *extra,
+    )
+    came = swap(away, "dom", lambda i: i ^ 1)
+    return small_call(add_kernel, "add_terms", pltpu.VMEM((half, latent), BF16), left, came, *last), came
 
 
 def sum_of_four(kept):
-    kept = (kept.astype(F32) + swap(kept, "dom", lambda i: 3 - i).astype(F32)).astype(BF16)
+    return (kept.astype(F32) + swap(kept, "dom", lambda i: 3 - i).astype(F32)).astype(BF16)
+
+
+def with_other_half(kept):
     return kept, swap(kept, "dom", lambda i: i ^ 1)
 
 
@@ -654,18 +653,44 @@
         name="rest_weights",
     )(*[in_vmem(array) for array in (node_v, edge_v, ext, grad_pre, sums)])
     if four:
-        sent_a, finish_a = sum_of_square(away_a, kept_a, cot_v)
+        came_a = swap(away_a, "dp", lambda i: i ^ 1)
+        away_a, kept_a, near, far = small_call(
+            functools.partial(send_back_kernel, nodes, block),
+            "halve",
+            (
+                pltpu.VMEM((1, 2 * unit, latent), BF16),
+                pltpu.VMEM((1, 2 * unit, latent), F32),
+                block_shape,
+                block_shape,
+            ),
+            came_a,
+            kept_a,
+            sums,
+        )
+        came_a = swap(away_a, "dp", lambda i: i ^ 2)
+        far = swap(far, "dom", lambda i: partners_of_four(2)[i])
+        near = swap(near, "dom", lambda i: partners_of_four(1)[i])
+        pair_a, beside = sum_of_pair(nodes, block, came_a, kept_a, sums, (), ())
+        four_a = sum_of_four(pair_a)
+        came_b = swap(away_b, "dp", lambda i: i ^ 1)
+        away_b, kept_b = halve(2, came_b, kept_b, near)
+        came_b = swap(away_b, "dp", lambda i: i ^ 2)
+        pair_b, _ = sum_of_pair(nodes, block, came_b, kept_b, None, (pair_a, far), (four_a,))
+        returned = [beside, near, far]
+        late, later, backs = pair_a, pair_b, 0
     else:
-        came_a, kept_a, sent_a = sum_over_dp(away_a, kept_a, cot_v)
+        came_a, kept_a, late = sum_over_dp(away_a, kept_a, cot_v)
+        came_b, kept_b, later = sum_over_dp(away_b, kept_b, cot_v)
+        backs = arrivals
     edge_grad, agg, *back_sums = pl.pallas_call(
         functools.partial(edge_grad_kernel, block, arrivals, four),
         out_shape=(
             jax.ShapeDtypeStruct((edges, latent), BF16),
             jax.ShapeDtypeStruct((nodes, latent), BF16),
         )
-        + (block_shape,) * arrivals,
+        + (block_shape,) * backs,
         in_specs=[HBM, SMEM] + [VMEM] * 7,
-        out_specs=(VMEM,) * (2 + arrivals),
+        out_specs=(VMEM,) * (2 + backs),
         scratch_shapes=[
             pltpu.SMEM((tiles,), jnp.int32),
             pltpu.VMEM((nodes, latent), F32),
@@ -679,20 +704,12 @@
     )(
         tile_dst,
         tile_count,
-        *[in_vmem(array) for array in (sent_a, grad_pre, sums, cot_v, win_v, edge_v, message)],
-    )
-    if four:
-        returned = exchange_of_four(*back_sums)
-        _, finish_b = sum_of_square(away_b, kept_b, back_sums[0])
-        pair_a = finish_a()
-        pair_b = finish_b(*returned)
-        late = pair_b
-    else:
+        *[in_vmem(array) for array in (late, grad_pre, sums, cot_v, win_v, edge_v, message)],
+    )
+    if not four:
         returned = [
             from_behind(back_sums[which], "dom", -OFFSET_LIST[which]) for which in range(4)
         ]
-        came_b, kept_b, _ = sum_over_dp(away_b, kept_b, back_sums[0])
-        late = sent_a
     node_out = pl.pallas_call(
         functools.partial(node_grad_kernel, arrivals, four),
         out_shape=jax.ShapeDtypeStruct((nodes, latent), BF16),
@@ -708,7 +725,7 @@
             flops=8 * nodes * latent * latent, bytes_accessed=2_000_000, transcendentals=0
         ),
         name="node_grads",
-    )(boundary, *[in_vmem(array) for array in (late, sums, win_v, *returned)])
+    )(boundary, *[in_vmem(array) for array in (later, sums, win_v, *returned)])
     if four:
         w_in_grad, w_out_grad = pl.pallas_call(
             last_kernel,
@@ -721,7 +738,7 @@
             compiler_params=small,
             cost_estimate=pl.CostEstimate(flops=0, bytes_accessed=1_500_000, transcendentals=0),
             name="widen",
-        )(in_hbm(node_out), *sum_of_four(pair_a), *sum_of_four(pair_b))
+        )(in_hbm(node_out), *with_other_half(four_a), *with_other_half(sum_of_four(pair_b)))
     else:
         sum_a = sum_over_dom(kept_a[0] + came_a[0].astype(F32))
         sum_b = sum_over_dom(kept_b[0] + came_b[0].astype(F32))

time: 60.1 us -> 66.5 us (1.11)
  waiting for transfers between devices: 17.2 us -> 28.1 us
  starting transfers between devices: 24.2 us -> 19.7 us
    ppermute x16 -> x15, waiting for transfers between devices: 17.2 us -> 28.1 us  [swap(): return lax.ppermute(array, axis, [(i, partner(i)) for i in range(devices)])]
    ppermute x16 -> x15, starting transfers between devices: 23.8 us -> 19.7 us  [swap(): return lax.ppermute(array, axis, [(i, partner(i)) for i in range(devices)])]
  transfers between devices with their start and end apart: 18 -> 15, of which waited for: 4 -> 7; matrix products, arithmetic and copies ran while one was open for 0% -> 0% of each run, Pallas kernels for 14% -> 13%
where the time goes in v8:
time: 66.5 us; the launch traced here: 66.3 us
  waiting for transfers between devices  28.1 us (42%)
  starting transfers between devices  19.7 us (30%)
  Pallas kernels  17 us (26%)
  between operations  1.45 us (2%)
    ppermute x15, waiting for transfers between devices, swap(): return lax.ppermute(array, axis, [(i, partner(i)) for i in range(devices)])  28.1 us
    ppermute x15, starting transfers between devices, swap(): return lax.ppermute(array, axis, [(i, partner(i)) for i in range(devices)])  19.7 us
    pallas_call x1, Pallas kernels, body(): pl.pallas_call(functools.partial(edge_kernel, ways, arrivals, four, block...  5.75 us
    pallas_call x1, Pallas kernels, body(): pl.pallas_call(functools.partial(prep_kernel, parts, arrivals), out_shape...  2.42 us
    pallas_call x1, Pallas kernels, body(): pl.pallas_call(functools.partial(edge_grad_kernel, block, arrivals, four)...  2.21 us
    pallas_call x1, Pallas kernels, body(): pl.pallas_call(functools.partial(node_grad_kernel, arrivals, four), out_s...  2.14 us
    pallas_call x1, Pallas kernels, body(): pl.pallas_call(functools.partial(pick_kernel, four, block), out_shape=(bl...  1.63 us
    pallas_call x1, Pallas kernels, body(): pl.pallas_call(functools.partial(rest_kernel, ways), out_shape=(sent_shap...  1.49 us
  transfers between devices with their start and end apart: 15, of which 7 were waited for; matrix products, arithmetic and copies ran while one was open for 0% of the time, Pallas kernels for 13%

profile of v8, /device:TPU:0, one launch (start us, length us, event | category | flops | bytes accessed | tf_op | source)
XLA Modules:
  0.0 66.3 jit_solution(17640174856123495550)
XLA Ops:
  0.6 1.6 %pick_blocks.1 = (bf16[64,512]{1,0:T(8,128)(2,1)S(1)}, bf16[64,512]{1,0:T(8,128)(2,1)S(1)}, bf16[64,512]{1,0:T(8,128)(2,1)S(1)}) custom-call(s32[1,4]{1,0:T(1,128)} %boundary_hbm.3, bf16[128,512]{1,0:T(8,128)(2,1)} %bitcast.7), custom_call_target="tpu_custom_call" | custom-call | bytes 400000 | tf_op jit(solution)/shard_map/pick_blocks/pallas_call | solution.py:552
  2.3 3.1 %collective-permute-start = (bf16[64,512]{1,0:T(8,128)(2,1)S(1)}, bf16[64,512]{1,0:T(8,128)(2,1)S(1)}, u32[]{:S(2)}, u32[]{:S(2)}) collective-permute-start(bf16[64,512]{1,0:T(8,128)(2,1)S(1)} %get-tuple-element.39), channel_id=1, source_target_pairs={{0,4},{4,0},{8,12},{12,8},{1,5},{5,1},{9,13},{13,9},{2,6},{6,2},{1... | collective-permute-start | bytes 196616 | tf_op jit(solution)/shard_map/ppermute | solution.py:429
  5.4 0.7 collective-permute-start.1
  6.0 3.9 %collective-permute-start.2 = (bf16[64,512]{1,0:T(8,128)(2,1)S(1)}, bf16[64,512]{1,0:T(8,128)(2,1)S(1)}, u32[]{:S(2)}, u32[]{:S(2)}) collective-permute-start(bf16[64,512]{1,0:T(8,128)(2,1)S(1)} %get-tuple-element.41), channel_id=1, source_target_pairs={{0,8},{4,12},{8,0},{12,4},{1,9},{5,13},{9,1},{13,5},{2,10},{6,14},... | collective-permute-start | bytes 196616 | tf_op jit(solution)/shard_map/ppermute | solution.py:429
  10.6 2.4 %prepare.1 = (bf16[128,512]{1,0:T(8,128)(2,1)S(1)}, bf16[768,512]{1,0:T(8,128)(2,1)S(1)}, bf16[128,512]{1,0:T(8,128)(2,1)S(1)}, bf16[1536,512]{1,0:T(8,128)(2,1)...) custom-call(s32[1]{0:T(128)S(6)} %copy.15.count_ref, ...), custom_call_target="tpu_custom_call" | custom-call | flops 402653184 | bytes 8000000 | tf_op jit(solution)/shard_map/prepare/pallas_call | solution.py:574
  13.0 0.0 collective-permute-done.refs_0_
  13.1 0.7 %collective-permute-done.2.refs_2_ = bf16[64,512]{1,0:T(8,128)(2,1)S(1)} collective-permute-done((bf16[64,512]{1,0:T(8,128)(2,1)S(1)}, bf16[64,512]{1,0:T(8,128)(2,1)S(1)}, u32[]{:S(2)}, u32[]{:S(2)}) %collective-permute-start.2) | collective-permute-done | bytes 65568 | tf_op jit(solution)/shard_map/ppermute | solution.py:429
  13.8 5.7 %edge_block.1 = (bf16[768,512]{1,0:T(8,128)(2,1)S(1)}, f32[768,512]{1,0:T(8,128)S(1)}, f32[512,512]{1,0:T(8,128)S(1)}, bf16[384,512]{1,0:T(8,128)(2,1)S(1)}, bf1...) custom-call(bf16[64,512]{1,0:T(8,128)(2,1)S(1)} %collective-permute-done.refs_0_, ...), custom_call_target="tpu_custom_call" | custom-call | flops 2415919104 | bytes 12000000 | tf_op jit(solution)/shard_map/edge_block/pallas_call | solution.py:615
  19.5 0.1 collective-permute-start.3
  19.6 1.5 %rest_weights.1 = (bf16[2,256,512]{2,1,0:T(8,128)(2,1)S(1)}, f32[2,256,512]{2,1,0:T(8,128)S(1)}) custom-call(bf16[128,512]{1,0:T(8,128)(2,1)S(1)} %get-tuple-element.42.refs_3_.node_ref, bf16[768,512]{1,0:T(8,128)(2,1)S(1)} %get-tuple-element.43.refs_4_.edge_ref, bf16[384,512]{1,0:T(8,128)(2,1)S(1)} %get-tuple-element.62.ext_ref, ...), custom_call_target="tpu_custom_call" | custom-call | flops 402653184 | bytes 4000000 | tf_op jit(solution)/shard_map/rest_weights/pallas_call | solution.py:644
  21.1 0.6 collective-permute-start.6
  21.7 0.1 halve.2
  21.8 1.6 %collective-permute-start.4 = (bf16[1,256,512]{2,1,0:T(8,128)(2,1)S(1)}, bf16[1,256,512]{2,1,0:T(8,128)(2,1)S(1)}, u32[]{:S(2)}, u32[]{:S(2)}) collective-permute-start(bf16[1,256,512]{2,1,0:T(8,128)(2,1)S(1)} %get-tuple-element.53), channel_id=1, source_target_pairs={{0,2},{1,3},{2,0},{3,1},{4,6},{5,7},{6,4},{7,5},{8,10},{9,11},{10,... | collective-permute-start | bytes 786440 | tf_op jit(solution)/shard_map/ppermute | solution.py:429
  23.4 0.7 collective-permute-start.7
  24.0 6.1 %collective-permute-done.4.came_ref = bf16[1,256,512]{2,1,0:T(8,128)(2,1)S(1)} collective-permute-done((bf16[1,256,512]{2,1,0:T(8,128)(2,1)S(1)}, bf16[1,256,512]{2,1,0:T(8,128)(2,1)S(1)}, u32[]{:S(2)}, u32[]{:S(2)}) %collective-permute-start.4) | collective-permute-done | bytes 262176 | tf_op jit(solution)/shard_map/ppermute | solution.py:429
  30.1 0.1 split.2
  30.2 2.0 %collective-permute-start.5 = (bf16[192,512]{1,0:T(8,128)(2,1)S(1)}, bf16[192,512]{1,0:T(8,128)(2,1)S(1)}, u32[]{:S(2)}, u32[]{:S(2)}) collective-permute-start(bf16[192,512]{1,0:T(8,128)(2,1)S(1)} %get-tuple-element.56), channel_id=1, source_target_pairs={{0,4},{4,0},{8,12},{12,8},{1,5},{5,1},{9,13},{13,9},{2,6},{6,2},{1... | collective-permute-start | bytes 589832 | tf_op jit(solution)/shard_map/ppermute | solution.py:429
  32.1 0.1 halve.3
  32.2 1.6 %collective-permute-start.8 = (bf16[1,256,512]{2,1,0:T(8,128)(2,1)S(1)}, bf16[1,256,512]{2,1,0:T(8,128)(2,1)S(1)}, u32[]{:S(2)}, u32[]{:S(2)}) collective-permute-start(bf16[1,256,512]{2,1,0:T(8,128)(2,1)S(1)} %get-tuple-element.66), channel_id=1, source_target_pairs={{0,2},{1,3},{2,0},{3,1},{4,6},{5,7},{6,4},{7,5},{8,10},{9,11},{10,... | collective-permute-start | bytes 786440 | tf_op jit(solution)/shard_map/ppermute | solution.py:429
  33.8 2.6 %collective-permute-done.5.came_ref.refs_0_ = bf16[192,512]{1,0:T(8,128)(2,1)S(1)} collective-permute-done((bf16[192,512]{1,0:T(8,128)(2,1)S(1)}, bf16[192,512]{1,0:T(8,128)(2,1)S(1)}, u32[]{:S(2)}, u32[]{:S(2)}) %collective-permute-start.5) | collective-permute-done | bytes 196640 | tf_op jit(solution)/shard_map/ppermute | solution.py:429
  36.4 3.3 %collective-permute-start.11 = (bf16[128,512]{1,0:T(8,128)(2,1)S(1)}, bf16[128,512]{1,0:T(8,128)(2,1)S(1)}, u32[]{:S(2)}, u32[]{:S(2)}) collective-permute-start(bf16[128,512]{1,0:T(8,128)(2,1)S(1)} %add_terms.2.after.refs_0_), channel_id=1, source_target_pairs={{0,12},{4,8},{8,4},{12,0},{1,13},{5,9},{9,5},{13,1},{2,14},{6,10},... | collective-permute-start | bytes 393224 | tf_op jit(solution)/shard_map/ppermute | solution.py:429
  39.7 0.0 collective-permute-start.9
  39.7 7.3 %collective-permute-done.9.refs_1_.refs_2_ = bf16[64,512]{1,0:T(8,128)(2,1)S(1)} collective-permute-done((bf16[64,512]{1,0:T(8,128)(2,1)S(1)}, bf16[64,512]{1,0:T(8,128)(2,1)S(1)}, u32[]{:S(2)}, u32[]{:S(2)}) %collective-permute-start.9) | collective-permute-done | bytes 65568 | tf_op jit(solution)/shard_map/ppermute | solution.py:429
  47.0 0.1 collective-permute-start.10
  47.2 4.9 %collective-permute-done.10.came_ref = bf16[128,512]{1,0:T(8,128)(2,1)S(1)} collective-permute-done((bf16[128,512]{1,0:T(8,128)(2,1)S(1)}, bf16[128,512]{1,0:T(8,128)(2,1)S(1)}, u32[]{:S(2)}, u32[]{:S(2)}) %collective-permute-start.10) | collective-permute-done | bytes 131104 | tf_op jit(solution)/shard_map/ppermute | solution.py:429
  52.1 2.2 %collective-permute-start.13 = (bf16[128,512]{1,0:T(8,128)(2,1)S(1)}, bf16[128,512]{1,0:T(8,128)(2,1)S(1)}, u32[]{:S(2)}, u32[]{:S(2)}) collective-permute-start(bf16[128,512]{1,0:T(8,128)(2,1)S(1)} %add_terms.3.after), channel_id=1, source_target_pairs={{0,12},{4,8},{8,4},{12,0},{1,13},{5,9},{9,5},{13,1},{2,14},{6,10},... | collective-permute-start | bytes 393224 | tf_op jit(solution)/shard_map/ppermute | solution.py:429
  54.3 5.9 %collective-permute-done.13 = bf16[128,512]{1,0:T(8,128)(2,1)S(1)} collective-permute-done((bf16[128,512]{1,0:T(8,128)(2,1)S(1)}, bf16[128,512]{1,0:T(8,128)(2,1)S(1)}, u32[]{:S(2)}, u32[]{:S(2)}) %collective-permute-start.13) | collective-permute-done | bytes 131104 | tf_op jit(solution)/shard_map/ppermute | solution.py:429
  60.2 0.1 collective-permute-start.14
  60.3 2.2 %edge_grads.1 = (bf16[768,512]{1,0:T(8,128)(2,1)}, bf16[128,512]{1,0:T(8,128)(2,1)}) custom-call(s32[12]{0:T(128)} %dst_hbm.3, s32[1]{0:T(128)S(6)} %copy.15.count_ref, bf16[128,512]{1,0:T(8,128)(2,1)S(1)} %add_terms.2.after.refs_0_, bf16[768,512]{1,0:T(8,128)(2,1)S(1)} %get-tuple-element.57.gpre_ref, f32[512,512]{1,0:T(8,128)S(1)} %get-tuple-element.52.sums_ref.refs_0_, ...), custom_call_target="tpu_custom_call" | custom-call | flops 402653184 | bytes 3000000 | tf_op jit(solution)/shard_map/edge_grads/pallas_call | solution.py:685
  62.5 2.1 %node_grads.1.after = bf16[128,512]{1,0:T(8,128)(2,1)} custom-call(s32[1,4]{1,0:T(1,128)} %boundary_hbm.3, bf16[128,512]{1,0:T(8,128)(2,1)S(1)} %add_terms.3.after, f32[512,512]{1,0:T(8,128)S(1)} %get-tuple-element.52.sums_ref.refs_0_, bf16[1536,512]{1,0:T(8,128)(2,1)S(1)} %get-tuple-element.44.refs_5_.win_ref, ...), custom_call_target="tpu_custom_call" | custom-call | flops 268435456 | bytes 2000000 | tf_op jit(solution)/shard_map/node_grads/pallas_call | solution.py:713
  64.7 0.6 collective-permute-done.14.other_b
  65.2 1.0 %widen.1 = (f32[384,512]{1,0:T(8,128)}, f32[128,512]{1,0:T(8,128)}) custom-call(bf16[128,512]{1,0:T(8,128)(2,1)} %node_grads.1.after, bf16[128,512]{1,0:T(8,128)(2,1)S(1)} %add_convert_fusion.1.refs_0_.own_a, bf16[128,512]{1,0:T(8,128)(2,1)S(1)} %collective-permute-done.12.other_a, bf16[128,512]{1,0:T(8,128)(2,1)S(1)} %add_convert_fusion.own_b, ...), custom_call_target="tpu_custom_call" | custom-call | bytes 1500000 | tf_op jit(solution)/shard_map/widen/pallas_call | solution.py:730
  (13 shorter events, 0.2 us)
Async XLA Ops:
  2.3 10.8 %collective-permute-start = (bf16[64,512]{1,0:T(8,128)(2,1)S(1)}, bf16[64,512]{1,0:T(8,128)(2,1)S(1)}, u32[]{:S(2)}, u32[]{:S(2)}) collective-permute-start(bf16[64,512]{1,0:T(8,128)(2,1)S(1)} %get-tuple-element.39), channel_id=1, source_target_pairs={{0,4},{4,0},{8,12},{12,8},{1,5},{5,1},{9,13},{13,9},{2,6},{6,2},{1... | collective-permute-start | bytes 196616 | tf_op jit(solution)/shard_map/ppermute | solution.py:429
  5.4 7.7 %collective-permute-start.1 = (bf16[64,512]{1,0:T(8,128)(2,1)S(1)}, bf16[64,512]{1,0:T(8,128)(2,1)S(1)}, u32[]{:S(2)}, u32[]{:S(2)}) collective-permute-start(bf16[64,512]{1,0:T(8,128)(2,1)S(1)} %get-tuple-element.40), channel_id=1, source_target_pairs={{0,0},{4,8},{8,4},{12,12},{1,1},{5,9},{9,5},{13,13},{2,2},{6,10},{... | collective-permute-start | bytes 196616 | tf_op jit(solution)/shard_map/ppermute | solution.py:429
  6.0 7.8 %collective-permute-start.2 = (bf16[64,512]{1,0:T(8,128)(2,1)S(1)}, bf16[64,512]{1,0:T(8,128)(2,1)S(1)}, u32[]{:S(2)}, u32[]{:S(2)}) collective-permute-start(bf16[64,512]{1,0:T(8,128)(2,1)S(1)} %get-tuple-element.41), channel_id=1, source_target_pairs={{0,8},{4,12},{8,0},{12,4},{1,9},{5,13},{9,1},{13,5},{2,10},{6,14},... | collective-permute-start | bytes 196616 | tf_op jit(solution)/shard_map/ppermute | solution.py:429
  19.5 2.2 %collective-permute-start.3 = (bf16[2,256,512]{2,1,0:T(8,128)(2,1)S(1)}, bf16[2,256,512]{2,1,0:T(8,128)(2,1)S(1)}, u32[]{:S(2)}, u32[]{:S(2)}) collective-permute-start(bf16[2,256,512]{2,1,0:T(8,128)(2,1)S(1)} %get-tuple-element.50), channel_id=1, source_target_pairs={{0,1},{1,0},{2,3},{3,2},{4,5},{5,4},{6,7},{7,6},{8,9},{9,8},{10,11... | collective-permute-start | bytes 1572872 | tf_op jit(solution)/shard_map/ppermute | solution.py:429
  21.1 11.0 %collective-permute-start.6 = (bf16[2,256,512]{2,1,0:T(8,128)(2,1)S(1)}, bf16[2,256,512]{2,1,0:T(8,128)(2,1)S(1)}, u32[]{:S(2)}, u32[]{:S(2)}) collective-permute-start(bf16[2,256,512]{2,1,0:T(8,128)(2,1)S(1)} %get-tuple-element.63), channel_id=1, source_target_pairs={{0,1},{1,0},{2,3},{3,2},{4,5},{5,4},{6,7},{7,6},{8,9},{9,8},{10,11... | collective-permute-start | bytes 1572872 | tf_op jit(solution)/shard_map/ppermute | solution.py:429
  21.8 8.3 %collective-permute-start.4 = (bf16[1,256,512]{2,1,0:T(8,128)(2,1)S(1)}, bf16[1,256,512]{2,1,0:T(8,128)(2,1)S(1)}, u32[]{:S(2)}, u32[]{:S(2)}) collective-permute-start(bf16[1,256,512]{2,1,0:T(8,128)(2,1)S(1)} %get-tuple-element.53), channel_id=1, source_target_pairs={{0,2},{1,3},{2,0},{3,1},{4,6},{5,7},{6,4},{7,5},{8,10},{9,11},{10,... | collective-permute-start | bytes 786440 | tf_op jit(solution)/shard_map/ppermute | solution.py:429
  23.4 8.8 %collective-permute-start.7 = (bf16[64,512]{1,0:T(8,128)(2,1)S(1)}, bf16[64,512]{1,0:T(8,128)(2,1)S(1)}, u32[]{:S(2)}, u32[]{:S(2)}) collective-permute-start(bf16[64,512]{1,0:T(8,128)(2,1)S(1)} %get-tuple-element.65), channel_id=1, source_target_pairs={{0,0},{4,8},{8,4},{12,12},{1,1},{5,9},{9,5},{13,13},{2,2},{6,10},{... | collective-permute-start | bytes 196616 | tf_op jit(solution)/shard_map/ppermute | solution.py:429
  30.2 6.2 %collective-permute-start.5 = (bf16[192,512]{1,0:T(8,128)(2,1)S(1)}, bf16[192,512]{1,0:T(8,128)(2,1)S(1)}, u32[]{:S(2)}, u32[]{:S(2)}) collective-permute-start(bf16[192,512]{1,0:T(8,128)(2,1)S(1)} %get-tuple-element.56), channel_id=1, source_target_pairs={{0,4},{4,0},{8,12},{12,8},{1,5},{5,1},{9,13},{13,9},{2,6},{6,2},{1... | collective-permute-start | bytes 589832 | tf_op jit(solution)/shard_map/ppermute | solution.py:429
  32.2 14.7 %collective-permute-start.8 = (bf16[1,256,512]{2,1,0:T(8,128)(2,1)S(1)}, bf16[1,256,512]{2,1,0:T(8,128)(2,1)S(1)}, u32[]{:S(2)}, u32[]{:S(2)}) collective-permute-start(bf16[1,256,512]{2,1,0:T(8,128)(2,1)S(1)} %get-tuple-element.66), channel_id=1, source_target_pairs={{0,2},{1,3},{2,0},{3,1},{4,6},{5,7},{6,4},{7,5},{8,10},{9,11},{10,... | collective-permute-start | bytes 786440 | tf_op jit(solution)/shard_map/ppermute | solution.py:429
  36.4 10.7 %collective-permute-start.11 = (bf16[128,512]{1,0:T(8,128)(2,1)S(1)}, bf16[128,512]{1,0:T(8,128)(2,1)S(1)}, u32[]{:S(2)}, u32[]{:S(2)}) collective-permute-start(bf16[128,512]{1,0:T(8,128)(2,1)S(1)} %add_terms.2.after.refs_0_), channel_id=1, source_target_pairs={{0,12},{4,8},{8,4},{12,0},{1,13},{5,9},{9,5},{13,1},{2,14},{6,10},... | collective-permute-start | bytes 393224 | tf_op jit(solution)/shard_map/ppermute | solution.py:429
  39.7 7.3 %collective-permute-start.9 = (bf16[64,512]{1,0:T(8,128)(2,1)S(1)}, bf16[64,512]{1,0:T(8,128)(2,1)S(1)}, u32[]{:S(2)}, u32[]{:S(2)}) collective-permute-start(bf16[64,512]{1,0:T(8,128)(2,1)S(1)} %get-tuple-element.68), channel_id=1, source_target_pairs={{0,8},{4,12},{8,0},{12,4},{1,9},{5,13},{9,1},{13,5},{2,10},{6,14},... | collective-permute-start | bytes 196616 | tf_op jit(solution)/shard_map/ppermute | solution.py:429
  47.0 5.0 %collective-permute-start.10 = (bf16[128,512]{1,0:T(8,128)(2,1)S(1)}, bf16[128,512]{1,0:T(8,128)(2,1)S(1)}, u32[]{:S(2)}, u32[]{:S(2)}) collective-permute-start(bf16[128,512]{1,0:T(8,128)(2,1)S(1)} %get-tuple-element.70), channel_id=1, source_target_pairs={{0,4},{4,0},{8,12},{12,8},{1,5},{5,1},{9,13},{13,9},{2,6},{6,2},{1... | collective-permute-start | bytes 393224 | tf_op jit(solution)/shard_map/ppermute | solution.py:429
  52.1 8.1 %collective-permute-start.13 = (bf16[128,512]{1,0:T(8,128)(2,1)S(1)}, bf16[128,512]{1,0:T(8,128)(2,1)S(1)}, u32[]{:S(2)}, u32[]{:S(2)}) collective-permute-start(bf16[128,512]{1,0:T(8,128)(2,1)S(1)} %add_terms.3.after), channel_id=1, source_target_pairs={{0,12},{4,8},{8,4},{12,0},{1,13},{5,9},{9,5},{13,1},{2,14},{6,10},... | collective-permute-start | bytes 393224 | tf_op jit(solution)/shard_map/ppermute | solution.py:429
  54.3 10.4 %collective-permute-start.12 = (bf16[128,512]{1,0:T(8,128)(2,1)S(1)}, bf16[128,512]{1,0:T(8,128)(2,1)S(1)}, u32[]{:S(2)}, u32[]{:S(2)}) collective-permute-start(bf16[128,512]{1,0:T(8,128)(2,1)S(1)} %add_convert_fusion.1.refs_0_.own_a), channel_id=1, source_target_pairs={{0,4},{4,0},{8,12},{12,8},{1,5},{5,1},{9,13},{13,9},{2,6},{6,2},{1... | collective-permute-start | bytes 393224 | tf_op jit(solution)/shard_map/ppermute | solution.py:429
  60.2 5.0 %collective-permute-start.14 = (bf16[128,512]{1,0:T(8,128)(2,1)S(1)}, bf16[128,512]{1,0:T(8,128)(2,1)S(1)}, u32[]{:S(2)}, u32[]{:S(2)}) collective-permute-start(bf16[128,512]{1,0:T(8,128)(2,1)S(1)} %add_convert_fusion.own_b), channel_id=1, source_target_pairs={{0,4},{4,0},{8,12},{12,8},{1,5},{5,1},{9,13},{13,9},{2,6},{6,2},{1... | collective-permute-start | bytes 393224 | tf_op jit(solution)/shard_map/ppermute | solution.py:429

commit v9 on v8

--- a/solution.py
+++ b/solution.py
@@ -351,33 +351,59 @@
         left_ref[slot] = kept_ref[here] + came_ref[here].astype(F32)
 
 
-def send_back_kernel(nodes, block, came_ref, kept_ref, sums_ref, away_ref, left_ref, *back_refs):
-    halve_kernel(2, came_ref, kept_ref, None, away_ref, left_ref)
-    for place, back_ref in zip(arrival_places(lax.axis_index("dom"), True, 3)[1:], back_refs):
-        at = pl.multiple_of(nodes + place * block, block)
-        back_ref[...] = sums_ref[pl.ds(at, block), :].astype(BF16)
-
-
-def split_kernel(nodes, block, came_ref, kept_ref, *refs):
-    away_ref, left_ref = refs[-2:]
+def half_rows(rows):
     part = lax.axis_index("dom")
     inner = (part == 1) | (part == 2)
-    rows = left_ref.shape[0]
     here = pl.ds(pl.multiple_of(jnp.where(inner, 0, rows), rows), rows)
     there = pl.ds(pl.multiple_of(jnp.where(inner, rows, 0), rows), rows)
-    away_ref[:rows, :] = (kept_ref[0, there, :] + came_ref[0, there, :].astype(F32)).astype(BF16)
+    return here, there
+
+
+def back_block(nodes, block, sums_ref, which):
+    place = arrival_places(lax.axis_index("dom"), True, 3)[which]
+    return sums_ref[pl.ds(pl.multiple_of(nodes + place * block, block), block), :].astype(BF16)
+
+
+def over_first_kernel(nodes, block, came_ref, kept_ref, sums_ref, away_ref, left_ref, *back_refs):
+    halve_kernel(2, came_ref, kept_ref, None, away_ref, left_ref)
+    for which, back_ref in enumerate(back_refs):
+        back_ref[...] = back_block(nodes, block, sums_ref, 1 + which)
+
+
+def beside_first_kernel(nodes, block, came_ref, kept_ref, sums_ref, away_ref, left_ref):
+    rows = left_ref.shape[1]
+    here, there = half_rows(rows)
+    for slot in range(2):
+        away_ref[slot * rows : (slot + 1) * rows, :] = (
+            kept_ref[slot, there, :] + came_ref[slot, there, :].astype(F32)
+        ).astype(BF16)
+        left_ref[slot] = kept_ref[slot, here, :] + came_ref[slot, here, :].astype(F32)
+    away_ref[2 * rows :, :] = back_block(nodes, block, sums_ref, 0)
+
+
+def beside_second_kernel(came_ref, kept_ref, *refs):
+    away_ref, left_ref = refs[-2:]
+    here, there = half_rows(left_ref.shape[0])
+    away_ref[...] = (kept_ref[0, there, :] + came_ref[0, there, :].astype(F32)).astype(BF16)
     left_ref[...] = kept_ref[0, here, :] + came_ref[0, here, :].astype(F32)
-    if away_ref.shape[0] > rows:
-        sums_ref = refs[0]
-        place = arrival_places(part, True, 3)[0]
-        at = pl.multiple_of(nodes + place * block, block)
-        away_ref[rows:, :] = sums_ref[pl.ds(at, block), :].astype(BF16)
+
+
+def over_second_kernel(came_ref, kept_ref, *refs):
+    away_ref, left_ref = refs[-2:]
+    mine = lax.axis_index("dp") // 2
+    rows = left_ref.shape[0]
+
+    def came(slot):
+        spot = pl.ds(pl.multiple_of(slot * rows, rows), rows)
+        return came_ref[spot, :].astype(F32)
+
+    away_ref[...] = (kept_ref[1 - mine] + came(1 - mine)).astype(BF16)
+    left_ref[...] = kept_ref[mine] + came(mine)
 
 
 def add_kernel(left_ref, came_ref, *refs):
     out_ref = refs[-1]
-    rows = out_ref.shape[0]
-    out_ref[...] = (left_ref[...] + came_ref[:rows, :].astype(F32)).astype(BF16)
+    out_ref[...] = (left_ref[...] + came_ref[...].astype(F32)).astype(BF16)
 
 
 def node_grad_kernel(arrivals, four, boundary_hbm, after, sums_ref, win_ref, *refs):
@@ -473,34 +499,17 @@
         away, kept = halve(bit, came, kept, after)
 
 
-def small_call(kernel, name, out_shape, *operands):
+def small_call(kernel, name, out_shape, *operands, after=()):
     many = isinstance(out_shape, tuple)
     return pl.pallas_call(
         kernel,
         out_shape=out_shape,
-        in_specs=[VMEM] * len(operands),
+        in_specs=[VMEM] * len(operands) + [HBM] * len(after),
         out_specs=(VMEM,) * len(out_shape) if many else VMEM,
         compiler_params=pltpu.CompilerParams(vmem_limit_bytes=4 * 1024 * 1024),
         cost_estimate=pl.CostEstimate(flops=0, bytes_accessed=500_000, transcendentals=0),
         name=name,
-    )(*[in_vmem(array) for array in operands])
-
-
-def sum_of_pair(nodes, block, came, kept, sums, after, last):
-    rows, latent = kept.shape[1:]
-    half = rows // 2
-    sent = half if sums is None else half + block
-    extra = after if sums is None else (sums, *after)
-    away, left = small_call(
-        functools.partial(split_kernel, nodes, block),
-        "split",
-        (pltpu.VMEM((sent, latent), BF16), pltpu.VMEM((half, latent), F32)),
-        came,
-        kept,
-        *extra,
-    )
-    came = swap(away, "dom", lambda i: i ^ 1)
-    return small_call(add_kernel, "add_terms", pltpu.VMEM((half, latent), BF16), left, came, *last), came
+    )(*[in_vmem(array) for array in operands], *[in_hbm(array) for array in after])
 
 
 def sum_of_four(kept):
@@ -653,13 +662,15 @@
         name="rest_weights",
     )(*[in_vmem(array) for array in (node_v, edge_v, ext, grad_pre, sums)])
     if four:
+        rows = 2 * unit
+        piece, wide = pltpu.VMEM((unit, latent), BF16), pltpu.VMEM((unit, latent), F32)
         came_a = swap(away_a, "dp", lambda i: i ^ 1)
         away_a, kept_a, near, far = small_call(
-            functools.partial(send_back_kernel, nodes, block),
-            "halve",
+            functools.partial(over_first_kernel, nodes, block),
+            "over_first",
             (
-                pltpu.VMEM((1, 2 * unit, latent), BF16),
-                pltpu.VMEM((1, 2 * unit, latent), F32),
+                pltpu.VMEM((1, rows, latent), BF16),
+                pltpu.VMEM((1, rows, latent), F32),
                 block_shape,
                 block_shape,
             ),
@@ -668,19 +679,32 @@
             sums,
         )
         came_a = swap(away_a, "dp", lambda i: i ^ 2)
+        came_b = swap(away_b, "dp", lambda i: i ^ 1)
+        away_b, kept_b = small_call(
+            functools.partial(beside_first_kernel, nodes, block),
+            "beside_first",
+            (pltpu.VMEM((rows + block, latent), BF16), pltpu.VMEM((2, unit, latent), F32)),
+            came_b,
+            kept_b,
+            sums,
+        )
+        beside = swap(away_b, "dom", lambda i: i ^ 1)
         far = swap(far, "dom", lambda i: partners_of_four(2)[i])
         near = swap(near, "dom", lambda i: partners_of_four(1)[i])
-        pair_a, beside = sum_of_pair(nodes, block, came_a, kept_a, sums, (), ())
-        four_a = sum_of_four(pair_a)
-        came_b = swap(away_b, "dp", lambda i: i ^ 1)
-        away_b, kept_b = halve(2, came_b, kept_b, near)
+        away_a, kept_a = small_call(
+            beside_second_kernel, "beside_second", (piece, wide), came_a, kept_a, near, far
+        )
+        came_a = swap(away_a, "dom", lambda i: i ^ 1)
+        away_b, kept_b = small_call(
+            over_second_kernel, "over_second", (piece, wide), beside, kept_b
+        )
         came_b = swap(away_b, "dp", lambda i: i ^ 2)
-        pair_b, _ = sum_of_pair(nodes, block, came_b, kept_b, None, (pair_a, far), (four_a,))
+        pair_a = small_call(add_kernel, "add_terms", piece, kept_a, came_a)
         returned = [beside, near, far]
-        late, later, backs = pair_a, pair_b, 0
+        late, backs = pair_a, 0
     else:
         came_a, kept_a, late = sum_over_dp(away_a, kept_a, cot_v)
-        came_b, kept_b, later = sum_over_dp(away_b, kept_b, cot_v)
+        came_b, kept_b, _ = sum_over_dp(away_b, kept_b, cot_v)
         backs = arrivals
     edge_grad, agg, *back_sums = pl.pallas_call(
         functools.partial(edge_grad_kernel, block, arrivals, four),
@@ -706,7 +730,11 @@
         tile_count,
         *[in_vmem(array) for array in (late, grad_pre, sums, cot_v, win_v, edge_v, message)],
     )
-    if not four:
+    if four:
+        pair_b = small_call(add_kernel, "add_terms", piece, kept_b, came_b, after=(edge_grad,))
+        later = pair_b
+    else:
+        later = late
         returned = [
             from_behind(back_sums[which], "dom", -OFFSET_LIST[which]) for which in range(4)
         ]
@@ -738,7 +766,7 @@
             compiler_params=small,
             cost_estimate=pl.CostEstimate(flops=0, bytes_accessed=1_500_000, transcendentals=0),
             name="widen",
-        )(in_hbm(node_out), *with_other_half(four_a), *with_other_half(sum_of_four(pair_b)))
+        )(in_hbm(node_out), *with_other_half(sum_of_four(pair_a)), *with_other_half(sum_of_four(pair_b)))
     else:
         sum_a = sum_over_dom(kept_a[0] + came_a[0].astype(F32))
         sum_b = sum_over_dom(kept_b[0] + came_b[0].astype(F32))

time: 66.5 us -> 60.4 us (0.908)
  waiting for transfers between devices: 28.1 us -> 10.5 us
  starting transfers between devices: 19.7 us -> 31.3 us
    ppermute x15, waiting for transfers between devices: 28.1 us -> 10.5 us  [swap(): return lax.ppermute(array, axis, [(i, partner(i)) for i in range(devices)])]
    ppermute x15, starting transfers between devices: 19.7 us -> 31.3 us  [swap(): return lax.ppermute(array, axis, [(i, partner(i)) for i in range(devices)])]
  transfers between devices with their start and end apart: 15 -> 15, of which waited for: 7 -> 6; matrix products, arithmetic and copies ran while one was open for 0% -> 0% of each run, Pallas kernels for 13% -> 14%
where the time goes in v9:
time: 60.4 us; the launch traced here: 60.2 us
  starting transfers between devices  31.3 us (52%)
  Pallas kernels  17 us (28%)
  waiting for transfers between devices  10.5 us (17%)
  between operations  1.43 us (2%)
    ppermute x15, starting transfers between devices, swap(): return lax.ppermute(array, axis, [(i, partner(i)) for i in range(devices)])  31.3 us
    ppermute x15, waiting for transfers between devices, swap(): return lax.ppermute(array, axis, [(i, partner(i)) for i in range(devices)])  10.5 us
    pallas_call x1, Pallas kernels, body(): pl.pallas_call(functools.partial(edge_kernel, ways, arrivals, four, block...  5.74 us
    pallas_call x1, Pallas kernels, body(): pl.pallas_call(functools.partial(prep_kernel, parts, arrivals), out_shape...  2.42 us
    pallas_call x1, Pallas kernels, body(): pl.pallas_call(functools.partial(edge_grad_kernel, block, arrivals, four)...  2.21 us
    pallas_call x1, Pallas kernels, body(): pl.pallas_call(functools.partial(node_grad_kernel, arrivals, four), out_s...  2.13 us
    pallas_call x1, Pallas kernels, body(): pl.pallas_call(functools.partial(pick_kernel, four, block), out_shape=(bl...  1.63 us
    pallas_call x1, Pallas kernels, body(): pl.pallas_call(functools.partial(rest_kernel, ways), out_shape=(sent_shap...  1.49 us
  transfers between devices with their start and end apart: 15, of which 6 were waited for; matrix products, arithmetic and copies ran while one was open for 0% of the time, Pallas kernels for 14%

profile of v9, /device:TPU:0, one launch (start us, length us, event | category | flops | bytes accessed | tf_op | source)
XLA Modules:
  0.0 60.2 jit_solution(12441270123944125526)
XLA Ops:
  0.6 1.6 %pick_blocks.1 = (bf16[64,512]{1,0:T(8,128)(2,1)S(1)}, bf16[64,512]{1,0:T(8,128)(2,1)S(1)}, bf16[64,512]{1,0:T(8,128)(2,1)S(1)}) custom-call(s32[1,4]{1,0:T(1,128)} %boundary_hbm.3, bf16[128,512]{1,0:T(8,128)(2,1)} %bitcast.9), custom_call_target="tpu_custom_call" | custom-call | bytes 400000 | tf_op jit(solution)/shard_map/pick_blocks/pallas_call | solution.py:561
  2.3 3.1 %collective-permute-start = (bf16[64,512]{1,0:T(8,128)(2,1)S(1)}, bf16[64,512]{1,0:T(8,128)(2,1)S(1)}, u32[]{:S(2)}, u32[]{:S(2)}) collective-permute-start(bf16[64,512]{1,0:T(8,128)(2,1)S(1)} %get-tuple-element.39), channel_id=1, source_target_pairs={{0,4},{4,0},{8,12},{12,8},{1,5},{5,1},{9,13},{13,9},{2,6},{6,2},{1... | collective-permute-start | bytes 196616 | tf_op jit(solution)/shard_map/ppermute | solution.py:455
  5.4 0.7 %collective-permute-start.1 = (bf16[64,512]{1,0:T(8,128)(2,1)S(1)}, bf16[64,512]{1,0:T(8,128)(2,1)S(1)}, u32[]{:S(2)}, u32[]{:S(2)}) collective-permute-start(bf16[64,512]{1,0:T(8,128)(2,1)S(1)} %get-tuple-element.40), channel_id=1, source_target_pairs={{0,0},{4,8},{8,4},{12,12},{1,1},{5,9},{9,5},{13,13},{2,2},{6,10},{... | collective-permute-start | bytes 196616 | tf_op jit(solution)/shard_map/ppermute | solution.py:455
  6.0 3.9 %collective-permute-start.2 = (bf16[64,512]{1,0:T(8,128)(2,1)S(1)}, bf16[64,512]{1,0:T(8,128)(2,1)S(1)}, u32[]{:S(2)}, u32[]{:S(2)}) collective-permute-start(bf16[64,512]{1,0:T(8,128)(2,1)S(1)} %get-tuple-element.41), channel_id=1, source_target_pairs={{0,8},{4,12},{8,0},{12,4},{1,9},{5,13},{9,1},{13,5},{2,10},{6,14},... | collective-permute-start | bytes 196616 | tf_op jit(solution)/shard_map/ppermute | solution.py:455
  10.6 2.4 %prepare.1 = (bf16[128,512]{1,0:T(8,128)(2,1)S(1)}, bf16[768,512]{1,0:T(8,128)(2,1)S(1)}, bf16[128,512]{1,0:T(8,128)(2,1)S(1)}, bf16[1536,512]{1,0:T(8,128)(2,1)...) custom-call(s32[1]{0:T(128)S(6)} %copy.15.count_ref, ...), custom_call_target="tpu_custom_call" | custom-call | flops 402653184 | bytes 8000000 | tf_op jit(solution)/shard_map/prepare/pallas_call | solution.py:583
  13.0 0.0 collective-permute-done.refs_0_
  13.0 0.0 collective-permute-done.1.refs_1_
  13.0 0.7 %collective-permute-done.2.refs_2_ = bf16[64,512]{1,0:T(8,128)(2,1)S(1)} collective-permute-done((bf16[64,512]{1,0:T(8,128)(2,1)S(1)}, bf16[64,512]{1,0:T(8,128)(2,1)S(1)}, u32[]{:S(2)}, u32[]{:S(2)}) %collective-permute-start.2) | collective-permute-done | bytes 65568 | tf_op jit(solution)/shard_map/ppermute | solution.py:455
  13.8 5.7 %edge_block.1 = (bf16[768,512]{1,0:T(8,128)(2,1)S(1)}, f32[768,512]{1,0:T(8,128)S(1)}, f32[512,512]{1,0:T(8,128)S(1)}, bf16[384,512]{1,0:T(8,128)(2,1)S(1)}, bf1...) custom-call(bf16[64,512]{1,0:T(8,128)(2,1)S(1)} %collective-permute-done.refs_0_, ...), custom_call_target="tpu_custom_call" | custom-call | flops 2415919104 | bytes 12000000 | tf_op jit(solution)/shard_map/edge_block/pallas_call | solution.py:624
  19.5 0.1 collective-permute-start.3
  19.6 1.5 %rest_weights.1 = (bf16[2,256,512]{2,1,0:T(8,128)(2,1)S(1)}, f32[2,256,512]{2,1,0:T(8,128)S(1)}) custom-call(bf16[128,512]{1,0:T(8,128)(2,1)S(1)} %get-tuple-element.42.refs_3_.node_ref, bf16[768,512]{1,0:T(8,128)(2,1)S(1)} %get-tuple-element.43.refs_4_.edge_ref, bf16[384,512]{1,0:T(8,128)(2,1)S(1)} %get-tuple-element.64.ext_ref, ...), custom_call_target="tpu_custom_call" | custom-call | flops 402653184 | bytes 4000000 | tf_op jit(solution)/shard_map/rest_weights/pallas_call | solution.py:653
  21.1 0.6 collective-permute-start.8
  21.7 0.1 over_first.1
  21.8 1.6 %collective-permute-start.4 = (bf16[1,256,512]{2,1,0:T(8,128)(2,1)S(1)}, bf16[1,256,512]{2,1,0:T(8,128)(2,1)S(1)}, u32[]{:S(2)}, u32[]{:S(2)}) collective-permute-start(bf16[1,256,512]{2,1,0:T(8,128)(2,1)S(1)} %get-tuple-element.53), channel_id=1, source_target_pairs={{0,2},{1,3},{2,0},{3,1},{4,6},{5,7},{6,4},{7,5},{8,10},{9,11},{10,... | collective-permute-start | bytes 786440 | tf_op jit(solution)/shard_map/ppermute | solution.py:455
  23.3 0.1 beside_first.1
  23.4 2.0 %collective-permute-start.9 = (bf16[320,512]{1,0:T(8,128)(2,1)S(1)}, bf16[320,512]{1,0:T(8,128)(2,1)S(1)}, u32[]{:S(2)}, u32[]{:S(2)}) collective-permute-start(bf16[320,512]{1,0:T(8,128)(2,1)S(1)} %get-tuple-element.67), channel_id=1, source_target_pairs={{0,4},{4,0},{8,12},{12,8},{1,5},{5,1},{9,13},{13,9},{2,6},{6,2},{1... | collective-permute-start | bytes 983048 | tf_op jit(solution)/shard_map/ppermute | solution.py:455
  25.4 0.7 %collective-permute-start.5 = (bf16[64,512]{1,0:T(8,128)(2,1)S(1)}, bf16[64,512]{1,0:T(8,128)(2,1)S(1)}, u32[]{:S(2)}, u32[]{:S(2)}) collective-permute-start(bf16[64,512]{1,0:T(8,128)(2,1)S(1)} %get-tuple-element.55), channel_id=1, source_target_pairs={{0,0},{4,8},{8,4},{12,12},{1,1},{5,9},{9,5},{13,13},{2,2},{6,10},{... | collective-permute-start | bytes 196616 | tf_op jit(solution)/shard_map/ppermute | solution.py:455
  26.1 3.3 %collective-permute-start.6 = (bf16[64,512]{1,0:T(8,128)(2,1)S(1)}, bf16[64,512]{1,0:T(8,128)(2,1)S(1)}, u32[]{:S(2)}, u32[]{:S(2)}) collective-permute-start(bf16[64,512]{1,0:T(8,128)(2,1)S(1)} %get-tuple-element.56), channel_id=1, source_target_pairs={{0,8},{4,12},{8,0},{12,4},{1,9},{5,13},{9,1},{13,5},{2,10},{6,14},... | collective-permute-start | bytes 196616 | tf_op jit(solution)/shard_map/ppermute | solution.py:455
  29.4 4.8 %collective-permute-done.6.refs_1_.refs_2_ = bf16[64,512]{1,0:T(8,128)(2,1)S(1)} collective-permute-done((bf16[64,512]{1,0:T(8,128)(2,1)S(1)}, bf16[64,512]{1,0:T(8,128)(2,1)S(1)}, u32[]{:S(2)}, u32[]{:S(2)}) %collective-permute-start.6) | collective-permute-done | bytes 65568 | tf_op jit(solution)/shard_map/ppermute | solution.py:455
  34.2 2.8 %collective-permute-start.7 = (bf16[128,512]{1,0:T(8,128)(2,1)S(1)}, bf16[128,512]{1,0:T(8,128)(2,1)S(1)}, u32[]{:S(2)}, u32[]{:S(2)}) collective-permute-start(bf16[128,512]{1,0:T(8,128)(2,1)S(1)} %get-tuple-element.58), channel_id=1, source_target_pairs={{0,4},{4,0},{8,12},{12,8},{1,5},{5,1},{9,13},{13,9},{2,6},{6,2},{1... | collective-permute-start | bytes 393224 | tf_op jit(solution)/shard_map/ppermute | solution.py:455
  37.1 1.5 %collective-permute-start.10 = (bf16[128,512]{1,0:T(8,128)(2,1)S(1)}, bf16[128,512]{1,0:T(8,128)(2,1)S(1)}, u32[]{:S(2)}, u32[]{:S(2)}) collective-permute-start(bf16[128,512]{1,0:T(8,128)(2,1)S(1)} %get-tuple-element.70), channel_id=1, source_target_pairs={{0,2},{1,3},{2,0},{3,1},{4,6},{5,7},{6,4},{7,5},{8,10},{9,11},{10,... | collective-permute-start | bytes 393224 | tf_op jit(solution)/shard_map/ppermute | solution.py:455
  38.6 1.8 %collective-permute-done.7.came_ref = bf16[128,512]{1,0:T(8,128)(2,1)S(1)} collective-permute-done((bf16[128,512]{1,0:T(8,128)(2,1)S(1)}, bf16[128,512]{1,0:T(8,128)(2,1)S(1)}, u32[]{:S(2)}, u32[]{:S(2)}) %collective-permute-start.7) | collective-permute-done | bytes 131104 | tf_op jit(solution)/shard_map/ppermute | solution.py:455
  40.5 1.7 %collective-permute-start.11 = (bf16[128,512]{1,0:T(8,128)(2,1)S(1)}, bf16[128,512]{1,0:T(8,128)(2,1)S(1)}, u32[]{:S(2)}, u32[]{:S(2)}) collective-permute-start(bf16[128,512]{1,0:T(8,128)(2,1)S(1)} %add_terms.2.after), channel_id=1, source_target_pairs={{0,12},{4,8},{8,4},{12,0},{1,13},{5,9},{9,5},{13,1},{2,14},{6,10},... | collective-permute-start | bytes 393224 | tf_op jit(solution)/shard_map/ppermute | solution.py:455
  42.2 2.2 %edge_grads.1 = (bf16[768,512]{1,0:T(8,128)(2,1)}, bf16[128,512]{1,0:T(8,128)(2,1)}) custom-call(s32[12]{0:T(128)} %dst_hbm.3, s32[1]{0:T(128)S(6)} %copy.15.count_ref, bf16[128,512]{1,0:T(8,128)(2,1)S(1)} %add_terms.2.after, bf16[768,512]{1,0:T(8,128)(2,1)S(1)} %get-tuple-element.59.gpre_ref, f32[512,512]{1,0:T(8,128)S(1)} %get-tuple-element.52.sums_ref, ...), custom_call_target="tpu_custom_call" | custom-call | flops 402653184 | bytes 3000000 | tf_op jit(solution)/shard_map/edge_grads/pallas_call | solution.py:709
  44.4 2.3 %collective-permute-start.13 = (bf16[128,512]{1,0:T(8,128)(2,1)S(1)}, bf16[128,512]{1,0:T(8,128)(2,1)S(1)}, u32[]{:S(2)}, u32[]{:S(2)}) collective-permute-start(bf16[128,512]{1,0:T(8,128)(2,1)S(1)} %add_terms.3.after), channel_id=1, source_target_pairs={{0,12},{4,8},{8,4},{12,0},{1,13},{5,9},{9,5},{13,1},{2,14},{6,10},... | collective-permute-start | bytes 393224 | tf_op jit(solution)/shard_map/ppermute | solution.py:455
  46.7 1.2 %collective-permute-done.11 = bf16[128,512]{1,0:T(8,128)(2,1)S(1)} collective-permute-done((bf16[128,512]{1,0:T(8,128)(2,1)S(1)}, bf16[128,512]{1,0:T(8,128)(2,1)S(1)}, u32[]{:S(2)}, u32[]{:S(2)}) %collective-permute-start.11) | collective-permute-done | bytes 131104 | tf_op jit(solution)/shard_map/ppermute | solution.py:455
  47.9 5.5 %collective-permute-start.12 = (bf16[128,512]{1,0:T(8,128)(2,1)S(1)}, bf16[128,512]{1,0:T(8,128)(2,1)S(1)}, u32[]{:S(2)}, u32[]{:S(2)}) collective-permute-start(bf16[128,512]{1,0:T(8,128)(2,1)S(1)} %add_convert_fusion.1.own_a), channel_id=1, source_target_pairs={{0,4},{4,0},{8,12},{12,8},{1,5},{5,1},{9,13},{13,9},{2,6},{6,2},{1... | collective-permute-start | bytes 393224 | tf_op jit(solution)/shard_map/ppermute | solution.py:455
  53.5 1.7 %collective-permute-start.14 = (bf16[128,512]{1,0:T(8,128)(2,1)S(1)}, bf16[128,512]{1,0:T(8,128)(2,1)S(1)}, u32[]{:S(2)}, u32[]{:S(2)}) collective-permute-start(bf16[128,512]{1,0:T(8,128)(2,1)S(1)} %add_convert_fusion.own_b), channel_id=1, source_target_pairs={{0,4},{4,0},{8,12},{12,8},{1,5},{5,1},{9,13},{13,9},{2,6},{6,2},{1... | collective-permute-start | bytes 393224 | tf_op jit(solution)/shard_map/ppermute | solution.py:455
  55.1 2.1 %node_grads.1.after = bf16[128,512]{1,0:T(8,128)(2,1)} custom-call(s32[1,4]{1,0:T(1,128)} %boundary_hbm.3, bf16[128,512]{1,0:T(8,128)(2,1)S(1)} %add_terms.3.after, f32[512,512]{1,0:T(8,128)S(1)} %get-tuple-element.52.sums_ref, bf16[1536,512]{1,0:T(8,128)(2,1)S(1)} %get-tuple-element.44.refs_5_.win_ref, ...), custom_call_target="tpu_custom_call" | custom-call | flops 268435456 | bytes 2000000 | tf_op jit(solution)/shard_map/node_grads/pallas_call | solution.py:741
  57.3 0.5 collective-permute-done.12.other_a
  57.7 1.4 %collective-permute-done.14.other_b = bf16[128,512]{1,0:T(8,128)(2,1)S(1)} collective-permute-done((bf16[128,512]{1,0:T(8,128)(2,1)S(1)}, bf16[128,512]{1,0:T(8,128)(2,1)S(1)}, u32[]{:S(2)}, u32[]{:S(2)}) %collective-permute-start.14) | collective-permute-done | bytes 131104 | tf_op jit(solution)/shard_map/ppermute | solution.py:455
  59.2 1.0 %widen.1 = (f32[384,512]{1,0:T(8,128)}, f32[128,512]{1,0:T(8,128)}) custom-call(bf16[128,512]{1,0:T(8,128)(2,1)} %node_grads.1.after, bf16[128,512]{1,0:T(8,128)(2,1)S(1)} %add_convert_fusion.1.own_a, bf16[128,512]{1,0:T(8,128)(2,1)S(1)} %collective-permute-done.12.other_a, bf16[128,512]{1,0:T(8,128)(2,1)S(1)} %add_convert_fusion.own_b, ...), custom_call_target="tpu_custom_call" | custom-call | bytes 1500000 | tf_op jit(solution)/shard_map/widen/pallas_call | solution.py:758
  (13 shorter events, 0.2 us)
Async XLA Ops:
  2.3 10.7 %collective-permute-start = (bf16[64,512]{1,0:T(8,128)(2,1)S(1)}, bf16[64,512]{1,0:T(8,128)(2,1)S(1)}, u32[]{:S(2)}, u32[]{:S(2)}) collective-permute-start(bf16[64,512]{1,0:T(8,128)(2,1)S(1)} %get-tuple-element.39), channel_id=1, source_target_pairs={{0,4},{4,0},{8,12},{12,8},{1,5},{5,1},{9,13},{13,9},{2,6},{6,2},{1... | collective-permute-start | bytes 196616 | tf_op jit(solution)/shard_map/ppermute | solution.py:455
  5.4 7.7 %collective-permute-start.1 = (bf16[64,512]{1,0:T(8,128)(2,1)S(1)}, bf16[64,512]{1,0:T(8,128)(2,1)S(1)}, u32[]{:S(2)}, u32[]{:S(2)}) collective-permute-start(bf16[64,512]{1,0:T(8,128)(2,1)S(1)} %get-tuple-element.40), channel_id=1, source_target_pairs={{0,0},{4,8},{8,4},{12,12},{1,1},{5,9},{9,5},{13,13},{2,2},{6,10},{... | collective-permute-start | bytes 196616 | tf_op jit(solution)/shard_map/ppermute | solution.py:455
  6.0 7.7 %collective-permute-start.2 = (bf16[64,512]{1,0:T(8,128)(2,1)S(1)}, bf16[64,512]{1,0:T(8,128)(2,1)S(1)}, u32[]{:S(2)}, u32[]{:S(2)}) collective-permute-start(bf16[64,512]{1,0:T(8,128)(2,1)S(1)} %get-tuple-element.41), channel_id=1, source_target_pairs={{0,8},{4,12},{8,0},{12,4},{1,9},{5,13},{9,1},{13,5},{2,10},{6,14},... | collective-permute-start | bytes 196616 | tf_op jit(solution)/shard_map/ppermute | solution.py:455
  19.5 2.2 %collective-permute-start.3 = (bf16[2,256,512]{2,1,0:T(8,128)(2,1)S(1)}, bf16[2,256,512]{2,1,0:T(8,128)(2,1)S(1)}, u32[]{:S(2)}, u32[]{:S(2)}) collective-permute-start(bf16[2,256,512]{2,1,0:T(8,128)(2,1)S(1)} %get-tuple-element.50), channel_id=1, source_target_pairs={{0,1},{1,0},{2,3},{3,2},{4,5},{5,4},{6,7},{7,6},{8,9},{9,8},{10,11... | collective-permute-start | bytes 1572872 | tf_op jit(solution)/shard_map/ppermute | solution.py:455
  21.1 2.3 %collective-permute-start.8 = (bf16[2,256,512]{2,1,0:T(8,128)(2,1)S(1)}, bf16[2,256,512]{2,1,0:T(8,128)(2,1)S(1)}, u32[]{:S(2)}, u32[]{:S(2)}) collective-permute-start(bf16[2,256,512]{2,1,0:T(8,128)(2,1)S(1)} %get-tuple-element.65), channel_id=1, source_target_pairs={{0,1},{1,0},{2,3},{3,2},{4,5},{5,4},{6,7},{7,6},{8,9},{9,8},{10,11... | collective-permute-start | bytes 1572872 | tf_op jit(solution)/shard_map/ppermute | solution.py:455
  21.8 12.4 %collective-permute-start.4 = (bf16[1,256,512]{2,1,0:T(8,128)(2,1)S(1)}, bf16[1,256,512]{2,1,0:T(8,128)(2,1)S(1)}, u32[]{:S(2)}, u32[]{:S(2)}) collective-permute-start(bf16[1,256,512]{2,1,0:T(8,128)(2,1)S(1)} %get-tuple-element.53), channel_id=1, source_target_pairs={{0,2},{1,3},{2,0},{3,1},{4,6},{5,7},{6,4},{7,5},{8,10},{9,11},{10,... | collective-permute-start | bytes 786440 | tf_op jit(solution)/shard_map/ppermute | solution.py:455
  23.4 13.6 %collective-permute-start.9 = (bf16[320,512]{1,0:T(8,128)(2,1)S(1)}, bf16[320,512]{1,0:T(8,128)(2,1)S(1)}, u32[]{:S(2)}, u32[]{:S(2)}) collective-permute-start(bf16[320,512]{1,0:T(8,128)(2,1)S(1)} %get-tuple-element.67), channel_id=1, source_target_pairs={{0,4},{4,0},{8,12},{12,8},{1,5},{5,1},{9,13},{13,9},{2,6},{6,2},{1... | collective-permute-start | bytes 983048 | tf_op jit(solution)/shard_map/ppermute | solution.py:455
  25.4 4.0 %collective-permute-start.5 = (bf16[64,512]{1,0:T(8,128)(2,1)S(1)}, bf16[64,512]{1,0:T(8,128)(2,1)S(1)}, u32[]{:S(2)}, u32[]{:S(2)}) collective-permute-start(bf16[64,512]{1,0:T(8,128)(2,1)S(1)} %get-tuple-element.55), channel_id=1, source_target_pairs={{0,0},{4,8},{8,4},{12,12},{1,1},{5,9},{9,5},{13,13},{2,2},{6,10},{... | collective-permute-start | bytes 196616 | tf_op jit(solution)/shard_map/ppermute | solution.py:455
  26.1 8.1 %collective-permute-start.6 = (bf16[64,512]{1,0:T(8,128)(2,1)S(1)}, bf16[64,512]{1,0:T(8,128)(2,1)S(1)}, u32[]{:S(2)}, u32[]{:S(2)}) collective-permute-start(bf16[64,512]{1,0:T(8,128)(2,1)S(1)} %get-tuple-element.56), channel_id=1, source_target_pairs={{0,8},{4,12},{8,0},{12,4},{1,9},{5,13},{9,1},{13,5},{2,10},{6,14},... | collective-permute-start | bytes 196616 | tf_op jit(solution)/shard_map/ppermute | solution.py:455
  34.2 6.3 %collective-permute-start.7 = (bf16[128,512]{1,0:T(8,128)(2,1)S(1)}, bf16[128,512]{1,0:T(8,128)(2,1)S(1)}, u32[]{:S(2)}, u32[]{:S(2)}) collective-permute-start(bf16[128,512]{1,0:T(8,128)(2,1)S(1)} %get-tuple-element.58), channel_id=1, source_target_pairs={{0,4},{4,0},{8,12},{12,8},{1,5},{5,1},{9,13},{13,9},{2,6},{6,2},{1... | collective-permute-start | bytes 393224 | tf_op jit(solution)/shard_map/ppermute | solution.py:455
  37.1 7.3 %collective-permute-start.10 = (bf16[128,512]{1,0:T(8,128)(2,1)S(1)}, bf16[128,512]{1,0:T(8,128)(2,1)S(1)}, u32[]{:S(2)}, u32[]{:S(2)}) collective-permute-start(bf16[128,512]{1,0:T(8,128)(2,1)S(1)} %get-tuple-element.70), channel_id=1, source_target_pairs={{0,2},{1,3},{2,0},{3,1},{4,6},{5,7},{6,4},{7,5},{8,10},{9,11},{10,... | collective-permute-start | bytes 393224 | tf_op jit(solution)/shard_map/ppermute | solution.py:455
  40.5 7.4 %collective-permute-start.11 = (bf16[128,512]{1,0:T(8,128)(2,1)S(1)}, bf16[128,512]{1,0:T(8,128)(2,1)S(1)}, u32[]{:S(2)}, u32[]{:S(2)}) collective-permute-start(bf16[128,512]{1,0:T(8,128)(2,1)S(1)} %add_terms.2.after), channel_id=1, source_target_pairs={{0,12},{4,8},{8,4},{12,0},{1,13},{5,9},{9,5},{13,1},{2,14},{6,10},... | collective-permute-start | bytes 393224 | tf_op jit(solution)/shard_map/ppermute | solution.py:455
  44.4 9.0 %collective-permute-start.13 = (bf16[128,512]{1,0:T(8,128)(2,1)S(1)}, bf16[128,512]{1,0:T(8,128)(2,1)S(1)}, u32[]{:S(2)}, u32[]{:S(2)}) collective-permute-start(bf16[128,512]{1,0:T(8,128)(2,1)S(1)} %add_terms.3.after), channel_id=1, source_target_pairs={{0,12},{4,8},{8,4},{12,0},{1,13},{5,9},{9,5},{13,1},{2,14},{6,10},... | collective-permute-start | bytes 393224 | tf_op jit(solution)/shard_map/ppermute | solution.py:455
  47.9 9.8 %collective-permute-start.12 = (bf16[128,512]{1,0:T(8,128)(2,1)S(1)}, bf16[128,512]{1,0:T(8,128)(2,1)S(1)}, u32[]{:S(2)}, u32[]{:S(2)}) collective-permute-start(bf16[128,512]{1,0:T(8,128)(2,1)S(1)} %add_convert_fusion.1.own_a), channel_id=1, source_target_pairs={{0,4},{4,0},{8,12},{12,8},{1,5},{5,1},{9,13},{13,9},{2,6},{6,2},{1... | collective-permute-start | bytes 393224 | tf_op jit(solution)/shard_map/ppermute | solution.py:455
  53.5 5.7 %collective-permute-start.14 = (bf16[128,512]{1,0:T(8,128)(2,1)S(1)}, bf16[128,512]{1,0:T(8,128)(2,1)S(1)}, u32[]{:S(2)}, u32[]{:S(2)}) collective-permute-start(bf16[128,512]{1,0:T(8,128)(2,1)S(1)} %add_convert_fusion.own_b), channel_id=1, source_target_pairs={{0,4},{4,0},{8,12},{12,8},{1,5},{5,1},{9,13},{13,9},{2,6},{6,2},{1... | collective-permute-start | bytes 393224 | tf_op jit(solution)/shard_map/ppermute | solution.py:455

commit v10 on v9

--- a/solution.py
+++ b/solution.py
@@ -65,15 +65,14 @@
 def pick_kernel(four, block, boundary_hbm, node_hbm, *refs):
     count = 3 if four else 4
     outs = refs[:count]
-    boundary_ref, small_sem, sems = refs[count:]
-    load_small(boundary_hbm, boundary_ref, small_sem).wait()
-    copies = []
-    for which, place in enumerate(boundary_places(boundary_ref, lax.axis_index("dom"), four)):
-        spot = pl.ds(pl.multiple_of(place * block, block), block)
-        copies.append(pltpu.make_async_copy(node_hbm.at[spot, :], outs[which], sems.at[which]))
-        copies[-1].start()
-    for copy in copies:
-        copy.wait()
+    boundary_ref, node_ref, sems = refs[count:]
+    small = load_small(boundary_hbm, boundary_ref, sems.at[0])
+    large = load_small(node_hbm, node_ref, sems.at[1])
+    small.wait()
+    places = boundary_places(boundary_ref, lax.axis_index("dom"), four)
+    large.wait()
+    for place, out in zip(places, outs):
+        out[...] = rows_of(node_ref, place, block)
 
 
 def prep_kernel(
@@ -220,7 +219,7 @@
 
 
 def edge_kernel(ways, arrivals, four, block, *refs):
-    arrived = refs[:arrivals]
+    arrived = refs[:arrivals][::-1]
     (
         node_ref,
         edge_ref,
@@ -364,12 +363,6 @@
     return sums_ref[pl.ds(pl.multiple_of(nodes + place * block, block), block), :].astype(BF16)
 
 
-def over_first_kernel(nodes, block, came_ref, kept_ref, sums_ref, away_ref, left_ref, *back_refs):
-    halve_kernel(2, came_ref, kept_ref, None, away_ref, left_ref)
-    for which, back_ref in enumerate(back_refs):
-        back_ref[...] = back_block(nodes, block, sums_ref, 1 + which)
-
-
 def beside_first_kernel(nodes, block, came_ref, kept_ref, sums_ref, away_ref, left_ref):
     rows = left_ref.shape[1]
     here, there = half_rows(rows)
@@ -388,8 +381,9 @@
     left_ref[...] = kept_ref[0, here, :] + came_ref[0, here, :].astype(F32)
 
 
-def over_second_kernel(came_ref, kept_ref, *refs):
-    away_ref, left_ref = refs[-2:]
+def over_second_kernel(
+    nodes, block, came_ref, kept_ref, sums_ref, away_ref, left_ref, near_ref, far_ref
+):
     mine = lax.axis_index("dp") // 2
     rows = left_ref.shape[0]
 
@@ -399,11 +393,15 @@
 
     away_ref[...] = (kept_ref[1 - mine] + came(1 - mine)).astype(BF16)
     left_ref[...] = kept_ref[mine] + came(mine)
-
-
-def add_kernel(left_ref, came_ref, *refs):
+    near_ref[...] = back_block(nodes, block, sums_ref, 1)
+    far_ref[...] = back_block(nodes, block, sums_ref, 2)
+
+
+def add_kernel(left_a, came_a, left_b, came_b, *refs):
     out_ref = refs[-1]
-    out_ref[...] = (left_ref[...] + came_ref[...].astype(F32)).astype(BF16)
+    rows = left_a.shape[0]
+    out_ref[:rows, :] = (left_a[...] + came_a[...].astype(F32)).astype(BF16)
+    out_ref[rows:, :] = (left_b[...] + came_b[...].astype(F32)).astype(BF16)
 
 
 def node_grad_kernel(arrivals, four, boundary_hbm, after, sums_ref, win_ref, *refs):
@@ -430,24 +428,24 @@
     ).astype(BF16)
 
 
-def last_kernel(after, own_a, other_a, own_b, other_b, in_ref, out_ref):
+def last_kernel(node_out, edge_grad, own_ref, other_ref, in_ref, out_ref):
     unit = out_ref.shape[0]
     part = lax.axis_index("dom")
     inner = (part == 1) | (part == 2)
 
-    def write(low_a, high_a, low_b, high_b):
-        out_ref[...] = low_a[...].astype(F32)
-        in_ref[:unit, :] = high_a[...].astype(F32)
-        in_ref[unit : 2 * unit, :] = low_b[...].astype(F32)
-        in_ref[2 * unit :, :] = high_b[...].astype(F32)
+    def write(low, high):
+        out_ref[...] = low[:unit, :].astype(F32)
+        in_ref[:unit, :] = high[:unit, :].astype(F32)
+        in_ref[unit : 2 * unit, :] = low[unit:, :].astype(F32)
+        in_ref[2 * unit :, :] = high[unit:, :].astype(F32)
 
     @pl.when(inner)
     def _():
-        write(own_a, other_a, own_b, other_b)
+        write(own_ref, other_ref)
 
     @pl.when(jnp.logical_not(inner))
     def _():
-        write(other_a, own_a, other_b, own_b)
+        write(other_ref, own_ref)
 
 
 def swap(array, axis, partner):
@@ -565,8 +563,8 @@
         out_specs=(VMEM,) * arrivals,
         scratch_shapes=[
             pltpu.SMEM(boundary.shape, jnp.int32),
-            pltpu.SemaphoreType.DMA,
-            pltpu.SemaphoreType.DMA((arrivals,)),
+            pltpu.VMEM((nodes, latent), BF16),
+            pltpu.SemaphoreType.DMA((2,)),
         ],
         compiler_params=small,
         cost_estimate=pl.CostEstimate(flops=0, bytes_accessed=400_000, transcendentals=0),
@@ -647,7 +645,7 @@
     )(
         *[
             in_vmem(array)
-            for array in (*came, node_v, edge_v, win_v, wout_v, pre, up, hot, turned)
+            for array in (*came[::-1], node_v, edge_v, win_v, wout_v, pre, up, hot, turned)
         ],
     )
     away_b, kept_b = pl.pallas_call(
@@ -665,19 +663,7 @@
         rows = 2 * unit
         piece, wide = pltpu.VMEM((unit, latent), BF16), pltpu.VMEM((unit, latent), F32)
         came_a = swap(away_a, "dp", lambda i: i ^ 1)
-        away_a, kept_a, near, far = small_call(
-            functools.partial(over_first_kernel, nodes, block),
-            "over_first",
-            (
-                pltpu.VMEM((1, rows, latent), BF16),
-                pltpu.VMEM((1, rows, latent), F32),
-                block_shape,
-                block_shape,
-            ),
-            came_a,
-            kept_a,
-            sums,
-        )
+        away_a, kept_a = halve(2, came_a, kept_a, cot_v)
         came_a = swap(away_a, "dp", lambda i: i ^ 2)
         came_b = swap(away_b, "dp", lambda i: i ^ 1)
         away_b, kept_b = small_call(
@@ -689,19 +675,34 @@
             sums,
         )
         beside = swap(away_b, "dom", lambda i: i ^ 1)
+        away_a, kept_a = small_call(
+            beside_second_kernel, "beside_second", (piece, wide), came_a, kept_a
+        )
+        came_a = swap(away_a, "dom", lambda i: i ^ 1)
+        away_b, kept_b, near, far = small_call(
+            functools.partial(over_second_kernel, nodes, block),
+            "over_second",
+            (piece, wide, block_shape, block_shape),
+            beside,
+            kept_b,
+            sums,
+        )
+        came_b = swap(away_b, "dp", lambda i: i ^ 2)
         far = swap(far, "dom", lambda i: partners_of_four(2)[i])
         near = swap(near, "dom", lambda i: partners_of_four(1)[i])
-        away_a, kept_a = small_call(
-            beside_second_kernel, "beside_second", (piece, wide), came_a, kept_a, near, far
+        pair = small_call(
+            add_kernel,
+            "add_terms",
+            pltpu.VMEM((rows, latent), BF16),
+            kept_a,
+            came_a,
+            kept_b,
+            came_b,
+            near,
+            far,
         )
-        came_a = swap(away_a, "dom", lambda i: i ^ 1)
-        away_b, kept_b = small_call(
-            over_second_kernel, "over_second", (piece, wide), beside, kept_b
-        )
-        came_b = swap(away_b, "dp", lambda i: i ^ 2)
-        pair_a = small_call(add_kernel, "add_terms", piece, kept_a, came_a)
         returned = [beside, near, far]
-        late, backs = pair_a, 0
+        late, backs = pair, 0
     else:
         came_a, kept_a, late = sum_over_dp(away_a, kept_a, cot_v)
         came_b, kept_b, _ = sum_over_dp(away_b, kept_b, cot_v)
@@ -730,11 +731,7 @@
         tile_count,
         *[in_vmem(array) for array in (late, grad_pre, sums, cot_v, win_v, edge_v, message)],
     )
-    if four:
-        pair_b = small_call(add_kernel, "add_terms", piece, kept_b, came_b, after=(edge_grad,))
-        later = pair_b
-    else:
-        later = late
+    if not four:
         returned = [
             from_behind(back_sums[which], "dom", -OFFSET_LIST[which]) for which in range(4)
         ]
@@ -753,7 +750,7 @@
             flops=8 * nodes * latent * latent, bytes_accessed=2_000_000, transcendentals=0
         ),
         name="node_grads",
-    )(boundary, *[in_vmem(array) for array in (later, sums, win_v, *returned)])
+    )(boundary, *[in_vmem(array) for array in (late, sums, win_v, *returned)])
     if four:
         w_in_grad, w_out_grad = pl.pallas_call(
             last_kernel,
@@ -761,12 +758,12 @@
                 jax.ShapeDtypeStruct((3 * unit, latent), F32),
                 jax.ShapeDtypeStruct((unit, latent), F32),
             ),
-            in_specs=[HBM] + [VMEM] * 4,
+            in_specs=[HBM] * 2 + [VMEM] * 2,
             out_specs=(VMEM,) * 2,
             compiler_params=small,
             cost_estimate=pl.CostEstimate(flops=0, bytes_accessed=1_500_000, transcendentals=0),
             name="widen",
-        )(in_hbm(node_out), *with_other_half(sum_of_four(pair_a)), *with_other_half(sum_of_four(pair_b)))
+        )(in_hbm(node_out), in_hbm(edge_grad), *with_other_half(sum_of_four(pair)))
     else:
         sum_a = sum_over_dom(kept_a[0] + came_a[0].astype(F32))
         sum_b = sum_over_dom(kept_b[0] + came_b[0].astype(F32))

time: 60.4 us -> 62 us (1.026)
  waiting for transfers between devices: 10.5 us -> 17.7 us
  starting transfers between devices: 31.3 us -> 26.3 us
  Pallas kernels: 17 us -> 16.3 us
    ppermute x15 -> x13, waiting for transfers between devices: 10.5 us -> 17.7 us  [swap(): return lax.ppermute(array, axis, [(i, partner(i)) for i in range(devices)])]
    ppermute x15 -> x13, starting transfers between devices: 31.3 us -> 26.3 us  [swap(): return lax.ppermute(array, axis, [(i, partner(i)) for i in range(devices)])]
    pallas_call x1, Pallas kernels: 1.63 us -> 0.94 us  [body(): pl.pallas_call(functools.partial(pick_kernel, four, block), out_shape=(bl...]
  transfers between devices with their start and end apart: 15 -> 13, of which waited for: 6 -> 5; matrix products, arithmetic and copies ran while one was open for 0% -> 0% of each run, Pallas kernels for 14% -> 11%
where the time goes in v10:
time: 62 us; the launch traced here: 61.8 us
  starting transfers between devices  26.3 us (42%)
  waiting for transfers between devices  17.7 us (29%)
  Pallas kernels  16.3 us (26%)
  between operations  1.41 us (2%)
    ppermute x13, starting transfers between devices, swap(): return lax.ppermute(array, axis, [(i, partner(i)) for i in range(devices)])  26.3 us
    ppermute x13, waiting for transfers between devices, swap(): return lax.ppermute(array, axis, [(i, partner(i)) for i in range(devices)])  17.7 us
    pallas_call x1, Pallas kernels, body(): pl.pallas_call(functools.partial(edge_kernel, ways, arrivals, four, block...  5.76 us
    pallas_call x1, Pallas kernels, body(): pl.pallas_call(functools.partial(prep_kernel, parts, arrivals), out_shape...  2.42 us
    pallas_call x1, Pallas kernels, body(): pl.pallas_call(functools.partial(edge_grad_kernel, block, arrivals, four)...  2.21 us
    pallas_call x1, Pallas kernels, body(): pl.pallas_call(functools.partial(node_grad_kernel, arrivals, four), out_s...  2.14 us
    pallas_call x1, Pallas kernels, body(): pl.pallas_call(functools.partial(rest_kernel, ways), out_shape=(sent_shap...  1.49 us
  transfers between devices with their start and end apart: 13, of which 5 were waited for; matrix products, arithmetic and copies ran while one was open for 0% of the time, Pallas kernels for 11%

profile of v10, /device:TPU:0, one launch (start us, length us, event | category | flops | bytes accessed | tf_op | source)
XLA Modules:
  0.0 61.8 jit_solution(4501033933507535128)
XLA Ops:
  0.6 0.9 %pick_blocks.1 = (bf16[64,512]{1,0:T(8,128)(2,1)S(1)}, bf16[64,512]{1,0:T(8,128)(2,1)S(1)}, bf16[64,512]{1,0:T(8,128)(2,1)S(1)}) custom-call(s32[1,4]{1,0:T(1,128)} %boundary_hbm.3, bf16[128,512]{1,0:T(8,128)(2,1)} %bitcast.8), custom_call_target="tpu_custom_call" | custom-call | bytes 400000 | tf_op jit(solution)/shard_map/pick_blocks/pallas_call | solution.py:559
  1.6 4.1 %collective-permute-start = (bf16[64,512]{1,0:T(8,128)(2,1)S(1)}, bf16[64,512]{1,0:T(8,128)(2,1)S(1)}, u32[]{:S(2)}, u32[]{:S(2)}) collective-permute-start(bf16[64,512]{1,0:T(8,128)(2,1)S(1)} %get-tuple-element.39), channel_id=1, source_target_pairs={{0,8},{4,12},{8,0},{12,4},{1,9},{5,13},{9,1},{13,5},{2,10},{6,14},... | collective-permute-start | bytes 196616 | tf_op jit(solution)/shard_map/ppermute | solution.py:453
  5.7 0.7 %collective-permute-start.1 = (bf16[64,512]{1,0:T(8,128)(2,1)S(1)}, bf16[64,512]{1,0:T(8,128)(2,1)S(1)}, u32[]{:S(2)}, u32[]{:S(2)}) collective-permute-start(bf16[64,512]{1,0:T(8,128)(2,1)S(1)} %get-tuple-element.40), channel_id=1, source_target_pairs={{0,0},{4,8},{8,4},{12,12},{1,1},{5,9},{9,5},{13,13},{2,2},{6,10},{... | collective-permute-start | bytes 196616 | tf_op jit(solution)/shard_map/ppermute | solution.py:453
  6.3 2.9 %collective-permute-start.2 = (bf16[64,512]{1,0:T(8,128)(2,1)S(1)}, bf16[64,512]{1,0:T(8,128)(2,1)S(1)}, u32[]{:S(2)}, u32[]{:S(2)}) collective-permute-start(bf16[64,512]{1,0:T(8,128)(2,1)S(1)} %get-tuple-element.41), channel_id=1, source_target_pairs={{0,4},{4,0},{8,12},{12,8},{1,5},{5,1},{9,13},{13,9},{2,6},{6,2},{1... | collective-permute-start | bytes 196616 | tf_op jit(solution)/shard_map/ppermute | solution.py:453
  9.9 2.4 %prepare.1 = (bf16[128,512]{1,0:T(8,128)(2,1)S(1)}, bf16[768,512]{1,0:T(8,128)(2,1)S(1)}, bf16[128,512]{1,0:T(8,128)(2,1)S(1)}, bf16[1536,512]{1,0:T(8,128)(2,1)...) custom-call(s32[1]{0:T(128)S(6)} %copy.15.count_ref, ...), custom_call_target="tpu_custom_call" | custom-call | flops 402653184 | bytes 8000000 | tf_op jit(solution)/shard_map/prepare/pallas_call | solution.py:581
  12.3 0.0 collective-permute-done.1.refs_1_
  12.3 0.0 collective-permute-done.2.refs_2_
  12.3 5.8 %edge_block.1 = (bf16[768,512]{1,0:T(8,128)(2,1)S(1)}, f32[768,512]{1,0:T(8,128)S(1)}, f32[512,512]{1,0:T(8,128)S(1)}, bf16[384,512]{1,0:T(8,128)(2,1)S(1)}, bf1...) custom-call(bf16[64,512]{1,0:T(8,128)(2,1)S(1)} %collective-permute-done.refs_0_, ...), custom_call_target="tpu_custom_call" | custom-call | flops 2415919104 | bytes 12000000 | tf_op jit(solution)/shard_map/edge_block/pallas_call | solution.py:622
  18.1 1.5 %rest_weights.1 = (bf16[2,256,512]{2,1,0:T(8,128)(2,1)S(1)}, f32[2,256,512]{2,1,0:T(8,128)S(1)}) custom-call(bf16[128,512]{1,0:T(8,128)(2,1)S(1)} %get-tuple-element.42.refs_3_.node_ref, bf16[768,512]{1,0:T(8,128)(2,1)S(1)} %get-tuple-element.43.refs_4_.edge_ref, bf16[384,512]{1,0:T(8,128)(2,1)S(1)} %get-tuple-element.57.ext_ref, ...), custom_call_target="tpu_custom_call" | custom-call | flops 402653184 | bytes 4000000 | tf_op jit(solution)/shard_map/rest_weights/pallas_call | solution.py:651
  19.6 0.1 collective-permute-start.6
  19.7 0.5 collective-permute-start.3
  20.2 1.4 %collective-permute-done.6.came_ref = bf16[2,256,512]{2,1,0:T(8,128)(2,1)S(1)} collective-permute-done((bf16[2,256,512]{2,1,0:T(8,128)(2,1)S(1)}, bf16[2,256,512]{2,1,0:T(8,128)(2,1)S(1)}, u32[]{:S(2)}, u32[]{:S(2)}) %collective-permute-start.6) | collective-permute-done | bytes 524320 | tf_op jit(solution)/shard_map/ppermute | solution.py:453
  21.6 0.1 beside_first.1
  21.7 1.2 %collective-permute-start.7 = (bf16[320,512]{1,0:T(8,128)(2,1)S(1)}, bf16[320,512]{1,0:T(8,128)(2,1)S(1)}, u32[]{:S(2)}, u32[]{:S(2)}) collective-permute-start(bf16[320,512]{1,0:T(8,128)(2,1)S(1)} %get-tuple-element.62), channel_id=1, source_target_pairs={{0,4},{4,0},{8,12},{12,8},{1,5},{5,1},{9,13},{13,9},{2,6},{6,2},{1... | collective-permute-start | bytes 983048 | tf_op jit(solution)/shard_map/ppermute | solution.py:453
  22.9 0.1 halve.1
  23.0 1.6 %collective-permute-start.4 = (bf16[1,256,512]{2,1,0:T(8,128)(2,1)S(1)}, bf16[1,256,512]{2,1,0:T(8,128)(2,1)S(1)}, u32[]{:S(2)}, u32[]{:S(2)}) collective-permute-start(bf16[1,256,512]{2,1,0:T(8,128)(2,1)S(1)} %get-tuple-element.53), channel_id=1, source_target_pairs={{0,2},{1,3},{2,0},{3,1},{4,6},{5,7},{6,4},{7,5},{8,10},{9,11},{10,... | collective-permute-start | bytes 786440 | tf_op jit(solution)/shard_map/ppermute | solution.py:453
  24.6 6.6 %collective-permute-done.4.came_ref = bf16[1,256,512]{2,1,0:T(8,128)(2,1)S(1)} collective-permute-done((bf16[1,256,512]{2,1,0:T(8,128)(2,1)S(1)}, bf16[1,256,512]{2,1,0:T(8,128)(2,1)S(1)}, u32[]{:S(2)}, u32[]{:S(2)}) %collective-permute-start.4) | collective-permute-done | bytes 262176 | tf_op jit(solution)/shard_map/ppermute | solution.py:453
  31.2 0.9 %collective-permute-start.5 = (bf16[128,512]{1,0:T(8,128)(2,1)S(1)}, bf16[128,512]{1,0:T(8,128)(2,1)S(1)}, u32[]{:S(2)}, u32[]{:S(2)}) collective-permute-start(bf16[128,512]{1,0:T(8,128)(2,1)S(1)} %get-tuple-element.56), channel_id=1, source_target_pairs={{0,4},{4,0},{8,12},{12,8},{1,5},{5,1},{9,13},{13,9},{2,6},{6,2},{1... | collective-permute-start | bytes 393224 | tf_op jit(solution)/shard_map/ppermute | solution.py:453
  32.1 0.0 collective-permute-done.7.came_ref.refs_0_
  32.1 0.1 over_second.1
  32.2 1.5 %collective-permute-start.8 = (bf16[128,512]{1,0:T(8,128)(2,1)S(1)}, bf16[128,512]{1,0:T(8,128)(2,1)S(1)}, u32[]{:S(2)}, u32[]{:S(2)}) collective-permute-start(bf16[128,512]{1,0:T(8,128)(2,1)S(1)} %get-tuple-element.65), channel_id=1, source_target_pairs={{0,2},{1,3},{2,0},{3,1},{4,6},{5,7},{6,4},{7,5},{8,10},{9,11},{10,... | collective-permute-start | bytes 393224 | tf_op jit(solution)/shard_map/ppermute | solution.py:453
  33.7 0.7 %collective-permute-start.9 = (bf16[64,512]{1,0:T(8,128)(2,1)S(1)}, bf16[64,512]{1,0:T(8,128)(2,1)S(1)}, u32[]{:S(2)}, u32[]{:S(2)}) collective-permute-start(bf16[64,512]{1,0:T(8,128)(2,1)S(1)} %get-tuple-element.66), channel_id=1, source_target_pairs={{0,0},{4,8},{8,4},{12,12},{1,1},{5,9},{9,5},{13,13},{2,2},{6,10},{... | collective-permute-start | bytes 196616 | tf_op jit(solution)/shard_map/ppermute | solution.py:453
  34.4 3.9 %collective-permute-start.10 = (bf16[64,512]{1,0:T(8,128)(2,1)S(1)}, bf16[64,512]{1,0:T(8,128)(2,1)S(1)}, u32[]{:S(2)}, u32[]{:S(2)}) collective-permute-start(bf16[64,512]{1,0:T(8,128)(2,1)S(1)} %get-tuple-element.67), channel_id=1, source_target_pairs={{0,8},{4,12},{8,0},{12,4},{1,9},{5,13},{9,1},{13,5},{2,10},{6,14},... | collective-permute-start | bytes 196616 | tf_op jit(solution)/shard_map/ppermute | solution.py:453
  38.3 3.5 %collective-permute-done.10.refs_1_.refs_2_ = bf16[64,512]{1,0:T(8,128)(2,1)S(1)} collective-permute-done((bf16[64,512]{1,0:T(8,128)(2,1)S(1)}, bf16[64,512]{1,0:T(8,128)(2,1)S(1)}, u32[]{:S(2)}, u32[]{:S(2)}) %collective-permute-start.10) | collective-permute-done | bytes 65568 | tf_op jit(solution)/shard_map/ppermute | solution.py:453
  41.9 3.2 %collective-permute-start.11 = (bf16[256,512]{1,0:T(8,128)(2,1)S(1)}, bf16[256,512]{1,0:T(8,128)(2,1)S(1)}, u32[]{:S(2)}, u32[]{:S(2)}) collective-permute-start(bf16[256,512]{1,0:T(8,128)(2,1)S(1)} %add_terms.1.after), channel_id=1, source_target_pairs={{0,12},{4,8},{8,4},{12,0},{1,13},{5,9},{9,5},{13,1},{2,14},{6,10},... | collective-permute-start | bytes 786440 | tf_op jit(solution)/shard_map/ppermute | solution.py:453
  45.2 5.1 %collective-permute-done.11 = bf16[256,512]{1,0:T(8,128)(2,1)S(1)} collective-permute-done((bf16[256,512]{1,0:T(8,128)(2,1)S(1)}, bf16[256,512]{1,0:T(8,128)(2,1)S(1)}, u32[]{:S(2)}, u32[]{:S(2)}) %collective-permute-start.11) | collective-permute-done | bytes 262176 | tf_op jit(solution)/shard_map/ppermute | solution.py:453
  50.3 0.1 add_convert_fusion.own_ref
  50.4 5.1 %collective-permute-start.12 = (bf16[256,512]{1,0:T(8,128)(2,1)S(1)}, bf16[256,512]{1,0:T(8,128)(2,1)S(1)}, u32[]{:S(2)}, u32[]{:S(2)}) collective-permute-start(bf16[256,512]{1,0:T(8,128)(2,1)S(1)} %add_convert_fusion.own_ref), channel_id=1, source_target_pairs={{0,4},{4,0},{8,12},{12,8},{1,5},{5,1},{9,13},{13,9},{2,6},{6,2},{1... | collective-permute-start | bytes 786440 | tf_op jit(solution)/shard_map/ppermute | solution.py:453
  55.4 2.1 %node_grads.1.node_out = bf16[128,512]{1,0:T(8,128)(2,1)} custom-call(s32[1,4]{1,0:T(1,128)} %boundary_hbm.3, bf16[256,512]{1,0:T(8,128)(2,1)S(1)} %add_terms.1.after, f32[512,512]{1,0:T(8,128)S(1)} %get-tuple-element.59.sums_ref, bf16[1536,512]{1,0:T(8,128)(2,1)S(1)} %get-tuple-element.44.refs_5_.win_ref, ...), custom_call_target="tpu_custom_call" | custom-call | flops 268435456 | bytes 2000000 | tf_op jit(solution)/shard_map/node_grads/pallas_call | solution.py:738
  57.6 2.2 %edge_grads.1 = (bf16[768,512]{1,0:T(8,128)(2,1)}, bf16[128,512]{1,0:T(8,128)(2,1)}) custom-call(s32[12]{0:T(128)} %dst_hbm.3, s32[1]{0:T(128)S(6)} %copy.15.count_ref, bf16[256,512]{1,0:T(8,128)(2,1)S(1)} %add_terms.1.after, bf16[768,512]{1,0:T(8,128)(2,1)S(1)} %get-tuple-element.58.gpre_ref, f32[512,512]{1,0:T(8,128)S(1)} %get-tuple-element.59.sums_ref, ...), custom_call_target="tpu_custom_call" | custom-call | flops 402653184 | bytes 3000000 | tf_op jit(solution)/shard_map/edge_grads/pallas_call | solution.py:710
  59.8 1.0 %collective-permute-done.12.other_ref = bf16[256,512]{1,0:T(8,128)(2,1)S(1)} collective-permute-done((bf16[256,512]{1,0:T(8,128)(2,1)S(1)}, bf16[256,512]{1,0:T(8,128)(2,1)S(1)}, u32[]{:S(2)}, u32[]{:S(2)}) %collective-permute-start.12) | collective-permute-done | bytes 262176 | tf_op jit(solution)/shard_map/ppermute | solution.py:453
  60.8 1.0 %widen.1 = (f32[384,512]{1,0:T(8,128)}, f32[128,512]{1,0:T(8,128)}) custom-call(bf16[128,512]{1,0:T(8,128)(2,1)} %node_grads.1.node_out, bf16[768,512]{1,0:T(8,128)(2,1)} %get-tuple-element.70.edge_grad, bf16[256,512]{1,0:T(8,128)(2,1)S(1)} %add_convert_fusion.own_ref, bf16[256,512]{1,0:T(8,128)(2,1)S(1)} %collective-permute-done.12.other_ref), custom_call_target="tpu_custom_call" | custom-call | bytes 1500000 | tf_op jit(solution)/shard_map/widen/pallas_call | solution.py:755
  (7 shorter events, 0.1 us)
Async XLA Ops:
  1.6 10.7 %collective-permute-start = (bf16[64,512]{1,0:T(8,128)(2,1)S(1)}, bf16[64,512]{1,0:T(8,128)(2,1)S(1)}, u32[]{:S(2)}, u32[]{:S(2)}) collective-permute-start(bf16[64,512]{1,0:T(8,128)(2,1)S(1)} %get-tuple-element.39), channel_id=1, source_target_pairs={{0,8},{4,12},{8,0},{12,4},{1,9},{5,13},{9,1},{13,5},{2,10},{6,14},... | collective-permute-start | bytes 196616 | tf_op jit(solution)/shard_map/ppermute | solution.py:453
  5.7 6.7 %collective-permute-start.1 = (bf16[64,512]{1,0:T(8,128)(2,1)S(1)}, bf16[64,512]{1,0:T(8,128)(2,1)S(1)}, u32[]{:S(2)}, u32[]{:S(2)}) collective-permute-start(bf16[64,512]{1,0:T(8,128)(2,1)S(1)} %get-tuple-element.40), channel_id=1, source_target_pairs={{0,0},{4,8},{8,4},{12,12},{1,1},{5,9},{9,5},{13,13},{2,2},{6,10},{... | collective-permute-start | bytes 196616 | tf_op jit(solution)/shard_map/ppermute | solution.py:453
  6.3 6.0 %collective-permute-start.2 = (bf16[64,512]{1,0:T(8,128)(2,1)S(1)}, bf16[64,512]{1,0:T(8,128)(2,1)S(1)}, u32[]{:S(2)}, u32[]{:S(2)}) collective-permute-start(bf16[64,512]{1,0:T(8,128)(2,1)S(1)} %get-tuple-element.41), channel_id=1, source_target_pairs={{0,4},{4,0},{8,12},{12,8},{1,5},{5,1},{9,13},{13,9},{2,6},{6,2},{1... | collective-permute-start | bytes 196616 | tf_op jit(solution)/shard_map/ppermute | solution.py:453
  19.6 2.0 %collective-permute-start.6 = (bf16[2,256,512]{2,1,0:T(8,128)(2,1)S(1)}, bf16[2,256,512]{2,1,0:T(8,128)(2,1)S(1)}, u32[]{:S(2)}, u32[]{:S(2)}) collective-permute-start(bf16[2,256,512]{2,1,0:T(8,128)(2,1)S(1)} %get-tuple-element.60), channel_id=1, source_target_pairs={{0,1},{1,0},{2,3},{3,2},{4,5},{5,4},{6,7},{7,6},{8,9},{9,8},{10,11... | collective-permute-start | bytes 1572872 | tf_op jit(solution)/shard_map/ppermute | solution.py:453
  19.7 3.2 %collective-permute-start.3 = (bf16[2,256,512]{2,1,0:T(8,128)(2,1)S(1)}, bf16[2,256,512]{2,1,0:T(8,128)(2,1)S(1)}, u32[]{:S(2)}, u32[]{:S(2)}) collective-permute-start(bf16[2,256,512]{2,1,0:T(8,128)(2,1)S(1)} %get-tuple-element.50), channel_id=1, source_target_pairs={{0,1},{1,0},{2,3},{3,2},{4,5},{5,4},{6,7},{7,6},{8,9},{9,8},{10,11... | collective-permute-start | bytes 1572872 | tf_op jit(solution)/shard_map/ppermute | solution.py:453
  21.7 10.4 %collective-permute-start.7 = (bf16[320,512]{1,0:T(8,128)(2,1)S(1)}, bf16[320,512]{1,0:T(8,128)(2,1)S(1)}, u32[]{:S(2)}, u32[]{:S(2)}) collective-permute-start(bf16[320,512]{1,0:T(8,128)(2,1)S(1)} %get-tuple-element.62), channel_id=1, source_target_pairs={{0,4},{4,0},{8,12},{12,8},{1,5},{5,1},{9,13},{13,9},{2,6},{6,2},{1... | collective-permute-start | bytes 983048 | tf_op jit(solution)/shard_map/ppermute | solution.py:453
  23.0 8.1 %collective-permute-start.4 = (bf16[1,256,512]{2,1,0:T(8,128)(2,1)S(1)}, bf16[1,256,512]{2,1,0:T(8,128)(2,1)S(1)}, u32[]{:S(2)}, u32[]{:S(2)}) collective-permute-start(bf16[1,256,512]{2,1,0:T(8,128)(2,1)S(1)} %get-tuple-element.53), channel_id=1, source_target_pairs={{0,2},{1,3},{2,0},{3,1},{4,6},{5,7},{6,4},{7,5},{8,10},{9,11},{10,... | collective-permute-start | bytes 786440 | tf_op jit(solution)/shard_map/ppermute | solution.py:453
  31.2 7.2 %collective-permute-start.5 = (bf16[128,512]{1,0:T(8,128)(2,1)S(1)}, bf16[128,512]{1,0:T(8,128)(2,1)S(1)}, u32[]{:S(2)}, u32[]{:S(2)}) collective-permute-start(bf16[128,512]{1,0:T(8,128)(2,1)S(1)} %get-tuple-element.56), channel_id=1, source_target_pairs={{0,4},{4,0},{8,12},{12,8},{1,5},{5,1},{9,13},{13,9},{2,6},{6,2},{1... | collective-permute-start | bytes 393224 | tf_op jit(solution)/shard_map/ppermute | solution.py:453
  32.2 9.7 %collective-permute-start.8 = (bf16[128,512]{1,0:T(8,128)(2,1)S(1)}, bf16[128,512]{1,0:T(8,128)(2,1)S(1)}, u32[]{:S(2)}, u32[]{:S(2)}) collective-permute-start(bf16[128,512]{1,0:T(8,128)(2,1)S(1)} %get-tuple-element.65), channel_id=1, source_target_pairs={{0,2},{1,3},{2,0},{3,1},{4,6},{5,7},{6,4},{7,5},{8,10},{9,11},{10,... | collective-permute-start | bytes 393224 | tf_op jit(solution)/shard_map/ppermute | solution.py:453
  33.7 4.6 %collective-permute-start.9 = (bf16[64,512]{1,0:T(8,128)(2,1)S(1)}, bf16[64,512]{1,0:T(8,128)(2,1)S(1)}, u32[]{:S(2)}, u32[]{:S(2)}) collective-permute-start(bf16[64,512]{1,0:T(8,128)(2,1)S(1)} %get-tuple-element.66), channel_id=1, source_target_pairs={{0,0},{4,8},{8,4},{12,12},{1,1},{5,9},{9,5},{13,13},{2,2},{6,10},{... | collective-permute-start | bytes 196616 | tf_op jit(solution)/shard_map/ppermute | solution.py:453
  34.4 7.5 %collective-permute-start.10 = (bf16[64,512]{1,0:T(8,128)(2,1)S(1)}, bf16[64,512]{1,0:T(8,128)(2,1)S(1)}, u32[]{:S(2)}, u32[]{:S(2)}) collective-permute-start(bf16[64,512]{1,0:T(8,128)(2,1)S(1)} %get-tuple-element.67), channel_id=1, source_target_pairs={{0,8},{4,12},{8,0},{12,4},{1,9},{5,13},{9,1},{13,5},{2,10},{6,14},... | collective-permute-start | bytes 196616 | tf_op jit(solution)/shard_map/ppermute | solution.py:453
  41.9 8.3 %collective-permute-start.11 = (bf16[256,512]{1,0:T(8,128)(2,1)S(1)}, bf16[256,512]{1,0:T(8,128)(2,1)S(1)}, u32[]{:S(2)}, u32[]{:S(2)}) collective-permute-start(bf16[256,512]{1,0:T(8,128)(2,1)S(1)} %add_terms.1.after), channel_id=1, source_target_pairs={{0,12},{4,8},{8,4},{12,0},{1,13},{5,9},{9,5},{13,1},{2,14},{6,10},... | collective-permute-start | bytes 786440 | tf_op jit(solution)/shard_map/ppermute | solution.py:453
  50.4 10.4 %collective-permute-start.12 = (bf16[256,512]{1,0:T(8,128)(2,1)S(1)}, bf16[256,512]{1,0:T(8,128)(2,1)S(1)}, u32[]{:S(2)}, u32[]{:S(2)}) collective-permute-start(bf16[256,512]{1,0:T(8,128)(2,1)S(1)} %add_convert_fusion.own_ref), channel_id=1, source_target_pairs={{0,4},{4,0},{8,12},{12,8},{1,5},{5,1},{9,13},{13,9},{2,6},{6,2},{1... | collective-permute-start | bytes 786440 | tf_op jit(solution)/shard_map/ppermute | solution.py:453

commit v11 on v10

--- a/solution.py
+++ b/solution.py
@@ -170,52 +170,30 @@
     copies[9].wait()
 
 
-def put_units(chunk, ways, bit, away, kept, sections):
+def put_units(ways, bit, targets, sections):
     latent = sections[0][0].shape[1]
     unit = latent // ways
-    step = 128
-
-    def wanted(number, start):
-        if number == 0:
-            return [(start + at) // unit for at in range(0, step, unit)] if chunk == 0 else []
-        found = []
-        for at in range(0, step, unit):
-            spot = ((number - 1) * latent + start + at) // unit
-            if (1 + spot % 3) // 2 == chunk:
-                found.append(spot)
-        return found
-
+    step = 256
     for number, (left, right) in enumerate(sections):
         value_right = right()
-        start = 0
-        while start < latent:
-            size = step
-            if start + 2 * step <= latent and wanted(number, start + step):
-                size = 2 * step
-            if wanted(number, start):
-                value = t_dot(left[:, start : start + size], value_right)
-                for at in range(0, size, unit):
-                    if number == 0:
-                        owner, spot = (start + at) // unit, 0
-                    else:
-                        place = ((number - 1) * latent + start + at) // unit
-                        owner, spot = place // 3, 1 + place % 3
-                    if spot // 2 != chunk:
-                        continue
-                    part = value[at : at + unit]
-                    where = slice((spot % 2) * unit, (spot % 2 + 1) * unit)
-
-                    @pl.when(bit == owner % 2)
-                    def _(owner=owner, where=where, part=part):
-                        kept[owner // 2, where, :] = part
-
-                    @pl.when(bit != owner % 2)
-                    def _(owner=owner, where=where, part=part):
-                        away[owner // 2, where, :] = part.astype(BF16)
-
-                start += size
-            else:
-                start += step
+        for start in range(0, latent, step):
+            value = t_dot(left[:, start : start + step], value_right)
+            for at in range(0, step, unit):
+                owner, spot = (start + at) // unit, 0
+                if number > 0:
+                    place = ((number - 1) * latent + start + at) // unit
+                    owner, spot = place // 3, 1 + place % 3
+                away, kept = targets[spot // 2]
+                part = value[at : at + unit]
+                where = slice((spot % 2) * unit, (spot % 2 + 1) * unit)
+
+                @pl.when(bit == owner % 2)
+                def _(kept=kept, owner=owner, where=where, part=part):
+                    kept[owner // 2, where, :] = part
+
+                @pl.when(bit != owner % 2)
+                def _(away=away, owner=owner, where=where, part=part):
+                    away[owner // 2, where, :] = part.astype(BF16)
 
 
 def edge_kernel(ways, arrivals, four, block, *refs):
@@ -232,9 +210,12 @@
         gpre_ref,
         message_ref,
         sums_ref,
+        away_a,
+        kept_a,
+        away_b,
+        kept_b,
+        *back_refs,
         ext_ref,
-        away_ref,
-        kept_ref,
         act_ref,
         proj_ref,
     ) = refs[arrivals:]
@@ -273,24 +254,16 @@
         gpre_ref[rows, :] = (dot_t(grad_project, wout_ref[...]) * slope).astype(BF16)
 
     sums_ref[...] = dot(hot_turned[...], gpre_ref[...])
+    for which, back_ref in enumerate(back_refs):
+        back_ref[...] = back_block(nodes, block, sums_ref, 1 + which)
     sections = (
         (act_ref, lambda: proj_ref[...]),
         (edge_ref, lambda: gpre_ref[...]),
         (ext_ref, lambda: sums_ref[:extent, :].astype(BF16)),
         (node_ref, lambda: sums_ref[extent:, :].astype(BF16)),
     )
-    put_units(0, ways, lax.axis_index("dp") % 2, away_ref, kept_ref, sections)
-
-
-def rest_kernel(ways, node_ref, edge_ref, ext_ref, gpre_ref, sums_ref, away_ref, kept_ref):
-    extent = ext_ref.shape[0]
-    sections = (
-        (edge_ref, lambda: None),
-        (edge_ref, lambda: gpre_ref[...]),
-        (ext_ref, lambda: sums_ref[:extent, :].astype(BF16)),
-        (node_ref, lambda: sums_ref[extent:, :].astype(BF16)),
-    )
-    put_units(1, ways, lax.axis_index("dp") % 2, away_ref, kept_ref, sections)
+    targets = ((away_a, kept_a), (away_b, kept_b))
+    put_units(ways, lax.axis_index("dp") % 2, targets, sections)
 
 
 def edge_grad_kernel(
@@ -381,9 +354,8 @@
     left_ref[...] = kept_ref[0, here, :] + came_ref[0, here, :].astype(F32)
 
 
-def over_second_kernel(
-    nodes, block, came_ref, kept_ref, sums_ref, away_ref, left_ref, near_ref, far_ref
-):
+def over_second_kernel(came_ref, kept_ref, *refs):
+    away_ref, left_ref = refs[-2:]
     mine = lax.axis_index("dp") // 2
     rows = left_ref.shape[0]
 
@@ -393,8 +365,6 @@
 
     away_ref[...] = (kept_ref[1 - mine] + came(1 - mine)).astype(BF16)
     left_ref[...] = kept_ref[mine] + came(mine)
-    near_ref[...] = back_block(nodes, block, sums_ref, 1)
-    far_ref[...] = back_block(nodes, block, sums_ref, 2)
 
 
 def add_kernel(left_a, came_a, left_b, came_b, *refs):
@@ -619,19 +589,22 @@
     )
     sent_shape = pltpu.VMEM((half, 2 * unit, latent), BF16)
     kept_shape = pltpu.VMEM((half, 2 * unit, latent), F32)
-    grad_pre, message, sums, ext, away_a, kept_a = pl.pallas_call(
+    grad_pre, message, sums, away_a, kept_a, away_b, kept_b, *outer = pl.pallas_call(
         functools.partial(edge_kernel, ways, arrivals, four, block),
         out_shape=(
             pltpu.VMEM((edges, latent), BF16),
             pltpu.VMEM((edges, latent), F32),
             pltpu.VMEM((extent + nodes, latent), F32),
-            pltpu.VMEM((extent, latent), BF16),
             sent_shape,
             kept_shape,
+            sent_shape,
+            kept_shape,
+            *[block_shape] * (2 if four else 0),
         ),
         in_specs=[VMEM] * (8 + arrivals),
-        out_specs=(VMEM,) * 6,
+        out_specs=(VMEM,) * (9 if four else 7),
         scratch_shapes=[
+            pltpu.VMEM((extent, latent), BF16),
             pltpu.VMEM((edges, latent), BF16),
             pltpu.VMEM((edges, latent), BF16),
         ],
@@ -648,17 +621,6 @@
             for array in (*came[::-1], node_v, edge_v, win_v, wout_v, pre, up, hot, turned)
         ],
     )
-    away_b, kept_b = pl.pallas_call(
-        functools.partial(rest_kernel, ways),
-        out_shape=(sent_shape, kept_shape),
-        in_specs=[VMEM] * 5,
-        out_specs=(VMEM,) * 2,
-        compiler_params=small,
-        cost_estimate=pl.CostEstimate(
-            flops=2 * edges * latent * latent, bytes_accessed=4_000_000, transcendentals=0
-        ),
-        name="rest_weights",
-    )(*[in_vmem(array) for array in (node_v, edge_v, ext, grad_pre, sums)])
     if four:
         rows = 2 * unit
         piece, wide = pltpu.VMEM((unit, latent), BF16), pltpu.VMEM((unit, latent), F32)
@@ -675,21 +637,16 @@
             sums,
         )
         beside = swap(away_b, "dom", lambda i: i ^ 1)
+        far = swap(outer[1], "dom", lambda i: partners_of_four(2)[i])
+        near = swap(outer[0], "dom", lambda i: partners_of_four(1)[i])
         away_a, kept_a = small_call(
-            beside_second_kernel, "beside_second", (piece, wide), came_a, kept_a
+            beside_second_kernel, "beside_second", (piece, wide), came_a, kept_a, far, near
         )
         came_a = swap(away_a, "dom", lambda i: i ^ 1)
-        away_b, kept_b, near, far = small_call(
-            functools.partial(over_second_kernel, nodes, block),
-            "over_second",
-            (piece, wide, block_shape, block_shape),
-            beside,
-            kept_b,
-            sums,
+        away_b, kept_b = small_call(
+            over_second_kernel, "over_second", (piece, wide), beside, kept_b
         )
         came_b = swap(away_b, "dp", lambda i: i ^ 2)
-        far = swap(far, "dom", lambda i: partners_of_four(2)[i])
-        near = swap(near, "dom", lambda i: partners_of_four(1)[i])
         pair = small_call(
             add_kernel,
             "add_terms",
@@ -698,8 +655,6 @@
             came_a,
             kept_b,
             came_b,
-            near,
-            far,
         )
         returned = [beside, near, far]
         late, backs = pair, 0

time: 62 us -> 57.9 us (0.934)
  starting transfers between devices: 26.3 us -> 24.1 us
  waiting for transfers between devices: 17.7 us -> 16.3 us
    ppermute x13, starting transfers between devices: 26.3 us -> 24.1 us  [swap(): return lax.ppermute(array, axis, [(i, partner(i)) for i in range(devices)])]
    pallas_call x1 -> x0, Pallas kernels: 1.49 us -> none  [body(): pl.pallas_call(functools.partial(rest_kernel, ways), out_shape=(sent_shap...]
    ppermute x13, waiting for transfers between devices: 17.7 us -> 16.3 us  [swap(): return lax.ppermute(array, axis, [(i, partner(i)) for i in range(devices)])]
    pallas_call x1, Pallas kernels: 5.76 us -> 6.79 us  [body(): pl.pallas_call(functools.partial(edge_kernel, ways, arrivals, four, block...]
  transfers between devices with their start and end apart: 13 -> 13, of which waited for: 5 -> 5; matrix products, arithmetic and copies ran while one was open for 0% -> 0% of each run, Pallas kernels for 11% -> 12%
where the time goes in v11:
time: 57.9 us; the launch traced here: 57.7 us
  starting transfers between devices  24.1 us (42%)
  waiting for transfers between devices  16.3 us (28%)
  Pallas kernels  15.9 us (27%)
  between operations  1.41 us (2%)
    ppermute x13, starting transfers between devices, swap(): return lax.ppermute(array, axis, [(i, partner(i)) for i in range(devices)])  24.1 us
    ppermute x13, waiting for transfers between devices, swap(): return lax.ppermute(array, axis, [(i, partner(i)) for i in range(devices)])  16.3 us
    pallas_call x1, Pallas kernels, body(): pl.pallas_call(functools.partial(edge_kernel, ways, arrivals, four, block...  6.79 us
    pallas_call x1, Pallas kernels, body(): pl.pallas_call(functools.partial(prep_kernel, parts, arrivals), out_shape...  2.42 us
    pallas_call x1, Pallas kernels, body(): pl.pallas_call(functools.partial(edge_grad_kernel, block, arrivals, four)...  2.21 us
    pallas_call x1, Pallas kernels, body(): pl.pallas_call(functools.partial(node_grad_kernel, arrivals, four), out_s...  2.14 us
  transfers between devices with their start and end apart: 13, of which 5 were waited for; matrix products, arithmetic and copies ran while one was open for 0% of the time, Pallas kernels for 12%

profile of v11, /device:TPU:0, one launch (start us, length us, event | category | flops | bytes accessed | tf_op | source)
XLA Modules:
  0.0 57.7 jit_solution(194746789485078620)
XLA Ops:
  0.6 0.9 %pick_blocks.1 = (bf16[64,512]{1,0:T(8,128)(2,1)S(1)}, bf16[64,512]{1,0:T(8,128)(2,1)S(1)}, bf16[64,512]{1,0:T(8,128)(2,1)S(1)}) custom-call(s32[1,4]{1,0:T(1,128)} %boundary_hbm.3, bf16[128,512]{1,0:T(8,128)(2,1)} %bitcast.8), custom_call_target="tpu_custom_call" | custom-call | bytes 400000 | tf_op jit(solution)/shard_map/pick_blocks/pallas_call | solution.py:529
  1.6 4.1 %collective-permute-start = (bf16[64,512]{1,0:T(8,128)(2,1)S(1)}, bf16[64,512]{1,0:T(8,128)(2,1)S(1)}, u32[]{:S(2)}, u32[]{:S(2)}) collective-permute-start(bf16[64,512]{1,0:T(8,128)(2,1)S(1)} %get-tuple-element.38), channel_id=1, source_target_pairs={{0,8},{4,12},{8,0},{12,4},{1,9},{5,13},{9,1},{13,5},{2,10},{6,14},... | collective-permute-start | bytes 196616 | tf_op jit(solution)/shard_map/ppermute | solution.py:423
  5.7 0.7 %collective-permute-start.1 = (bf16[64,512]{1,0:T(8,128)(2,1)S(1)}, bf16[64,512]{1,0:T(8,128)(2,1)S(1)}, u32[]{:S(2)}, u32[]{:S(2)}) collective-permute-start(bf16[64,512]{1,0:T(8,128)(2,1)S(1)} %get-tuple-element.39), channel_id=1, source_target_pairs={{0,0},{4,8},{8,4},{12,12},{1,1},{5,9},{9,5},{13,13},{2,2},{6,10},{... | collective-permute-start | bytes 196616 | tf_op jit(solution)/shard_map/ppermute | solution.py:423
  6.3 2.9 %collective-permute-start.2 = (bf16[64,512]{1,0:T(8,128)(2,1)S(1)}, bf16[64,512]{1,0:T(8,128)(2,1)S(1)}, u32[]{:S(2)}, u32[]{:S(2)}) collective-permute-start(bf16[64,512]{1,0:T(8,128)(2,1)S(1)} %get-tuple-element.40), channel_id=1, source_target_pairs={{0,4},{4,0},{8,12},{12,8},{1,5},{5,1},{9,13},{13,9},{2,6},{6,2},{1... | collective-permute-start | bytes 196616 | tf_op jit(solution)/shard_map/ppermute | solution.py:423
  9.9 2.4 %prepare.1 = (bf16[128,512]{1,0:T(8,128)(2,1)S(1)}, bf16[768,512]{1,0:T(8,128)(2,1)S(1)}, bf16[128,512]{1,0:T(8,128)(2,1)S(1)}, bf16[1536,512]{1,0:T(8,128)(2,1)...) custom-call(s32[1]{0:T(128)S(6)} %copy.15.count_ref, ...), custom_call_target="tpu_custom_call" | custom-call | flops 402653184 | bytes 8000000 | tf_op jit(solution)/shard_map/prepare/pallas_call | solution.py:551
  12.3 0.0 collective-permute-done.refs_0_
  12.3 0.0 collective-permute-done.1.refs_1_
  12.3 6.8 %edge_block.1 = (bf16[768,512]{1,0:T(8,128)(2,1)S(1)}, f32[768,512]{1,0:T(8,128)S(1)}, f32[512,512]{1,0:T(8,128)S(1)}, bf16[2,256,512]{2,1,0:T(8,128)(2,1)S(1)},...) custom-call(bf16[64,512]{1,0:T(8,128)(2,1)S(1)} %collective-permute-, ...), custom_call_target="tpu_custom_call" | custom-call | flops 2415919104 | bytes 12000000 | tf_op jit(solution)/shard_map/edge_block/pallas_call | solution.py:592
  19.1 0.1 collective-permute-start.8
  19.2 0.5 collective-permute-start.3
  19.7 1.4 %collective-permute-done.8.came_ref = bf16[2,256,512]{2,1,0:T(8,128)(2,1)S(1)} collective-permute-done((bf16[2,256,512]{2,1,0:T(8,128)(2,1)S(1)}, bf16[2,256,512]{2,1,0:T(8,128)(2,1)S(1)}, u32[]{:S(2)}, u32[]{:S(2)}) %collective-permute-start.8) | collective-permute-done | bytes 524320 | tf_op jit(solution)/shard_map/ppermute | solution.py:423
  21.1 0.1 beside_first.1
  21.2 1.2 %collective-permute-start.9 = (bf16[320,512]{1,0:T(8,128)(2,1)S(1)}, bf16[320,512]{1,0:T(8,128)(2,1)S(1)}, u32[]{:S(2)}, u32[]{:S(2)}) collective-permute-start(bf16[320,512]{1,0:T(8,128)(2,1)S(1)} %get-tuple-element.61), channel_id=1, source_target_pairs={{0,4},{4,0},{8,12},{12,8},{1,5},{5,1},{9,13},{13,9},{2,6},{6,2},{1... | collective-permute-start | bytes 983048 | tf_op jit(solution)/shard_map/ppermute | solution.py:423
  22.4 0.0 collective-permute-done.3.came_ref
  22.4 0.1 halve.1
  22.5 1.6 %collective-permute-start.4 = (bf16[1,256,512]{2,1,0:T(8,128)(2,1)S(1)}, bf16[1,256,512]{2,1,0:T(8,128)(2,1)S(1)}, u32[]{:S(2)}, u32[]{:S(2)}) collective-permute-start(bf16[1,256,512]{2,1,0:T(8,128)(2,1)S(1)} %get-tuple-element.52), channel_id=1, source_target_pairs={{0,2},{1,3},{2,0},{3,1},{4,6},{5,7},{6,4},{7,5},{8,10},{9,11},{10,... | collective-permute-start | bytes 786440 | tf_op jit(solution)/shard_map/ppermute | solution.py:423
  24.1 2.3 %collective-permute-start.5 = (bf16[64,512]{1,0:T(8,128)(2,1)S(1)}, bf16[64,512]{1,0:T(8,128)(2,1)S(1)}, u32[]{:S(2)}, u32[]{:S(2)}) collective-permute-start(bf16[64,512]{1,0:T(8,128)(2,1)S(1)} %get-tuple-element.54), channel_id=1, source_target_pairs={{0,8},{4,12},{8,0},{12,4},{1,9},{5,13},{9,1},{13,5},{2,10},{6,14},... | collective-permute-start | bytes 196616 | tf_op jit(solution)/shard_map/ppermute | solution.py:423
  26.4 0.7 %collective-permute-start.6 = (bf16[64,512]{1,0:T(8,128)(2,1)S(1)}, bf16[64,512]{1,0:T(8,128)(2,1)S(1)}, u32[]{:S(2)}, u32[]{:S(2)}) collective-permute-start(bf16[64,512]{1,0:T(8,128)(2,1)S(1)} %get-tuple-element.55), channel_id=1, source_target_pairs={{0,0},{4,8},{8,4},{12,12},{1,1},{5,9},{9,5},{13,13},{2,2},{6,10},{... | collective-permute-start | bytes 196616 | tf_op jit(solution)/shard_map/ppermute | solution.py:423
  27.1 4.0 %collective-permute-done.5.refs_0_.refs_2_ = bf16[64,512]{1,0:T(8,128)(2,1)S(1)} collective-permute-done((bf16[64,512]{1,0:T(8,128)(2,1)S(1)}, bf16[64,512]{1,0:T(8,128)(2,1)S(1)}, u32[]{:S(2)}, u32[]{:S(2)}) %collective-permute-start.5) | collective-permute-done | bytes 65568 | tf_op jit(solution)/shard_map/ppermute | solution.py:423
  31.1 0.0 collective-permute-done.6.refs_1_
  31.2 4.0 %collective-permute-start.7 = (bf16[128,512]{1,0:T(8,128)(2,1)S(1)}, bf16[128,512]{1,0:T(8,128)(2,1)S(1)}, u32[]{:S(2)}, u32[]{:S(2)}) collective-permute-start(bf16[128,512]{1,0:T(8,128)(2,1)S(1)} %get-tuple-element.57), channel_id=1, source_target_pairs={{0,4},{4,0},{8,12},{12,8},{1,5},{5,1},{9,13},{13,9},{2,6},{6,2},{1... | collective-permute-start | bytes 393224 | tf_op jit(solution)/shard_map/ppermute | solution.py:423
  35.2 0.1 over_second.1
  35.2 1.6 %collective-permute-start.10 = (bf16[128,512]{1,0:T(8,128)(2,1)S(1)}, bf16[128,512]{1,0:T(8,128)(2,1)S(1)}, u32[]{:S(2)}, u32[]{:S(2)}) collective-permute-start(bf16[128,512]{1,0:T(8,128)(2,1)S(1)} %get-tuple-element.64), channel_id=1, source_target_pairs={{0,2},{1,3},{2,0},{3,1},{4,6},{5,7},{6,4},{7,5},{8,10},{9,11},{10,... | collective-permute-start | bytes 393224 | tf_op jit(solution)/shard_map/ppermute | solution.py:423
  36.8 1.3 %collective-permute-done.7.came_a = bf16[128,512]{1,0:T(8,128)(2,1)S(1)} collective-permute-done((bf16[128,512]{1,0:T(8,128)(2,1)S(1)}, bf16[128,512]{1,0:T(8,128)(2,1)S(1)}, u32[]{:S(2)}, u32[]{:S(2)}) %collective-permute-start.7) | collective-permute-done | bytes 131104 | tf_op jit(solution)/shard_map/ppermute | solution.py:423
  38.1 2.1 %collective-permute-done.10.came_b = bf16[128,512]{1,0:T(8,128)(2,1)S(1)} collective-permute-done((bf16[128,512]{1,0:T(8,128)(2,1)S(1)}, bf16[128,512]{1,0:T(8,128)(2,1)S(1)}, u32[]{:S(2)}, u32[]{:S(2)}) %collective-permute-start.10) | collective-permute-done | bytes 131104 | tf_op jit(solution)/shard_map/ppermute | solution.py:423
  40.3 1.0 %collective-permute-start.11 = (bf16[256,512]{1,0:T(8,128)(2,1)S(1)}, bf16[256,512]{1,0:T(8,128)(2,1)S(1)}, u32[]{:S(2)}, u32[]{:S(2)}) collective-permute-start(bf16[256,512]{1,0:T(8,128)(2,1)S(1)} %add_terms.1.after), channel_id=1, source_target_pairs={{0,12},{4,8},{8,4},{12,0},{1,13},{5,9},{9,5},{13,1},{2,14},{6,10},... | collective-permute-start | bytes 786440 | tf_op jit(solution)/shard_map/ppermute | solution.py:423
  41.3 7.3 %collective-permute-done.11 = bf16[256,512]{1,0:T(8,128)(2,1)S(1)} collective-permute-done((bf16[256,512]{1,0:T(8,128)(2,1)S(1)}, bf16[256,512]{1,0:T(8,128)(2,1)S(1)}, u32[]{:S(2)}, u32[]{:S(2)}) %collective-permute-start.11) | collective-permute-done | bytes 262176 | tf_op jit(solution)/shard_map/ppermute | solution.py:423
  48.6 0.1 add_convert_fusion.own_ref
  48.7 3.6 %collective-permute-start.12 = (bf16[256,512]{1,0:T(8,128)(2,1)S(1)}, bf16[256,512]{1,0:T(8,128)(2,1)S(1)}, u32[]{:S(2)}, u32[]{:S(2)}) collective-permute-start(bf16[256,512]{1,0:T(8,128)(2,1)S(1)} %add_convert_fusion.own_ref), channel_id=1, source_target_pairs={{0,4},{4,0},{8,12},{12,8},{1,5},{5,1},{9,13},{13,9},{2,6},{6,2},{1... | collective-permute-start | bytes 786440 | tf_op jit(solution)/shard_map/ppermute | solution.py:423
  52.2 2.1 %node_grads.1.node_out = bf16[128,512]{1,0:T(8,128)(2,1)} custom-call(s32[1,4]{1,0:T(1,128)} %boundary_hbm.3, bf16[256,512]{1,0:T(8,128)(2,1)S(1)} %add_terms.1.after, f32[512,512]{1,0:T(8,128)S(1)} %get-tuple-element.60.sums_ref, bf16[1536,512]{1,0:T(8,128)(2,1)S(1)} %get-tuple-element.43.refs_5_.win_ref, ...), custom_call_target="tpu_custom_call" | custom-call | flops 268435456 | bytes 2000000 | tf_op jit(solution)/shard_map/node_grads/pallas_call | solution.py:693
  54.4 2.2 %edge_grads.1 = (bf16[768,512]{1,0:T(8,128)(2,1)}, bf16[128,512]{1,0:T(8,128)(2,1)}) custom-call(s32[12]{0:T(128)} %dst_hbm.3, s32[1]{0:T(128)S(6)} %copy.15.count_ref, bf16[256,512]{1,0:T(8,128)(2,1)S(1)} %add_terms.1.after, bf16[768,512]{1,0:T(8,128)(2,1)S(1)} %get-tuple-element.65.gpre_ref, f32[512,512]{1,0:T(8,128)S(1)} %get-tuple-element.60.sums_ref, ...), custom_call_target="tpu_custom_call" | custom-call | flops 402653184 | bytes 3000000 | tf_op jit(solution)/shard_map/edge_grads/pallas_call | solution.py:665
  56.6 1.0 %widen.1 = (f32[384,512]{1,0:T(8,128)}, f32[128,512]{1,0:T(8,128)}) custom-call(bf16[128,512]{1,0:T(8,128)(2,1)} %node_grads.1.node_out, bf16[768,512]{1,0:T(8,128)(2,1)} %get-tuple-element.68.edge_grad, bf16[256,512]{1,0:T(8,128)(2,1)S(1)} %add_convert_fusion.own_ref, bf16[256,512]{1,0:T(8,128)(2,1)S(1)} %collective-permute-done.12.other_ref), custom_call_target="tpu_custom_call" | custom-call | bytes 1500000 | tf_op jit(solution)/shard_map/widen/pallas_call | solution.py:710
  (6 shorter events, 0.1 us)
Async XLA Ops:
  1.6 10.7 %collective-permute-start = (bf16[64,512]{1,0:T(8,128)(2,1)S(1)}, bf16[64,512]{1,0:T(8,128)(2,1)S(1)}, u32[]{:S(2)}, u32[]{:S(2)}) collective-permute-start(bf16[64,512]{1,0:T(8,128)(2,1)S(1)} %get-tuple-element.38), channel_id=1, source_target_pairs={{0,8},{4,12},{8,0},{12,4},{1,9},{5,13},{9,1},{13,5},{2,10},{6,14},... | collective-permute-start | bytes 196616 | tf_op jit(solution)/shard_map/ppermute | solution.py:423
  5.7 6.7 %collective-permute-start.1 = (bf16[64,512]{1,0:T(8,128)(2,1)S(1)}, bf16[64,512]{1,0:T(8,128)(2,1)S(1)}, u32[]{:S(2)}, u32[]{:S(2)}) collective-permute-start(bf16[64,512]{1,0:T(8,128)(2,1)S(1)} %get-tuple-element.39), channel_id=1, source_target_pairs={{0,0},{4,8},{8,4},{12,12},{1,1},{5,9},{9,5},{13,13},{2,2},{6,10},{... | collective-permute-start | bytes 196616 | tf_op jit(solution)/shard_map/ppermute | solution.py:423
  6.3 6.0 %collective-permute-start.2 = (bf16[64,512]{1,0:T(8,128)(2,1)S(1)}, bf16[64,512]{1,0:T(8,128)(2,1)S(1)}, u32[]{:S(2)}, u32[]{:S(2)}) collective-permute-start(bf16[64,512]{1,0:T(8,128)(2,1)S(1)} %get-tuple-element.40), channel_id=1, source_target_pairs={{0,4},{4,0},{8,12},{12,8},{1,5},{5,1},{9,13},{13,9},{2,6},{6,2},{1... | collective-permute-start | bytes 196616 | tf_op jit(solution)/shard_map/ppermute | solution.py:423
  19.1 2.0 %collective-permute-start.8 = (bf16[2,256,512]{2,1,0:T(8,128)(2,1)S(1)}, bf16[2,256,512]{2,1,0:T(8,128)(2,1)S(1)}, u32[]{:S(2)}, u32[]{:S(2)}) collective-permute-start(bf16[2,256,512]{2,1,0:T(8,128)(2,1)S(1)} %get-tuple-element.58), channel_id=1, source_target_pairs={{0,1},{1,0},{2,3},{3,2},{4,5},{5,4},{6,7},{7,6},{8,9},{9,8},{10,11... | collective-permute-start | bytes 1572872 | tf_op jit(solution)/shard_map/ppermute | solution.py:423
  19.2 3.2 %collective-permute-start.3 = (bf16[2,256,512]{2,1,0:T(8,128)(2,1)S(1)}, bf16[2,256,512]{2,1,0:T(8,128)(2,1)S(1)}, u32[]{:S(2)}, u32[]{:S(2)}) collective-permute-start(bf16[2,256,512]{2,1,0:T(8,128)(2,1)S(1)} %get-tuple-element.49), channel_id=1, source_target_pairs={{0,1},{1,0},{2,3},{3,2},{4,5},{5,4},{6,7},{7,6},{8,9},{9,8},{10,11... | collective-permute-start | bytes 1572872 | tf_op jit(solution)/shard_map/ppermute | solution.py:423
  21.2 13.9 %collective-permute-start.9 = (bf16[320,512]{1,0:T(8,128)(2,1)S(1)}, bf16[320,512]{1,0:T(8,128)(2,1)S(1)}, u32[]{:S(2)}, u32[]{:S(2)}) collective-permute-start(bf16[320,512]{1,0:T(8,128)(2,1)S(1)} %get-tuple-element.61), channel_id=1, source_target_pairs={{0,4},{4,0},{8,12},{12,8},{1,5},{5,1},{9,13},{13,9},{2,6},{6,2},{1... | collective-permute-start | bytes 983048 | tf_op jit(solution)/shard_map/ppermute | solution.py:423
  22.5 8.6 %collective-permute-start.4 = (bf16[1,256,512]{2,1,0:T(8,128)(2,1)S(1)}, bf16[1,256,512]{2,1,0:T(8,128)(2,1)S(1)}, u32[]{:S(2)}, u32[]{:S(2)}) collective-permute-start(bf16[1,256,512]{2,1,0:T(8,128)(2,1)S(1)} %get-tuple-element.52), channel_id=1, source_target_pairs={{0,2},{1,3},{2,0},{3,1},{4,6},{5,7},{6,4},{7,5},{8,10},{9,11},{10,... | collective-permute-start | bytes 786440 | tf_op jit(solution)/shard_map/ppermute | solution.py:423
  24.1 7.0 %collective-permute-start.5 = (bf16[64,512]{1,0:T(8,128)(2,1)S(1)}, bf16[64,512]{1,0:T(8,128)(2,1)S(1)}, u32[]{:S(2)}, u32[]{:S(2)}) collective-permute-start(bf16[64,512]{1,0:T(8,128)(2,1)S(1)} %get-tuple-element.54), channel_id=1, source_target_pairs={{0,8},{4,12},{8,0},{12,4},{1,9},{5,13},{9,1},{13,5},{2,10},{6,14},... | collective-permute-start | bytes 196616 | tf_op jit(solution)/shard_map/ppermute | solution.py:423
  26.4 4.7 %collective-permute-start.6 = (bf16[64,512]{1,0:T(8,128)(2,1)S(1)}, bf16[64,512]{1,0:T(8,128)(2,1)S(1)}, u32[]{:S(2)}, u32[]{:S(2)}) collective-permute-start(bf16[64,512]{1,0:T(8,128)(2,1)S(1)} %get-tuple-element.55), channel_id=1, source_target_pairs={{0,0},{4,8},{8,4},{12,12},{1,1},{5,9},{9,5},{13,13},{2,2},{6,10},{... | collective-permute-start | bytes 196616 | tf_op jit(solution)/shard_map/ppermute | solution.py:423
  31.2 6.9 %collective-permute-start.7 = (bf16[128,512]{1,0:T(8,128)(2,1)S(1)}, bf16[128,512]{1,0:T(8,128)(2,1)S(1)}, u32[]{:S(2)}, u32[]{:S(2)}) collective-permute-start(bf16[128,512]{1,0:T(8,128)(2,1)S(1)} %get-tuple-element.57), channel_id=1, source_target_pairs={{0,4},{4,0},{8,12},{12,8},{1,5},{5,1},{9,13},{13,9},{2,6},{6,2},{1... | collective-permute-start | bytes 393224 | tf_op jit(solution)/shard_map/ppermute | solution.py:423
  35.2 5.0 %collective-permute-start.10 = (bf16[128,512]{1,0:T(8,128)(2,1)S(1)}, bf16[128,512]{1,0:T(8,128)(2,1)S(1)}, u32[]{:S(2)}, u32[]{:S(2)}) collective-permute-start(bf16[128,512]{1,0:T(8,128)(2,1)S(1)} %get-tuple-element.64), channel_id=1, source_target_pairs={{0,2},{1,3},{2,0},{3,1},{4,6},{5,7},{6,4},{7,5},{8,10},{9,11},{10,... | collective-permute-start | bytes 393224 | tf_op jit(solution)/shard_map/ppermute | solution.py:423
  40.3 8.3 %collective-permute-start.11 = (bf16[256,512]{1,0:T(8,128)(2,1)S(1)}, bf16[256,512]{1,0:T(8,128)(2,1)S(1)}, u32[]{:S(2)}, u32[]{:S(2)}) collective-permute-start(bf16[256,512]{1,0:T(8,128)(2,1)S(1)} %add_terms.1.after), channel_id=1, source_target_pairs={{0,12},{4,8},{8,4},{12,0},{1,13},{5,9},{9,5},{13,1},{2,14},{6,10},... | collective-permute-start | bytes 786440 | tf_op jit(solution)/shard_map/ppermute | solution.py:423
  48.7 7.9 %collective-permute-start.12 = (bf16[256,512]{1,0:T(8,128)(2,1)S(1)}, bf16[256,512]{1,0:T(8,128)(2,1)S(1)}, u32[]{:S(2)}, u32[]{:S(2)}) collective-permute-start(bf16[256,512]{1,0:T(8,128)(2,1)S(1)} %add_convert_fusion.own_ref), channel_id=1, source_target_pairs={{0,4},{4,0},{8,12},{12,8},{1,5},{5,1},{9,13},{13,9},{2,6},{6,2},{1... | collective-permute-start | bytes 786440 | tf_op jit(solution)/shard_map/ppermute | solution.py:423

commit v12 on v11

--- a/solution.py
+++ b/solution.py
@@ -196,8 +196,12 @@
                     away[owner // 2, where, :] = part.astype(BF16)
 
 
+def arrival_order(arrivals):
+    return (2, 0, 1) if arrivals == 3 else tuple(range(arrivals))
+
+
 def edge_kernel(ways, arrivals, four, block, *refs):
-    arrived = refs[:arrivals][::-1]
+    arrived = [refs[which] for which in arrival_order(arrivals)]
     (
         node_ref,
         edge_ref,
@@ -232,7 +236,7 @@
     if filled < extent:
         ext_ref[filled:, :] = jnp.zeros((extent - filled, latent), BF16)
 
-    span = 256 if edges % 256 == 0 else block
+    span = 384 if edges % 384 == 0 else block
     for start in range(0, edges, span):
         rows = slice(start, start + span)
         senders = dot(hot_ref[rows, :], ext_ref[...]).astype(BF16)
@@ -336,7 +340,7 @@
     return sums_ref[pl.ds(pl.multiple_of(nodes + place * block, block), block), :].astype(BF16)
 
 
-def beside_first_kernel(nodes, block, came_ref, kept_ref, sums_ref, away_ref, left_ref):
+def beside_first_kernel(came_ref, kept_ref, away_ref, left_ref):
     rows = left_ref.shape[1]
     here, there = half_rows(rows)
     for slot in range(2):
@@ -344,13 +348,14 @@
             kept_ref[slot, there, :] + came_ref[slot, there, :].astype(F32)
         ).astype(BF16)
         left_ref[slot] = kept_ref[slot, here, :] + came_ref[slot, here, :].astype(F32)
-    away_ref[2 * rows :, :] = back_block(nodes, block, sums_ref, 0)
-
-
-def beside_second_kernel(came_ref, kept_ref, *refs):
+
+
+def beside_second_kernel(nodes, block, came_ref, kept_ref, sums_ref, *refs):
     away_ref, left_ref = refs[-2:]
-    here, there = half_rows(left_ref.shape[0])
-    away_ref[...] = (kept_ref[0, there, :] + came_ref[0, there, :].astype(F32)).astype(BF16)
+    rows = left_ref.shape[0]
+    here, there = half_rows(rows)
+    away_ref[:rows, :] = (kept_ref[0, there, :] + came_ref[0, there, :].astype(F32)).astype(BF16)
+    away_ref[rows:, :] = back_block(nodes, block, sums_ref, 0)
     left_ref[...] = kept_ref[0, here, :] + came_ref[0, here, :].astype(F32)
 
 
@@ -370,7 +375,7 @@
 def add_kernel(left_a, came_a, left_b, came_b, *refs):
     out_ref = refs[-1]
     rows = left_a.shape[0]
-    out_ref[:rows, :] = (left_a[...] + came_a[...].astype(F32)).astype(BF16)
+    out_ref[:rows, :] = (left_a[...] + came_a[:rows, :].astype(F32)).astype(BF16)
     out_ref[rows:, :] = (left_b[...] + came_b[...].astype(F32)).astype(BF16)
 
 
@@ -589,6 +594,9 @@
     )
     sent_shape = pltpu.VMEM((half, 2 * unit, latent), BF16)
     kept_shape = pltpu.VMEM((half, 2 * unit, latent), F32)
+    ordered = [None] * arrivals
+    for array, which in zip(came, arrival_order(arrivals)):
+        ordered[which] = array
     grad_pre, message, sums, away_a, kept_a, away_b, kept_b, *outer = pl.pallas_call(
         functools.partial(edge_kernel, ways, arrivals, four, block),
         out_shape=(
@@ -618,7 +626,7 @@
     )(
         *[
             in_vmem(array)
-            for array in (*came[::-1], node_v, edge_v, win_v, wout_v, pre, up, hot, turned)
+            for array in (*ordered, node_v, edge_v, win_v, wout_v, pre, up, hot, turned)
         ],
     )
     if four:
@@ -629,18 +637,24 @@
         came_a = swap(away_a, "dp", lambda i: i ^ 2)
         came_b = swap(away_b, "dp", lambda i: i ^ 1)
         away_b, kept_b = small_call(
-            functools.partial(beside_first_kernel, nodes, block),
+            beside_first_kernel,
             "beside_first",
-            (pltpu.VMEM((rows + block, latent), BF16), pltpu.VMEM((2, unit, latent), F32)),
+            (pltpu.VMEM((rows, latent), BF16), pltpu.VMEM((2, unit, latent), F32)),
             came_b,
             kept_b,
-            sums,
         )
         beside = swap(away_b, "dom", lambda i: i ^ 1)
         far = swap(outer[1], "dom", lambda i: partners_of_four(2)[i])
         near = swap(outer[0], "dom", lambda i: partners_of_four(1)[i])
         away_a, kept_a = small_call(
-            beside_second_kernel, "beside_second", (piece, wide), came_a, kept_a, far, near
+            functools.partial(beside_second_kernel, nodes, block),
+            "beside_second",
+            (pltpu.VMEM((unit + block, latent), BF16), wide),
+            came_a,
+            kept_a,
+            sums,
+            far,
+            near,
         )
         came_a = swap(away_a, "dom", lambda i: i ^ 1)
         away_b, kept_b = small_call(
@@ -656,7 +670,7 @@
             kept_b,
             came_b,
         )
-        returned = [beside, near, far]
+        returned = [came_a, near, far]
         late, backs = pair, 0
     else:
         came_a, kept_a, late = sum_over_dp(away_a, kept_a, cot_v)

time: 57.9 us -> 57.3 us (0.990)
  starting transfers between devices: 24.1 us -> 22.8 us
  waiting for transfers between devices: 16.3 us -> 17.5 us
  Pallas kernels: 15.9 us -> 15.1 us
    ppermute x13, starting transfers between devices: 24.1 us -> 22.8 us  [swap(): return lax.ppermute(array, axis, [(i, partner(i)) for i in range(devices)])]
    ppermute x13, waiting for transfers between devices: 16.3 us -> 17.5 us  [swap(): return lax.ppermute(array, axis, [(i, partner(i)) for i in range(devices)])]
    pallas_call x1, Pallas kernels: 6.79 us -> 6.09 us  [body(): pl.pallas_call(functools.partial(edge_kernel, ways, arrivals, four, block...]
  transfers between devices with their start and end apart: 13 -> 13, of which waited for: 5 -> 7; matrix products, arithmetic and copies ran while one was open for 0% -> 0% of each run, Pallas kernels for 12% -> 12%
where the time goes in v12:
time: 57.3 us; the launch traced here: 56.8 us
  starting transfers between devices  22.8 us (40%)
  waiting for transfers between devices  17.5 us (31%)
  Pallas kernels  15.1 us (26%)
  between operations  1.39 us (2%)
    ppermute x13, starting transfers between devices, swap(): return lax.ppermute(array, axis, [(i, partner(i)) for i in range(devices)])  22.8 us
    ppermute x13, waiting for transfers between devices, swap(): return lax.ppermute(array, axis, [(i, partner(i)) for i in range(devices)])  17.5 us
    pallas_call x1, Pallas kernels, body(): pl.pallas_call(functools.partial(edge_kernel, ways, arrivals, four, block...  6.09 us
    pallas_call x1, Pallas kernels, body(): pl.pallas_call(functools.partial(prep_kernel, parts, arrivals), out_shape...  2.42 us
    pallas_call x1, Pallas kernels, body(): pl.pallas_call(functools.partial(edge_grad_kernel, block, arrivals, four)...  2.21 us
    pallas_call x1, Pallas kernels, body(): pl.pallas_call(functools.partial(node_grad_kernel, arrivals, four), out_s...  2.13 us
  transfers between devices with their start and end apart: 13, of which 7 were waited for; matrix products, arithmetic and copies ran while one was open for 0% of the time, Pallas kernels for 12%

profile of v12, /device:TPU:0, one launch (start us, length us, event | category | flops | bytes accessed | tf_op | source)
XLA Modules:
  0.0 56.8 jit_solution(12788553206058189346)
XLA Ops:
  0.6 0.9 %pick_blocks.1 = (bf16[64,512]{1,0:T(8,128)(2,1)S(1)}, bf16[64,512]{1,0:T(8,128)(2,1)S(1)}, bf16[64,512]{1,0:T(8,128)(2,1)S(1)}) custom-call(s32[1,4]{1,0:T(1,128)} %boundary_hbm.3, bf16[128,512]{1,0:T(8,128)(2,1)} %bitcast.8), custom_call_target="tpu_custom_call" | custom-call | bytes 400000 | tf_op jit(solution)/shard_map/pick_blocks/pallas_call | solution.py:534
  1.6 0.7 %collective-permute-start = (bf16[64,512]{1,0:T(8,128)(2,1)S(1)}, bf16[64,512]{1,0:T(8,128)(2,1)S(1)}, u32[]{:S(2)}, u32[]{:S(2)}) collective-permute-start(bf16[64,512]{1,0:T(8,128)(2,1)S(1)} %get-tuple-element.38), channel_id=1, source_target_pairs={{0,0},{4,8},{8,4},{12,12},{1,1},{5,9},{9,5},{13,13},{2,2},{6,10},{... | collective-permute-start | bytes 196616 | tf_op jit(solution)/shard_map/ppermute | solution.py:428
  2.2 5.8 %collective-permute-start.1 = (bf16[64,512]{1,0:T(8,128)(2,1)S(1)}, bf16[64,512]{1,0:T(8,128)(2,1)S(1)}, u32[]{:S(2)}, u32[]{:S(2)}) collective-permute-start(bf16[64,512]{1,0:T(8,128)(2,1)S(1)} %get-tuple-element.39), channel_id=1, source_target_pairs={{0,8},{4,12},{8,0},{12,4},{1,9},{5,13},{9,1},{13,5},{2,10},{6,14},... | collective-permute-start | bytes 196616 | tf_op jit(solution)/shard_map/ppermute | solution.py:428
  8.0 0.2 collective-permute-start.2
  8.9 2.4 %prepare.1 = (bf16[128,512]{1,0:T(8,128)(2,1)S(1)}, bf16[768,512]{1,0:T(8,128)(2,1)S(1)}, bf16[128,512]{1,0:T(8,128)(2,1)S(1)}, bf16[1536,512]{1,0:T(8,128)(2,1)...) custom-call(s32[1]{0:T(128)S(6)} %copy.15.count_ref, ...), custom_call_target="tpu_custom_call" | custom-call | flops 402653184 | bytes 8000000 | tf_op jit(solution)/shard_map/prepare/pallas_call | solution.py:556
  11.3 0.0 collective-permute-done.refs_0_
  11.3 0.6 %collective-permute-done.1.refs_1_ = bf16[64,512]{1,0:T(8,128)(2,1)S(1)} collective-permute-done((bf16[64,512]{1,0:T(8,128)(2,1)S(1)}, bf16[64,512]{1,0:T(8,128)(2,1)S(1)}, u32[]{:S(2)}, u32[]{:S(2)}) %collective-permute-start.1) | collective-permute-done | bytes 65568 | tf_op jit(solution)/shard_map/ppermute | solution.py:428
  11.9 0.7 %collective-permute-done.2.refs_2_ = bf16[64,512]{1,0:T(8,128)(2,1)S(1)} collective-permute-done((bf16[64,512]{1,0:T(8,128)(2,1)S(1)}, bf16[64,512]{1,0:T(8,128)(2,1)S(1)}, u32[]{:S(2)}, u32[]{:S(2)}) %collective-permute-start.2) | collective-permute-done | bytes 65568 | tf_op jit(solution)/shard_map/ppermute | solution.py:428
  12.6 6.1 %edge_block.1 = (bf16[768,512]{1,0:T(8,128)(2,1)S(1)}, f32[768,512]{1,0:T(8,128)S(1)}, f32[512,512]{1,0:T(8,128)S(1)}, bf16[2,256,512]{2,1,0:T(8,128)(2,1)S(1)},...) custom-call(bf16[64,512]{1,0:T(8,128)(2,1)S(1)} %collective-permute-, ...), custom_call_target="tpu_custom_call" | custom-call | flops 2415919104 | bytes 12000000 | tf_op jit(solution)/shard_map/edge_block/pallas_call | solution.py:600
  18.7 0.1 collective-permute-start.3
  18.8 0.5 collective-permute-start.8
  19.2 1.4 %collective-permute-done.3.came_ref = bf16[2,256,512]{2,1,0:T(8,128)(2,1)S(1)} collective-permute-done((bf16[2,256,512]{2,1,0:T(8,128)(2,1)S(1)}, bf16[2,256,512]{2,1,0:T(8,128)(2,1)S(1)}, u32[]{:S(2)}, u32[]{:S(2)}) %collective-permute-start.3) | collective-permute-done | bytes 524320 | tf_op jit(solution)/shard_map/ppermute | solution.py:428
  20.6 0.1 halve.1
  20.7 1.5 %collective-permute-start.4 = (bf16[1,256,512]{2,1,0:T(8,128)(2,1)S(1)}, bf16[1,256,512]{2,1,0:T(8,128)(2,1)S(1)}, u32[]{:S(2)}, u32[]{:S(2)}) collective-permute-start(bf16[1,256,512]{2,1,0:T(8,128)(2,1)S(1)} %get-tuple-element.52), channel_id=1, source_target_pairs={{0,2},{1,3},{2,0},{3,1},{4,6},{5,7},{6,4},{7,5},{8,10},{9,11},{10,... | collective-permute-start | bytes 786440 | tf_op jit(solution)/shard_map/ppermute | solution.py:428
  22.3 0.1 beside_first.1
  22.4 0.8 %collective-permute-start.9 = (bf16[256,512]{1,0:T(8,128)(2,1)S(1)}, bf16[256,512]{1,0:T(8,128)(2,1)S(1)}, u32[]{:S(2)}, u32[]{:S(2)}) collective-permute-start(bf16[256,512]{1,0:T(8,128)(2,1)S(1)} %get-tuple-element.61), channel_id=1, source_target_pairs={{0,4},{4,0},{8,12},{12,8},{1,5},{5,1},{9,13},{13,9},{2,6},{6,2},{1... | collective-permute-start | bytes 786440 | tf_op jit(solution)/shard_map/ppermute | solution.py:428
  23.2 2.7 %collective-permute-start.5 = (bf16[64,512]{1,0:T(8,128)(2,1)S(1)}, bf16[64,512]{1,0:T(8,128)(2,1)S(1)}, u32[]{:S(2)}, u32[]{:S(2)}) collective-permute-start(bf16[64,512]{1,0:T(8,128)(2,1)S(1)} %get-tuple-element.55), channel_id=1, source_target_pairs={{0,8},{4,12},{8,0},{12,4},{1,9},{5,13},{9,1},{13,5},{2,10},{6,14},... | collective-permute-start | bytes 196616 | tf_op jit(solution)/shard_map/ppermute | solution.py:428
  25.9 0.7 %collective-permute-start.6 = (bf16[64,512]{1,0:T(8,128)(2,1)S(1)}, bf16[64,512]{1,0:T(8,128)(2,1)S(1)}, u32[]{:S(2)}, u32[]{:S(2)}) collective-permute-start(bf16[64,512]{1,0:T(8,128)(2,1)S(1)} %get-tuple-element.56), channel_id=1, source_target_pairs={{0,0},{4,8},{8,4},{12,12},{1,1},{5,9},{9,5},{13,13},{2,2},{6,10},{... | collective-permute-start | bytes 196616 | tf_op jit(solution)/shard_map/ppermute | solution.py:428
  26.6 3.6 %collective-permute-done.5.refs_0_.refs_2_ = bf16[64,512]{1,0:T(8,128)(2,1)S(1)} collective-permute-done((bf16[64,512]{1,0:T(8,128)(2,1)S(1)}, bf16[64,512]{1,0:T(8,128)(2,1)S(1)}, u32[]{:S(2)}, u32[]{:S(2)}) %collective-permute-start.5) | collective-permute-done | bytes 65568 | tf_op jit(solution)/shard_map/ppermute | solution.py:428
  30.2 0.0 collective-permute-done.6.refs_1_
  30.2 3.5 %collective-permute-start.7 = (bf16[192,512]{1,0:T(8,128)(2,1)S(1)}, bf16[192,512]{1,0:T(8,128)(2,1)S(1)}, u32[]{:S(2)}, u32[]{:S(2)}) collective-permute-start(bf16[192,512]{1,0:T(8,128)(2,1)S(1)} %get-tuple-element.58), channel_id=1, source_target_pairs={{0,4},{4,0},{8,12},{12,8},{1,5},{5,1},{9,13},{13,9},{2,6},{6,2},{1... | collective-permute-start | bytes 589832 | tf_op jit(solution)/shard_map/ppermute | solution.py:428
  33.8 0.9 %collective-permute-start.10 = (bf16[128,512]{1,0:T(8,128)(2,1)S(1)}, bf16[128,512]{1,0:T(8,128)(2,1)S(1)}, u32[]{:S(2)}, u32[]{:S(2)}) collective-permute-start(bf16[128,512]{1,0:T(8,128)(2,1)S(1)} %get-tuple-element.64), channel_id=1, source_target_pairs={{0,2},{1,3},{2,0},{3,1},{4,6},{5,7},{6,4},{7,5},{8,10},{9,11},{10,... | collective-permute-start | bytes 393224 | tf_op jit(solution)/shard_map/ppermute | solution.py:428
  34.8 4.1 %collective-permute-done.10.came_b = bf16[128,512]{1,0:T(8,128)(2,1)S(1)} collective-permute-done((bf16[128,512]{1,0:T(8,128)(2,1)S(1)}, bf16[128,512]{1,0:T(8,128)(2,1)S(1)}, u32[]{:S(2)}, u32[]{:S(2)}) %collective-permute-start.10) | collective-permute-done | bytes 131104 | tf_op jit(solution)/shard_map/ppermute | solution.py:428
  38.9 0.1 add_terms.1.after
  38.9 1.4 %collective-permute-start.11 = (bf16[256,512]{1,0:T(8,128)(2,1)S(1)}, bf16[256,512]{1,0:T(8,128)(2,1)S(1)}, u32[]{:S(2)}, u32[]{:S(2)}) collective-permute-start(bf16[256,512]{1,0:T(8,128)(2,1)S(1)} %add_terms.1.after), channel_id=1, source_target_pairs={{0,12},{4,8},{8,4},{12,0},{1,13},{5,9},{9,5},{13,1},{2,14},{6,10},... | collective-permute-start | bytes 786440 | tf_op jit(solution)/shard_map/ppermute | solution.py:428
  40.4 6.9 %collective-permute-done.11 = bf16[256,512]{1,0:T(8,128)(2,1)S(1)} collective-permute-done((bf16[256,512]{1,0:T(8,128)(2,1)S(1)}, bf16[256,512]{1,0:T(8,128)(2,1)S(1)}, u32[]{:S(2)}, u32[]{:S(2)}) %collective-permute-start.11) | collective-permute-done | bytes 262176 | tf_op jit(solution)/shard_map/ppermute | solution.py:428
  47.2 0.1 add_convert_fusion.own_ref
  47.3 3.9 %collective-permute-start.12 = (bf16[256,512]{1,0:T(8,128)(2,1)S(1)}, bf16[256,512]{1,0:T(8,128)(2,1)S(1)}, u32[]{:S(2)}, u32[]{:S(2)}) collective-permute-start(bf16[256,512]{1,0:T(8,128)(2,1)S(1)} %add_convert_fusion.own_ref), channel_id=1, source_target_pairs={{0,4},{4,0},{8,12},{12,8},{1,5},{5,1},{9,13},{13,9},{2,6},{6,2},{1... | collective-permute-start | bytes 786440 | tf_op jit(solution)/shard_map/ppermute | solution.py:428
  51.2 2.1 %node_grads.1.node_out = bf16[128,512]{1,0:T(8,128)(2,1)} custom-call(s32[1,4]{1,0:T(1,128)} %boundary_hbm.3, bf16[256,512]{1,0:T(8,128)(2,1)S(1)} %add_terms.1.after, f32[512,512]{1,0:T(8,128)S(1)} %get-tuple-element.54.sums_ref, bf16[1536,512]{1,0:T(8,128)(2,1)S(1)} %get-tuple-element.43.refs_5_.win_ref, ...), custom_call_target="tpu_custom_call" | custom-call | flops 268435456 | bytes 2000000 | tf_op jit(solution)/shard_map/node_grads/pallas_call | solution.py:707
  53.3 2.2 %edge_grads.1 = (bf16[768,512]{1,0:T(8,128)(2,1)}, bf16[128,512]{1,0:T(8,128)(2,1)}) custom-call(s32[12]{0:T(128)} %dst_hbm.3, s32[1]{0:T(128)S(6)} %copy.15.count_ref, bf16[256,512]{1,0:T(8,128)(2,1)S(1)} %add_terms.1.after, bf16[768,512]{1,0:T(8,128)(2,1)S(1)} %get-tuple-element.65.gpre_ref, f32[512,512]{1,0:T(8,128)S(1)} %get-tuple-element.54.sums_ref, ...), custom_call_target="tpu_custom_call" | custom-call | flops 402653184 | bytes 3000000 | tf_op jit(solution)/shard_map/edge_grads/pallas_call | solution.py:679
  55.5 0.3 collective-permute-done.12.other_ref
  55.8 1.0 %widen.1 = (f32[384,512]{1,0:T(8,128)}, f32[128,512]{1,0:T(8,128)}) custom-call(bf16[128,512]{1,0:T(8,128)(2,1)} %node_grads.1.node_out, bf16[768,512]{1,0:T(8,128)(2,1)} %get-tuple-element.68.edge_grad, bf16[256,512]{1,0:T(8,128)(2,1)S(1)} %add_convert_fusion.own_ref, bf16[256,512]{1,0:T(8,128)(2,1)S(1)} %collective-permute-done.12.other_ref), custom_call_target="tpu_custom_call" | custom-call | bytes 1500000 | tf_op jit(solution)/shard_map/widen/pallas_call | solution.py:724
  (6 shorter events, 0.1 us)
Async XLA Ops:
  1.6 9.7 %collective-permute-start = (bf16[64,512]{1,0:T(8,128)(2,1)S(1)}, bf16[64,512]{1,0:T(8,128)(2,1)S(1)}, u32[]{:S(2)}, u32[]{:S(2)}) collective-permute-start(bf16[64,512]{1,0:T(8,128)(2,1)S(1)} %get-tuple-element.38), channel_id=1, source_target_pairs={{0,0},{4,8},{8,4},{12,12},{1,1},{5,9},{9,5},{13,13},{2,2},{6,10},{... | collective-permute-start | bytes 196616 | tf_op jit(solution)/shard_map/ppermute | solution.py:428
  2.2 9.6 %collective-permute-start.1 = (bf16[64,512]{1,0:T(8,128)(2,1)S(1)}, bf16[64,512]{1,0:T(8,128)(2,1)S(1)}, u32[]{:S(2)}, u32[]{:S(2)}) collective-permute-start(bf16[64,512]{1,0:T(8,128)(2,1)S(1)} %get-tuple-element.39), channel_id=1, source_target_pairs={{0,8},{4,12},{8,0},{12,4},{1,9},{5,13},{9,1},{13,5},{2,10},{6,14},... | collective-permute-start | bytes 196616 | tf_op jit(solution)/shard_map/ppermute | solution.py:428
  8.0 4.5 %collective-permute-start.2 = (bf16[64,512]{1,0:T(8,128)(2,1)S(1)}, bf16[64,512]{1,0:T(8,128)(2,1)S(1)}, u32[]{:S(2)}, u32[]{:S(2)}) collective-permute-start(bf16[64,512]{1,0:T(8,128)(2,1)S(1)} %get-tuple-element.40), channel_id=1, source_target_pairs={{0,4},{4,0},{8,12},{12,8},{1,5},{5,1},{9,13},{13,9},{2,6},{6,2},{1... | collective-permute-start | bytes 196616 | tf_op jit(solution)/shard_map/ppermute | solution.py:428
  18.7 2.0 %collective-permute-start.3 = (bf16[2,256,512]{2,1,0:T(8,128)(2,1)S(1)}, bf16[2,256,512]{2,1,0:T(8,128)(2,1)S(1)}, u32[]{:S(2)}, u32[]{:S(2)}) collective-permute-start(bf16[2,256,512]{2,1,0:T(8,128)(2,1)S(1)} %get-tuple-element.49), channel_id=1, source_target_pairs={{0,1},{1,0},{2,3},{3,2},{4,5},{5,4},{6,7},{7,6},{8,9},{9,8},{10,11... | collective-permute-start | bytes 1572872 | tf_op jit(solution)/shard_map/ppermute | solution.py:428
  18.8 3.5 %collective-permute-start.8 = (bf16[2,256,512]{2,1,0:T(8,128)(2,1)S(1)}, bf16[2,256,512]{2,1,0:T(8,128)(2,1)S(1)}, u32[]{:S(2)}, u32[]{:S(2)}) collective-permute-start(bf16[2,256,512]{2,1,0:T(8,128)(2,1)S(1)} %get-tuple-element.59), channel_id=1, source_target_pairs={{0,1},{1,0},{2,3},{3,2},{4,5},{5,4},{6,7},{7,6},{8,9},{9,8},{10,11... | collective-permute-start | bytes 1572872 | tf_op jit(solution)/shard_map/ppermute | solution.py:428
  20.7 9.4 %collective-permute-start.4 = (bf16[1,256,512]{2,1,0:T(8,128)(2,1)S(1)}, bf16[1,256,512]{2,1,0:T(8,128)(2,1)S(1)}, u32[]{:S(2)}, u32[]{:S(2)}) collective-permute-start(bf16[1,256,512]{2,1,0:T(8,128)(2,1)S(1)} %get-tuple-element.52), channel_id=1, source_target_pairs={{0,2},{1,3},{2,0},{3,1},{4,6},{5,7},{6,4},{7,5},{8,10},{9,11},{10,... | collective-permute-start | bytes 786440 | tf_op jit(solution)/shard_map/ppermute | solution.py:428
  22.4 11.4 %collective-permute-start.9 = (bf16[256,512]{1,0:T(8,128)(2,1)S(1)}, bf16[256,512]{1,0:T(8,128)(2,1)S(1)}, u32[]{:S(2)}, u32[]{:S(2)}) collective-permute-start(bf16[256,512]{1,0:T(8,128)(2,1)S(1)} %get-tuple-element.61), channel_id=1, source_target_pairs={{0,4},{4,0},{8,12},{12,8},{1,5},{5,1},{9,13},{13,9},{2,6},{6,2},{1... | collective-permute-start | bytes 786440 | tf_op jit(solution)/shard_map/ppermute | solution.py:428
  23.2 7.0 %collective-permute-start.5 = (bf16[64,512]{1,0:T(8,128)(2,1)S(1)}, bf16[64,512]{1,0:T(8,128)(2,1)S(1)}, u32[]{:S(2)}, u32[]{:S(2)}) collective-permute-start(bf16[64,512]{1,0:T(8,128)(2,1)S(1)} %get-tuple-element.55), channel_id=1, source_target_pairs={{0,8},{4,12},{8,0},{12,4},{1,9},{5,13},{9,1},{13,5},{2,10},{6,14},... | collective-permute-start | bytes 196616 | tf_op jit(solution)/shard_map/ppermute | solution.py:428
  25.9 4.3 %collective-permute-start.6 = (bf16[64,512]{1,0:T(8,128)(2,1)S(1)}, bf16[64,512]{1,0:T(8,128)(2,1)S(1)}, u32[]{:S(2)}, u32[]{:S(2)}) collective-permute-start(bf16[64,512]{1,0:T(8,128)(2,1)S(1)} %get-tuple-element.56), channel_id=1, source_target_pairs={{0,0},{4,8},{8,4},{12,12},{1,1},{5,9},{9,5},{13,13},{2,2},{6,10},{... | collective-permute-start | bytes 196616 | tf_op jit(solution)/shard_map/ppermute | solution.py:428
  30.2 8.6 %collective-permute-start.7 = (bf16[192,512]{1,0:T(8,128)(2,1)S(1)}, bf16[192,512]{1,0:T(8,128)(2,1)S(1)}, u32[]{:S(2)}, u32[]{:S(2)}) collective-permute-start(bf16[192,512]{1,0:T(8,128)(2,1)S(1)} %get-tuple-element.58), channel_id=1, source_target_pairs={{0,4},{4,0},{8,12},{12,8},{1,5},{5,1},{9,13},{13,9},{2,6},{6,2},{1... | collective-permute-start | bytes 589832 | tf_op jit(solution)/shard_map/ppermute | solution.py:428
  33.8 5.0 %collective-permute-start.10 = (bf16[128,512]{1,0:T(8,128)(2,1)S(1)}, bf16[128,512]{1,0:T(8,128)(2,1)S(1)}, u32[]{:S(2)}, u32[]{:S(2)}) collective-permute-start(bf16[128,512]{1,0:T(8,128)(2,1)S(1)} %get-tuple-element.64), channel_id=1, source_target_pairs={{0,2},{1,3},{2,0},{3,1},{4,6},{5,7},{6,4},{7,5},{8,10},{9,11},{10,... | collective-permute-start | bytes 393224 | tf_op jit(solution)/shard_map/ppermute | solution.py:428
  38.9 8.3 %collective-permute-start.11 = (bf16[256,512]{1,0:T(8,128)(2,1)S(1)}, bf16[256,512]{1,0:T(8,128)(2,1)S(1)}, u32[]{:S(2)}, u32[]{:S(2)}) collective-permute-start(bf16[256,512]{1,0:T(8,128)(2,1)S(1)} %add_terms.1.after), channel_id=1, source_target_pairs={{0,12},{4,8},{8,4},{12,0},{1,13},{5,9},{9,5},{13,1},{2,14},{6,10},... | collective-permute-start | bytes 786440 | tf_op jit(solution)/shard_map/ppermute | solution.py:428
  47.3 8.5 %collective-permute-start.12 = (bf16[256,512]{1,0:T(8,128)(2,1)S(1)}, bf16[256,512]{1,0:T(8,128)(2,1)S(1)}, u32[]{:S(2)}, u32[]{:S(2)}) collective-permute-start(bf16[256,512]{1,0:T(8,128)(2,1)S(1)} %add_convert_fusion.own_ref), channel_id=1, source_target_pairs={{0,4},{4,0},{8,12},{12,8},{1,5},{5,1},{9,13},{13,9},{2,6},{6,2},{1... | collective-permute-start | bytes 786440 | tf_op jit(solution)/shard_map/ppermute | solution.py:428

commit v13 on v12

--- a/solution.py
+++ b/solution.py
@@ -236,7 +236,7 @@
     if filled < extent:
         ext_ref[filled:, :] = jnp.zeros((extent - filled, latent), BF16)
 
-    span = 384 if edges % 384 == 0 else block
+    span = edges
     for start in range(0, edges, span):
         rows = slice(start, start + span)
         senders = dot(hot_ref[rows, :], ext_ref[...]).astype(BF16)
@@ -654,7 +654,6 @@
             kept_a,
             sums,
             far,
-            near,
         )
         came_a = swap(away_a, "dom", lambda i: i ^ 1)
         away_b, kept_b = small_call(
@@ -669,6 +668,7 @@
             came_a,
             kept_b,
             came_b,
+            near,
         )
         returned = [came_a, near, far]
         late, backs = pair, 0

time: 57.3 us -> 60.2 us (1.051)
  starting transfers between devices: 22.8 us -> 24.6 us
  waiting for transfers between devices: 17.5 us -> 19.2 us
    ppermute x13, starting transfers between devices: 22.8 us -> 24.6 us  [swap(): return lax.ppermute(array, axis, [(i, partner(i)) for i in range(devices)])]
    ppermute x13, waiting for transfers between devices: 17.5 us -> 19.2 us  [swap(): return lax.ppermute(array, axis, [(i, partner(i)) for i in range(devices)])]
where the time goes in v13:
time: 60.2 us; the launch traced here: 60 us
  starting transfers between devices  24.6 us (41%)
  waiting for transfers between devices  19.2 us (32%)
  Pallas kernels  14.8 us (25%)
  between operations  1.4 us (2%)
    ppermute x13, starting transfers between devices, swap(): return lax.ppermute(array, axis, [(i, partner(i)) for i in range(devices)])  24.6 us
    ppermute x13, waiting for transfers between devices, swap(): return lax.ppermute(array, axis, [(i, partner(i)) for i in range(devices)])  19.2 us
    pallas_call x1, Pallas kernels, body(): pl.pallas_call(functools.partial(edge_kernel, ways, arrivals, four, block...  5.75 us
    pallas_call x1, Pallas kernels, body(): pl.pallas_call(functools.partial(prep_kernel, parts, arrivals), out_shape...  2.42 us
    pallas_call x1, Pallas kernels, body(): pl.pallas_call(functools.partial(edge_grad_kernel, block, arrivals, four)...  2.21 us
    pallas_call x1, Pallas kernels, body(): pl.pallas_call(functools.partial(node_grad_kernel, arrivals, four), out_s...  2.13 us
  transfers between devices with their start and end apart: 13, of which 7 were waited for; matrix products, arithmetic and copies ran while one was open for 0% of the time, Pallas kernels for 12%

profile of v13, /device:TPU:0, one launch (start us, length us, event | category | flops | bytes accessed | tf_op | source)
XLA Modules:
  0.0 60.0 jit_solution(15704416169207608174)
XLA Ops:
  0.6 0.9 %pick_blocks.1 = (bf16[64,512]{1,0:T(8,128)(2,1)S(1)}, bf16[64,512]{1,0:T(8,128)(2,1)S(1)}, bf16[64,512]{1,0:T(8,128)(2,1)S(1)}) custom-call(s32[1,4]{1,0:T(1,128)} %boundary_hbm.3, bf16[128,512]{1,0:T(8,128)(2,1)} %bitcast.8), custom_call_target="tpu_custom_call" | custom-call | bytes 400000 | tf_op jit(solution)/shard_map/pick_blocks/pallas_call | solution.py:534
  1.6 0.7 %collective-permute-start = (bf16[64,512]{1,0:T(8,128)(2,1)S(1)}, bf16[64,512]{1,0:T(8,128)(2,1)S(1)}, u32[]{:S(2)}, u32[]{:S(2)}) collective-permute-start(bf16[64,512]{1,0:T(8,128)(2,1)S(1)} %get-tuple-element.38), channel_id=1, source_target_pairs={{0,0},{4,8},{8,4},{12,12},{1,1},{5,9},{9,5},{13,13},{2,2},{6,10},{... | collective-permute-start | bytes 196616 | tf_op jit(solution)/shard_map/ppermute | solution.py:428
  2.2 5.8 %collective-permute-start.1 = (bf16[64,512]{1,0:T(8,128)(2,1)S(1)}, bf16[64,512]{1,0:T(8,128)(2,1)S(1)}, u32[]{:S(2)}, u32[]{:S(2)}) collective-permute-start(bf16[64,512]{1,0:T(8,128)(2,1)S(1)} %get-tuple-element.39), channel_id=1, source_target_pairs={{0,8},{4,12},{8,0},{12,4},{1,9},{5,13},{9,1},{13,5},{2,10},{6,14},... | collective-permute-start | bytes 196616 | tf_op jit(solution)/shard_map/ppermute | solution.py:428
  8.0 0.2 collective-permute-start.2
  8.9 2.4 %prepare.1 = (bf16[128,512]{1,0:T(8,128)(2,1)S(1)}, bf16[768,512]{1,0:T(8,128)(2,1)S(1)}, bf16[128,512]{1,0:T(8,128)(2,1)S(1)}, bf16[1536,512]{1,0:T(8,128)(2,1)...) custom-call(s32[1]{0:T(128)S(6)} %copy.15.count_ref, ...), custom_call_target="tpu_custom_call" | custom-call | flops 402653184 | bytes 8000000 | tf_op jit(solution)/shard_map/prepare/pallas_call | solution.py:556
  11.3 0.0 collective-permute-done.refs_0_
  11.3 0.6 collective-permute-done.1.refs_1_
  11.9 0.7 %collective-permute-done.2.refs_2_ = bf16[64,512]{1,0:T(8,128)(2,1)S(1)} collective-permute-done((bf16[64,512]{1,0:T(8,128)(2,1)S(1)}, bf16[64,512]{1,0:T(8,128)(2,1)S(1)}, u32[]{:S(2)}, u32[]{:S(2)}) %collective-permute-start.2) | collective-permute-done | bytes 65568 | tf_op jit(solution)/shard_map/ppermute | solution.py:428
  12.6 5.7 %edge_block.1 = (bf16[768,512]{1,0:T(8,128)(2,1)S(1)}, f32[768,512]{1,0:T(8,128)S(1)}, f32[512,512]{1,0:T(8,128)S(1)}, bf16[2,256,512]{2,1,0:T(8,128)(2,1)S(1)},...) custom-call(bf16[64,512]{1,0:T(8,128)(2,1)S(1)} %collective-permute-, ...), custom_call_target="tpu_custom_call" | custom-call | flops 2415919104 | bytes 12000000 | tf_op jit(solution)/shard_map/edge_block/pallas_call | solution.py:600
  18.3 0.1 collective-permute-start.3
  18.4 0.5 collective-permute-start.7
  18.9 1.4 %collective-permute-done.3.came_ref = bf16[2,256,512]{2,1,0:T(8,128)(2,1)S(1)} collective-permute-done((bf16[2,256,512]{2,1,0:T(8,128)(2,1)S(1)}, bf16[2,256,512]{2,1,0:T(8,128)(2,1)S(1)}, u32[]{:S(2)}, u32[]{:S(2)}) %collective-permute-start.3) | collective-permute-done | bytes 524320 | tf_op jit(solution)/shard_map/ppermute | solution.py:428
  20.3 0.1 halve.1
  20.4 1.5 %collective-permute-start.4 = (bf16[1,256,512]{2,1,0:T(8,128)(2,1)S(1)}, bf16[1,256,512]{2,1,0:T(8,128)(2,1)S(1)}, u32[]{:S(2)}, u32[]{:S(2)}) collective-permute-start(bf16[1,256,512]{2,1,0:T(8,128)(2,1)S(1)} %get-tuple-element.52), channel_id=1, source_target_pairs={{0,2},{1,3},{2,0},{3,1},{4,6},{5,7},{6,4},{7,5},{8,10},{9,11},{10,... | collective-permute-start | bytes 786440 | tf_op jit(solution)/shard_map/ppermute | solution.py:428
  21.9 0.1 beside_first.1
  22.0 0.8 %collective-permute-start.8 = (bf16[256,512]{1,0:T(8,128)(2,1)S(1)}, bf16[256,512]{1,0:T(8,128)(2,1)S(1)}, u32[]{:S(2)}, u32[]{:S(2)}) collective-permute-start(bf16[256,512]{1,0:T(8,128)(2,1)S(1)} %get-tuple-element.60), channel_id=1, source_target_pairs={{0,4},{4,0},{8,12},{12,8},{1,5},{5,1},{9,13},{13,9},{2,6},{6,2},{1... | collective-permute-start | bytes 786440 | tf_op jit(solution)/shard_map/ppermute | solution.py:428
  22.9 2.7 %collective-permute-start.5 = (bf16[64,512]{1,0:T(8,128)(2,1)S(1)}, bf16[64,512]{1,0:T(8,128)(2,1)S(1)}, u32[]{:S(2)}, u32[]{:S(2)}) collective-permute-start(bf16[64,512]{1,0:T(8,128)(2,1)S(1)} %get-tuple-element.55), channel_id=1, source_target_pairs={{0,8},{4,12},{8,0},{12,4},{1,9},{5,13},{9,1},{13,5},{2,10},{6,14},... | collective-permute-start | bytes 196616 | tf_op jit(solution)/shard_map/ppermute | solution.py:428
  25.6 4.3 %collective-permute-done.5.refs_0_.refs_2_ = bf16[64,512]{1,0:T(8,128)(2,1)S(1)} collective-permute-done((bf16[64,512]{1,0:T(8,128)(2,1)S(1)}, bf16[64,512]{1,0:T(8,128)(2,1)S(1)}, u32[]{:S(2)}, u32[]{:S(2)}) %collective-permute-start.5) | collective-permute-done | bytes 65568 | tf_op jit(solution)/shard_map/ppermute | solution.py:428
  29.8 0.0 collective-permute-done.4.came_ref
  29.9 3.5 %collective-permute-start.6 = (bf16[192,512]{1,0:T(8,128)(2,1)S(1)}, bf16[192,512]{1,0:T(8,128)(2,1)S(1)}, u32[]{:S(2)}, u32[]{:S(2)}) collective-permute-start(bf16[192,512]{1,0:T(8,128)(2,1)S(1)} %get-tuple-element.57), channel_id=1, source_target_pairs={{0,4},{4,0},{8,12},{12,8},{1,5},{5,1},{9,13},{13,9},{2,6},{6,2},{1... | collective-permute-start | bytes 589832 | tf_op jit(solution)/shard_map/ppermute | solution.py:428
  33.5 0.9 %collective-permute-start.9 = (bf16[128,512]{1,0:T(8,128)(2,1)S(1)}, bf16[128,512]{1,0:T(8,128)(2,1)S(1)}, u32[]{:S(2)}, u32[]{:S(2)}) collective-permute-start(bf16[128,512]{1,0:T(8,128)(2,1)S(1)} %get-tuple-element.63), channel_id=1, source_target_pairs={{0,2},{1,3},{2,0},{3,1},{4,6},{5,7},{6,4},{7,5},{8,10},{9,11},{10,... | collective-permute-start | bytes 393224 | tf_op jit(solution)/shard_map/ppermute | solution.py:428
  34.4 0.7 %collective-permute-start.10 = (bf16[64,512]{1,0:T(8,128)(2,1)S(1)}, bf16[64,512]{1,0:T(8,128)(2,1)S(1)}, u32[]{:S(2)}, u32[]{:S(2)}) collective-permute-start(bf16[64,512]{1,0:T(8,128)(2,1)S(1)} %get-tuple-element.64), channel_id=1, source_target_pairs={{0,0},{4,8},{8,4},{12,12},{1,1},{5,9},{9,5},{13,13},{2,2},{6,10},{... | collective-permute-start | bytes 196616 | tf_op jit(solution)/shard_map/ppermute | solution.py:428
  35.1 3.4 %collective-permute-done.9.came_b = bf16[128,512]{1,0:T(8,128)(2,1)S(1)} collective-permute-done((bf16[128,512]{1,0:T(8,128)(2,1)S(1)}, bf16[128,512]{1,0:T(8,128)(2,1)S(1)}, u32[]{:S(2)}, u32[]{:S(2)}) %collective-permute-start.9) | collective-permute-done | bytes 131104 | tf_op jit(solution)/shard_map/ppermute | solution.py:428
  38.5 0.1 add_terms.1.after
  38.6 1.4 %collective-permute-start.11 = (bf16[256,512]{1,0:T(8,128)(2,1)S(1)}, bf16[256,512]{1,0:T(8,128)(2,1)S(1)}, u32[]{:S(2)}, u32[]{:S(2)}) collective-permute-start(bf16[256,512]{1,0:T(8,128)(2,1)S(1)} %add_terms.1.after), channel_id=1, source_target_pairs={{0,12},{4,8},{8,4},{12,0},{1,13},{5,9},{9,5},{13,1},{2,14},{6,10},... | collective-permute-start | bytes 786440 | tf_op jit(solution)/shard_map/ppermute | solution.py:428
  40.0 6.8 %collective-permute-done.11 = bf16[256,512]{1,0:T(8,128)(2,1)S(1)} collective-permute-done((bf16[256,512]{1,0:T(8,128)(2,1)S(1)}, bf16[256,512]{1,0:T(8,128)(2,1)S(1)}, u32[]{:S(2)}, u32[]{:S(2)}) %collective-permute-start.11) | collective-permute-done | bytes 262176 | tf_op jit(solution)/shard_map/ppermute | solution.py:428
  46.9 0.1 add_convert_fusion.own_ref
  46.9 5.7 %collective-permute-start.12 = (bf16[256,512]{1,0:T(8,128)(2,1)S(1)}, bf16[256,512]{1,0:T(8,128)(2,1)S(1)}, u32[]{:S(2)}, u32[]{:S(2)}) collective-permute-start(bf16[256,512]{1,0:T(8,128)(2,1)S(1)} %add_convert_fusion.own_ref), channel_id=1, source_target_pairs={{0,4},{4,0},{8,12},{12,8},{1,5},{5,1},{9,13},{13,9},{2,6},{6,2},{1... | collective-permute-start | bytes 786440 | tf_op jit(solution)/shard_map/ppermute | solution.py:428
  52.6 2.1 %node_grads.1.node_out = bf16[128,512]{1,0:T(8,128)(2,1)} custom-call(s32[1,4]{1,0:T(1,128)} %boundary_hbm.3, bf16[256,512]{1,0:T(8,128)(2,1)S(1)} %add_terms.1.after, f32[512,512]{1,0:T(8,128)S(1)} %get-tuple-element.54.sums_ref, bf16[1536,512]{1,0:T(8,128)(2,1)S(1)} %get-tuple-element.43.refs_5_.win_ref, ...), custom_call_target="tpu_custom_call" | custom-call | flops 268435456 | bytes 2000000 | tf_op jit(solution)/shard_map/node_grads/pallas_call | solution.py:707
  54.8 2.2 %edge_grads.1 = (bf16[768,512]{1,0:T(8,128)(2,1)}, bf16[128,512]{1,0:T(8,128)(2,1)}) custom-call(s32[12]{0:T(128)} %dst_hbm.3, s32[1]{0:T(128)S(6)} %copy.15.count_ref, bf16[256,512]{1,0:T(8,128)(2,1)S(1)} %add_terms.1.after, bf16[768,512]{1,0:T(8,128)(2,1)S(1)} %get-tuple-element.65.gpre_ref, f32[512,512]{1,0:T(8,128)S(1)} %get-tuple-element.54.sums_ref, ...), custom_call_target="tpu_custom_call" | custom-call | flops 402653184 | bytes 3000000 | tf_op jit(solution)/shard_map/edge_grads/pallas_call | solution.py:679
  57.0 2.0 %collective-permute-done.12.other_ref = bf16[256,512]{1,0:T(8,128)(2,1)S(1)} collective-permute-done((bf16[256,512]{1,0:T(8,128)(2,1)S(1)}, bf16[256,512]{1,0:T(8,128)(2,1)S(1)}, u32[]{:S(2)}, u32[]{:S(2)}) %collective-permute-start.12) | collective-permute-done | bytes 262176 | tf_op jit(solution)/shard_map/ppermute | solution.py:428
  59.0 1.0 %widen.1 = (f32[384,512]{1,0:T(8,128)}, f32[128,512]{1,0:T(8,128)}) custom-call(bf16[128,512]{1,0:T(8,128)(2,1)} %node_grads.1.node_out, bf16[768,512]{1,0:T(8,128)(2,1)} %get-tuple-element.68.edge_grad, bf16[256,512]{1,0:T(8,128)(2,1)S(1)} %add_convert_fusion.own_ref, bf16[256,512]{1,0:T(8,128)(2,1)S(1)} %collective-permute-done.12.other_ref), custom_call_target="tpu_custom_call" | custom-call | bytes 1500000 | tf_op jit(solution)/shard_map/widen/pallas_call | solution.py:724
  (6 shorter events, 0.1 us)
Async XLA Ops:
  1.6 9.7 %collective-permute-start = (bf16[64,512]{1,0:T(8,128)(2,1)S(1)}, bf16[64,512]{1,0:T(8,128)(2,1)S(1)}, u32[]{:S(2)}, u32[]{:S(2)}) collective-permute-start(bf16[64,512]{1,0:T(8,128)(2,1)S(1)} %get-tuple-element.38), channel_id=1, source_target_pairs={{0,0},{4,8},{8,4},{12,12},{1,1},{5,9},{9,5},{13,13},{2,2},{6,10},{... | collective-permute-start | bytes 196616 | tf_op jit(solution)/shard_map/ppermute | solution.py:428
  2.2 9.6 %collective-permute-start.1 = (bf16[64,512]{1,0:T(8,128)(2,1)S(1)}, bf16[64,512]{1,0:T(8,128)(2,1)S(1)}, u32[]{:S(2)}, u32[]{:S(2)}) collective-permute-start(bf16[64,512]{1,0:T(8,128)(2,1)S(1)} %get-tuple-element.39), channel_id=1, source_target_pairs={{0,8},{4,12},{8,0},{12,4},{1,9},{5,13},{9,1},{13,5},{2,10},{6,14},... | collective-permute-start | bytes 196616 | tf_op jit(solution)/shard_map/ppermute | solution.py:428
  8.0 4.5 %collective-permute-start.2 = (bf16[64,512]{1,0:T(8,128)(2,1)S(1)}, bf16[64,512]{1,0:T(8,128)(2,1)S(1)}, u32[]{:S(2)}, u32[]{:S(2)}) collective-permute-start(bf16[64,512]{1,0:T(8,128)(2,1)S(1)} %get-tuple-element.40), channel_id=1, source_target_pairs={{0,4},{4,0},{8,12},{12,8},{1,5},{5,1},{9,13},{13,9},{2,6},{6,2},{1... | collective-permute-start | bytes 196616 | tf_op jit(solution)/shard_map/ppermute | solution.py:428
  18.3 2.0 %collective-permute-start.3 = (bf16[2,256,512]{2,1,0:T(8,128)(2,1)S(1)}, bf16[2,256,512]{2,1,0:T(8,128)(2,1)S(1)}, u32[]{:S(2)}, u32[]{:S(2)}) collective-permute-start(bf16[2,256,512]{2,1,0:T(8,128)(2,1)S(1)} %get-tuple-element.49), channel_id=1, source_target_pairs={{0,1},{1,0},{2,3},{3,2},{4,5},{5,4},{6,7},{7,6},{8,9},{9,8},{10,11... | collective-permute-start | bytes 1572872 | tf_op jit(solution)/shard_map/ppermute | solution.py:428
  18.4 3.5 %collective-permute-start.7 = (bf16[2,256,512]{2,1,0:T(8,128)(2,1)S(1)}, bf16[2,256,512]{2,1,0:T(8,128)(2,1)S(1)}, u32[]{:S(2)}, u32[]{:S(2)}) collective-permute-start(bf16[2,256,512]{2,1,0:T(8,128)(2,1)S(1)} %get-tuple-element.58), channel_id=1, source_target_pairs={{0,1},{1,0},{2,3},{3,2},{4,5},{5,4},{6,7},{7,6},{8,9},{9,8},{10,11... | collective-permute-start | bytes 1572872 | tf_op jit(solution)/shard_map/ppermute | solution.py:428
  20.4 9.5 %collective-permute-start.4 = (bf16[1,256,512]{2,1,0:T(8,128)(2,1)S(1)}, bf16[1,256,512]{2,1,0:T(8,128)(2,1)S(1)}, u32[]{:S(2)}, u32[]{:S(2)}) collective-permute-start(bf16[1,256,512]{2,1,0:T(8,128)(2,1)S(1)} %get-tuple-element.52), channel_id=1, source_target_pairs={{0,2},{1,3},{2,0},{3,1},{4,6},{5,7},{6,4},{7,5},{8,10},{9,11},{10,... | collective-permute-start | bytes 786440 | tf_op jit(solution)/shard_map/ppermute | solution.py:428
  22.0 11.4 %collective-permute-start.8 = (bf16[256,512]{1,0:T(8,128)(2,1)S(1)}, bf16[256,512]{1,0:T(8,128)(2,1)S(1)}, u32[]{:S(2)}, u32[]{:S(2)}) collective-permute-start(bf16[256,512]{1,0:T(8,128)(2,1)S(1)} %get-tuple-element.60), channel_id=1, source_target_pairs={{0,4},{4,0},{8,12},{12,8},{1,5},{5,1},{9,13},{13,9},{2,6},{6,2},{1... | collective-permute-start | bytes 786440 | tf_op jit(solution)/shard_map/ppermute | solution.py:428
  22.9 7.0 %collective-permute-start.5 = (bf16[64,512]{1,0:T(8,128)(2,1)S(1)}, bf16[64,512]{1,0:T(8,128)(2,1)S(1)}, u32[]{:S(2)}, u32[]{:S(2)}) collective-permute-start(bf16[64,512]{1,0:T(8,128)(2,1)S(1)} %get-tuple-element.55), channel_id=1, source_target_pairs={{0,8},{4,12},{8,0},{12,4},{1,9},{5,13},{9,1},{13,5},{2,10},{6,14},... | collective-permute-start | bytes 196616 | tf_op jit(solution)/shard_map/ppermute | solution.py:428
  29.9 8.6 %collective-permute-start.6 = (bf16[192,512]{1,0:T(8,128)(2,1)S(1)}, bf16[192,512]{1,0:T(8,128)(2,1)S(1)}, u32[]{:S(2)}, u32[]{:S(2)}) collective-permute-start(bf16[192,512]{1,0:T(8,128)(2,1)S(1)} %get-tuple-element.57), channel_id=1, source_target_pairs={{0,4},{4,0},{8,12},{12,8},{1,5},{5,1},{9,13},{13,9},{2,6},{6,2},{1... | collective-permute-start | bytes 589832 | tf_op jit(solution)/shard_map/ppermute | solution.py:428
  33.5 5.0 %collective-permute-start.9 = (bf16[128,512]{1,0:T(8,128)(2,1)S(1)}, bf16[128,512]{1,0:T(8,128)(2,1)S(1)}, u32[]{:S(2)}, u32[]{:S(2)}) collective-permute-start(bf16[128,512]{1,0:T(8,128)(2,1)S(1)} %get-tuple-element.63), channel_id=1, source_target_pairs={{0,2},{1,3},{2,0},{3,1},{4,6},{5,7},{6,4},{7,5},{8,10},{9,11},{10,... | collective-permute-start | bytes 393224 | tf_op jit(solution)/shard_map/ppermute | solution.py:428
  34.4 0.7 %collective-permute-start.10 = (bf16[64,512]{1,0:T(8,128)(2,1)S(1)}, bf16[64,512]{1,0:T(8,128)(2,1)S(1)}, u32[]{:S(2)}, u32[]{:S(2)}) collective-permute-start(bf16[64,512]{1,0:T(8,128)(2,1)S(1)} %get-tuple-element.64), channel_id=1, source_target_pairs={{0,0},{4,8},{8,4},{12,12},{1,1},{5,9},{9,5},{13,13},{2,2},{6,10},{... | collective-permute-start | bytes 196616 | tf_op jit(solution)/shard_map/ppermute | solution.py:428
  38.6 8.3 %collective-permute-start.11 = (bf16[256,512]{1,0:T(8,128)(2,1)S(1)}, bf16[256,512]{1,0:T(8,128)(2,1)S(1)}, u32[]{:S(2)}, u32[]{:S(2)}) collective-permute-start(bf16[256,512]{1,0:T(8,128)(2,1)S(1)} %add_terms.1.after), channel_id=1, source_target_pairs={{0,12},{4,8},{8,4},{12,0},{1,13},{5,9},{9,5},{13,1},{2,14},{6,10},... | collective-permute-start | bytes 786440 | tf_op jit(solution)/shard_map/ppermute | solution.py:428
  46.9 12.0 %collective-permute-start.12 = (bf16[256,512]{1,0:T(8,128)(2,1)S(1)}, bf16[256,512]{1,0:T(8,128)(2,1)S(1)}, u32[]{:S(2)}, u32[]{:S(2)}) collective-permute-start(bf16[256,512]{1,0:T(8,128)(2,1)S(1)} %add_convert_fusion.own_ref), channel_id=1, source_target_pairs={{0,4},{4,0},{8,12},{12,8},{1,5},{5,1},{9,13},{13,9},{2,6},{6,2},{1... | collective-permute-start | bytes 786440 | tf_op jit(solution)/shard_map/ppermute | solution.py:428

commit v14 on v13

--- a/solution.py
+++ b/solution.py
@@ -654,6 +654,7 @@
             kept_a,
             sums,
             far,
+            near,
         )
         came_a = swap(away_a, "dom", lambda i: i ^ 1)
         away_b, kept_b = small_call(
@@ -668,7 +669,6 @@
             came_a,
             kept_b,
             came_b,
-            near,
         )
         returned = [came_a, near, far]
         late, backs = pair, 0

time: 60.2 us -> 56.7 us (0.942)
  starting transfers between devices: 24.6 us -> 22.8 us
  waiting for transfers between devices: 19.2 us -> 17.5 us
    ppermute x13, starting transfers between devices: 24.6 us -> 22.8 us  [swap(): return lax.ppermute(array, axis, [(i, partner(i)) for i in range(devices)])]
    ppermute x13, waiting for transfers between devices: 19.2 us -> 17.5 us  [swap(): return lax.ppermute(array, axis, [(i, partner(i)) for i in range(devices)])]
where the time goes in v14:
time: 56.7 us; the launch traced here: 56.5 us
  starting transfers between devices  22.8 us (40%)
  waiting for transfers between devices  17.5 us (31%)
  Pallas kernels  14.8 us (26%)
  between operations  1.39 us (2%)
    ppermute x13, starting transfers between devices, swap(): return lax.ppermute(array, axis, [(i, partner(i)) for i in range(devices)])  22.8 us
    ppermute x13, waiting for transfers between devices, swap(): return lax.ppermute(array, axis, [(i, partner(i)) for i in range(devices)])  17.5 us
    pallas_call x1, Pallas kernels, body(): pl.pallas_call(functools.partial(edge_kernel, ways, arrivals, four, block...  5.75 us
    pallas_call x1, Pallas kernels, body(): pl.pallas_call(functools.partial(prep_kernel, parts, arrivals), out_shape...  2.42 us
    pallas_call x1, Pallas kernels, body(): pl.pallas_call(functools.partial(edge_grad_kernel, block, arrivals, four)...  2.21 us
    pallas_call x1, Pallas kernels, body(): pl.pallas_call(functools.partial(node_grad_kernel, arrivals, four), out_s...  2.14 us
  transfers between devices with their start and end apart: 13, of which 7 were waited for; matrix products, arithmetic and copies ran while one was open for 0% of the time, Pallas kernels for 12%

profile of v14, /device:TPU:0, one launch (start us, length us, event | category | flops | bytes accessed | tf_op | source)
XLA Modules:
  0.0 56.5 jit_solution(1911912360670880943)
XLA Ops:
  0.6 0.9 %pick_blocks.1 = (bf16[64,512]{1,0:T(8,128)(2,1)S(1)}, bf16[64,512]{1,0:T(8,128)(2,1)S(1)}, bf16[64,512]{1,0:T(8,128)(2,1)S(1)}) custom-call(s32[1,4]{1,0:T(1,128)} %boundary_hbm.3, bf16[128,512]{1,0:T(8,128)(2,1)} %bitcast.8), custom_call_target="tpu_custom_call" | custom-call | bytes 400000 | tf_op jit(solution)/shard_map/pick_blocks/pallas_call | solution.py:534
  1.6 0.7 %collective-permute-start = (bf16[64,512]{1,0:T(8,128)(2,1)S(1)}, bf16[64,512]{1,0:T(8,128)(2,1)S(1)}, u32[]{:S(2)}, u32[]{:S(2)}) collective-permute-start(bf16[64,512]{1,0:T(8,128)(2,1)S(1)} %get-tuple-element.38), channel_id=1, source_target_pairs={{0,0},{4,8},{8,4},{12,12},{1,1},{5,9},{9,5},{13,13},{2,2},{6,10},{... | collective-permute-start | bytes 196616 | tf_op jit(solution)/shard_map/ppermute | solution.py:428
  2.2 5.8 %collective-permute-start.1 = (bf16[64,512]{1,0:T(8,128)(2,1)S(1)}, bf16[64,512]{1,0:T(8,128)(2,1)S(1)}, u32[]{:S(2)}, u32[]{:S(2)}) collective-permute-start(bf16[64,512]{1,0:T(8,128)(2,1)S(1)} %get-tuple-element.39), channel_id=1, source_target_pairs={{0,8},{4,12},{8,0},{12,4},{1,9},{5,13},{9,1},{13,5},{2,10},{6,14},... | collective-permute-start | bytes 196616 | tf_op jit(solution)/shard_map/ppermute | solution.py:428
  8.0 0.2 collective-permute-start.2
  8.9 2.4 %prepare.1 = (bf16[128,512]{1,0:T(8,128)(2,1)S(1)}, bf16[768,512]{1,0:T(8,128)(2,1)S(1)}, bf16[128,512]{1,0:T(8,128)(2,1)S(1)}, bf16[1536,512]{1,0:T(8,128)(2,1)...) custom-call(s32[1]{0:T(128)S(6)} %copy.15.count_ref, ...), custom_call_target="tpu_custom_call" | custom-call | flops 402653184 | bytes 8000000 | tf_op jit(solution)/shard_map/prepare/pallas_call | solution.py:556
  11.3 0.0 collective-permute-done.refs_0_
  11.3 0.6 %collective-permute-done.1.refs_1_ = bf16[64,512]{1,0:T(8,128)(2,1)S(1)} collective-permute-done((bf16[64,512]{1,0:T(8,128)(2,1)S(1)}, bf16[64,512]{1,0:T(8,128)(2,1)S(1)}, u32[]{:S(2)}, u32[]{:S(2)}) %collective-permute-start.1) | collective-permute-done | bytes 65568 | tf_op jit(solution)/shard_map/ppermute | solution.py:428
  11.9 0.7 %collective-permute-done.2.refs_2_ = bf16[64,512]{1,0:T(8,128)(2,1)S(1)} collective-permute-done((bf16[64,512]{1,0:T(8,128)(2,1)S(1)}, bf16[64,512]{1,0:T(8,128)(2,1)S(1)}, u32[]{:S(2)}, u32[]{:S(2)}) %collective-permute-start.2) | collective-permute-done | bytes 65568 | tf_op jit(solution)/shard_map/ppermute | solution.py:428
  12.6 5.7 %edge_block.1 = (bf16[768,512]{1,0:T(8,128)(2,1)S(1)}, f32[768,512]{1,0:T(8,128)S(1)}, f32[512,512]{1,0:T(8,128)S(1)}, bf16[2,256,512]{2,1,0:T(8,128)(2,1)S(1)},...) custom-call(bf16[64,512]{1,0:T(8,128)(2,1)S(1)} %collective-permute-, ...), custom_call_target="tpu_custom_call" | custom-call | flops 2415919104 | bytes 12000000 | tf_op jit(solution)/shard_map/edge_block/pallas_call | solution.py:600
  18.3 0.1 collective-permute-start.3
  18.4 0.5 collective-permute-start.8
  18.9 1.4 %collective-permute-done.3.came_ref = bf16[2,256,512]{2,1,0:T(8,128)(2,1)S(1)} collective-permute-done((bf16[2,256,512]{2,1,0:T(8,128)(2,1)S(1)}, bf16[2,256,512]{2,1,0:T(8,128)(2,1)S(1)}, u32[]{:S(2)}, u32[]{:S(2)}) %collective-permute-start.3) | collective-permute-done | bytes 524320 | tf_op jit(solution)/shard_map/ppermute | solution.py:428
  20.3 0.1 halve.1
  20.4 1.5 %collective-permute-start.4 = (bf16[1,256,512]{2,1,0:T(8,128)(2,1)S(1)}, bf16[1,256,512]{2,1,0:T(8,128)(2,1)S(1)}, u32[]{:S(2)}, u32[]{:S(2)}) collective-permute-start(bf16[1,256,512]{2,1,0:T(8,128)(2,1)S(1)} %get-tuple-element.52), channel_id=1, source_target_pairs={{0,2},{1,3},{2,0},{3,1},{4,6},{5,7},{6,4},{7,5},{8,10},{9,11},{10,... | collective-permute-start | bytes 786440 | tf_op jit(solution)/shard_map/ppermute | solution.py:428
  21.9 0.1 beside_first.1
  22.0 0.8 %collective-permute-start.9 = (bf16[256,512]{1,0:T(8,128)(2,1)S(1)}, bf16[256,512]{1,0:T(8,128)(2,1)S(1)}, u32[]{:S(2)}, u32[]{:S(2)}) collective-permute-start(bf16[256,512]{1,0:T(8,128)(2,1)S(1)} %get-tuple-element.61), channel_id=1, source_target_pairs={{0,4},{4,0},{8,12},{12,8},{1,5},{5,1},{9,13},{13,9},{2,6},{6,2},{1... | collective-permute-start | bytes 786440 | tf_op jit(solution)/shard_map/ppermute | solution.py:428
  22.9 2.7 %collective-permute-start.5 = (bf16[64,512]{1,0:T(8,128)(2,1)S(1)}, bf16[64,512]{1,0:T(8,128)(2,1)S(1)}, u32[]{:S(2)}, u32[]{:S(2)}) collective-permute-start(bf16[64,512]{1,0:T(8,128)(2,1)S(1)} %get-tuple-element.55), channel_id=1, source_target_pairs={{0,8},{4,12},{8,0},{12,4},{1,9},{5,13},{9,1},{13,5},{2,10},{6,14},... | collective-permute-start | bytes 196616 | tf_op jit(solution)/shard_map/ppermute | solution.py:428
  25.6 0.7 %collective-permute-start.6 = (bf16[64,512]{1,0:T(8,128)(2,1)S(1)}, bf16[64,512]{1,0:T(8,128)(2,1)S(1)}, u32[]{:S(2)}, u32[]{:S(2)}) collective-permute-start(bf16[64,512]{1,0:T(8,128)(2,1)S(1)} %get-tuple-element.56), channel_id=1, source_target_pairs={{0,0},{4,8},{8,4},{12,12},{1,1},{5,9},{9,5},{13,13},{2,2},{6,10},{... | collective-permute-start | bytes 196616 | tf_op jit(solution)/shard_map/ppermute | solution.py:428
  26.2 3.6 %collective-permute-done.5.refs_0_.refs_2_ = bf16[64,512]{1,0:T(8,128)(2,1)S(1)} collective-permute-done((bf16[64,512]{1,0:T(8,128)(2,1)S(1)}, bf16[64,512]{1,0:T(8,128)(2,1)S(1)}, u32[]{:S(2)}, u32[]{:S(2)}) %collective-permute-start.5) | collective-permute-done | bytes 65568 | tf_op jit(solution)/shard_map/ppermute | solution.py:428
  29.8 0.0 collective-permute-done.6.refs_1_
  29.9 3.5 %collective-permute-start.7 = (bf16[192,512]{1,0:T(8,128)(2,1)S(1)}, bf16[192,512]{1,0:T(8,128)(2,1)S(1)}, u32[]{:S(2)}, u32[]{:S(2)}) collective-permute-start(bf16[192,512]{1,0:T(8,128)(2,1)S(1)} %get-tuple-element.58), channel_id=1, source_target_pairs={{0,4},{4,0},{8,12},{12,8},{1,5},{5,1},{9,13},{13,9},{2,6},{6,2},{1... | collective-permute-start | bytes 589832 | tf_op jit(solution)/shard_map/ppermute | solution.py:428
  33.5 0.9 %collective-permute-start.10 = (bf16[128,512]{1,0:T(8,128)(2,1)S(1)}, bf16[128,512]{1,0:T(8,128)(2,1)S(1)}, u32[]{:S(2)}, u32[]{:S(2)}) collective-permute-start(bf16[128,512]{1,0:T(8,128)(2,1)S(1)} %get-tuple-element.64), channel_id=1, source_target_pairs={{0,2},{1,3},{2,0},{3,1},{4,6},{5,7},{6,4},{7,5},{8,10},{9,11},{10,... | collective-permute-start | bytes 393224 | tf_op jit(solution)/shard_map/ppermute | solution.py:428
  34.4 4.1 %collective-permute-done.10.came_b = bf16[128,512]{1,0:T(8,128)(2,1)S(1)} collective-permute-done((bf16[128,512]{1,0:T(8,128)(2,1)S(1)}, bf16[128,512]{1,0:T(8,128)(2,1)S(1)}, u32[]{:S(2)}, u32[]{:S(2)}) %collective-permute-start.10) | collective-permute-done | bytes 131104 | tf_op jit(solution)/shard_map/ppermute | solution.py:428
  38.5 0.1 add_terms.1.after
  38.6 1.4 %collective-permute-start.11 = (bf16[256,512]{1,0:T(8,128)(2,1)S(1)}, bf16[256,512]{1,0:T(8,128)(2,1)S(1)}, u32[]{:S(2)}, u32[]{:S(2)}) collective-permute-start(bf16[256,512]{1,0:T(8,128)(2,1)S(1)} %add_terms.1.after), channel_id=1, source_target_pairs={{0,12},{4,8},{8,4},{12,0},{1,13},{5,9},{9,5},{13,1},{2,14},{6,10},... | collective-permute-start | bytes 786440 | tf_op jit(solution)/shard_map/ppermute | solution.py:428
  40.0 6.8 %collective-permute-done.11 = bf16[256,512]{1,0:T(8,128)(2,1)S(1)} collective-permute-done((bf16[256,512]{1,0:T(8,128)(2,1)S(1)}, bf16[256,512]{1,0:T(8,128)(2,1)S(1)}, u32[]{:S(2)}, u32[]{:S(2)}) %collective-permute-start.11) | collective-permute-done | bytes 262176 | tf_op jit(solution)/shard_map/ppermute | solution.py:428
  46.9 0.1 add_convert_fusion.own_ref
  46.9 3.9 %collective-permute-start.12 = (bf16[256,512]{1,0:T(8,128)(2,1)S(1)}, bf16[256,512]{1,0:T(8,128)(2,1)S(1)}, u32[]{:S(2)}, u32[]{:S(2)}) collective-permute-start(bf16[256,512]{1,0:T(8,128)(2,1)S(1)} %add_convert_fusion.own_ref), channel_id=1, source_target_pairs={{0,4},{4,0},{8,12},{12,8},{1,5},{5,1},{9,13},{13,9},{2,6},{6,2},{1... | collective-permute-start | bytes 786440 | tf_op jit(solution)/shard_map/ppermute | solution.py:428
  50.8 2.1 %node_grads.1.node_out = bf16[128,512]{1,0:T(8,128)(2,1)} custom-call(s32[1,4]{1,0:T(1,128)} %boundary_hbm.3, bf16[256,512]{1,0:T(8,128)(2,1)S(1)} %add_terms.1.after, f32[512,512]{1,0:T(8,128)S(1)} %get-tuple-element.54.sums_ref, bf16[1536,512]{1,0:T(8,128)(2,1)S(1)} %get-tuple-element.43.refs_5_.win_ref, ...), custom_call_target="tpu_custom_call" | custom-call | flops 268435456 | bytes 2000000 | tf_op jit(solution)/shard_map/node_grads/pallas_call | solution.py:707
  53.0 2.2 %edge_grads.1 = (bf16[768,512]{1,0:T(8,128)(2,1)}, bf16[128,512]{1,0:T(8,128)(2,1)}) custom-call(s32[12]{0:T(128)} %dst_hbm.3, s32[1]{0:T(128)S(6)} %copy.15.count_ref, bf16[256,512]{1,0:T(8,128)(2,1)S(1)} %add_terms.1.after, bf16[768,512]{1,0:T(8,128)(2,1)S(1)} %get-tuple-element.65.gpre_ref, f32[512,512]{1,0:T(8,128)S(1)} %get-tuple-element.54.sums_ref, ...), custom_call_target="tpu_custom_call" | custom-call | flops 402653184 | bytes 3000000 | tf_op jit(solution)/shard_map/edge_grads/pallas_call | solution.py:679
  55.2 0.3 collective-permute-done.12.other_ref
  55.5 1.0 %widen.1 = (f32[384,512]{1,0:T(8,128)}, f32[128,512]{1,0:T(8,128)}) custom-call(bf16[128,512]{1,0:T(8,128)(2,1)} %node_grads.1.node_out, bf16[768,512]{1,0:T(8,128)(2,1)} %get-tuple-element.68.edge_grad, bf16[256,512]{1,0:T(8,128)(2,1)S(1)} %add_convert_fusion.own_ref, bf16[256,512]{1,0:T(8,128)(2,1)S(1)} %collective-permute-done.12.other_ref), custom_call_target="tpu_custom_call" | custom-call | bytes 1500000 | tf_op jit(solution)/shard_map/widen/pallas_call | solution.py:724
  (6 shorter events, 0.1 us)
Async XLA Ops:
  1.6 9.7 %collective-permute-start = (bf16[64,512]{1,0:T(8,128)(2,1)S(1)}, bf16[64,512]{1,0:T(8,128)(2,1)S(1)}, u32[]{:S(2)}, u32[]{:S(2)}) collective-permute-start(bf16[64,512]{1,0:T(8,128)(2,1)S(1)} %get-tuple-element.38), channel_id=1, source_target_pairs={{0,0},{4,8},{8,4},{12,12},{1,1},{5,9},{9,5},{13,13},{2,2},{6,10},{... | collective-permute-start | bytes 196616 | tf_op jit(solution)/shard_map/ppermute | solution.py:428
  2.2 9.6 %collective-permute-start.1 = (bf16[64,512]{1,0:T(8,128)(2,1)S(1)}, bf16[64,512]{1,0:T(8,128)(2,1)S(1)}, u32[]{:S(2)}, u32[]{:S(2)}) collective-permute-start(bf16[64,512]{1,0:T(8,128)(2,1)S(1)} %get-tuple-element.39), channel_id=1, source_target_pairs={{0,8},{4,12},{8,0},{12,4},{1,9},{5,13},{9,1},{13,5},{2,10},{6,14},... | collective-permute-start | bytes 196616 | tf_op jit(solution)/shard_map/ppermute | solution.py:428
  8.0 4.5 %collective-permute-start.2 = (bf16[64,512]{1,0:T(8,128)(2,1)S(1)}, bf16[64,512]{1,0:T(8,128)(2,1)S(1)}, u32[]{:S(2)}, u32[]{:S(2)}) collective-permute-start(bf16[64,512]{1,0:T(8,128)(2,1)S(1)} %get-tuple-element.40), channel_id=1, source_target_pairs={{0,4},{4,0},{8,12},{12,8},{1,5},{5,1},{9,13},{13,9},{2,6},{6,2},{1... | collective-permute-start | bytes 196616 | tf_op jit(solution)/shard_map/ppermute | solution.py:428
  18.3 2.0 %collective-permute-start.3 = (bf16[2,256,512]{2,1,0:T(8,128)(2,1)S(1)}, bf16[2,256,512]{2,1,0:T(8,128)(2,1)S(1)}, u32[]{:S(2)}, u32[]{:S(2)}) collective-permute-start(bf16[2,256,512]{2,1,0:T(8,128)(2,1)S(1)} %get-tuple-element.49), channel_id=1, source_target_pairs={{0,1},{1,0},{2,3},{3,2},{4,5},{5,4},{6,7},{7,6},{8,9},{9,8},{10,11... | collective-permute-start | bytes 1572872 | tf_op jit(solution)/shard_map/ppermute | solution.py:428
  18.4 3.5 %collective-permute-start.8 = (bf16[2,256,512]{2,1,0:T(8,128)(2,1)S(1)}, bf16[2,256,512]{2,1,0:T(8,128)(2,1)S(1)}, u32[]{:S(2)}, u32[]{:S(2)}) collective-permute-start(bf16[2,256,512]{2,1,0:T(8,128)(2,1)S(1)} %get-tuple-element.59), channel_id=1, source_target_pairs={{0,1},{1,0},{2,3},{3,2},{4,5},{5,4},{6,7},{7,6},{8,9},{9,8},{10,11... | collective-permute-start | bytes 1572872 | tf_op jit(solution)/shard_map/ppermute | solution.py:428
  20.4 9.5 %collective-permute-start.4 = (bf16[1,256,512]{2,1,0:T(8,128)(2,1)S(1)}, bf16[1,256,512]{2,1,0:T(8,128)(2,1)S(1)}, u32[]{:S(2)}, u32[]{:S(2)}) collective-permute-start(bf16[1,256,512]{2,1,0:T(8,128)(2,1)S(1)} %get-tuple-element.52), channel_id=1, source_target_pairs={{0,2},{1,3},{2,0},{3,1},{4,6},{5,7},{6,4},{7,5},{8,10},{9,11},{10,... | collective-permute-start | bytes 786440 | tf_op jit(solution)/shard_map/ppermute | solution.py:428
  22.0 11.4 %collective-permute-start.9 = (bf16[256,512]{1,0:T(8,128)(2,1)S(1)}, bf16[256,512]{1,0:T(8,128)(2,1)S(1)}, u32[]{:S(2)}, u32[]{:S(2)}) collective-permute-start(bf16[256,512]{1,0:T(8,128)(2,1)S(1)} %get-tuple-element.61), channel_id=1, source_target_pairs={{0,4},{4,0},{8,12},{12,8},{1,5},{5,1},{9,13},{13,9},{2,6},{6,2},{1... | collective-permute-start | bytes 786440 | tf_op jit(solution)/shard_map/ppermute | solution.py:428
  22.9 7.0 %collective-permute-start.5 = (bf16[64,512]{1,0:T(8,128)(2,1)S(1)}, bf16[64,512]{1,0:T(8,128)(2,1)S(1)}, u32[]{:S(2)}, u32[]{:S(2)}) collective-permute-start(bf16[64,512]{1,0:T(8,128)(2,1)S(1)} %get-tuple-element.55), channel_id=1, source_target_pairs={{0,8},{4,12},{8,0},{12,4},{1,9},{5,13},{9,1},{13,5},{2,10},{6,14},... | collective-permute-start | bytes 196616 | tf_op jit(solution)/shard_map/ppermute | solution.py:428
  25.6 4.3 %collective-permute-start.6 = (bf16[64,512]{1,0:T(8,128)(2,1)S(1)}, bf16[64,512]{1,0:T(8,128)(2,1)S(1)}, u32[]{:S(2)}, u32[]{:S(2)}) collective-permute-start(bf16[64,512]{1,0:T(8,128)(2,1)S(1)} %get-tuple-element.56), channel_id=1, source_target_pairs={{0,0},{4,8},{8,4},{12,12},{1,1},{5,9},{9,5},{13,13},{2,2},{6,10},{... | collective-permute-start | bytes 196616 | tf_op jit(solution)/shard_map/ppermute | solution.py:428
  29.9 8.6 %collective-permute-start.7 = (bf16[192,512]{1,0:T(8,128)(2,1)S(1)}, bf16[192,512]{1,0:T(8,128)(2,1)S(1)}, u32[]{:S(2)}, u32[]{:S(2)}) collective-permute-start(bf16[192,512]{1,0:T(8,128)(2,1)S(1)} %get-tuple-element.58), channel_id=1, source_target_pairs={{0,4},{4,0},{8,12},{12,8},{1,5},{5,1},{9,13},{13,9},{2,6},{6,2},{1... | collective-permute-start | bytes 589832 | tf_op jit(solution)/shard_map/ppermute | solution.py:428
  33.5 5.0 %collective-permute-start.10 = (bf16[128,512]{1,0:T(8,128)(2,1)S(1)}, bf16[128,512]{1,0:T(8,128)(2,1)S(1)}, u32[]{:S(2)}, u32[]{:S(2)}) collective-permute-start(bf16[128,512]{1,0:T(8,128)(2,1)S(1)} %get-tuple-element.64), channel_id=1, source_target_pairs={{0,2},{1,3},{2,0},{3,1},{4,6},{5,7},{6,4},{7,5},{8,10},{9,11},{10,... | collective-permute-start | bytes 393224 | tf_op jit(solution)/shard_map/ppermute | solution.py:428
  38.6 8.3 %collective-permute-start.11 = (bf16[256,512]{1,0:T(8,128)(2,1)S(1)}, bf16[256,512]{1,0:T(8,128)(2,1)S(1)}, u32[]{:S(2)}, u32[]{:S(2)}) collective-permute-start(bf16[256,512]{1,0:T(8,128)(2,1)S(1)} %add_terms.1.after), channel_id=1, source_target_pairs={{0,12},{4,8},{8,4},{12,0},{1,13},{5,9},{9,5},{13,1},{2,14},{6,10},... | collective-permute-start | bytes 786440 | tf_op jit(solution)/shard_map/ppermute | solution.py:428
  46.9 8.5 %collective-permute-start.12 = (bf16[256,512]{1,0:T(8,128)(2,1)S(1)}, bf16[256,512]{1,0:T(8,128)(2,1)S(1)}, u32[]{:S(2)}, u32[]{:S(2)}) collective-permute-start(bf16[256,512]{1,0:T(8,128)(2,1)S(1)} %add_convert_fusion.own_ref), channel_id=1, source_target_pairs={{0,4},{4,0},{8,12},{12,8},{1,5},{5,1},{9,13},{13,9},{2,6},{6,2},{1... | collective-permute-start | bytes 786440 | tf_op jit(solution)/shard_map/ppermute | solution.py:428

commit v15 on v14

--- a/solution.py
+++ b/solution.py
@@ -96,6 +96,7 @@
     up_ref,
     hot_ref,
     hot_turned,
+    edge_turned,
     src_ref,
     dst_ref,
     slot_ref,
@@ -166,6 +167,7 @@
     for tile in range(tiles):
         live = jnp.where(tile < count_ref[0], 1.0, 0.0)
         up_ref[tile * block : (tile + 1) * block, :] = rows_of(mid_ref, dst_ref[tile], block) * live
+    edge_turned[...] = edge_ref[...].T
     copies[8].wait()
     copies[9].wait()
 
@@ -174,10 +176,13 @@
     latent = sections[0][0].shape[1]
     unit = latent // ways
     step = 256
-    for number, (left, right) in enumerate(sections):
+    for number, (left, right, turned) in enumerate(sections):
         value_right = right()
         for start in range(0, latent, step):
-            value = t_dot(left[:, start : start + step], value_right)
+            if turned:
+                value = dot(left[start : start + step, :], value_right)
+            else:
+                value = t_dot(left[:, start : start + step], value_right)
             for at in range(0, step, unit):
                 owner, spot = (start + at) // unit, 0
                 if number > 0:
@@ -211,6 +216,7 @@
         up_ref,
         hot_ref,
         hot_turned,
+        edge_turned,
         gpre_ref,
         message_ref,
         sums_ref,
@@ -261,10 +267,10 @@
     for which, back_ref in enumerate(back_refs):
         back_ref[...] = back_block(nodes, block, sums_ref, 1 + which)
     sections = (
-        (act_ref, lambda: proj_ref[...]),
-        (edge_ref, lambda: gpre_ref[...]),
-        (ext_ref, lambda: sums_ref[:extent, :].astype(BF16)),
-        (node_ref, lambda: sums_ref[extent:, :].astype(BF16)),
+        (act_ref, lambda: proj_ref[...], False),
+        (edge_turned, lambda: gpre_ref[...], True),
+        (ext_ref, lambda: sums_ref[:extent, :].astype(BF16), False),
+        (node_ref, lambda: sums_ref[extent:, :].astype(BF16), False),
     )
     targets = ((away_a, kept_a), (away_b, kept_b))
     put_units(ways, lax.axis_index("dp") % 2, targets, sections)
@@ -553,7 +559,7 @@
     half = ways // 2
     extent = -(-(nodes + arrivals * block) // 128) * 128
 
-    node_v, edge_v, cot_v, win_v, wout_v, pre, up, hot, turned = pl.pallas_call(
+    node_v, edge_v, cot_v, win_v, wout_v, pre, up, hot, turned, edge_t = pl.pallas_call(
         functools.partial(prep_kernel, parts, arrivals),
         out_shape=(
             pltpu.VMEM((nodes, latent), BF16),
@@ -565,9 +571,10 @@
             pltpu.VMEM((edges, latent), F32),
             pltpu.VMEM((edges, extent), BF16),
             pltpu.VMEM((extent + nodes, edges), BF16),
+            pltpu.VMEM((latent, edges), BF16),
         ),
         in_specs=[SMEM] + [HBM] * 8,
-        out_specs=(VMEM,) * 9,
+        out_specs=(VMEM,) * 10,
         scratch_shapes=[
             pltpu.SMEM((tiles,), jnp.int32),
             pltpu.SMEM((tiles,), jnp.int32),
@@ -609,7 +616,7 @@
             kept_shape,
             *[block_shape] * (2 if four else 0),
         ),
-        in_specs=[VMEM] * (8 + arrivals),
+        in_specs=[VMEM] * (9 + arrivals),
         out_specs=(VMEM,) * (9 if four else 7),
         scratch_shapes=[
             pltpu.VMEM((extent, latent), BF16),
@@ -626,7 +633,7 @@
     )(
         *[
             in_vmem(array)
-            for array in (*ordered, node_v, edge_v, win_v, wout_v, pre, up, hot, turned)
+            for array in (*ordered, node_v, edge_v, win_v, wout_v, pre, up, hot, turned, edge_t)
         ],
     )
     if four:

time: 56.7 us -> 56.6 us (level)
  transfers between devices with their start and end apart: 13 -> 13, of which waited for: 7 -> 7; matrix products, arithmetic and copies ran while one was open for 0% -> 0% of each run, Pallas kernels for 12% -> 13%
where the time goes in v15:
time: 56.6 us; the launch traced here: 56.4 us
  starting transfers between devices  22.6 us (40%)
  waiting for transfers between devices  17.4 us (31%)
  Pallas kernels  14.9 us (26%)
  between operations  1.39 us (2%)
    ppermute x13, starting transfers between devices, swap(): return lax.ppermute(array, axis, [(i, partner(i)) for i in range(devices)])  22.6 us
    ppermute x13, waiting for transfers between devices, swap(): return lax.ppermute(array, axis, [(i, partner(i)) for i in range(devices)])  17.4 us
    pallas_call x1, Pallas kernels, body(): pl.pallas_call(functools.partial(edge_kernel, ways, arrivals, four, block...  5.68 us
    pallas_call x1, Pallas kernels, body(): pl.pallas_call(functools.partial(prep_kernel, parts, arrivals), out_shape...  2.62 us
    pallas_call x1, Pallas kernels, body(): pl.pallas_call(functools.partial(edge_grad_kernel, block, arrivals, four)...  2.21 us
    pallas_call x1, Pallas kernels, body(): pl.pallas_call(functools.partial(node_grad_kernel, arrivals, four), out_s...  2.13 us
  transfers between devices with their start and end apart: 13, of which 7 were waited for; matrix products, arithmetic and copies ran while one was open for 0% of the time, Pallas kernels for 13%

profile of v15, /device:TPU:0, one launch (start us, length us, event | category | flops | bytes accessed | tf_op | source)
XLA Modules:
  0.0 56.4 jit_solution(16164972396802212657)
XLA Ops:
  0.6 0.9 %pick_blocks.1 = (bf16[64,512]{1,0:T(8,128)(2,1)S(1)}, bf16[64,512]{1,0:T(8,128)(2,1)S(1)}, bf16[64,512]{1,0:T(8,128)(2,1)S(1)}) custom-call(s32[1,4]{1,0:T(1,128)} %boundary_hbm.3, bf16[128,512]{1,0:T(8,128)(2,1)} %bitcast.8), custom_call_target="tpu_custom_call" | custom-call | bytes 400000 | tf_op jit(solution)/shard_map/pick_blocks/pallas_call | solution.py:540
  1.6 0.7 %collective-permute-start = (bf16[64,512]{1,0:T(8,128)(2,1)S(1)}, bf16[64,512]{1,0:T(8,128)(2,1)S(1)}, u32[]{:S(2)}, u32[]{:S(2)}) collective-permute-start(bf16[64,512]{1,0:T(8,128)(2,1)S(1)} %get-tuple-element.39), channel_id=1, source_target_pairs={{0,0},{4,8},{8,4},{12,12},{1,1},{5,9},{9,5},{13,13},{2,2},{6,10},{... | collective-permute-start | bytes 196616 | tf_op jit(solution)/shard_map/ppermute | solution.py:434
  2.2 5.8 %collective-permute-start.1 = (bf16[64,512]{1,0:T(8,128)(2,1)S(1)}, bf16[64,512]{1,0:T(8,128)(2,1)S(1)}, u32[]{:S(2)}, u32[]{:S(2)}) collective-permute-start(bf16[64,512]{1,0:T(8,128)(2,1)S(1)} %get-tuple-element.40), channel_id=1, source_target_pairs={{0,8},{4,12},{8,0},{12,4},{1,9},{5,13},{9,1},{13,5},{2,10},{6,14},... | collective-permute-start | bytes 196616 | tf_op jit(solution)/shard_map/ppermute | solution.py:434
  8.0 0.2 collective-permute-start.2
  8.9 2.6 %prepare.1 = (bf16[128,512]{1,0:T(8,128)(2,1)S(1)}, bf16[768,512]{1,0:T(8,128)(2,1)S(1)}, bf16[128,512]{1,0:T(8,128)(2,1)S(1)}, bf16[1536,512]{1,0:T(8,128)(2,1)...) custom-call(s32[1]{0:T(128)S(6)} %copy.15.count_ref, ...), custom_call_target="tpu_custom_call" | custom-call | flops 402653184 | bytes 8000000 | tf_op jit(solution)/shard_map/prepare/pallas_call | solution.py:562
  11.5 0.4 collective-permute-done.1.refs_1_
  11.9 0.7 %collective-permute-done.2.refs_2_ = bf16[64,512]{1,0:T(8,128)(2,1)S(1)} collective-permute-done((bf16[64,512]{1,0:T(8,128)(2,1)S(1)}, bf16[64,512]{1,0:T(8,128)(2,1)S(1)}, u32[]{:S(2)}, u32[]{:S(2)}) %collective-permute-start.2) | collective-permute-done | bytes 65568 | tf_op jit(solution)/shard_map/ppermute | solution.py:434
  12.6 5.7 %edge_block.1 = (bf16[768,512]{1,0:T(8,128)(2,1)S(1)}, f32[768,512]{1,0:T(8,128)S(1)}, f32[512,512]{1,0:T(8,128)S(1)}, bf16[2,256,512]{2,1,0:T(8,128)(2,1)S(1)},...) custom-call(bf16[64,512]{1,0:T(8,128)(2,1)S(1)} %collective-permute-, ...), custom_call_target="tpu_custom_call" | custom-call | flops 2415919104 | bytes 12000000 | tf_op jit(solution)/shard_map/edge_block/pallas_call | solution.py:607
  18.3 0.1 collective-permute-start.3
  18.3 0.5 collective-permute-start.8
  18.8 1.4 %collective-permute-done.3.came_ref = bf16[2,256,512]{2,1,0:T(8,128)(2,1)S(1)} collective-permute-done((bf16[2,256,512]{2,1,0:T(8,128)(2,1)S(1)}, bf16[2,256,512]{2,1,0:T(8,128)(2,1)S(1)}, u32[]{:S(2)}, u32[]{:S(2)}) %collective-permute-start.3) | collective-permute-done | bytes 524320 | tf_op jit(solution)/shard_map/ppermute | solution.py:434
  20.2 0.1 halve.1
  20.3 1.5 %collective-permute-start.4 = (bf16[1,256,512]{2,1,0:T(8,128)(2,1)S(1)}, bf16[1,256,512]{2,1,0:T(8,128)(2,1)S(1)}, u32[]{:S(2)}, u32[]{:S(2)}) collective-permute-start(bf16[1,256,512]{2,1,0:T(8,128)(2,1)S(1)} %get-tuple-element.54), channel_id=1, source_target_pairs={{0,2},{1,3},{2,0},{3,1},{4,6},{5,7},{6,4},{7,5},{8,10},{9,11},{10,... | collective-permute-start | bytes 786440 | tf_op jit(solution)/shard_map/ppermute | solution.py:434
  21.9 0.0 collective-permute-done.8.came_ref
  21.9 0.1 beside_first.1
  22.0 0.9 %collective-permute-start.9 = (bf16[256,512]{1,0:T(8,128)(2,1)S(1)}, bf16[256,512]{1,0:T(8,128)(2,1)S(1)}, u32[]{:S(2)}, u32[]{:S(2)}) collective-permute-start(bf16[256,512]{1,0:T(8,128)(2,1)S(1)} %get-tuple-element.63), channel_id=1, source_target_pairs={{0,4},{4,0},{8,12},{12,8},{1,5},{5,1},{9,13},{13,9},{2,6},{6,2},{1... | collective-permute-start | bytes 786440 | tf_op jit(solution)/shard_map/ppermute | solution.py:434
  22.9 2.6 %collective-permute-start.5 = (bf16[64,512]{1,0:T(8,128)(2,1)S(1)}, bf16[64,512]{1,0:T(8,128)(2,1)S(1)}, u32[]{:S(2)}, u32[]{:S(2)}) collective-permute-start(bf16[64,512]{1,0:T(8,128)(2,1)S(1)} %get-tuple-element.57), channel_id=1, source_target_pairs={{0,8},{4,12},{8,0},{12,4},{1,9},{5,13},{9,1},{13,5},{2,10},{6,14},... | collective-permute-start | bytes 196616 | tf_op jit(solution)/shard_map/ppermute | solution.py:434
  25.5 0.7 %collective-permute-start.6 = (bf16[64,512]{1,0:T(8,128)(2,1)S(1)}, bf16[64,512]{1,0:T(8,128)(2,1)S(1)}, u32[]{:S(2)}, u32[]{:S(2)}) collective-permute-start(bf16[64,512]{1,0:T(8,128)(2,1)S(1)} %get-tuple-element.58), channel_id=1, source_target_pairs={{0,0},{4,8},{8,4},{12,12},{1,1},{5,9},{9,5},{13,13},{2,2},{6,10},{... | collective-permute-start | bytes 196616 | tf_op jit(solution)/shard_map/ppermute | solution.py:434
  26.2 3.7 %collective-permute-done.5.refs_0_.refs_2_ = bf16[64,512]{1,0:T(8,128)(2,1)S(1)} collective-permute-done((bf16[64,512]{1,0:T(8,128)(2,1)S(1)}, bf16[64,512]{1,0:T(8,128)(2,1)S(1)}, u32[]{:S(2)}, u32[]{:S(2)}) %collective-permute-start.5) | collective-permute-done | bytes 65568 | tf_op jit(solution)/shard_map/ppermute | solution.py:434
  29.9 0.0 collective-permute-done.6.refs_1_
  29.9 3.6 %collective-permute-start.7 = (bf16[192,512]{1,0:T(8,128)(2,1)S(1)}, bf16[192,512]{1,0:T(8,128)(2,1)S(1)}, u32[]{:S(2)}, u32[]{:S(2)}) collective-permute-start(bf16[192,512]{1,0:T(8,128)(2,1)S(1)} %get-tuple-element.60), channel_id=1, source_target_pairs={{0,4},{4,0},{8,12},{12,8},{1,5},{5,1},{9,13},{13,9},{2,6},{6,2},{1... | collective-permute-start | bytes 589832 | tf_op jit(solution)/shard_map/ppermute | solution.py:434
  33.5 0.9 %collective-permute-start.10 = (bf16[128,512]{1,0:T(8,128)(2,1)S(1)}, bf16[128,512]{1,0:T(8,128)(2,1)S(1)}, u32[]{:S(2)}, u32[]{:S(2)}) collective-permute-start(bf16[128,512]{1,0:T(8,128)(2,1)S(1)} %get-tuple-element.66), channel_id=1, source_target_pairs={{0,2},{1,3},{2,0},{3,1},{4,6},{5,7},{6,4},{7,5},{8,10},{9,11},{10,... | collective-permute-start | bytes 393224 | tf_op jit(solution)/shard_map/ppermute | solution.py:434
  34.5 4.1 %collective-permute-done.10.came_b = bf16[128,512]{1,0:T(8,128)(2,1)S(1)} collective-permute-done((bf16[128,512]{1,0:T(8,128)(2,1)S(1)}, bf16[128,512]{1,0:T(8,128)(2,1)S(1)}, u32[]{:S(2)}, u32[]{:S(2)}) %collective-permute-start.10) | collective-permute-done | bytes 131104 | tf_op jit(solution)/shard_map/ppermute | solution.py:434
  38.6 0.1 add_terms.1.after
  38.6 1.4 %collective-permute-start.11 = (bf16[256,512]{1,0:T(8,128)(2,1)S(1)}, bf16[256,512]{1,0:T(8,128)(2,1)S(1)}, u32[]{:S(2)}, u32[]{:S(2)}) collective-permute-start(bf16[256,512]{1,0:T(8,128)(2,1)S(1)} %add_terms.1.after), channel_id=1, source_target_pairs={{0,12},{4,8},{8,4},{12,0},{1,13},{5,9},{9,5},{13,1},{2,14},{6,10},... | collective-permute-start | bytes 786440 | tf_op jit(solution)/shard_map/ppermute | solution.py:434
  40.0 6.9 %collective-permute-done.11 = bf16[256,512]{1,0:T(8,128)(2,1)S(1)} collective-permute-done((bf16[256,512]{1,0:T(8,128)(2,1)S(1)}, bf16[256,512]{1,0:T(8,128)(2,1)S(1)}, u32[]{:S(2)}, u32[]{:S(2)}) %collective-permute-start.11) | collective-permute-done | bytes 262176 | tf_op jit(solution)/shard_map/ppermute | solution.py:434
  47.0 0.1 add_convert_fusion.own_ref
  47.0 3.7 %collective-permute-start.12 = (bf16[256,512]{1,0:T(8,128)(2,1)S(1)}, bf16[256,512]{1,0:T(8,128)(2,1)S(1)}, u32[]{:S(2)}, u32[]{:S(2)}) collective-permute-start(bf16[256,512]{1,0:T(8,128)(2,1)S(1)} %add_convert_fusion.own_ref), channel_id=1, source_target_pairs={{0,4},{4,0},{8,12},{12,8},{1,5},{5,1},{9,13},{13,9},{2,6},{6,2},{1... | collective-permute-start | bytes 786440 | tf_op jit(solution)/shard_map/ppermute | solution.py:434
  50.8 2.1 %node_grads.1.node_out = bf16[128,512]{1,0:T(8,128)(2,1)} custom-call(s32[1,4]{1,0:T(1,128)} %boundary_hbm.3, bf16[256,512]{1,0:T(8,128)(2,1)S(1)} %add_terms.1.after, f32[512,512]{1,0:T(8,128)S(1)} %get-tuple-element.56.sums_ref, bf16[1536,512]{1,0:T(8,128)(2,1)S(1)} %get-tuple-element.44.refs_5_.win_ref, ...), custom_call_target="tpu_custom_call" | custom-call | flops 268435456 | bytes 2000000 | tf_op jit(solution)/shard_map/node_grads/pallas_call | solution.py:714
  52.9 2.2 %edge_grads.1 = (bf16[768,512]{1,0:T(8,128)(2,1)}, bf16[128,512]{1,0:T(8,128)(2,1)}) custom-call(s32[12]{0:T(128)} %dst_hbm.3, s32[1]{0:T(128)S(6)} %copy.15.count_ref, bf16[256,512]{1,0:T(8,128)(2,1)S(1)} %add_terms.1.after, bf16[768,512]{1,0:T(8,128)(2,1)S(1)} %get-tuple-element.67.gpre_ref, f32[512,512]{1,0:T(8,128)S(1)} %get-tuple-element.56.sums_ref, ...), custom_call_target="tpu_custom_call" | custom-call | flops 402653184 | bytes 3000000 | tf_op jit(solution)/shard_map/edge_grads/pallas_call | solution.py:686
  55.1 0.3 collective-permute-done.12.other_ref
  55.4 1.0 %widen.1 = (f32[384,512]{1,0:T(8,128)}, f32[128,512]{1,0:T(8,128)}) custom-call(bf16[128,512]{1,0:T(8,128)(2,1)} %node_grads.1.node_out, bf16[768,512]{1,0:T(8,128)(2,1)} %get-tuple-element.70.edge_grad, bf16[256,512]{1,0:T(8,128)(2,1)S(1)} %add_convert_fusion.own_ref, bf16[256,512]{1,0:T(8,128)(2,1)S(1)} %collective-permute-done.12.other_ref), custom_call_target="tpu_custom_call" | custom-call | bytes 1500000 | tf_op jit(solution)/shard_map/widen/pallas_call | solution.py:731
  (6 shorter events, 0.1 us)
Async XLA Ops:
  1.6 9.9 %collective-permute-start = (bf16[64,512]{1,0:T(8,128)(2,1)S(1)}, bf16[64,512]{1,0:T(8,128)(2,1)S(1)}, u32[]{:S(2)}, u32[]{:S(2)}) collective-permute-start(bf16[64,512]{1,0:T(8,128)(2,1)S(1)} %get-tuple-element.39), channel_id=1, source_target_pairs={{0,0},{4,8},{8,4},{12,12},{1,1},{5,9},{9,5},{13,13},{2,2},{6,10},{... | collective-permute-start | bytes 196616 | tf_op jit(solution)/shard_map/ppermute | solution.py:434
  2.2 9.6 %collective-permute-start.1 = (bf16[64,512]{1,0:T(8,128)(2,1)S(1)}, bf16[64,512]{1,0:T(8,128)(2,1)S(1)}, u32[]{:S(2)}, u32[]{:S(2)}) collective-permute-start(bf16[64,512]{1,0:T(8,128)(2,1)S(1)} %get-tuple-element.40), channel_id=1, source_target_pairs={{0,8},{4,12},{8,0},{12,4},{1,9},{5,13},{9,1},{13,5},{2,10},{6,14},... | collective-permute-start | bytes 196616 | tf_op jit(solution)/shard_map/ppermute | solution.py:434
  8.0 4.5 %collective-permute-start.2 = (bf16[64,512]{1,0:T(8,128)(2,1)S(1)}, bf16[64,512]{1,0:T(8,128)(2,1)S(1)}, u32[]{:S(2)}, u32[]{:S(2)}) collective-permute-start(bf16[64,512]{1,0:T(8,128)(2,1)S(1)} %get-tuple-element.41), channel_id=1, source_target_pairs={{0,4},{4,0},{8,12},{12,8},{1,5},{5,1},{9,13},{13,9},{2,6},{6,2},{1... | collective-permute-start | bytes 196616 | tf_op jit(solution)/shard_map/ppermute | solution.py:434
  18.3 2.0 %collective-permute-start.3 = (bf16[2,256,512]{2,1,0:T(8,128)(2,1)S(1)}, bf16[2,256,512]{2,1,0:T(8,128)(2,1)S(1)}, u32[]{:S(2)}, u32[]{:S(2)}) collective-permute-start(bf16[2,256,512]{2,1,0:T(8,128)(2,1)S(1)} %get-tuple-element.51), channel_id=1, source_target_pairs={{0,1},{1,0},{2,3},{3,2},{4,5},{5,4},{6,7},{7,6},{8,9},{9,8},{10,11... | collective-permute-start | bytes 1572872 | tf_op jit(solution)/shard_map/ppermute | solution.py:434
  18.3 3.5 %collective-permute-start.8 = (bf16[2,256,512]{2,1,0:T(8,128)(2,1)S(1)}, bf16[2,256,512]{2,1,0:T(8,128)(2,1)S(1)}, u32[]{:S(2)}, u32[]{:S(2)}) collective-permute-start(bf16[2,256,512]{2,1,0:T(8,128)(2,1)S(1)} %get-tuple-element.61), channel_id=1, source_target_pairs={{0,1},{1,0},{2,3},{3,2},{4,5},{5,4},{6,7},{7,6},{8,9},{9,8},{10,11... | collective-permute-start | bytes 1572872 | tf_op jit(solution)/shard_map/ppermute | solution.py:434
  20.3 9.5 %collective-permute-start.4 = (bf16[1,256,512]{2,1,0:T(8,128)(2,1)S(1)}, bf16[1,256,512]{2,1,0:T(8,128)(2,1)S(1)}, u32[]{:S(2)}, u32[]{:S(2)}) collective-permute-start(bf16[1,256,512]{2,1,0:T(8,128)(2,1)S(1)} %get-tuple-element.54), channel_id=1, source_target_pairs={{0,2},{1,3},{2,0},{3,1},{4,6},{5,7},{6,4},{7,5},{8,10},{9,11},{10,... | collective-permute-start | bytes 786440 | tf_op jit(solution)/shard_map/ppermute | solution.py:434
  22.0 11.5 %collective-permute-start.9 = (bf16[256,512]{1,0:T(8,128)(2,1)S(1)}, bf16[256,512]{1,0:T(8,128)(2,1)S(1)}, u32[]{:S(2)}, u32[]{:S(2)}) collective-permute-start(bf16[256,512]{1,0:T(8,128)(2,1)S(1)} %get-tuple-element.63), channel_id=1, source_target_pairs={{0,4},{4,0},{8,12},{12,8},{1,5},{5,1},{9,13},{13,9},{2,6},{6,2},{1... | collective-permute-start | bytes 786440 | tf_op jit(solution)/shard_map/ppermute | solution.py:434
  22.9 7.0 %collective-permute-start.5 = (bf16[64,512]{1,0:T(8,128)(2,1)S(1)}, bf16[64,512]{1,0:T(8,128)(2,1)S(1)}, u32[]{:S(2)}, u32[]{:S(2)}) collective-permute-start(bf16[64,512]{1,0:T(8,128)(2,1)S(1)} %get-tuple-element.57), channel_id=1, source_target_pairs={{0,8},{4,12},{8,0},{12,4},{1,9},{5,13},{9,1},{13,5},{2,10},{6,14},... | collective-permute-start | bytes 196616 | tf_op jit(solution)/shard_map/ppermute | solution.py:434
  25.5 4.4 %collective-permute-start.6 = (bf16[64,512]{1,0:T(8,128)(2,1)S(1)}, bf16[64,512]{1,0:T(8,128)(2,1)S(1)}, u32[]{:S(2)}, u32[]{:S(2)}) collective-permute-start(bf16[64,512]{1,0:T(8,128)(2,1)S(1)} %get-tuple-element.58), channel_id=1, source_target_pairs={{0,0},{4,8},{8,4},{12,12},{1,1},{5,9},{9,5},{13,13},{2,2},{6,10},{... | collective-permute-start | bytes 196616 | tf_op jit(solution)/shard_map/ppermute | solution.py:434
  29.9 8.6 %collective-permute-start.7 = (bf16[192,512]{1,0:T(8,128)(2,1)S(1)}, bf16[192,512]{1,0:T(8,128)(2,1)S(1)}, u32[]{:S(2)}, u32[]{:S(2)}) collective-permute-start(bf16[192,512]{1,0:T(8,128)(2,1)S(1)} %get-tuple-element.60), channel_id=1, source_target_pairs={{0,4},{4,0},{8,12},{12,8},{1,5},{5,1},{9,13},{13,9},{2,6},{6,2},{1... | collective-permute-start | bytes 589832 | tf_op jit(solution)/shard_map/ppermute | solution.py:434
  33.5 5.0 %collective-permute-start.10 = (bf16[128,512]{1,0:T(8,128)(2,1)S(1)}, bf16[128,512]{1,0:T(8,128)(2,1)S(1)}, u32[]{:S(2)}, u32[]{:S(2)}) collective-permute-start(bf16[128,512]{1,0:T(8,128)(2,1)S(1)} %get-tuple-element.66), channel_id=1, source_target_pairs={{0,2},{1,3},{2,0},{3,1},{4,6},{5,7},{6,4},{7,5},{8,10},{9,11},{10,... | collective-permute-start | bytes 393224 | tf_op jit(solution)/shard_map/ppermute | solution.py:434
  38.6 8.3 %collective-permute-start.11 = (bf16[256,512]{1,0:T(8,128)(2,1)S(1)}, bf16[256,512]{1,0:T(8,128)(2,1)S(1)}, u32[]{:S(2)}, u32[]{:S(2)}) collective-permute-start(bf16[256,512]{1,0:T(8,128)(2,1)S(1)} %add_terms.1.after), channel_id=1, source_target_pairs={{0,12},{4,8},{8,4},{12,0},{1,13},{5,9},{9,5},{13,1},{2,14},{6,10},... | collective-permute-start | bytes 786440 | tf_op jit(solution)/shard_map/ppermute | solution.py:434
  47.0 8.4 %collective-permute-start.12 = (bf16[256,512]{1,0:T(8,128)(2,1)S(1)}, bf16[256,512]{1,0:T(8,128)(2,1)S(1)}, u32[]{:S(2)}, u32[]{:S(2)}) collective-permute-start(bf16[256,512]{1,0:T(8,128)(2,1)S(1)} %add_convert_fusion.own_ref), channel_id=1, source_target_pairs={{0,4},{4,0},{8,12},{12,8},{1,5},{5,1},{9,13},{13,9},{2,6},{6,2},{1... | collective-permute-start | bytes 786440 | tf_op jit(solution)/shard_map/ppermute | solution.py:434
